TPU v7x, 256 devices: a whole 4x4x8 slice. The times are simulated.
256 devices in a mesh: row: 16 (over z, y_lo), col: 16 (over x, y_hi, core).
Axes of the slice: x: 4, y: 4 (y_hi: 2, y_lo: 2; y = y_hi * 2 + y_lo), z: 8, core: 2. Of those that a mesh axis runs over, the one named last changes fastest.
Arguments:
- matrix: float32 [4096, 8192], P('row', 'col'), may hold values from -30 to 30
- shifts: int32 [2, 8], replicated, may hold values from 0 to 255
Outputs:
- rotated: float32 [4096, 8192], P('row', 'col')
All inputs are finite; a program needn't handle non-finite values.
Results may differ from a plain program's by a relative error of at most 0.0003.
Values sent between devices are 32-bit elements; how exact they have to be, the bound alone decides.
No kernel may reach another device: no remote copies, remote signals or barrier semaphores. Data moves between devices by JAX's collectives and lax.ppermute only.
A program may use at most 64 MiB of HBM per device.

v0:
```python
import jax
import jax.numpy as jnp
from jax import lax
from jax.sharding import PartitionSpec as P

STEPS = 2


def passed_along(block, axis, distance):
    devices = range(lax.axis_size(axis))
    route = [((i - distance) % len(devices), i) for i in devices]
    return lax.ppermute(block, axis, route)


def turn_bottom(gram_blocks, rotation, advance):
    upper_rows = gram_blocks[0]
    lower_rows = jnp.roll(gram_blocks[1], -advance, axis=1)
    stacked = jnp.stack([upper_rows, lower_rows])
    left_cols = stacked[:, 0]
    right_cols = jnp.roll(stacked[:, 1], -advance, axis=2)
    gram_blocks = jnp.stack([left_cols, right_cols], axis=1)
    rotation = jnp.stack([rotation[:, 0], jnp.roll(rotation[:, 1], -advance, axis=1)], axis=1)
    return (gram_blocks, rotation)


def turn_pairs(gram_blocks, rotation, cosine, sine_part):
    cos_rows = cosine[:, None]
    sin_rows = sine_part[:, None]
    top_left = cos_rows * gram_blocks[0, 0] + sin_rows * gram_blocks[1, 0]
    top_right = cos_rows * gram_blocks[0, 1] + sin_rows * gram_blocks[1, 1]
    low_left = cos_rows * gram_blocks[1, 0] - sin_rows * gram_blocks[0, 0]
    low_right = cos_rows * gram_blocks[1, 1] - sin_rows * gram_blocks[0, 1]
    cos_cols = cosine[None, :]
    sin_cols = sine_part[None, :]
    new_tl = top_left * cos_cols + top_right * sin_cols
    new_tr = top_right * cos_cols - top_left * sin_cols
    new_ll = low_left * cos_cols + low_right * sin_cols
    new_lr = low_right * cos_cols - low_left * sin_cols
    gram_blocks = jnp.stack([jnp.stack([new_tl, new_tr]), jnp.stack([new_ll, new_lr])])
    first_half = rotation[:, 0] * cos_cols + rotation[:, 1] * sin_cols
    second_half = rotation[:, 1] * cos_cols - rotation[:, 0] * sin_cols
    rotation = jnp.stack([first_half, second_half], axis=1)
    return (gram_blocks, rotation)


def jacobi_pairs(gram_matrix, shift_row):
    block_width = gram_matrix.shape[0] // 2
    gram_blocks = gram_matrix.reshape(2, block_width, 2, block_width).transpose(0, 2, 1, 3)
    rotation = jnp.eye(2 * block_width, dtype=gram_matrix.dtype).reshape(
        2 * block_width, 2, block_width
    )
    offset = jnp.zeros((), jnp.int32)
    for inner_index in range(shift_row.shape[0]):
        target = shift_row[inner_index]
        gram_blocks, rotation = turn_bottom(gram_blocks, rotation, target - offset)
        offset = target
        upper_diag = jnp.diagonal(gram_blocks[0, 0])
        lower_diag = jnp.diagonal(gram_blocks[1, 1])
        coupling = jnp.diagonal(gram_blocks[0, 1])
        angles = 0.5 * jnp.arctan2(2.0 * coupling, upper_diag - lower_diag)
        gram_blocks, rotation = turn_pairs(gram_blocks, rotation, jnp.cos(angles), jnp.sin(angles))
    gram_blocks, rotation = turn_bottom(gram_blocks, rotation, -offset)
    return (gram_blocks, rotation.reshape(2 * block_width, 2 * block_width))


def local_gram(left_part, right_part):
    return lax.dot_general(
        left_part,
        right_part,
        (((0,), (0,)), ((), ())),
        precision=lax.Precision.HIGHEST,
        preferred_element_type=jnp.float32,
    )


def whole_gram(column_pair):
    return lax.psum(local_gram(column_pair, column_pair), "row")


def apply_rotation(column_pair, rotation):
    return jnp.dot(
        column_pair, rotation, precision=lax.Precision.HIGHEST, preferred_element_type=jnp.float32
    )


def trade_blocks(upper_rows, lower_rows):
    upper_rows = passed_along(upper_rows, "col", 1)
    lower_rows = passed_along(lower_rows, "col", -1)
    return (upper_rows, lower_rows)


def per_device(matrix, shifts):
    block_width = matrix.shape[1] // 2
    column_pair = matrix
    for section_index in range(STEPS):
        gram_matrix = whole_gram(column_pair)
        final_blocks, rotation = jacobi_pairs(gram_matrix, shifts[section_index])
        column_pair = apply_rotation(column_pair, rotation)
        upper_rows, lower_rows = trade_blocks(
            column_pair[:, :block_width], column_pair[:, block_width:]
        )
        column_pair = jnp.concatenate([upper_rows, lower_rows], axis=1)
    return column_pair


def solution(mesh):
    in_specs = (P("row", "col"), P())
    out_specs = P("row", "col")
    return jax.shard_map(
        per_device, mesh=mesh, in_specs=in_specs, out_specs=out_specs, check_vma=False
    )
```

profile of v0, /device:TPU:8, one launch (start us, length us, event | category | flops | bytes accessed | tf_op | source)
XLA Modules:
  0.0 510.6 jit_solution(11311594564352847269)
XLA Ops:
  24.2 128.5 %all-reduce.3.cloned.1.call-done = f32[2,2,256,256]{3,2,1,0:T(8,128)} async-done(((f32[2,2,256,256]{3,2,1,0:T(8,128)}), f32[2,2,256,256]{3,2,1,0:T(8,128)}) %all-reduce.3.cloned.1.call-update) | async-done | bytes 1048592 | tf_op jit(solution)/shard_map/psum | solution.py:77
  152.7 1.3 fusion.186
  156.3 2.5 gather_fusion.1
  158.9 2.3 gather_fusion.2
  161.2 2.3 gather_fusion
  167.0 2.3 gather_fusion.4
  169.8 2.3 gather_fusion.5
  172.2 2.3 gather_fusion.3
  174.6 1.2 multiply_subtract_fusion.52
  177.9 2.3 gather_fusion.7
  180.7 2.3 gather_fusion.8
  183.1 2.3 gather_fusion.6
  188.9 2.3 gather_fusion.10
  191.7 2.3 gather_fusion.11
  194.0 2.3 gather_fusion.9
  196.5 1.2 multiply_subtract_fusion.46
  199.8 2.3 gather_fusion.13
  202.6 2.3 gather_fusion.14
  205.0 2.6 gather_fusion.12
  211.0 2.3 gather_fusion.16
  213.7 2.3 gather_fusion.17
  216.1 2.3 gather_fusion.15
  218.6 1.2 multiply_subtract_fusion.40
  221.9 2.3 gather_fusion.19
  224.7 2.3 gather_fusion.20
  227.0 2.3 gather_fusion.18
  231.0 2.3 gather_fusion.22
  233.7 2.3 gather_fusion.23
  236.1 2.7 gather_fusion.21
  243.7 5.3 %collective-permute-start.1 = (f32[256,256]{0,1:T(8,128)S(1)}, f32[256,256]{0,1:T(8,128)S(1)}, u32[]{:S(2)}, u32[]{:S(2)}) collective-permute-start(f32[256,256]{0,1:T(8,128)S(1)} %get-tuple-element.126), channel_id=1, source_target_pairs={{1,0},{2,1},{3,2},{4,3},{5,4},{6,5},{7,6},{8,7},{9,8},{10,9},{11,1... | collective-permute-start | bytes 786440 | tf_op jit(solution)/shard_map/ppermute | solution.py:12
  249.1 4.1 collective-permute-done
  253.3 2.0 fusion.191
  255.3 1.9 reshape.6122
  270.2 127.9 %all-reduce.5.cloned.1.call-done = f32[2,2,256,256]{3,2,1,0:T(8,128)} async-done(((f32[2,2,256,256]{3,2,1,0:T(8,128)}), f32[2,2,256,256]{3,2,1,0:T(8,128)}) %all-reduce.5.cloned.1.call-update) | async-done | bytes 1048592 | tf_op jit(solution)/shard_map/psum | solution.py:77
  399.2 2.5 gather_fusion.25
  403.2 2.3 gather_fusion.26
  405.5 2.3 gather_fusion.24
  411.3 2.3 gather_fusion.28
  414.1 2.3 gather_fusion.29
  416.5 2.3 gather_fusion.27
  418.9 1.2 multiply_subtract_fusion.31
  422.2 2.3 gather_fusion.31
  425.0 2.3 gather_fusion.32
  427.4 2.3 gather_fusion.30
  433.2 2.3 gather_fusion.34
  436.0 2.3 gather_fusion.35
  438.3 2.3 gather_fusion.33
  444.1 2.3 gather_fusion.37
  446.9 2.6 gather_fusion.38
  449.5 2.3 gather_fusion.36
  455.2 2.3 gather_fusion.40
  458.0 2.3 gather_fusion.41
  460.4 2.3 gather_fusion.39
  467.2 2.3 gather_fusion.43
  471.7 2.3 gather_fusion.44
  474.0 2.3 gather_fusion.42
  476.5 2.1 multiply_subtract_fusion.16
  478.7 2.3 gather_fusion.46
  481.0 1.3 fusion.7
  482.7 2.3 gather_fusion.47
  485.1 2.6 gather_fusion.45
  491.1 1.9 fusion.192
  493.6 3.4 collective-permute-done.3
  497.0 5.6 %collective-permute-done.2 = f32[256,256]{1,0:T(8,128)S(1)} collective-permute-done((f32[256,256]{1,0:T(8,128)S(1)}, f32[256,256]{1,0:T(8,128)S(1)}, u32[]{:S(2)}, u32[]{:S(2)}) %collective-permute-start.2) | collective-permute-done | bytes 262176 | tf_op jit(solution)/shard_map/ppermute | solution.py:12
  (241 shorter events, 66.8 us)
Async XLA Ops:
  6.5 1.0 copy-start
  6.5 146.2 %all-reduce.3.cloned.1.call-start = ((), (), s32[]{:S(2)}) async-start(), calls=%async_computation | async-start | bytes 2097152 | tf_op jit(solution)/shard_map/psum | solution.py:77
  10.4 0.7 copy-start.32
  10.4 387.7 %all-reduce.5.cloned.1.call-start = ((), (), s32[]{:S(2)}) async-start(), calls=%async_computation.1 | async-start | bytes 2097152 | tf_op jit(solution)/shard_map/psum | solution.py:77
  154.2 0.8 copy-start.4
  161.2 2.4 copy-start.5
  166.2 0.8 copy-start.9
  172.2 2.4 copy-start.10
  177.1 0.8 copy-start.11
  183.1 2.4 copy-start.12
  188.1 0.8 copy-start.13
  194.0 2.4 copy-start.14
  199.0 0.8 copy-start.15
  205.0 2.7 copy-start.16
  210.1 0.8 copy-start.17
  216.1 2.4 copy-start.18
  221.1 0.8 copy-start.19
  227.0 2.4 copy-start.20
  243.6 9.6 %collective-permute-start = (f32[256,256]{0,1:T(8,128)S(1)}, f32[256,256]{0,1:T(8,128)S(1)}, u32[]{:S(2)}, u32[]{:S(2)}) collective-permute-start(f32[256,256]{0,1:T(8,128)S(1)} %get-tuple-element.127), channel_id=1, source_target_pairs={{15,0},{0,1},{1,2},{2,3},{3,4},{4,5},{5,6},{6,7},{7,8},{8,9},{9,10... | collective-permute-start | bytes 786440 | tf_op jit(solution)/shard_map/ppermute | solution.py:12
  243.7 9.5 %collective-permute-start.1 = (f32[256,256]{0,1:T(8,128)S(1)}, f32[256,256]{0,1:T(8,128)S(1)}, u32[]{:S(2)}, u32[]{:S(2)}) collective-permute-start(f32[256,256]{0,1:T(8,128)S(1)} %get-tuple-element.126), channel_id=1, source_target_pairs={{1,0},{2,1},{3,2},{4,3},{5,4},{6,5},{7,6},{8,7},{9,8},{10,9},{11,1... | collective-permute-start | bytes 786440 | tf_op jit(solution)/shard_map/ppermute | solution.py:12
  398.1 3.6 copy-start.8
  402.0 0.8 copy-start.6
  405.5 2.4 copy-start.7
  410.5 0.8 copy-start.21
  416.4 2.4 copy-start.22
  421.4 0.8 copy-start.23
  427.4 2.4 copy-start.24
  432.3 0.8 copy-start.25
  438.3 2.4 copy-start.26
  443.3 0.8 copy-start.27
  449.5 2.4 copy-start.28
  454.4 0.8 copy-start.29
  460.4 2.4 copy-start.30
  466.3 0.8 copy-start.31
  470.9 0.8 copy-start.2
  474.0 2.4 copy-start.3
  493.0 4.0 collective-permute-start.3
  493.1 10.4 %copy-start.1 = (f32[256,512]{1,0:T(8,128)S(1)}, f32[256,512]{1,0:T(8,128)}, u32[]{:S(2)}) copy-start(f32[256,512]{1,0:T(8,128)} %param.8) | copy-start | bytes 1572868
  493.2 9.5 %collective-permute-start.2 = (f32[256,256]{1,0:T(8,128)S(1)}, f32[256,256]{1,0:T(8,128)S(1)}, u32[]{:S(2)}, u32[]{:S(2)}) collective-permute-start(f32[256,256]{1,0:T(8,128)S(1)} %get-tuple-element.96), channel_id=1, source_target_pairs={{15,0},{0,1},{1,2},{2,3},{3,4},{4,5},{5,6},{6,7},{7,8},{8,9},{9,10... | collective-permute-start | bytes 786440 | tf_op jit(solution)/shard_map/ppermute | solution.py:12
Sparse Core Ops, SparseCore 0:
  10.5 142.1 all-reduce.2
  258.4 139.6 all-reduce.4
where the time goes:
time: 516 us; the launch traced here: 511 us
  waiting for transfers between devices  270 us (52%)
  local copies, waits for them, and re-layouts  137 us (27%)
  other arithmetic  52.3 us (10%)
  between operations  39.7 us (8%)
  starting transfers between devices  6.04 us (1%)
  matrix products  5.95 us (1%)
    psum x2, waiting for transfers between devices, whole_gram(): return lax.psum(local_gram(column_pair, column_pair), 'row')  256 us
    gather x16, local copies, waits for them, and re-layouts, jacobi_pairs(): coupling = jnp.diagonal(gram_blocks[0, 1])  38.4 us
    gather x16, local copies, waits for them, and re-layouts, jacobi_pairs(): upper_diag = jnp.diagonal(gram_blocks[0, 0])  37.8 us
    gather x16, local copies, waits for them, and re-layouts, jacobi_pairs(): lower_diag = jnp.diagonal(gram_blocks[1, 1])  37.7 us
    sub x14, other arithmetic, turn_pairs(): new_lr = low_right * cos_cols - low_left * sin_cols  18.3 us
    another operation x28, other arithmetic, turn_bottom(): stacked = jnp.stack([upper_rows, lower_rows])  16.6 us
    unnamed x67, local copies, waits for them, and re-layouts  13.5 us
    ppermute x4, waiting for transfers between devices, passed_along(): return lax.ppermute(block, axis, route)  13.2 us
  transfers between devices with their start and end apart: 6, of which 5 were waited for; matrix products, arithmetic and copies ran while one was open for 0% of the time, Pallas kernels for 0%

commit v1 on v0

v1 whole, which is shorter than its diff:
```python
import jax
import jax.numpy as jnp
from jax import lax
from jax.experimental import pallas as pl
from jax.experimental.pallas import tpu as pltpu
from jax.sharding import PartitionSpec as P

STEPS = 2


def passed_along(block, axis, distance):
    devices = range(lax.axis_size(axis))
    route = [((i - distance) % len(devices), i) for i in devices]
    return lax.ppermute(block, axis, route)


def half_angle(x, y):
    scale = jnp.maximum(jnp.abs(x), jnp.abs(y))
    flat = scale == 0.0
    inverse = 1.0 / jnp.where(flat, 1.0, scale)
    xs = x * inverse
    ys = y * inverse
    norm = lax.rsqrt(jnp.where(flat, 1.0, xs * xs + ys * ys))
    major = jnp.sqrt(0.5 + 0.5 * jnp.abs(xs * norm))
    minor = 0.5 * jnp.abs(ys * norm) / major
    negative = (y < 0.0) | ((y == 0.0) & (1.0 / y < 0.0))
    ahead = x >= 0.0
    cosine = jnp.where(flat, 1.0, jnp.where(ahead, major, minor))
    sine = jnp.where(ahead, minor, major)
    sine = jnp.where(negative, -sine, sine)
    return cosine, jnp.where(flat, 0.0, sine)


def inner_kernel(shift_ref, gram_ref, pair_ref, out_ref, tl, tr, lr):
    w = tl.shape[0]
    tl[...] = gram_ref[:w, :w]
    tr[...] = gram_ref[:w, w:]
    lr[...] = gram_ref[w:, w:]
    out_ref[...] = pair_ref[...]
    rows = lax.broadcasted_iota(jnp.int32, (w, w), 0)
    cols = lax.broadcasted_iota(jnp.int32, (w, w), 1)
    eye = rows == cols

    def diagonal(block):
        return jnp.sum(jnp.where(eye, block, 0.0), axis=0, keepdims=True)

    def as_rows(vector):
        half = jnp.transpose(jnp.broadcast_to(vector, (w // 2, w)))
        return jnp.concatenate([half, half], axis=1)

    def one_round(r, offset):
        target = shift_ref[r]
        back = lax.rem(offset - target + 2 * w, w)
        top_left = tl[...]
        top_right = pltpu.roll(tr[...], back, 1)
        low_right = pltpu.roll(pltpu.roll(lr[...], back, 1), back, 0)
        c, s = half_angle(
            diagonal(top_left) - diagonal(low_right), 2.0 * diagonal(top_right)
        )
        c_rows = as_rows(c)
        s_rows = as_rows(s)
        low_left = jnp.transpose(top_right)
        half_tl = c_rows * top_left + s_rows * low_left
        half_tr = c_rows * top_right + s_rows * low_right
        half_ll = c_rows * low_left - s_rows * top_left
        half_lr = c_rows * low_right - s_rows * top_right
        tl[...] = half_tl * c + half_tr * s
        tr[...] = half_tr * c - half_tl * s
        lr[...] = half_lr * c - half_ll * s
        upper = out_ref[:, :w]
        lower = pltpu.roll(out_ref[:, w:], back, 1)
        out_ref[:, :w] = upper * c + lower * s
        out_ref[:, w:] = lower * c - upper * s
        return target

    last = lax.fori_loop(0, shift_ref.shape[0], one_round, jnp.int32(0))
    out_ref[:, w:] = pltpu.roll(out_ref[:, w:], last, 1)


def rotated_pair(shift_row, gram_matrix, column_pair):
    w = column_pair.shape[1] // 2
    return pl.pallas_call(
        inner_kernel,
        out_shape=jax.ShapeDtypeStruct(column_pair.shape, jnp.float32),
        in_specs=[
            pl.BlockSpec(memory_space=pltpu.SMEM),
            pl.BlockSpec(memory_space=pltpu.VMEM),
            pl.BlockSpec(memory_space=pltpu.VMEM),
        ],
        out_specs=pl.BlockSpec(memory_space=pltpu.VMEM),
        scratch_shapes=[pltpu.VMEM((w, w), jnp.float32)] * 3,
        compiler_params=pltpu.CompilerParams(vmem_limit_bytes=32 * 1024 * 1024),
    )(shift_row, gram_matrix, column_pair)


def local_gram(left_part, right_part):
    return lax.dot_general(
        left_part,
        right_part,
        (((0,), (0,)), ((), ())),
        precision=lax.Precision.HIGHEST,
        preferred_element_type=jnp.float32,
    )


def whole_gram(column_pair):
    return lax.psum(local_gram(column_pair, column_pair), "row")


def trade_blocks(upper_rows, lower_rows):
    upper_rows = passed_along(upper_rows, "col", 1)
    lower_rows = passed_along(lower_rows, "col", -1)
    return (upper_rows, lower_rows)


def per_device(matrix, shifts):
    block_width = matrix.shape[1] // 2
    column_pair = matrix
    for section_index in range(STEPS):
        gram_matrix = whole_gram(column_pair)
        column_pair = rotated_pair(shifts[section_index], gram_matrix, column_pair)
        upper_rows, lower_rows = trade_blocks(
            column_pair[:, :block_width], column_pair[:, block_width:]
        )
        column_pair = jnp.concatenate([upper_rows, lower_rows], axis=1)
    return column_pair


def solution(mesh):
    in_specs = (P("row", "col"), P())
    out_specs = P("row", "col")
    return jax.shard_map(
        per_device, mesh=mesh, in_specs=in_specs, out_specs=out_specs, check_vma=False
    )
```

time: 516 us -> 341 us (0.66)
  local copies, waits for them, and re-layouts: 137 us -> 3.17 us
  other arithmetic: 52.3 us -> 0.85 us
  between operations: 39.7 us -> 13.5 us
  waiting for transfers between devices: 270 us -> 290 us
  Pallas kernels: 0 us -> 13.7 us
    gather x48 -> x0, local copies, waits for them, and re-layouts: 114 us -> none  [the longest x16 38.4 us: jacobi_pairs(): coupling = jnp.diagonal(gram_blocks[0, 1])]
    psum x2, waiting for transfers between devices: 256 us -> 282 us  [whole_gram(): return lax.psum(local_gram(column_pair, column_pair), 'row')]
    sub x30 -> x0, other arithmetic: 24.1 us -> none  [the longest x14 18.3 us: turn_pairs(): new_lr = low_right * cos_cols - low_left * sin_cols]
    another operation x47 -> x0, other arithmetic: 18.9 us -> none  [the longest x28 16.6 us: turn_bottom(): stacked = jnp.stack([upper_rows, lower_rows])]
    pallas_call x0 -> x2, Pallas kernels: none -> 13.7 us  [rotated_pair(): pl.pallas_call(inner_kernel, out_shape=jax.ShapeDtypeStruct(column_pair.s...]
    unnamed x67 -> x9, local copies, waits for them, and re-layouts: 13.5 us -> 3.07 us
    concatenate x17 -> x0, other arithmetic: 5.59 us -> none  [the longest x16 5.58 us: turn_bottom(): right_cols = jnp.roll(stacked[:, 1], -advance, axis=2)]
  transfers between devices with their start and end apart: 6 -> 6, of which waited for: 5 -> 4; matrix products, arithmetic and copies ran while one was open for 0% -> 0% of each run, Pallas kernels for 0% -> 0%
where the time goes in v1:
time: 341 us; the launch traced here: 337 us
  waiting for transfers between devices  290 us (85%)
  Pallas kernels  13.7 us (4%)
  between operations  13.5 us (4%)
  starting transfers between devices  10.9 us (3%)
  matrix products  5.27 us (2%)
    psum x2, waiting for transfers between devices, whole_gram(): return lax.psum(local_gram(column_pair, column_pair), 'row')  282 us
    pallas_call x2, Pallas kernels, rotated_pair(): pl.pallas_call(inner_kernel, out_shape=jax.ShapeDtypeStruct(column_pair.s...  13.7 us
    ppermute x4, starting transfers between devices, passed_along(): return lax.ppermute(block, axis, route)  10.9 us
    ppermute x4, waiting for transfers between devices, passed_along(): return lax.ppermute(block, axis, route)  8.3 us
  transfers between devices with their start and end apart: 6, of which 4 were waited for; matrix products, arithmetic and copies ran while one was open for 0% of the time, Pallas kernels for 0%

profile of v1, /device:TPU:8, one launch (start us, length us, event | category | flops | bytes accessed | tf_op | source)
XLA Modules:
  0.0 337.4 jit_solution(10553458687114654359)
XLA Ops:
  6.5 0.0 all-reduce.3.cloned.1.call-start
  6.5 3.2 fusion.2
  9.8 0.0 copy-start.3
  9.8 0.0 copy-start
  9.8 0.0 all-reduce.3.cloned.1.call-update
  9.8 0.0 all-reduce.5.cloned.1.call-start
  9.8 0.6 copy-done.3
  10.4 141.9 %all-reduce.3.cloned.1.call-done.gram_ref = f32[512,512]{1,0:T(8,128)} async-done(((f32[512,512]{1,0:T(8,128)}), f32[512,512]{1,0:T(8,128)}) %all-reduce.3.cloned.1.call-update) | async-done | bytes 1048592 | tf_op jit(solution)/shard_map/psum | solution.py:107
  152.3 0.0 copy-done
  152.3 0.0 copy-start.1
  152.3 1.2 copy-done.1
  153.5 6.9 %shard_map.28 = f32[256,512]{1,0:T(8,128)S(1)} custom-call(s32[8]{0:T(128)S(1)} %get-tuple-element.9.shift_ref, f32[512,512]{1,0:T(8,128)S(1)} %copy-done.1, f32[256,512]{1,0:T(8,128)S(1)} %copy-done), custom_call_target="tpu_custom_call" | custom-call | tf_op jit(solution)/shard_map/pallas_call | solution.py:82
  160.5 0.1 collective-permute-start
  160.6 5.3 %collective-permute-start.1 = (f32[256,256]{1,0:T(8,128)S(1)}, f32[256,256]{1,0:T(8,128)S(1)}, u32[]{:S(2)}, u32[]{:S(2)}) collective-permute-start(f32[256,256]{1,0:T(8,128)S(1)} %get-tuple-element.7), channel_id=1, source_target_pairs={{1,0},{2,1},{3,2},{4,3},{5,4},{6,5},{7,6},{8,7},{9,8},{10,9},{11,1... | collective-permute-start | bytes 786440 | tf_op jit(solution)/shard_map/ppermute | solution.py:14
  165.9 4.1 %collective-permute-done = f32[256,256]{1,0:T(8,128)S(1)} collective-permute-done((f32[256,256]{1,0:T(8,128)S(1)}, f32[256,256]{1,0:T(8,128)S(1)}, u32[]{:S(2)}, u32[]{:S(2)}) %collective-permute-start) | collective-permute-done | bytes 262176 | tf_op jit(solution)/shard_map/ppermute | solution.py:14
  170.1 0.0 collective-permute-done.1
  170.1 2.0 fusion.3
  172.2 0.0 all-reduce.5.cloned.1.call-update
  172.2 139.8 %all-reduce.5.cloned.1.call-done.gram_ref = f32[512,512]{1,0:T(8,128)} async-done(((f32[512,512]{1,0:T(8,128)}), f32[512,512]{1,0:T(8,128)}) %all-reduce.5.cloned.1.call-update) | async-done | bytes 1048592 | tf_op jit(solution)/shard_map/psum | solution.py:107
  312.0 0.0 copy-start.2
  312.0 1.2 copy-done.2
  313.2 6.9 %shard_map.29 = f32[256,512]{1,0:T(8,128)S(1)} custom-call(s32[8]{0:T(128)S(1)} %get-tuple-element.10.shift_ref, f32[512,512]{1,0:T(8,128)S(1)} %copy-done.2, f32[256,512]{1,0:T(8,128)S(1)} %constant_dynamic-update-slice_fusion.pair_ref), custom_call_target="tpu_custom_call" | custom-call | tf_op jit(solution)/shard_map/pallas_call | solution.py:82
  320.1 0.1 collective-permute-start.2
  320.2 5.3 %collective-permute-start.3 = (f32[256,256]{1,0:T(8,128)S(1)}, f32[256,256]{1,0:T(8,128)S(1)}, u32[]{:S(2)}, u32[]{:S(2)}) collective-permute-start(f32[256,256]{1,0:T(8,128)S(1)} %get-tuple-element.6), channel_id=1, source_target_pairs={{1,0},{2,1},{3,2},{4,3},{5,4},{6,5},{7,6},{8,7},{9,8},{10,9},{11,1... | collective-permute-start | bytes 786440 | tf_op jit(solution)/shard_map/ppermute | solution.py:14
  325.6 4.1 %collective-permute-done.2 = f32[256,256]{1,0:T(8,128)S(1)} collective-permute-done((f32[256,256]{1,0:T(8,128)S(1)}, f32[256,256]{1,0:T(8,128)S(1)}, u32[]{:S(2)}, u32[]{:S(2)}) %collective-permute-start.2) | collective-permute-done | bytes 262176 | tf_op jit(solution)/shard_map/ppermute | solution.py:14
  329.7 0.0 collective-permute-done.3
  329.7 0.9 pad_maximum_fusion
  (5 shorter events, 0.1 us)
Async XLA Ops:
  6.5 145.8 %all-reduce.3.cloned.1.call-start = ((), (), s32[]{:S(2)}) async-start(), calls=%async_computation | async-start | bytes 2097152 | tf_op jit(solution)/shard_map/psum | solution.py:107
  9.8 0.7 copy-start.3
  9.8 142.5 %copy-start = (f32[256,512]{1,0:T(8,128)S(1)}, f32[256,512]{1,0:T(8,128)}, u32[]{:S(2)}) copy-start(f32[256,512]{1,0:T(8,128)} %pair_ref.1) | copy-start | bytes 1572868
  9.8 302.2 %all-reduce.5.cloned.1.call-start = ((), (), s32[]{:S(2)}) async-start(), calls=%async_computation.1 | async-start | bytes 2097152 | tf_op jit(solution)/shard_map/psum | solution.py:107
  152.3 1.2 copy-start.1
  160.5 9.6 %collective-permute-start = (f32[256,256]{1,0:T(8,128)S(1)}, f32[256,256]{1,0:T(8,128)S(1)}, u32[]{:S(2)}, u32[]{:S(2)}) collective-permute-start(f32[256,256]{1,0:T(8,128)S(1)} %get-tuple-element.8), channel_id=1, source_target_pairs={{15,0},{0,1},{1,2},{2,3},{3,4},{4,5},{5,6},{6,7},{7,8},{8,9},{9,10... | collective-permute-start | bytes 786440 | tf_op jit(solution)/shard_map/ppermute | solution.py:14
  160.6 9.5 %collective-permute-start.1 = (f32[256,256]{1,0:T(8,128)S(1)}, f32[256,256]{1,0:T(8,128)S(1)}, u32[]{:S(2)}, u32[]{:S(2)}) collective-permute-start(f32[256,256]{1,0:T(8,128)S(1)} %get-tuple-element.7), channel_id=1, source_target_pairs={{1,0},{2,1},{3,2},{4,3},{5,4},{6,5},{7,6},{8,7},{9,8},{10,9},{11,1... | collective-permute-start | bytes 786440 | tf_op jit(solution)/shard_map/ppermute | solution.py:14
  312.0 1.2 copy-start.2
  320.1 9.6 %collective-permute-start.2 = (f32[256,256]{1,0:T(8,128)S(1)}, f32[256,256]{1,0:T(8,128)S(1)}, u32[]{:S(2)}, u32[]{:S(2)}) collective-permute-start(f32[256,256]{1,0:T(8,128)S(1)} %get-tuple-element.5), channel_id=1, source_target_pairs={{15,0},{0,1},{1,2},{2,3},{3,4},{4,5},{5,6},{6,7},{7,8},{8,9},{9,10... | collective-permute-start | bytes 786440 | tf_op jit(solution)/shard_map/ppermute | solution.py:14
  320.2 9.5 %collective-permute-start.3 = (f32[256,256]{1,0:T(8,128)S(1)}, f32[256,256]{1,0:T(8,128)S(1)}, u32[]{:S(2)}, u32[]{:S(2)}) collective-permute-start(f32[256,256]{1,0:T(8,128)S(1)} %get-tuple-element.6), channel_id=1, source_target_pairs={{1,0},{2,1},{3,2},{4,3},{5,4},{6,5},{7,6},{8,7},{9,8},{10,9},{11,1... | collective-permute-start | bytes 786440 | tf_op jit(solution)/shard_map/ppermute | solution.py:14
Sparse Core Ops, SparseCore 0:
  10.0 142.2 all-reduce.2
  172.3 139.6 all-reduce.4

commit v2 on v1

v2 whole, which is shorter than its diff:
```python
import jax
import jax.numpy as jnp
from jax import lax
from jax.experimental import pallas as pl
from jax.experimental.pallas import tpu as pltpu
from jax.sharding import PartitionSpec as P

LANES = 128
VMEM = pl.BlockSpec(memory_space=pltpu.VMEM)
SMEM = pl.BlockSpec(memory_space=pltpu.SMEM)


def kernel_call(kernel, outs, ins, scratch=()):
    return pl.pallas_call(
        kernel,
        out_shape=[jax.ShapeDtypeStruct(shape, jnp.float32) for shape in outs],
        in_specs=ins,
        out_specs=[VMEM] * len(outs),
        scratch_shapes=[pltpu.VMEM(shape, jnp.float32) for shape in scratch],
        compiler_params=pltpu.CompilerParams(vmem_limit_bytes=32 * 1024 * 1024),
    )


def half_angle(x, y):
    scale = jnp.maximum(jnp.abs(x), jnp.abs(y))
    flat = scale == 0.0
    inverse = 1.0 / jnp.where(flat, 1.0, scale)
    xs = x * inverse
    ys = y * inverse
    norm = lax.rsqrt(jnp.where(flat, 1.0, xs * xs + ys * ys))
    major = jnp.sqrt(0.5 + 0.5 * jnp.abs(xs * norm))
    minor = 0.5 * jnp.abs(ys * norm) / major
    negative = (y < 0.0) | ((y == 0.0) & (1.0 / y < 0.0))
    ahead = x >= 0.0
    cosine = jnp.where(flat, 1.0, jnp.where(ahead, major, minor))
    sine = jnp.where(ahead, minor, major)
    sine = jnp.where(negative, -sine, sine)
    return cosine, jnp.where(flat, 0.0, sine)


def grid_of(w):
    rows = lax.broadcasted_iota(jnp.int32, (w, w), 0)
    cols = lax.broadcasted_iota(jnp.int32, (w, w), 1)
    return rows, cols


def diagonal(block):
    rows, cols = grid_of(block.shape[0])
    return jnp.sum(jnp.where(rows == cols, block, 0.0), axis=0, keepdims=True)


def inner_rounds(shift_ref, tl, tr, lr, upper_ref, lower_ref):
    w = tl.shape[0]

    def as_rows(vector):
        half = jnp.transpose(jnp.broadcast_to(vector, (LANES, w)))
        return jnp.concatenate([half] * (w // LANES), axis=1)

    def one_round(r, offset):
        target = shift_ref[r]
        back = lax.rem(offset - target + 2 * w, w)
        top_left = tl[...]
        top_right = pltpu.roll(tr[...], back, 1)
        low_right = pltpu.roll(pltpu.roll(lr[...], back, 1), back, 0)
        c, s = half_angle(
            diagonal(top_left) - diagonal(low_right), 2.0 * diagonal(top_right)
        )
        c_rows = as_rows(c)
        s_rows = as_rows(s)
        low_left = jnp.transpose(top_right)
        half_tl = c_rows * top_left + s_rows * low_left
        half_tr = c_rows * top_right + s_rows * low_right
        half_ll = c_rows * low_left - s_rows * top_left
        half_lr = c_rows * low_right - s_rows * top_right
        tl[...] = half_tl * c + half_tr * s
        tr[...] = half_tr * c - half_tl * s
        lr[...] = half_lr * c - half_ll * s
        upper = upper_ref[...]
        lower = pltpu.roll(lower_ref[...], back, 1)
        upper_ref[...] = upper * c + lower * s
        lower_ref[...] = lower * c - upper * s
        return target

    last = lax.fori_loop(0, shift_ref.shape[0], one_round, jnp.int32(0))
    lower_ref[...] = pltpu.roll(lower_ref[...], last, 1)
    lr[...] = pltpu.roll(pltpu.roll(lr[...], last, 1), last, 0)


def full_dot(left, right):
    return lax.dot_general(
        left,
        right,
        (((0,), (0,)), ((), ())),
        precision=lax.Precision.HIGHEST,
        preferred_element_type=jnp.float32,
    )


def write_pieces(out_ref, block, start):
    pieces = out_ref.shape[0]
    share = block.shape[0] // pieces
    for p in range(pieces):
        for t in range(block.shape[1] // LANES):
            out_ref[p, start + t * share : start + (t + 1) * share, :] = block[
                p * share : (p + 1) * share, t * LANES : (t + 1) * LANES
            ]


def read_pieces(in_ref, out_ref, start):
    pieces = in_ref.shape[0]
    share = out_ref.shape[0] // pieces
    for p in range(pieces):
        for t in range(out_ref.shape[1] // LANES):
            out_ref[p * share : (p + 1) * share, t * LANES : (t + 1) * LANES] = in_ref[
                p, start + t * share : start + (t + 1) * share, :
            ]


def gram_kernel(pair_ref, out_ref):
    w = pair_ref.shape[1] // 2
    rows, cols = grid_of(w)
    upper = pair_ref[:, :w]
    lower = pair_ref[:, w:]
    low_right = full_dot(lower, lower)
    write_pieces(out_ref, jnp.where(rows <= cols, full_dot(upper, upper), low_right), 0)
    write_pieces(out_ref, full_dot(upper, lower), 2 * w * w // (out_ref.shape[0] * 2 * LANES))
    low_diag = diagonal(low_right)
    end = out_ref.shape[1] - 8
    for p in range(out_ref.shape[0]):
        out_ref[p, end:, :] = jnp.zeros((8, LANES), jnp.float32)
        for t in range(w // LANES):
            out_ref[p, end + t : end + t + 1, :] = low_diag[:, t * LANES : (t + 1) * LANES]


def cross_kernel(upper_ref, lower_ref, out_ref):
    write_pieces(out_ref, full_dot(upper_ref[...], lower_ref[...]), 0)


def first_kernel(shift_ref, gram_ref, pair_ref, upper_ref, lower_ref, tl, lr, tr):
    w = tl.shape[0]
    rows, cols = grid_of(w)
    read_pieces(gram_ref, tl, 0)
    read_pieces(gram_ref, tr, w * w // (gram_ref.shape[0] * LANES))
    square = tl[...]
    turned = jnp.transpose(square)
    end = gram_ref.shape[1] - 8
    low_diag = jnp.concatenate(
        [gram_ref[0, end + t : end + t + 1, :] for t in range(w // LANES)], axis=1
    )
    lr[...] = jnp.where(rows == cols, low_diag, jnp.where(rows > cols, square, turned))
    tl[...] = jnp.where(rows <= cols, square, turned)
    upper_ref[...] = pair_ref[:, :w]
    lower_ref[...] = pair_ref[:, w:]
    inner_rounds(shift_ref, tl, tr, lr, upper_ref, lower_ref)


def second_kernel(
    shift_ref, tl_ref, cross_ref, lr_ref, upper_in, lower_in, upper_ref, lower_ref, tl, tr, lr
):
    tl[...] = tl_ref[...]
    lr[...] = lr_ref[...]
    read_pieces(cross_ref, tr, 0)
    upper_ref[...] = upper_in[...]
    lower_ref[...] = lower_in[...]
    inner_rounds(shift_ref, tl, tr, lr, upper_ref, lower_ref)


def passed_along(block, axis, distance):
    devices = range(lax.axis_size(axis))
    route = [((i - distance) % len(devices), i) for i in devices]
    return lax.ppermute(block, axis, route)


def summed_pieces(pieces, axis):
    mine = lax.all_to_all(pieces, axis, 0, 0, tiled=True).sum(0, keepdims=True)
    return lax.all_to_all(jnp.broadcast_to(mine, pieces.shape), axis, 0, 0, tiled=True)


def per_device(matrix, shifts):
    rows, width = matrix.shape
    w = width // 2
    n = lax.axis_size("row")
    block = (rows, w)
    square = (w, w)
    share = w * w // (n * LANES)

    (pieces,) = kernel_call(gram_kernel, [(n, 2 * share + 8, LANES)], [VMEM])(matrix)
    upper, lower, tl, lr = kernel_call(
        first_kernel, [block, block, square, square], [SMEM, VMEM, VMEM], [square]
    )(shifts[0], summed_pieces(pieces, "row"), matrix)
    upper = passed_along(upper, "col", 1)
    lower = passed_along(lower, "col", -1)
    tl = passed_along(tl, "col", 1)
    lr = passed_along(lr, "col", -1)

    (pieces,) = kernel_call(cross_kernel, [(n, share, LANES)], [VMEM, VMEM])(upper, lower)
    upper, lower = kernel_call(
        second_kernel, [block, block], [SMEM] + [VMEM] * 5, [square] * 3
    )(shifts[1], tl, summed_pieces(pieces, "row"), lr, upper, lower)
    upper = passed_along(upper, "col", 1)
    lower = passed_along(lower, "col", -1)
    return jnp.concatenate([upper, lower], axis=1)


def solution(mesh):
    in_specs = (P("row", "col"), P())
    out_specs = P("row", "col")
    return jax.shard_map(
        per_device, mesh=mesh, in_specs=in_specs, out_specs=out_specs, check_vma=False
    )
```

time: 341 us -> 122 us (0.36)
  the two profiles are of different devices: /device:TPU:8 before, /device:TPU:1 now
where the time goes in v2:
time: 122 us
  blocking collectives  42 us (34%)
  waiting for transfers between devices  41.7 us (34%)
  starting transfers between devices  19.4 us (16%)
  Pallas kernels  15.1 us (12%)
  local copies, waits for them, and re-layouts  2.63 us (2%)
    all_to_all x2, blocking collectives, summed_pieces(): mine = lax.all_to_all(pieces, axis, 0, 0, tiled=True).sum(0, keepdims=True)  42 us
    ppermute x6, waiting for transfers between devices, passed_along(): return lax.ppermute(block, axis, route)  25.9 us
    all_to_all x2, waiting for transfers between devices, summed_pieces(): lax.all_to_all(jnp.broadcast_to(mine, pieces.shape), axis, 0, 0, tiled=True)  15.9 us
    ppermute x6, starting transfers between devices, passed_along(): return lax.ppermute(block, axis, route)  12.2 us
    all_to_all x2, starting transfers between devices, summed_pieces(): lax.all_to_all(jnp.broadcast_to(mine, pieces.shape), axis, 0, 0, tiled=True)  7.25 us
    pallas_call x1, Pallas kernels, per_device(): kernel_call(first_kernel, [block, block, square, square], [SMEM, VMEM, VM...  7.08 us
    pallas_call x1, Pallas kernels, per_device(): kernel_call(second_kernel, [block, block], [SMEM] + [VMEM] * 5, [square]...  6.81 us
  transfers between devices with their start and end apart: 8, of which 7 were waited for; matrix products, arithmetic and copies ran while one was open for 0% of the time, Pallas kernels for 0%

profile of v2, /device:TPU:1, one launch (start us, length us, event | category | flops | bytes accessed | tf_op | source)
XLA Modules:
  0.0 121.9 jit_solution(1856375569829247141)
XLA Ops:
  0.0 0.0 copy-start
  0.0 1.0 copy-done
  1.0 0.8 shard_map.28
  1.9 28.4 %all_to_all.20 = f32[16,72,128]{2,1,0:T(8,128)S(1)} all-to-all(f32[16,72,128]{2,1,0:T(8,128)S(1)} %shard_map.28), channel_id=1, replica_groups=mesh['row'=16,'col'=16] {'row'}, dimensions={0} | all-to-all | bytes 1179648 | tf_op jit(solution)/shard_map/all_to_all | solution.py:175
  30.4 0.9 broadcast_in_dim.4
  31.2 0.0 copy-start.2
  31.2 0.0 copy-start.1
  31.2 3.7 %all-to-all-start.1 = ((f32[16,72,128]{2,1,0:T(8,128)}), f32[16,72,128]{2,1,0:T(8,128)S(1)}, u32[]{:S(2)}, u32[]{:S(2)}) async-start(f32[16,72,128]{2,1,0:T(8,128)} %broadcast_in_dim.4), calls=%async_computation.1 | async-start | bytes 1179648 | tf_op jit(solution)/shard_map/all_to_all | solution.py:176
  34.9 0.0 copy-done.2
  35.0 15.8 %all-to-all-done.1.gram_ref = f32[16,72,128]{2,1,0:T(8,128)S(1)} async-done(((f32[16,72,128]{2,1,0:T(8,128)}), f32[16,72,128]{2,1,0:T(8,128)S(1)}, u32[]{:S(2)}, u32[]{:S(2)}) %all-to-all-start.1) | async-done | bytes 589856 | tf_op jit(solution)/shard_map/all_to_all | solution.py:176
  50.8 0.0 copy-done.1
  50.8 7.1 %shard_map.29 = (f32[256,256]{1,0:T(8,128)S(1)}, f32[256,256]{1,0:T(8,128)S(1)}, f32[256,256]{1,0:T(8,128)S(1)}, f32[256,256]{1,0:T(8,128)S(1)}) custom-call(s32[8]{0:T(128)S(1)} %get-tuple-element.17.shift_ref, f32[16,72,128]{2,1,0:T(8,128)S(1)} %all-to-all-done.1.gram_ref, f32[256,512]{1,0:T(8,128)S(1)} %copy-done.1), custom_call_target="tpu_custom_call" | custom-call | tf_op jit(solution)/shard_map/pallas_call | solution.py:188
  57.9 6.6 %collective-permute-start.1 = (f32[256,256]{1,0:T(8,128)S(1)}, f32[256,256]{1,0:T(8,128)S(1)}, u32[]{:S(2)}, u32[]{:S(2)}) collective-permute-start(f32[256,256]{1,0:T(8,128)S(1)} %get-tuple-element.12), channel_id=1, source_target_pairs={{15,0},{0,1},{1,2},{2,3},{3,4},{4,5},{5,6},{6,7},{7,8},{8,9},{9,10... | collective-permute-start | bytes 786440 | tf_op jit(solution)/shard_map/ppermute | solution.py:171
  64.5 0.0 collective-permute-start.2
  64.5 3.3 %collective-permute-done.1.upper_ref.upper_in = f32[256,256]{1,0:T(8,128)S(1)} collective-permute-done((f32[256,256]{1,0:T(8,128)S(1)}, f32[256,256]{1,0:T(8,128)S(1)}, u32[]{:S(2)}, u32[]{:S(2)}) %collective-permute-start.1) | collective-permute-done | bytes 262176 | tf_op jit(solution)/shard_map/ppermute | solution.py:171
  67.8 5.7 %collective-permute-done.2.lower_ref.lower_in = f32[256,256]{1,0:T(8,128)S(1)} collective-permute-done((f32[256,256]{1,0:T(8,128)S(1)}, f32[256,256]{1,0:T(8,128)S(1)}, u32[]{:S(2)}, u32[]{:S(2)}) %collective-permute-start.2) | collective-permute-done | bytes 262176 | tf_op jit(solution)/shard_map/ppermute | solution.py:171
  73.5 0.4 shard_map.30
  73.9 13.6 %all_to_all.21 = f32[16,32,128]{2,1,0:T(8,128)S(1)} all-to-all(f32[16,32,128]{2,1,0:T(8,128)S(1)} %shard_map.30), channel_id=1, replica_groups=mesh['row'=16,'col'=16] {'row'}, dimensions={0} | all-to-all | bytes 524288 | tf_op jit(solution)/shard_map/all_to_all | solution.py:175
  87.5 0.7 broadcast_in_dim.5
  88.2 3.5 %all-to-all-start.3 = ((f32[16,32,128]{2,1,0:T(8,128)}), f32[16,32,128]{2,1,0:T(8,128)S(1)}, u32[]{:S(2)}, u32[]{:S(2)}) async-start(f32[16,32,128]{2,1,0:T(8,128)} %broadcast_in_dim.5), calls=%async_computation.3 | async-start | bytes 524288 | tf_op jit(solution)/shard_map/all_to_all | solution.py:176
  91.8 3.1 %collective-permute-start = (f32[256,256]{1,0:T(8,128)S(1)}, f32[256,256]{1,0:T(8,128)S(1)}, u32[]{:S(2)}, u32[]{:S(2)}) collective-permute-start(f32[256,256]{1,0:T(8,128)S(1)} %get-tuple-element.11), channel_id=1, source_target_pairs={{15,0},{0,1},{1,2},{2,3},{3,4},{4,5},{5,6},{6,7},{7,8},{8,9},{9,10... | collective-permute-start | bytes 786440 | tf_op jit(solution)/shard_map/ppermute | solution.py:171
  94.9 0.0 collective-permute-start.3
  94.9 8.0 %collective-permute-done.tl_ref = f32[256,256]{1,0:T(8,128)S(1)} collective-permute-done((f32[256,256]{1,0:T(8,128)S(1)}, f32[256,256]{1,0:T(8,128)S(1)}, u32[]{:S(2)}, u32[]{:S(2)}) %collective-permute-start) | collective-permute-done | bytes 262176 | tf_op jit(solution)/shard_map/ppermute | solution.py:171
  102.9 1.6 %collective-permute-done.3.lr_ref = f32[256,256]{1,0:T(8,128)S(1)} collective-permute-done((f32[256,256]{1,0:T(8,128)S(1)}, f32[256,256]{1,0:T(8,128)S(1)}, u32[]{:S(2)}, u32[]{:S(2)}) %collective-permute-start.3) | collective-permute-done | bytes 262176 | tf_op jit(solution)/shard_map/ppermute | solution.py:171
  104.5 0.0 all-to-all-done.3.cross_ref
  104.5 6.8 %shard_map.31 = (f32[256,256]{1,0:T(8,128)S(1)}, f32[256,256]{1,0:T(8,128)S(1)}) custom-call(s32[8]{0:T(128)S(1)} %get-tuple-element.18.shift_ref, f32[256,256]{1,0:T(8,128)S(1)} %collective-permute-done.tl_ref, f32[16,32,128]{2,1,0:T(8,128)S(1)} %all-to-all-done.3.cross_ref, f32[256,256]{1,0:T(8,128)S(1)} %collective-permute-done.3.lr_ref, ...), custom_call_target="tpu_custom_call" | custom-call | tf_op jit(solution)/shard_map/pallas_call | solution.py:197
  111.3 2.5 %collective-permute-start.4 = (f32[256,256]{1,0:T(8,128)S(1)}, f32[256,256]{1,0:T(8,128)S(1)}, u32[]{:S(2)}, u32[]{:S(2)}) collective-permute-start(f32[256,256]{1,0:T(8,128)S(1)} %get-tuple-element.15), channel_id=1, source_target_pairs={{15,0},{0,1},{1,2},{2,3},{3,4},{4,5},{5,6},{6,7},{7,8},{8,9},{9,10... | collective-permute-start | bytes 786440 | tf_op jit(solution)/shard_map/ppermute | solution.py:171
  113.8 0.0 collective-permute-start.5
  113.8 6.1 %collective-permute-done.4 = f32[256,256]{1,0:T(8,128)S(1)} collective-permute-done((f32[256,256]{1,0:T(8,128)S(1)}, f32[256,256]{1,0:T(8,128)S(1)}, u32[]{:S(2)}, u32[]{:S(2)}) %collective-permute-start.4) | collective-permute-done | bytes 262176 | tf_op jit(solution)/shard_map/ppermute | solution.py:171
  119.9 1.2 collective-permute-done.5
  121.1 0.9 pad_maximum_fusion
  (3 shorter events, 0.1 us)
Async XLA Ops:
  0.0 1.0 copy-start
  31.2 3.7 %copy-start.2 = (s32[2,8]{1,0:T(2,128)S(1)}, s32[2,8]{1,0:T(2,128)}, u32[]{:S(2)}) copy-start(s32[2,8]{1,0:T(2,128)} %param.3) | copy-start | bytes 196
  31.2 19.6 %copy-start.1 = (f32[256,512]{1,0:T(8,128)S(1)}, f32[256,512]{1,0:T(8,128)}, u32[]{:S(2)}) copy-start(f32[256,512]{1,0:T(8,128)} %pair_ref.3) | copy-start | bytes 1572868
  31.2 19.6 %all-to-all-start.1 = ((f32[16,72,128]{2,1,0:T(8,128)}), f32[16,72,128]{2,1,0:T(8,128)S(1)}, u32[]{:S(2)}, u32[]{:S(2)}) async-start(f32[16,72,128]{2,1,0:T(8,128)} %broadcast_in_dim.4), calls=%async_computation.1 | async-start | bytes 1179648 | tf_op jit(solution)/shard_map/all_to_all | solution.py:176
  57.9 9.9 %collective-permute-start.1 = (f32[256,256]{1,0:T(8,128)S(1)}, f32[256,256]{1,0:T(8,128)S(1)}, u32[]{:S(2)}, u32[]{:S(2)}) collective-permute-start(f32[256,256]{1,0:T(8,128)S(1)} %get-tuple-element.12), channel_id=1, source_target_pairs={{15,0},{0,1},{1,2},{2,3},{3,4},{4,5},{5,6},{6,7},{7,8},{8,9},{9,10... | collective-permute-start | bytes 786440 | tf_op jit(solution)/shard_map/ppermute | solution.py:171
  64.5 9.0 %collective-permute-start.2 = (f32[256,256]{1,0:T(8,128)S(1)}, f32[256,256]{1,0:T(8,128)S(1)}, u32[]{:S(2)}, u32[]{:S(2)}) collective-permute-start(f32[256,256]{1,0:T(8,128)S(1)} %get-tuple-element.13), channel_id=1, source_target_pairs={{1,0},{2,1},{3,2},{4,3},{5,4},{6,5},{7,6},{8,7},{9,8},{10,9},{11,1... | collective-permute-start | bytes 786440 | tf_op jit(solution)/shard_map/ppermute | solution.py:171
  88.2 16.2 %all-to-all-start.3 = ((f32[16,32,128]{2,1,0:T(8,128)}), f32[16,32,128]{2,1,0:T(8,128)S(1)}, u32[]{:S(2)}, u32[]{:S(2)}) async-start(f32[16,32,128]{2,1,0:T(8,128)} %broadcast_in_dim.5), calls=%async_computation.3 | async-start | bytes 524288 | tf_op jit(solution)/shard_map/all_to_all | solution.py:176
  91.8 11.1 %collective-permute-start = (f32[256,256]{1,0:T(8,128)S(1)}, f32[256,256]{1,0:T(8,128)S(1)}, u32[]{:S(2)}, u32[]{:S(2)}) collective-permute-start(f32[256,256]{1,0:T(8,128)S(1)} %get-tuple-element.11), channel_id=1, source_target_pairs={{15,0},{0,1},{1,2},{2,3},{3,4},{4,5},{5,6},{6,7},{7,8},{8,9},{9,10... | collective-permute-start | bytes 786440 | tf_op jit(solution)/shard_map/ppermute | solution.py:171
  94.9 9.6 %collective-permute-start.3 = (f32[256,256]{1,0:T(8,128)S(1)}, f32[256,256]{1,0:T(8,128)S(1)}, u32[]{:S(2)}, u32[]{:S(2)}) collective-permute-start(f32[256,256]{1,0:T(8,128)S(1)} %get-tuple-element.14), channel_id=1, source_target_pairs={{1,0},{2,1},{3,2},{4,3},{5,4},{6,5},{7,6},{8,7},{9,8},{10,9},{11,1... | collective-permute-start | bytes 786440 | tf_op jit(solution)/shard_map/ppermute | solution.py:171
  111.3 8.6 %collective-permute-start.4 = (f32[256,256]{1,0:T(8,128)S(1)}, f32[256,256]{1,0:T(8,128)S(1)}, u32[]{:S(2)}, u32[]{:S(2)}) collective-permute-start(f32[256,256]{1,0:T(8,128)S(1)} %get-tuple-element.15), channel_id=1, source_target_pairs={{15,0},{0,1},{1,2},{2,3},{3,4},{4,5},{5,6},{6,7},{7,8},{8,9},{9,10... | collective-permute-start | bytes 786440 | tf_op jit(solution)/shard_map/ppermute | solution.py:171
  113.8 7.3 %collective-permute-start.5 = (f32[256,256]{1,0:T(8,128)S(1)}, f32[256,256]{1,0:T(8,128)S(1)}, u32[]{:S(2)}, u32[]{:S(2)}) collective-permute-start(f32[256,256]{1,0:T(8,128)S(1)} %get-tuple-element.16), channel_id=1, source_target_pairs={{1,0},{2,1},{3,2},{4,3},{5,4},{6,5},{7,6},{8,7},{9,8},{10,9},{11,1... | collective-permute-start | bytes 786440 | tf_op jit(solution)/shard_map/ppermute | solution.py:171

commit v3 on v2

--- a/solution.py
+++ b/solution.py
@@ -96,58 +96,53 @@
     )
 
 
-def write_pieces(out_ref, block, start):
-    pieces = out_ref.shape[0]
-    share = block.shape[0] // pieces
-    for p in range(pieces):
-        for t in range(block.shape[1] // LANES):
-            out_ref[p, start + t * share : start + (t + 1) * share, :] = block[
-                p * share : (p + 1) * share, t * LANES : (t + 1) * LANES
-            ]
-
-
-def read_pieces(in_ref, out_ref, start):
-    pieces = in_ref.shape[0]
-    share = out_ref.shape[0] // pieces
-    for p in range(pieces):
-        for t in range(out_ref.shape[1] // LANES):
-            out_ref[p * share : (p + 1) * share, t * LANES : (t + 1) * LANES] = in_ref[
-                p, start + t * share : start + (t + 1) * share, :
-            ]
-
-
-def gram_kernel(pair_ref, out_ref):
+def hand_out(place_ref, blocks, outs):
+    for k, out in enumerate(outs):
+        start = 0
+        for block in blocks:
+            share = block.shape[0] // len(outs)
+            quarter = (place_ref[0] ^ k) * share
+            out[start : start + share, :] = block[pl.ds(pl.multiple_of(quarter, 8), share), :]
+            start += share
+
+
+def take_in(place_ref, ins, blocks):
+    for k, piece in enumerate(ins):
+        start = 0
+        for block in blocks:
+            share = block.shape[0] // len(ins)
+            quarter = (place_ref[0] ^ k) * share
+            block[pl.ds(pl.multiple_of(quarter, 8), share), :] = piece[start : start + share, :]
+            start += share
+
+
+def gram_kernel(place_ref, pair_ref, out0, out1, out2, out3, square, cross, diag):
+    outs = (out0, out1, out2, out3)
     w = pair_ref.shape[1] // 2
     rows, cols = grid_of(w)
     upper = pair_ref[:, :w]
     lower = pair_ref[:, w:]
     low_right = full_dot(lower, lower)
-    write_pieces(out_ref, jnp.where(rows <= cols, full_dot(upper, upper), low_right), 0)
-    write_pieces(out_ref, full_dot(upper, lower), 2 * w * w // (out_ref.shape[0] * 2 * LANES))
-    low_diag = diagonal(low_right)
-    end = out_ref.shape[1] - 8
-    for p in range(out_ref.shape[0]):
-        out_ref[p, end:, :] = jnp.zeros((8, LANES), jnp.float32)
-        for t in range(w // LANES):
-            out_ref[p, end + t : end + t + 1, :] = low_diag[:, t * LANES : (t + 1) * LANES]
-
-
-def cross_kernel(upper_ref, lower_ref, out_ref):
-    write_pieces(out_ref, full_dot(upper_ref[...], lower_ref[...]), 0)
-
-
-def first_kernel(shift_ref, gram_ref, pair_ref, upper_ref, lower_ref, tl, lr, tr):
+    square[...] = jnp.where(rows <= cols, full_dot(upper, upper), low_right)
+    cross[...] = full_dot(upper, lower)
+    diag[...] = jnp.broadcast_to(diagonal(low_right), diag.shape)
+    hand_out(place_ref, (square, cross, diag), outs)
+
+
+def cross_kernel(place_ref, upper_ref, lower_ref, out0, out1, out2, out3, cross):
+    cross[...] = full_dot(upper_ref[...], lower_ref[...])
+    hand_out(place_ref, (cross,), (out0, out1, out2, out3))
+
+
+def first_kernel(
+    place_ref, shift_ref, in0, in1, in2, in3, pair_ref, upper_ref, lower_ref, tl, lr, tr, diag
+):
     w = tl.shape[0]
     rows, cols = grid_of(w)
-    read_pieces(gram_ref, tl, 0)
-    read_pieces(gram_ref, tr, w * w // (gram_ref.shape[0] * LANES))
+    take_in(place_ref, (in0, in1, in2, in3), (tl, tr, diag))
     square = tl[...]
     turned = jnp.transpose(square)
-    end = gram_ref.shape[1] - 8
-    low_diag = jnp.concatenate(
-        [gram_ref[0, end + t : end + t + 1, :] for t in range(w // LANES)], axis=1
-    )
-    lr[...] = jnp.where(rows == cols, low_diag, jnp.where(rows > cols, square, turned))
+    lr[...] = jnp.where(rows == cols, diag[:1, :], jnp.where(rows > cols, square, turned))
     tl[...] = jnp.where(rows <= cols, square, turned)
     upper_ref[...] = pair_ref[:, :w]
     lower_ref[...] = pair_ref[:, w:]
@@ -155,11 +150,25 @@
 
 
 def second_kernel(
-    shift_ref, tl_ref, cross_ref, lr_ref, upper_in, lower_in, upper_ref, lower_ref, tl, tr, lr
+    place_ref,
+    shift_ref,
+    in0,
+    in1,
+    in2,
+    in3,
+    tl_ref,
+    lr_ref,
+    upper_in,
+    lower_in,
+    upper_ref,
+    lower_ref,
+    tl,
+    tr,
+    lr,
 ):
     tl[...] = tl_ref[...]
     lr[...] = lr_ref[...]
-    read_pieces(cross_ref, tr, 0)
+    take_in(place_ref, (in0, in1, in2, in3), (tr,))
     upper_ref[...] = upper_in[...]
     lower_ref[...] = lower_in[...]
     inner_rounds(shift_ref, tl, tr, lr, upper_ref, lower_ref)
@@ -171,32 +180,44 @@
     return lax.ppermute(block, axis, route)
 
 
-def summed_pieces(pieces, axis):
-    mine = lax.all_to_all(pieces, axis, 0, 0, tiled=True).sum(0, keepdims=True)
-    return lax.all_to_all(jnp.broadcast_to(mine, pieces.shape), axis, 0, 0, tiled=True)
+def swapped(block, axis, bits):
+    return lax.ppermute(block, axis, [(i, i ^ bits) for i in range(lax.axis_size(axis))])
+
+
+def summed_quarters(outs, axis):
+    sent = [swapped(outs[k], axis, k) for k in (3, 1, 2)]
+    mine = (outs[0] + sent[1]) + (sent[2] + sent[0])
+    met = [swapped(mine, axis, k) for k in (8, 4, 12)]
+    mine = (mine + met[1]) + (met[0] + met[2])
+    shared = [swapped(mine, axis, k) for k in (3, 1, 2)]
+    return (mine, shared[1], shared[2], shared[0])
 
 
 def per_device(matrix, shifts):
     rows, width = matrix.shape
     w = width // 2
-    n = lax.axis_size("row")
     block = (rows, w)
     square = (w, w)
-    share = w * w // (n * LANES)
-
-    (pieces,) = kernel_call(gram_kernel, [(n, 2 * share + 8, LANES)], [VMEM])(matrix)
+    diag = (32, w)
+    place = (lax.axis_index("row") % 4).astype(jnp.int32).reshape(1)
+
+    quarters = kernel_call(
+        gram_kernel, [(2 * w // 4 + 8, w)] * 4, [SMEM, VMEM], [square, square, diag]
+    )(place, matrix)
     upper, lower, tl, lr = kernel_call(
-        first_kernel, [block, block, square, square], [SMEM, VMEM, VMEM], [square]
-    )(shifts[0], summed_pieces(pieces, "row"), matrix)
+        first_kernel, [block, block, square, square], [SMEM, SMEM] + [VMEM] * 5, [square, diag]
+    )(place, shifts[0], *summed_quarters(quarters, "row"), matrix)
     upper = passed_along(upper, "col", 1)
     lower = passed_along(lower, "col", -1)
     tl = passed_along(tl, "col", 1)
     lr = passed_along(lr, "col", -1)
 
-    (pieces,) = kernel_call(cross_kernel, [(n, share, LANES)], [VMEM, VMEM])(upper, lower)
+    quarters = kernel_call(
+        cross_kernel, [(w // 4, w)] * 4, [SMEM, VMEM, VMEM], [square]
+    )(place, upper, lower)
     upper, lower = kernel_call(
-        second_kernel, [block, block], [SMEM] + [VMEM] * 5, [square] * 3
-    )(shifts[1], tl, summed_pieces(pieces, "row"), lr, upper, lower)
+        second_kernel, [block, block], [SMEM, SMEM] + [VMEM] * 8, [square] * 3
+    )(place, shifts[1], *summed_quarters(quarters, "row"), tl, lr, upper, lower)
     upper = passed_along(upper, "col", 1)
     lower = passed_along(lower, "col", -1)
     return jnp.concatenate([upper, lower], axis=1)

time: 122 us -> 108 us (0.89)
  blocking collectives: 42 us -> 0 us
  starting transfers between devices: 19.4 us -> 41.4 us
  waiting for transfers between devices: 41.7 us -> 48.9 us
  local copies, waits for them, and re-layouts: 2.63 us -> 1.05 us
    all_to_all x2 -> x0, blocking collectives: 42 us -> none  [summed_pieces(): mine = lax.all_to_all(pieces, axis, 0, 0, tiled=True).sum(0, keepdims=True)]
    ppermute x0 -> x18, starting transfers between devices: none -> 28.8 us  [swapped(): lax.ppermute(block, axis, [(i, i ^ bits) for i in range(lax.axis_size(axi...]
    ppermute x0 -> x18, waiting for transfers between devices: none -> 24.7 us  [swapped(): lax.ppermute(block, axis, [(i, i ^ bits) for i in range(lax.axis_size(axi...]
    all_to_all x2 -> x0, waiting for transfers between devices: 15.9 us -> none  [summed_pieces(): lax.all_to_all(jnp.broadcast_to(mine, pieces.shape), axis, 0, 0, tiled=True)]
    all_to_all x2 -> x0, starting transfers between devices: 7.25 us -> none  [summed_pieces(): lax.all_to_all(jnp.broadcast_to(mine, pieces.shape), axis, 0, 0, tiled=True)]
    ppermute x6, waiting for transfers between devices: 25.9 us -> 24.2 us  [passed_along(): return lax.ppermute(block, axis, route)]
    broadcast_in_dim x2 -> x0, local copies, waits for them, and re-layouts: 1.58 us -> none  [summed_pieces(): jnp.broadcast_to(mine, pieces.shape)]
  transfers between devices with their start and end apart: 8 -> 24, of which waited for: 7 -> 20; matrix products, arithmetic and copies ran while one was open for 0% -> 0% of each run, Pallas kernels for 0% -> 0%
where the time goes in v3:
time: 108 us
  waiting for transfers between devices  48.9 us (45%)
  starting transfers between devices  41.4 us (38%)
  Pallas kernels  15.5 us (14%)
    ppermute x18, starting transfers between devices, swapped(): lax.ppermute(block, axis, [(i, i ^ bits) for i in range(lax.axis_size(axi...  28.8 us
    ppermute x18, waiting for transfers between devices, swapped(): lax.ppermute(block, axis, [(i, i ^ bits) for i in range(lax.axis_size(axi...  24.7 us
    ppermute x6, waiting for transfers between devices, passed_along(): return lax.ppermute(block, axis, route)  24.2 us
    ppermute x6, starting transfers between devices, passed_along(): return lax.ppermute(block, axis, route)  12.7 us
    pallas_call x1, Pallas kernels, per_device(): kernel_call(first_kernel, [block, block, square, square], [SMEM, SMEM] +...  7.21 us
    pallas_call x1, Pallas kernels, per_device(): kernel_call(second_kernel, [block, block], [SMEM, SMEM] + [VMEM] * 8, [sq...  6.93 us
  transfers between devices with their start and end apart: 24, of which 20 were waited for; matrix products, arithmetic and copies ran while one was open for 0% of the time, Pallas kernels for 0%

profile of v3, /device:TPU:1, one launch (start us, length us, event | category | flops | bytes accessed | tf_op | source)
XLA Modules:
  0.0 107.8 jit_solution(13133252839508287045)
XLA Ops:
  0.0 0.0 copy-start
  0.0 1.0 copy-done
  1.0 0.9 shard_map.28
  1.9 2.2 %collective-permute-start = (f32[136,256]{1,0:T(8,128)S(1)}, f32[136,256]{1,0:T(8,128)S(1)}, u32[]{:S(2)}, u32[]{:S(2)}) collective-permute-start(f32[136,256]{1,0:T(8,128)S(1)} %get-tuple-element.20), channel_id=1, source_target_pairs={{0,16},{16,0},{32,48},{48,32},{64,80},{80,64},{96,112},{112,96},{1... | collective-permute-start | bytes 417800 | tf_op jit(solution)/shard_map/ppermute | solution.py:184
  4.1 1.7 %collective-permute-start.1 = (f32[136,256]{1,0:T(8,128)S(1)}, f32[136,256]{1,0:T(8,128)S(1)}, u32[]{:S(2)}, u32[]{:S(2)}) collective-permute-start(f32[136,256]{1,0:T(8,128)S(1)} %get-tuple-element.21), channel_id=1, source_target_pairs={{0,32},{16,48},{32,0},{48,16},{64,96},{80,112},{96,64},{112,80},{1... | collective-permute-start | bytes 417800 | tf_op jit(solution)/shard_map/ppermute | solution.py:184
  5.8 0.0 collective-permute-start.2
  5.8 0.8 collective-permute-done
  6.6 1.9 %collective-permute-done.1 = f32[136,256]{1,0:T(8,128)S(1)} collective-permute-done((f32[136,256]{1,0:T(8,128)S(1)}, f32[136,256]{1,0:T(8,128)S(1)}, u32[]{:S(2)}, u32[]{:S(2)}) %collective-permute-start.1) | collective-permute-done | bytes 139296 | tf_op jit(solution)/shard_map/ppermute | solution.py:184
  8.5 3.1 %collective-permute-done.2 = f32[136,256]{1,0:T(8,128)S(1)} collective-permute-done((f32[136,256]{1,0:T(8,128)S(1)}, f32[136,256]{1,0:T(8,128)S(1)}, u32[]{:S(2)}, u32[]{:S(2)}) %collective-permute-start.2) | collective-permute-done | bytes 139296 | tf_op jit(solution)/shard_map/ppermute | solution.py:184
  11.7 0.0 copy-start.1
  11.7 5.9 %collective-permute-start.5 = (f32[136,256]{1,0:T(8,128)S(1)}, f32[136,256]{1,0:T(8,128)S(1)}, u32[]{:S(2)}, u32[]{:S(2)}) collective-permute-start(f32[136,256]{1,0:T(8,128)S(1)} %add_add_fusion.1), channel_id=1, source_target_pairs={{0,192},{16,208},{32,224},{48,240},{64,128},{80,144},{96,160},{112... | collective-permute-start | bytes 417800 | tf_op jit(solution)/shard_map/ppermute | solution.py:184
  17.6 1.0 collective-permute-start.4
  18.6 1.2 %collective-permute-start.3 = (f32[136,256]{1,0:T(8,128)S(1)}, f32[136,256]{1,0:T(8,128)S(1)}, u32[]{:S(2)}, u32[]{:S(2)}) collective-permute-start(f32[136,256]{1,0:T(8,128)S(1)} %add_add_fusion.1), channel_id=1, source_target_pairs={{0,64},{16,80},{32,96},{48,112},{64,0},{80,16},{96,32},{112,48},{1... | collective-permute-start | bytes 417800 | tf_op jit(solution)/shard_map/ppermute | solution.py:184
  19.8 7.0 %collective-permute-done.5 = f32[136,256]{1,0:T(8,128)S(1)} collective-permute-done((f32[136,256]{1,0:T(8,128)S(1)}, f32[136,256]{1,0:T(8,128)S(1)}, u32[]{:S(2)}, u32[]{:S(2)}) %collective-permute-start.5) | collective-permute-done | bytes 139296 | tf_op jit(solution)/shard_map/ppermute | solution.py:184
  26.8 0.0 collective-permute-done.4
  26.8 2.7 %collective-permute-done.3 = f32[136,256]{1,0:T(8,128)S(1)} collective-permute-done((f32[136,256]{1,0:T(8,128)S(1)}, f32[136,256]{1,0:T(8,128)S(1)}, u32[]{:S(2)}, u32[]{:S(2)}) %collective-permute-start.3) | collective-permute-done | bytes 139296 | tf_op jit(solution)/shard_map/ppermute | solution.py:184
  29.5 2.3 %collective-permute-start.8 = (f32[136,256]{1,0:T(8,128)S(1)}, f32[136,256]{1,0:T(8,128)S(1)}, u32[]{:S(2)}, u32[]{:S(2)}) collective-permute-start(f32[136,256]{1,0:T(8,128)S(1)} %add_add_fusion.in0), channel_id=1, source_target_pairs={{0,48},{16,32},{32,16},{48,0},{64,112},{80,96},{96,80},{112,64},{1... | collective-permute-start | bytes 417800 | tf_op jit(solution)/shard_map/ppermute | solution.py:184
  31.9 0.1 collective-permute-start.7
  32.0 1.1 %collective-permute-start.6 = (f32[136,256]{1,0:T(8,128)S(1)}, f32[136,256]{1,0:T(8,128)S(1)}, u32[]{:S(2)}, u32[]{:S(2)}) collective-permute-start(f32[136,256]{1,0:T(8,128)S(1)} %add_add_fusion.in0), channel_id=1, source_target_pairs={{0,16},{16,0},{32,48},{48,32},{64,80},{80,64},{96,112},{112,96},{1... | collective-permute-start | bytes 417800 | tf_op jit(solution)/shard_map/ppermute | solution.py:184
  33.0 0.0 copy-done.1
  33.1 2.3 %collective-permute-done.8.in3 = f32[136,256]{1,0:T(8,128)S(1)} collective-permute-done((f32[136,256]{1,0:T(8,128)S(1)}, f32[136,256]{1,0:T(8,128)S(1)}, u32[]{:S(2)}, u32[]{:S(2)}) %collective-permute-start.8) | collective-permute-done | bytes 139296 | tf_op jit(solution)/shard_map/ppermute | solution.py:184
  35.3 1.0 collective-permute-done.7.in2
  36.4 0.4 collective-permute-done.6.in1
  36.7 7.2 %shard_map.29 = (f32[256,256]{1,0:T(8,128)S(1)}, f32[256,256]{1,0:T(8,128)S(1)}, f32[256,256]{1,0:T(8,128)S(1)}, f32[256,256]{1,0:T(8,128)S(1)}) custom-call(s32[1]{0:T(128)} %bitcast.place_ref, s32[8]{0:T(128)S(1)} %get-tuple-element.33.shift_ref, f32[136,256]{1,0:T(8,128)S(1)} %add_add_fusion.in0, f32[136,256]{1,0:T(8,128)S(1)} %collective-permute-done.6.in1, ...), custom_call_target="tpu_custom_call" | custom-call | tf_op jit(solution)/shard_map/pallas_call | solution.py:207
  44.0 8.4 %collective-permute-start.9 = (f32[256,256]{1,0:T(8,128)S(1)}, f32[256,256]{1,0:T(8,128)S(1)}, u32[]{:S(2)}, u32[]{:S(2)}) collective-permute-start(f32[256,256]{1,0:T(8,128)S(1)} %get-tuple-element.23), channel_id=1, source_target_pairs={{15,0},{0,1},{1,2},{2,3},{3,4},{4,5},{5,6},{6,7},{7,8},{8,9},{9,10... | collective-permute-start | bytes 786440 | tf_op jit(solution)/shard_map/ppermute | solution.py:180
  52.3 0.0 collective-permute-start.10
  52.3 3.3 %collective-permute-done.9.upper_ref.upper_in = f32[256,256]{1,0:T(8,128)S(1)} collective-permute-done((f32[256,256]{1,0:T(8,128)S(1)}, f32[256,256]{1,0:T(8,128)S(1)}, u32[]{:S(2)}, u32[]{:S(2)}) %collective-permute-start.9) | collective-permute-done | bytes 262176 | tf_op jit(solution)/shard_map/ppermute | solution.py:180
  55.7 5.5 %collective-permute-done.10.lower_ref.lower_in = f32[256,256]{1,0:T(8,128)S(1)} collective-permute-done((f32[256,256]{1,0:T(8,128)S(1)}, f32[256,256]{1,0:T(8,128)S(1)}, u32[]{:S(2)}, u32[]{:S(2)}) %collective-permute-start.10) | collective-permute-done | bytes 262176 | tf_op jit(solution)/shard_map/ppermute | solution.py:180
  61.1 0.4 shard_map.30
  61.6 0.7 collective-permute-start.11
  62.3 0.0 collective-permute-start.12
  62.3 2.0 %collective-permute-start.13 = (f32[64,256]{1,0:T(8,128)S(1)}, f32[64,256]{1,0:T(8,128)S(1)}, u32[]{:S(2)}, u32[]{:S(2)}) collective-permute-start(f32[64,256]{1,0:T(8,128)S(1)} %get-tuple-element.28), channel_id=1, source_target_pairs={{0,48},{16,32},{32,16},{48,0},{64,112},{80,96},{96,80},{112,64},{1... | collective-permute-start | bytes 196616 | tf_op jit(solution)/shard_map/ppermute | solution.py:184
  64.3 0.8 collective-permute-done.11
  65.1 0.7 collective-permute-done.12
  65.8 1.0 collective-permute-done.13
  66.8 4.9 %collective-permute-start.16 = (f32[64,256]{1,0:T(8,128)S(1)}, f32[64,256]{1,0:T(8,128)S(1)}, u32[]{:S(2)}, u32[]{:S(2)}) collective-permute-start(f32[64,256]{1,0:T(8,128)S(1)} %add_add_fusion.3), channel_id=1, source_target_pairs={{0,192},{16,208},{32,224},{48,240},{64,128},{80,144},{96,160},{112... | collective-permute-start | bytes 196616 | tf_op jit(solution)/shard_map/ppermute | solution.py:184
  71.7 0.0 collective-permute-start.15
  71.7 2.2 %collective-permute-start.14 = (f32[64,256]{1,0:T(8,128)S(1)}, f32[64,256]{1,0:T(8,128)S(1)}, u32[]{:S(2)}, u32[]{:S(2)}) collective-permute-start(f32[64,256]{1,0:T(8,128)S(1)} %add_add_fusion.3), channel_id=1, source_target_pairs={{0,64},{16,80},{32,96},{48,112},{64,0},{80,16},{96,32},{112,48},{1... | collective-permute-start | bytes 196616 | tf_op jit(solution)/shard_map/ppermute | solution.py:184
  73.9 2.3 %collective-permute-start.20 = (f32[256,256]{1,0:T(8,128)S(1)}, f32[256,256]{1,0:T(8,128)S(1)}, u32[]{:S(2)}, u32[]{:S(2)}) collective-permute-start(f32[256,256]{1,0:T(8,128)S(1)} %get-tuple-element.29), channel_id=1, source_target_pairs={{15,0},{0,1},{1,2},{2,3},{3,4},{4,5},{5,6},{6,7},{7,8},{8,9},{9,10... | collective-permute-start | bytes 786440 | tf_op jit(solution)/shard_map/ppermute | solution.py:180
  76.1 0.0 collective-permute-start.21
  76.1 1.4 %collective-permute-done.16 = f32[64,256]{1,0:T(8,128)S(1)} collective-permute-done((f32[64,256]{1,0:T(8,128)S(1)}, f32[64,256]{1,0:T(8,128)S(1)}, u32[]{:S(2)}, u32[]{:S(2)}) %collective-permute-start.16) | collective-permute-done | bytes 65568 | tf_op jit(solution)/shard_map/ppermute | solution.py:184
  77.5 1.4 %collective-permute-done.15 = f32[64,256]{1,0:T(8,128)S(1)} collective-permute-done((f32[64,256]{1,0:T(8,128)S(1)}, f32[64,256]{1,0:T(8,128)S(1)}, u32[]{:S(2)}, u32[]{:S(2)}) %collective-permute-start.15) | collective-permute-done | bytes 65568 | tf_op jit(solution)/shard_map/ppermute | solution.py:184
  78.9 0.1 collective-permute-done.14
  79.1 2.7 %collective-permute-start.19 = (f32[64,256]{1,0:T(8,128)S(1)}, f32[64,256]{1,0:T(8,128)S(1)}, u32[]{:S(2)}, u32[]{:S(2)}) collective-permute-start(f32[64,256]{1,0:T(8,128)S(1)} %add_add_fusion.2.in0), channel_id=1, source_target_pairs={{0,48},{16,32},{32,16},{48,0},{64,112},{80,96},{96,80},{112,64},{1... | collective-permute-start | bytes 196616 | tf_op jit(solution)/shard_map/ppermute | solution.py:184
  81.8 0.0 collective-permute-start.18
  81.8 0.8 collective-permute-start.17
  82.6 0.4 collective-permute-done.20.tl_ref
  83.0 5.4 %collective-permute-done.21.lr_ref = f32[256,256]{1,0:T(8,128)S(1)} collective-permute-done((f32[256,256]{1,0:T(8,128)S(1)}, f32[256,256]{1,0:T(8,128)S(1)}, u32[]{:S(2)}, u32[]{:S(2)}) %collective-permute-start.21) | collective-permute-done | bytes 262176 | tf_op jit(solution)/shard_map/ppermute | solution.py:180
  88.4 0.0 collective-permute-done.19.in3
  88.4 0.0 collective-permute-done.18.in2
  88.4 0.0 collective-permute-done.17.in1
  88.4 6.9 %shard_map.31 = (f32[256,256]{1,0:T(8,128)S(1)}, f32[256,256]{1,0:T(8,128)S(1)}) custom-call(s32[1]{0:T(128)} %bitcast.place_ref, s32[8]{0:T(128)S(1)} %get-tuple-element.34.shift_ref, f32[64,256]{1,0:T(8,128)S(1)} %add_add_fusion.2.in0, f32[64,256]{1,0:T(8,128)S(1)} %collective-permute-done.17.in1, f32[64,256]{1,0:T(8,128)S(1)} %collective-permute-done.18.in2, ...), custom_call_target="tpu_custom_call" | custom-call | tf_op jit(solution)/shard_map/pallas_call | solution.py:218
  95.3 2.0 %collective-permute-start.22 = (f32[256,256]{1,0:T(8,128)S(1)}, f32[256,256]{1,0:T(8,128)S(1)}, u32[]{:S(2)}, u32[]{:S(2)}) collective-permute-start(f32[256,256]{1,0:T(8,128)S(1)} %get-tuple-element.31), channel_id=1, source_target_pairs={{15,0},{0,1},{1,2},{2,3},{3,4},{4,5},{5,6},{6,7},{7,8},{8,9},{9,10... | collective-permute-start | bytes 786440 | tf_op jit(solution)/shard_map/ppermute | solution.py:180
  97.3 0.0 collective-permute-start.23
  97.3 6.1 %collective-permute-done.22 = f32[256,256]{1,0:T(8,128)S(1)} collective-permute-done((f32[256,256]{1,0:T(8,128)S(1)}, f32[256,256]{1,0:T(8,128)S(1)}, u32[]{:S(2)}, u32[]{:S(2)}) %collective-permute-start.22) | collective-permute-done | bytes 262176 | tf_op jit(solution)/shard_map/ppermute | solution.py:180
  103.4 3.6 %collective-permute-done.23 = f32[256,256]{1,0:T(8,128)S(1)} collective-permute-done((f32[256,256]{1,0:T(8,128)S(1)}, f32[256,256]{1,0:T(8,128)S(1)}, u32[]{:S(2)}, u32[]{:S(2)}) %collective-permute-start.23) | collective-permute-done | bytes 262176 | tf_op jit(solution)/shard_map/ppermute | solution.py:180
  107.0 0.9 pad_maximum_fusion
  (5 shorter events, 0.1 us)
Async XLA Ops:
  0.0 1.0 copy-start
  1.9 4.6 %collective-permute-start = (f32[136,256]{1,0:T(8,128)S(1)}, f32[136,256]{1,0:T(8,128)S(1)}, u32[]{:S(2)}, u32[]{:S(2)}) collective-permute-start(f32[136,256]{1,0:T(8,128)S(1)} %get-tuple-element.20), channel_id=1, source_target_pairs={{0,16},{16,0},{32,48},{48,32},{64,80},{80,64},{96,112},{112,96},{1... | collective-permute-start | bytes 417800 | tf_op jit(solution)/shard_map/ppermute | solution.py:184
  4.1 4.4 %collective-permute-start.1 = (f32[136,256]{1,0:T(8,128)S(1)}, f32[136,256]{1,0:T(8,128)S(1)}, u32[]{:S(2)}, u32[]{:S(2)}) collective-permute-start(f32[136,256]{1,0:T(8,128)S(1)} %get-tuple-element.21), channel_id=1, source_target_pairs={{0,32},{16,48},{32,0},{48,16},{64,96},{80,112},{96,64},{112,80},{1... | collective-permute-start | bytes 417800 | tf_op jit(solution)/shard_map/ppermute | solution.py:184
  5.8 5.9 %collective-permute-start.2 = (f32[136,256]{1,0:T(8,128)S(1)}, f32[136,256]{1,0:T(8,128)S(1)}, u32[]{:S(2)}, u32[]{:S(2)}) collective-permute-start(f32[136,256]{1,0:T(8,128)S(1)} %get-tuple-element.22), channel_id=1, source_target_pairs={{0,48},{16,32},{32,16},{48,0},{64,112},{80,96},{96,80},{112,64},{1... | collective-permute-start | bytes 417800 | tf_op jit(solution)/shard_map/ppermute | solution.py:184
  11.7 21.4 %copy-start.1 = (s32[2,8]{1,0:T(2,128)S(1)}, s32[2,8]{1,0:T(2,128)}, u32[]{:S(2)}) copy-start(s32[2,8]{1,0:T(2,128)} %param.3) | copy-start | bytes 196
  11.7 15.1 %collective-permute-start.5 = (f32[136,256]{1,0:T(8,128)S(1)}, f32[136,256]{1,0:T(8,128)S(1)}, u32[]{:S(2)}, u32[]{:S(2)}) collective-permute-start(f32[136,256]{1,0:T(8,128)S(1)} %add_add_fusion.1), channel_id=1, source_target_pairs={{0,192},{16,208},{32,224},{48,240},{64,128},{80,144},{96,160},{112... | collective-permute-start | bytes 417800 | tf_op jit(solution)/shard_map/ppermute | solution.py:184
  17.6 9.2 %collective-permute-start.4 = (f32[136,256]{1,0:T(8,128)S(1)}, f32[136,256]{1,0:T(8,128)S(1)}, u32[]{:S(2)}, u32[]{:S(2)}) collective-permute-start(f32[136,256]{1,0:T(8,128)S(1)} %add_add_fusion.1), channel_id=1, source_target_pairs={{0,128},{16,144},{32,160},{48,176},{64,192},{80,208},{96,224},{112... | collective-permute-start | bytes 417800 | tf_op jit(solution)/shard_map/ppermute | solution.py:184
  18.6 10.9 %collective-permute-start.3 = (f32[136,256]{1,0:T(8,128)S(1)}, f32[136,256]{1,0:T(8,128)S(1)}, u32[]{:S(2)}, u32[]{:S(2)}) collective-permute-start(f32[136,256]{1,0:T(8,128)S(1)} %add_add_fusion.1), channel_id=1, source_target_pairs={{0,64},{16,80},{32,96},{48,112},{64,0},{80,16},{96,32},{112,48},{1... | collective-permute-start | bytes 417800 | tf_op jit(solution)/shard_map/ppermute | solution.py:184
  29.5 5.8 %collective-permute-start.8 = (f32[136,256]{1,0:T(8,128)S(1)}, f32[136,256]{1,0:T(8,128)S(1)}, u32[]{:S(2)}, u32[]{:S(2)}) collective-permute-start(f32[136,256]{1,0:T(8,128)S(1)} %add_add_fusion.in0), channel_id=1, source_target_pairs={{0,48},{16,32},{32,16},{48,0},{64,112},{80,96},{96,80},{112,64},{1... | collective-permute-start | bytes 417800 | tf_op jit(solution)/shard_map/ppermute | solution.py:184
  31.9 4.5 %collective-permute-start.7 = (f32[136,256]{1,0:T(8,128)S(1)}, f32[136,256]{1,0:T(8,128)S(1)}, u32[]{:S(2)}, u32[]{:S(2)}) collective-permute-start(f32[136,256]{1,0:T(8,128)S(1)} %add_add_fusion.in0), channel_id=1, source_target_pairs={{0,32},{16,48},{32,0},{48,16},{64,96},{80,112},{96,64},{112,80},{1... | collective-permute-start | bytes 417800 | tf_op jit(solution)/shard_map/ppermute | solution.py:184
  32.0 4.8 %collective-permute-start.6 = (f32[136,256]{1,0:T(8,128)S(1)}, f32[136,256]{1,0:T(8,128)S(1)}, u32[]{:S(2)}, u32[]{:S(2)}) collective-permute-start(f32[136,256]{1,0:T(8,128)S(1)} %add_add_fusion.in0), channel_id=1, source_target_pairs={{0,16},{16,0},{32,48},{48,32},{64,80},{80,64},{96,112},{112,96},{1... | collective-permute-start | bytes 417800 | tf_op jit(solution)/shard_map/ppermute | solution.py:184
  44.0 11.7 %collective-permute-start.9 = (f32[256,256]{1,0:T(8,128)S(1)}, f32[256,256]{1,0:T(8,128)S(1)}, u32[]{:S(2)}, u32[]{:S(2)}) collective-permute-start(f32[256,256]{1,0:T(8,128)S(1)} %get-tuple-element.23), channel_id=1, source_target_pairs={{15,0},{0,1},{1,2},{2,3},{3,4},{4,5},{5,6},{6,7},{7,8},{8,9},{9,10... | collective-permute-start | bytes 786440 | tf_op jit(solution)/shard_map/ppermute | solution.py:180
  52.3 8.8 %collective-permute-start.10 = (f32[256,256]{1,0:T(8,128)S(1)}, f32[256,256]{1,0:T(8,128)S(1)}, u32[]{:S(2)}, u32[]{:S(2)}) collective-permute-start(f32[256,256]{1,0:T(8,128)S(1)} %get-tuple-element.24), channel_id=1, source_target_pairs={{1,0},{2,1},{3,2},{4,3},{5,4},{6,5},{7,6},{8,7},{9,8},{10,9},{11,1... | collective-permute-start | bytes 786440 | tf_op jit(solution)/shard_map/ppermute | solution.py:180
  61.6 3.5 %collective-permute-start.11 = (f32[64,256]{1,0:T(8,128)S(1)}, f32[64,256]{1,0:T(8,128)S(1)}, u32[]{:S(2)}, u32[]{:S(2)}) collective-permute-start(f32[64,256]{1,0:T(8,128)S(1)} %get-tuple-element.26), channel_id=1, source_target_pairs={{0,16},{16,0},{32,48},{48,32},{64,80},{80,64},{96,112},{112,96},{1... | collective-permute-start | bytes 196616 | tf_op jit(solution)/shard_map/ppermute | solution.py:184
  62.3 3.5 %collective-permute-start.12 = (f32[64,256]{1,0:T(8,128)S(1)}, f32[64,256]{1,0:T(8,128)S(1)}, u32[]{:S(2)}, u32[]{:S(2)}) collective-permute-start(f32[64,256]{1,0:T(8,128)S(1)} %get-tuple-element.27), channel_id=1, source_target_pairs={{0,32},{16,48},{32,0},{48,16},{64,96},{80,112},{96,64},{112,80},{1... | collective-permute-start | bytes 196616 | tf_op jit(solution)/shard_map/ppermute | solution.py:184
  62.3 4.5 %collective-permute-start.13 = (f32[64,256]{1,0:T(8,128)S(1)}, f32[64,256]{1,0:T(8,128)S(1)}, u32[]{:S(2)}, u32[]{:S(2)}) collective-permute-start(f32[64,256]{1,0:T(8,128)S(1)} %get-tuple-element.28), channel_id=1, source_target_pairs={{0,48},{16,32},{32,16},{48,0},{64,112},{80,96},{96,80},{112,64},{1... | collective-permute-start | bytes 196616 | tf_op jit(solution)/shard_map/ppermute | solution.py:184
  66.8 10.7 %collective-permute-start.16 = (f32[64,256]{1,0:T(8,128)S(1)}, f32[64,256]{1,0:T(8,128)S(1)}, u32[]{:S(2)}, u32[]{:S(2)}) collective-permute-start(f32[64,256]{1,0:T(8,128)S(1)} %add_add_fusion.3), channel_id=1, source_target_pairs={{0,192},{16,208},{32,224},{48,240},{64,128},{80,144},{96,160},{112... | collective-permute-start | bytes 196616 | tf_op jit(solution)/shard_map/ppermute | solution.py:184
  71.7 7.3 %collective-permute-start.15 = (f32[64,256]{1,0:T(8,128)S(1)}, f32[64,256]{1,0:T(8,128)S(1)}, u32[]{:S(2)}, u32[]{:S(2)}) collective-permute-start(f32[64,256]{1,0:T(8,128)S(1)} %add_add_fusion.3), channel_id=1, source_target_pairs={{0,128},{16,144},{32,160},{48,176},{64,192},{80,208},{96,224},{112... | collective-permute-start | bytes 196616 | tf_op jit(solution)/shard_map/ppermute | solution.py:184
  71.7 7.4 %collective-permute-start.14 = (f32[64,256]{1,0:T(8,128)S(1)}, f32[64,256]{1,0:T(8,128)S(1)}, u32[]{:S(2)}, u32[]{:S(2)}) collective-permute-start(f32[64,256]{1,0:T(8,128)S(1)} %add_add_fusion.3), channel_id=1, source_target_pairs={{0,64},{16,80},{32,96},{48,112},{64,0},{80,16},{96,32},{112,48},{1... | collective-permute-start | bytes 196616 | tf_op jit(solution)/shard_map/ppermute | solution.py:184
  73.9 9.1 %collective-permute-start.20 = (f32[256,256]{1,0:T(8,128)S(1)}, f32[256,256]{1,0:T(8,128)S(1)}, u32[]{:S(2)}, u32[]{:S(2)}) collective-permute-start(f32[256,256]{1,0:T(8,128)S(1)} %get-tuple-element.29), channel_id=1, source_target_pairs={{15,0},{0,1},{1,2},{2,3},{3,4},{4,5},{5,6},{6,7},{7,8},{8,9},{9,10... | collective-permute-start | bytes 786440 | tf_op jit(solution)/shard_map/ppermute | solution.py:180
  76.1 12.2 %collective-permute-start.21 = (f32[256,256]{1,0:T(8,128)S(1)}, f32[256,256]{1,0:T(8,128)S(1)}, u32[]{:S(2)}, u32[]{:S(2)}) collective-permute-start(f32[256,256]{1,0:T(8,128)S(1)} %get-tuple-element.30), channel_id=1, source_target_pairs={{1,0},{2,1},{3,2},{4,3},{5,4},{6,5},{7,6},{8,7},{9,8},{10,9},{11,1... | collective-permute-start | bytes 786440 | tf_op jit(solution)/shard_map/ppermute | solution.py:180
  79.1 9.3 %collective-permute-start.19 = (f32[64,256]{1,0:T(8,128)S(1)}, f32[64,256]{1,0:T(8,128)S(1)}, u32[]{:S(2)}, u32[]{:S(2)}) collective-permute-start(f32[64,256]{1,0:T(8,128)S(1)} %add_add_fusion.2.in0), channel_id=1, source_target_pairs={{0,48},{16,32},{32,16},{48,0},{64,112},{80,96},{96,80},{112,64},{1... | collective-permute-start | bytes 196616 | tf_op jit(solution)/shard_map/ppermute | solution.py:184
  81.8 6.5 %collective-permute-start.18 = (f32[64,256]{1,0:T(8,128)S(1)}, f32[64,256]{1,0:T(8,128)S(1)}, u32[]{:S(2)}, u32[]{:S(2)}) collective-permute-start(f32[64,256]{1,0:T(8,128)S(1)} %add_add_fusion.2.in0), channel_id=1, source_target_pairs={{0,32},{16,48},{32,0},{48,16},{64,96},{80,112},{96,64},{112,80},{1... | collective-permute-start | bytes 196616 | tf_op jit(solution)/shard_map/ppermute | solution.py:184
  81.8 6.5 %collective-permute-start.17 = (f32[64,256]{1,0:T(8,128)S(1)}, f32[64,256]{1,0:T(8,128)S(1)}, u32[]{:S(2)}, u32[]{:S(2)}) collective-permute-start(f32[64,256]{1,0:T(8,128)S(1)} %add_add_fusion.2.in0), channel_id=1, source_target_pairs={{0,16},{16,0},{32,48},{48,32},{64,80},{80,64},{96,112},{112,96},{1... | collective-permute-start | bytes 196616 | tf_op jit(solution)/shard_map/ppermute | solution.py:184
  95.3 8.1 %collective-permute-start.22 = (f32[256,256]{1,0:T(8,128)S(1)}, f32[256,256]{1,0:T(8,128)S(1)}, u32[]{:S(2)}, u32[]{:S(2)}) collective-permute-start(f32[256,256]{1,0:T(8,128)S(1)} %get-tuple-element.31), channel_id=1, source_target_pairs={{15,0},{0,1},{1,2},{2,3},{3,4},{4,5},{5,6},{6,7},{7,8},{8,9},{9,10... | collective-permute-start | bytes 786440 | tf_op jit(solution)/shard_map/ppermute | solution.py:180
  97.3 9.7 %collective-permute-start.23 = (f32[256,256]{1,0:T(8,128)S(1)}, f32[256,256]{1,0:T(8,128)S(1)}, u32[]{:S(2)}, u32[]{:S(2)}) collective-permute-start(f32[256,256]{1,0:T(8,128)S(1)} %get-tuple-element.32), channel_id=1, source_target_pairs={{1,0},{2,1},{3,2},{4,3},{5,4},{6,5},{7,6},{8,7},{9,8},{10,9},{11,1... | collective-permute-start | bytes 786440 | tf_op jit(solution)/shard_map/ppermute | solution.py:180

commit v4 on v3

--- a/solution.py
+++ b/solution.py
@@ -45,8 +45,16 @@
 
 
 def diagonal(block):
-    rows, cols = grid_of(block.shape[0])
-    return jnp.sum(jnp.where(rows == cols, block, 0.0), axis=0, keepdims=True)
+    rows, cols = grid_of(LANES)
+    parts = [
+        jnp.sum(jnp.where(rows == cols, block[t : t + LANES, t : t + LANES], 0.0), 0, keepdims=True)
+        for t in range(0, block.shape[0], LANES)
+    ]
+    return jnp.concatenate(parts, axis=1)
+
+
+def turned_along(vector, back):
+    return pltpu.roll(jnp.broadcast_to(vector, (8, vector.shape[1])), back, 1)[:1]
 
 
 def inner_rounds(shift_ref, tl, tr, lr, upper_ref, lower_ref):
@@ -56,14 +64,22 @@
         half = jnp.transpose(jnp.broadcast_to(vector, (LANES, w)))
         return jnp.concatenate([half] * (w // LANES), axis=1)
 
-    def one_round(r, offset):
+    offset = jnp.int32(0)
+    a = diagonal(tl[...])
+    b = diagonal(lr[...])
+    for r in range(shift_ref.shape[0]):
         target = shift_ref[r]
         back = lax.rem(offset - target + 2 * w, w)
+        offset = target
         top_left = tl[...]
         top_right = pltpu.roll(tr[...], back, 1)
         low_right = pltpu.roll(pltpu.roll(lr[...], back, 1), back, 0)
-        c, s = half_angle(
-            diagonal(top_left) - diagonal(low_right), 2.0 * diagonal(top_right)
+        g = diagonal(top_right)
+        b = turned_along(b, back)
+        c, s = half_angle(a - b, 2.0 * g)
+        a, b = (
+            (c * a + s * g) * c + (c * g + s * b) * s,
+            (c * b - s * g) * c - (c * g - s * a) * s,
         )
         c_rows = as_rows(c)
         s_rows = as_rows(s)
@@ -79,11 +95,8 @@
         lower = pltpu.roll(lower_ref[...], back, 1)
         upper_ref[...] = upper * c + lower * s
         lower_ref[...] = lower * c - upper * s
-        return target
-
-    last = lax.fori_loop(0, shift_ref.shape[0], one_round, jnp.int32(0))
-    lower_ref[...] = pltpu.roll(lower_ref[...], last, 1)
-    lr[...] = pltpu.roll(pltpu.roll(lr[...], last, 1), last, 0)
+    lower_ref[...] = pltpu.roll(lower_ref[...], offset, 1)
+    lr[...] = pltpu.roll(pltpu.roll(lr[...], offset, 1), offset, 0)
 
 
 def full_dot(left, right):
@@ -207,10 +220,8 @@
     upper, lower, tl, lr = kernel_call(
         first_kernel, [block, block, square, square], [SMEM, SMEM] + [VMEM] * 5, [square, diag]
     )(place, shifts[0], *summed_quarters(quarters, "row"), matrix)
-    upper = passed_along(upper, "col", 1)
-    lower = passed_along(lower, "col", -1)
-    tl = passed_along(tl, "col", 1)
-    lr = passed_along(lr, "col", -1)
+    upper = passed_along(upper, "col", 2)
+    tl = passed_along(tl, "col", 2)
 
     quarters = kernel_call(
         cross_kernel, [(w // 4, w)] * 4, [SMEM, VMEM, VMEM], [square]
@@ -218,8 +229,7 @@
     upper, lower = kernel_call(
         second_kernel, [block, block], [SMEM, SMEM] + [VMEM] * 8, [square] * 3
     )(place, shifts[1], *summed_quarters(quarters, "row"), tl, lr, upper, lower)
-    upper = passed_along(upper, "col", 1)
-    lower = passed_along(lower, "col", -1)
+    lower = passed_along(lower, "col", -2)
     return jnp.concatenate([upper, lower], axis=1)
 
 

time: 108 us -> 101 us (0.935)
  the two profiles are of different devices: /device:TPU:1 before, /device:TPU:8 now
where the time goes in v4:
time: 101 us; the launch traced here: 100 us
  waiting for transfers between devices  50.3 us (50%)
  starting transfers between devices  35.4 us (35%)
  Pallas kernels  12.6 us (12%)
  local copies, waits for them, and re-layouts  1.05 us (1%)
    ppermute x18, waiting for transfers between devices, swapped(): lax.ppermute(block, axis, [(i, i ^ bits) for i in range(lax.axis_size(axi...  34.5 us
    ppermute x18, starting transfers between devices, swapped(): lax.ppermute(block, axis, [(i, i ^ bits) for i in range(lax.axis_size(axi...  32.6 us
    ppermute x3, waiting for transfers between devices, passed_along(): return lax.ppermute(block, axis, route)  15.8 us
    pallas_call x1, Pallas kernels, per_device(): kernel_call(first_kernel, [block, block, square, square], [SMEM, SMEM] +...  5.78 us
    pallas_call x1, Pallas kernels, per_device(): kernel_call(second_kernel, [block, block], [SMEM, SMEM] + [VMEM] * 8, [sq...  5.51 us
    ppermute x3, starting transfers between devices, passed_along(): return lax.ppermute(block, axis, route)  2.71 us
  transfers between devices with their start and end apart: 21, of which 19 were waited for; matrix products, arithmetic and copies ran while one was open for 0% of the time, Pallas kernels for 0%

profile of v4, /device:TPU:8, one launch (start us, length us, event | category | flops | bytes accessed | tf_op | source)
XLA Modules:
  0.0 100.4 jit_solution(13130052017083269063)
XLA Ops:
  0.0 0.0 copy-start
  0.0 1.0 %copy-done = f32[256,512]{1,0:T(8,128)S(1)} copy-done((f32[256,512]{1,0:T(8,128)S(1)}, f32[256,512]{1,0:T(8,128)}, u32[]{:S(2)}) %copy-start) | copy-done | bytes 524312
  1.0 0.9 shard_map.28
  1.9 2.3 %collective-permute-start = (f32[136,256]{1,0:T(8,128)S(1)}, f32[136,256]{1,0:T(8,128)S(1)}, u32[]{:S(2)}, u32[]{:S(2)}) collective-permute-start(f32[136,256]{1,0:T(8,128)S(1)} %get-tuple-element.20), channel_id=1, source_target_pairs={{0,16},{16,0},{32,48},{48,32},{64,80},{80,64},{96,112},{112,96},{1... | collective-permute-start | bytes 417800 | tf_op jit(solution)/shard_map/ppermute | solution.py:197
  4.2 0.2 collective-permute-start.1
  4.4 1.4 %collective-permute-start.2 = (f32[136,256]{1,0:T(8,128)S(1)}, f32[136,256]{1,0:T(8,128)S(1)}, u32[]{:S(2)}, u32[]{:S(2)}) collective-permute-start(f32[136,256]{1,0:T(8,128)S(1)} %get-tuple-element.22), channel_id=1, source_target_pairs={{0,48},{16,32},{32,16},{48,0},{64,112},{80,96},{96,80},{112,64},{1... | collective-permute-start | bytes 417800 | tf_op jit(solution)/shard_map/ppermute | solution.py:197
  5.8 1.8 %collective-permute-done = f32[136,256]{1,0:T(8,128)S(1)} collective-permute-done((f32[136,256]{1,0:T(8,128)S(1)}, f32[136,256]{1,0:T(8,128)S(1)}, u32[]{:S(2)}, u32[]{:S(2)}) %collective-permute-start) | collective-permute-done | bytes 139296 | tf_op jit(solution)/shard_map/ppermute | solution.py:197
  7.6 2.6 %collective-permute-done.1 = f32[136,256]{1,0:T(8,128)S(1)} collective-permute-done((f32[136,256]{1,0:T(8,128)S(1)}, f32[136,256]{1,0:T(8,128)S(1)}, u32[]{:S(2)}, u32[]{:S(2)}) %collective-permute-start.1) | collective-permute-done | bytes 139296 | tf_op jit(solution)/shard_map/ppermute | solution.py:197
  10.3 1.5 %collective-permute-done.2 = f32[136,256]{1,0:T(8,128)S(1)} collective-permute-done((f32[136,256]{1,0:T(8,128)S(1)}, f32[136,256]{1,0:T(8,128)S(1)}, u32[]{:S(2)}, u32[]{:S(2)}) %collective-permute-start.2) | collective-permute-done | bytes 139296 | tf_op jit(solution)/shard_map/ppermute | solution.py:197
  11.8 0.0 copy-start.1
  11.8 6.2 %collective-permute-start.5 = (f32[136,256]{1,0:T(8,128)S(1)}, f32[136,256]{1,0:T(8,128)S(1)}, u32[]{:S(2)}, u32[]{:S(2)}) collective-permute-start(f32[136,256]{1,0:T(8,128)S(1)} %add_add_fusion.1), channel_id=1, source_target_pairs={{0,192},{16,208},{32,224},{48,240},{64,128},{80,144},{96,160},{112... | collective-permute-start | bytes 417800 | tf_op jit(solution)/shard_map/ppermute | solution.py:197
  18.0 1.0 collective-permute-start.4
  19.0 1.5 %collective-permute-start.3 = (f32[136,256]{1,0:T(8,128)S(1)}, f32[136,256]{1,0:T(8,128)S(1)}, u32[]{:S(2)}, u32[]{:S(2)}) collective-permute-start(f32[136,256]{1,0:T(8,128)S(1)} %add_add_fusion.1), channel_id=1, source_target_pairs={{0,64},{16,80},{32,96},{48,112},{64,0},{80,16},{96,32},{112,48},{1... | collective-permute-start | bytes 417800 | tf_op jit(solution)/shard_map/ppermute | solution.py:197
  20.5 8.1 %collective-permute-done.5 = f32[136,256]{1,0:T(8,128)S(1)} collective-permute-done((f32[136,256]{1,0:T(8,128)S(1)}, f32[136,256]{1,0:T(8,128)S(1)}, u32[]{:S(2)}, u32[]{:S(2)}) %collective-permute-start.5) | collective-permute-done | bytes 139296 | tf_op jit(solution)/shard_map/ppermute | solution.py:197
  28.6 3.9 %collective-permute-done.4 = f32[136,256]{1,0:T(8,128)S(1)} collective-permute-done((f32[136,256]{1,0:T(8,128)S(1)}, f32[136,256]{1,0:T(8,128)S(1)}, u32[]{:S(2)}, u32[]{:S(2)}) %collective-permute-start.4) | collective-permute-done | bytes 139296 | tf_op jit(solution)/shard_map/ppermute | solution.py:197
  32.6 0.0 collective-permute-done.3
  32.6 0.1 collective-permute-start.8
  32.7 2.4 %collective-permute-start.7 = (f32[136,256]{1,0:T(8,128)S(1)}, f32[136,256]{1,0:T(8,128)S(1)}, u32[]{:S(2)}, u32[]{:S(2)}) collective-permute-start(f32[136,256]{1,0:T(8,128)S(1)} %add_add_fusion.in0), channel_id=1, source_target_pairs={{0,32},{16,48},{32,0},{48,16},{64,96},{80,112},{96,64},{112,80},{1... | collective-permute-start | bytes 417800 | tf_op jit(solution)/shard_map/ppermute | solution.py:197
  35.1 1.1 %collective-permute-start.6 = (f32[136,256]{1,0:T(8,128)S(1)}, f32[136,256]{1,0:T(8,128)S(1)}, u32[]{:S(2)}, u32[]{:S(2)}) collective-permute-start(f32[136,256]{1,0:T(8,128)S(1)} %add_add_fusion.in0), channel_id=1, source_target_pairs={{0,16},{16,0},{32,48},{48,32},{64,80},{80,64},{96,112},{112,96},{1... | collective-permute-start | bytes 417800 | tf_op jit(solution)/shard_map/ppermute | solution.py:197
  36.2 0.0 copy-done.1
  36.2 2.5 %collective-permute-done.8.in3 = f32[136,256]{1,0:T(8,128)S(1)} collective-permute-done((f32[136,256]{1,0:T(8,128)S(1)}, f32[136,256]{1,0:T(8,128)S(1)}, u32[]{:S(2)}, u32[]{:S(2)}) %collective-permute-start.8) | collective-permute-done | bytes 139296 | tf_op jit(solution)/shard_map/ppermute | solution.py:197
  38.6 1.0 collective-permute-done.7.in2
  39.6 0.5 collective-permute-done.6.in1
  40.1 5.8 %shard_map.29 = (f32[256,256]{1,0:T(8,128)S(1)}, f32[256,256]{1,0:T(8,128)S(1)}, f32[256,256]{1,0:T(8,128)S(1)}, f32[256,256]{1,0:T(8,128)S(1)}) custom-call(s32[1]{0:T(128)} %bitcast.place_ref, s32[8]{0:T(128)S(1)} %get-tuple-element.33.shift_ref, f32[136,256]{1,0:T(8,128)S(1)} %add_add_fusion.in0, f32[136,256]{1,0:T(8,128)S(1)} %collective-permute-done.6.in1, ...), custom_call_target="tpu_custom_call" | custom-call | tf_op jit(solution)/shard_map/pallas_call | solution.py:220
  45.9 2.6 %collective-permute-start.9 = (f32[256,256]{1,0:T(8,128)S(1)}, f32[256,256]{1,0:T(8,128)S(1)}, u32[]{:S(2)}, u32[]{:S(2)}) collective-permute-start(f32[256,256]{1,0:T(8,128)S(1)} %get-tuple-element.23), channel_id=1, source_target_pairs={{14,0},{15,1},{0,2},{1,3},{2,4},{3,5},{4,6},{5,7},{6,8},{7,9},{8,1... | collective-permute-start | bytes 786440 | tf_op jit(solution)/shard_map/ppermute | solution.py:193
  48.6 7.5 %collective-permute-done.9.upper_ref.upper_in = f32[256,256]{1,0:T(8,128)S(1)} collective-permute-done((f32[256,256]{1,0:T(8,128)S(1)}, f32[256,256]{1,0:T(8,128)S(1)}, u32[]{:S(2)}, u32[]{:S(2)}) %collective-permute-start.9) | collective-permute-done | bytes 262176 | tf_op jit(solution)/shard_map/ppermute | solution.py:193
  56.1 0.4 shard_map.30
  56.6 1.4 %collective-permute-start.10 = (f32[64,256]{1,0:T(8,128)S(1)}, f32[64,256]{1,0:T(8,128)S(1)}, u32[]{:S(2)}, u32[]{:S(2)}) collective-permute-start(f32[64,256]{1,0:T(8,128)S(1)} %get-tuple-element.26), channel_id=1, source_target_pairs={{0,16},{16,0},{32,48},{48,32},{64,80},{80,64},{96,112},{112,96},{1... | collective-permute-start | bytes 196616 | tf_op jit(solution)/shard_map/ppermute | solution.py:197
  57.9 0.0 collective-permute-start.11
  57.9 2.4 %collective-permute-start.12 = (f32[64,256]{1,0:T(8,128)S(1)}, f32[64,256]{1,0:T(8,128)S(1)}, u32[]{:S(2)}, u32[]{:S(2)}) collective-permute-start(f32[64,256]{1,0:T(8,128)S(1)} %get-tuple-element.28), channel_id=1, source_target_pairs={{0,48},{16,32},{32,16},{48,0},{64,112},{80,96},{96,80},{112,64},{1... | collective-permute-start | bytes 196616 | tf_op jit(solution)/shard_map/ppermute | solution.py:197
  60.3 0.8 collective-permute-done.10
  61.1 1.1 %collective-permute-done.11 = f32[64,256]{1,0:T(8,128)S(1)} collective-permute-done((f32[64,256]{1,0:T(8,128)S(1)}, f32[64,256]{1,0:T(8,128)S(1)}, u32[]{:S(2)}, u32[]{:S(2)}) %collective-permute-start.11) | collective-permute-done | bytes 65568 | tf_op jit(solution)/shard_map/ppermute | solution.py:197
  62.2 1.1 %collective-permute-done.12 = f32[64,256]{1,0:T(8,128)S(1)} collective-permute-done((f32[64,256]{1,0:T(8,128)S(1)}, f32[64,256]{1,0:T(8,128)S(1)}, u32[]{:S(2)}, u32[]{:S(2)}) %collective-permute-start.12) | collective-permute-done | bytes 65568 | tf_op jit(solution)/shard_map/ppermute | solution.py:197
  63.3 6.8 %collective-permute-start.15 = (f32[64,256]{1,0:T(8,128)S(1)}, f32[64,256]{1,0:T(8,128)S(1)}, u32[]{:S(2)}, u32[]{:S(2)}) collective-permute-start(f32[64,256]{1,0:T(8,128)S(1)} %add_add_fusion.3), channel_id=1, source_target_pairs={{0,192},{16,208},{32,224},{48,240},{64,128},{80,144},{96,160},{112... | collective-permute-start | bytes 196616 | tf_op jit(solution)/shard_map/ppermute | solution.py:197
  70.1 0.0 collective-permute-start.14
  70.1 2.5 %collective-permute-start.13 = (f32[64,256]{1,0:T(8,128)S(1)}, f32[64,256]{1,0:T(8,128)S(1)}, u32[]{:S(2)}, u32[]{:S(2)}) collective-permute-start(f32[64,256]{1,0:T(8,128)S(1)} %add_add_fusion.3), channel_id=1, source_target_pairs={{0,64},{16,80},{32,96},{48,112},{64,0},{80,16},{96,32},{112,48},{1... | collective-permute-start | bytes 196616 | tf_op jit(solution)/shard_map/ppermute | solution.py:197
  72.5 0.0 collective-permute-start.19
  72.5 1.3 %collective-permute-done.15 = f32[64,256]{1,0:T(8,128)S(1)} collective-permute-done((f32[64,256]{1,0:T(8,128)S(1)}, f32[64,256]{1,0:T(8,128)S(1)}, u32[]{:S(2)}, u32[]{:S(2)}) %collective-permute-start.15) | collective-permute-done | bytes 65568 | tf_op jit(solution)/shard_map/ppermute | solution.py:197
  73.8 5.5 %collective-permute-done.14 = f32[64,256]{1,0:T(8,128)S(1)} collective-permute-done((f32[64,256]{1,0:T(8,128)S(1)}, f32[64,256]{1,0:T(8,128)S(1)}, u32[]{:S(2)}, u32[]{:S(2)}) %collective-permute-start.14) | collective-permute-done | bytes 65568 | tf_op jit(solution)/shard_map/ppermute | solution.py:197
  79.3 0.0 collective-permute-done.13
  79.3 0.1 collective-permute-start.18
  79.4 2.4 %collective-permute-start.17 = (f32[64,256]{1,0:T(8,128)S(1)}, f32[64,256]{1,0:T(8,128)S(1)}, u32[]{:S(2)}, u32[]{:S(2)}) collective-permute-start(f32[64,256]{1,0:T(8,128)S(1)} %add_add_fusion.2.in0), channel_id=1, source_target_pairs={{0,32},{16,48},{32,0},{48,16},{64,96},{80,112},{96,64},{112,80},{1... | collective-permute-start | bytes 196616 | tf_op jit(solution)/shard_map/ppermute | solution.py:197
  81.8 1.1 %collective-permute-start.16 = (f32[64,256]{1,0:T(8,128)S(1)}, f32[64,256]{1,0:T(8,128)S(1)}, u32[]{:S(2)}, u32[]{:S(2)}) collective-permute-start(f32[64,256]{1,0:T(8,128)S(1)} %add_add_fusion.2.in0), channel_id=1, source_target_pairs={{0,16},{16,0},{32,48},{48,32},{64,80},{80,64},{96,112},{112,96},{1... | collective-permute-start | bytes 196616 | tf_op jit(solution)/shard_map/ppermute | solution.py:197
  82.9 0.4 collective-permute-done.19.tl_ref
  83.3 1.3 %collective-permute-done.18.in3 = f32[64,256]{1,0:T(8,128)S(1)} collective-permute-done((f32[64,256]{1,0:T(8,128)S(1)}, f32[64,256]{1,0:T(8,128)S(1)}, u32[]{:S(2)}, u32[]{:S(2)}) %collective-permute-start.18) | collective-permute-done | bytes 65568 | tf_op jit(solution)/shard_map/ppermute | solution.py:197
  84.6 0.2 collective-permute-done.17.in2
  84.8 1.3 %collective-permute-done.16.in1 = f32[64,256]{1,0:T(8,128)S(1)} collective-permute-done((f32[64,256]{1,0:T(8,128)S(1)}, f32[64,256]{1,0:T(8,128)S(1)}, u32[]{:S(2)}, u32[]{:S(2)}) %collective-permute-start.16) | collective-permute-done | bytes 65568 | tf_op jit(solution)/shard_map/ppermute | solution.py:197
  86.1 5.5 %shard_map.31 = (f32[256,256]{1,0:T(8,128)S(1)}, f32[256,256]{1,0:T(8,128)S(1)}) custom-call(s32[1]{0:T(128)} %bitcast.place_ref, s32[8]{0:T(128)S(1)} %get-tuple-element.34.shift_ref, f32[64,256]{1,0:T(8,128)S(1)} %add_add_fusion.2.in0, f32[64,256]{1,0:T(8,128)S(1)} %collective-permute-done.16.in1, f32[64,256]{1,0:T(8,128)S(1)} %collective-permute-done.17.in2, ...), custom_call_target="tpu_custom_call" | custom-call | tf_op jit(solution)/shard_map/pallas_call | solution.py:229
  91.6 0.1 collective-permute-start.20
  91.7 7.9 %collective-permute-done.20 = f32[256,256]{1,0:T(8,128)S(1)} collective-permute-done((f32[256,256]{1,0:T(8,128)S(1)}, f32[256,256]{1,0:T(8,128)S(1)}, u32[]{:S(2)}, u32[]{:S(2)}) %collective-permute-start.20) | collective-permute-done | bytes 262176 | tf_op jit(solution)/shard_map/ppermute | solution.py:193
  99.6 0.9 pad_maximum_fusion
  (5 shorter events, 0.1 us)
Async XLA Ops:
  0.0 1.0 %copy-start = (f32[256,512]{1,0:T(8,128)S(1)}, f32[256,512]{1,0:T(8,128)}, u32[]{:S(2)}) copy-start(f32[256,512]{1,0:T(8,128)} %pair_ref.3) | copy-start | bytes 1572868
  1.9 5.7 %collective-permute-start = (f32[136,256]{1,0:T(8,128)S(1)}, f32[136,256]{1,0:T(8,128)S(1)}, u32[]{:S(2)}, u32[]{:S(2)}) collective-permute-start(f32[136,256]{1,0:T(8,128)S(1)} %get-tuple-element.20), channel_id=1, source_target_pairs={{0,16},{16,0},{32,48},{48,32},{64,80},{80,64},{96,112},{112,96},{1... | collective-permute-start | bytes 417800 | tf_op jit(solution)/shard_map/ppermute | solution.py:197
  4.2 6.0 %collective-permute-start.1 = (f32[136,256]{1,0:T(8,128)S(1)}, f32[136,256]{1,0:T(8,128)S(1)}, u32[]{:S(2)}, u32[]{:S(2)}) collective-permute-start(f32[136,256]{1,0:T(8,128)S(1)} %get-tuple-element.21), channel_id=1, source_target_pairs={{0,32},{16,48},{32,0},{48,16},{64,96},{80,112},{96,64},{112,80},{1... | collective-permute-start | bytes 417800 | tf_op jit(solution)/shard_map/ppermute | solution.py:197
  4.4 7.4 %collective-permute-start.2 = (f32[136,256]{1,0:T(8,128)S(1)}, f32[136,256]{1,0:T(8,128)S(1)}, u32[]{:S(2)}, u32[]{:S(2)}) collective-permute-start(f32[136,256]{1,0:T(8,128)S(1)} %get-tuple-element.22), channel_id=1, source_target_pairs={{0,48},{16,32},{32,16},{48,0},{64,112},{80,96},{96,80},{112,64},{1... | collective-permute-start | bytes 417800 | tf_op jit(solution)/shard_map/ppermute | solution.py:197
  11.8 24.4 %copy-start.1 = (s32[2,8]{1,0:T(2,128)S(1)}, s32[2,8]{1,0:T(2,128)}, u32[]{:S(2)}) copy-start(s32[2,8]{1,0:T(2,128)} %param.3) | copy-start | bytes 196
  11.8 16.8 %collective-permute-start.5 = (f32[136,256]{1,0:T(8,128)S(1)}, f32[136,256]{1,0:T(8,128)S(1)}, u32[]{:S(2)}, u32[]{:S(2)}) collective-permute-start(f32[136,256]{1,0:T(8,128)S(1)} %add_add_fusion.1), channel_id=1, source_target_pairs={{0,192},{16,208},{32,224},{48,240},{64,128},{80,144},{96,160},{112... | collective-permute-start | bytes 417800 | tf_op jit(solution)/shard_map/ppermute | solution.py:197
  18.0 14.5 %collective-permute-start.4 = (f32[136,256]{1,0:T(8,128)S(1)}, f32[136,256]{1,0:T(8,128)S(1)}, u32[]{:S(2)}, u32[]{:S(2)}) collective-permute-start(f32[136,256]{1,0:T(8,128)S(1)} %add_add_fusion.1), channel_id=1, source_target_pairs={{0,128},{16,144},{32,160},{48,176},{64,192},{80,208},{96,224},{112... | collective-permute-start | bytes 417800 | tf_op jit(solution)/shard_map/ppermute | solution.py:197
  19.0 13.5 %collective-permute-start.3 = (f32[136,256]{1,0:T(8,128)S(1)}, f32[136,256]{1,0:T(8,128)S(1)}, u32[]{:S(2)}, u32[]{:S(2)}) collective-permute-start(f32[136,256]{1,0:T(8,128)S(1)} %add_add_fusion.1), channel_id=1, source_target_pairs={{0,64},{16,80},{32,96},{48,112},{64,0},{80,16},{96,32},{112,48},{1... | collective-permute-start | bytes 417800 | tf_op jit(solution)/shard_map/ppermute | solution.py:197
  32.6 6.0 %collective-permute-start.8 = (f32[136,256]{1,0:T(8,128)S(1)}, f32[136,256]{1,0:T(8,128)S(1)}, u32[]{:S(2)}, u32[]{:S(2)}) collective-permute-start(f32[136,256]{1,0:T(8,128)S(1)} %add_add_fusion.in0), channel_id=1, source_target_pairs={{0,48},{16,32},{32,16},{48,0},{64,112},{80,96},{96,80},{112,64},{1... | collective-permute-start | bytes 417800 | tf_op jit(solution)/shard_map/ppermute | solution.py:197
  32.7 6.9 %collective-permute-start.7 = (f32[136,256]{1,0:T(8,128)S(1)}, f32[136,256]{1,0:T(8,128)S(1)}, u32[]{:S(2)}, u32[]{:S(2)}) collective-permute-start(f32[136,256]{1,0:T(8,128)S(1)} %add_add_fusion.in0), channel_id=1, source_target_pairs={{0,32},{16,48},{32,0},{48,16},{64,96},{80,112},{96,64},{112,80},{1... | collective-permute-start | bytes 417800 | tf_op jit(solution)/shard_map/ppermute | solution.py:197
  35.1 5.1 %collective-permute-start.6 = (f32[136,256]{1,0:T(8,128)S(1)}, f32[136,256]{1,0:T(8,128)S(1)}, u32[]{:S(2)}, u32[]{:S(2)}) collective-permute-start(f32[136,256]{1,0:T(8,128)S(1)} %add_add_fusion.in0), channel_id=1, source_target_pairs={{0,16},{16,0},{32,48},{48,32},{64,80},{80,64},{96,112},{112,96},{1... | collective-permute-start | bytes 417800 | tf_op jit(solution)/shard_map/ppermute | solution.py:197
  45.9 10.2 %collective-permute-start.9 = (f32[256,256]{1,0:T(8,128)S(1)}, f32[256,256]{1,0:T(8,128)S(1)}, u32[]{:S(2)}, u32[]{:S(2)}) collective-permute-start(f32[256,256]{1,0:T(8,128)S(1)} %get-tuple-element.23), channel_id=1, source_target_pairs={{14,0},{15,1},{0,2},{1,3},{2,4},{3,5},{4,6},{5,7},{6,8},{7,9},{8,1... | collective-permute-start | bytes 786440 | tf_op jit(solution)/shard_map/ppermute | solution.py:193
  56.6 4.5 %collective-permute-start.10 = (f32[64,256]{1,0:T(8,128)S(1)}, f32[64,256]{1,0:T(8,128)S(1)}, u32[]{:S(2)}, u32[]{:S(2)}) collective-permute-start(f32[64,256]{1,0:T(8,128)S(1)} %get-tuple-element.26), channel_id=1, source_target_pairs={{0,16},{16,0},{32,48},{48,32},{64,80},{80,64},{96,112},{112,96},{1... | collective-permute-start | bytes 196616 | tf_op jit(solution)/shard_map/ppermute | solution.py:197
  57.9 4.3 %collective-permute-start.11 = (f32[64,256]{1,0:T(8,128)S(1)}, f32[64,256]{1,0:T(8,128)S(1)}, u32[]{:S(2)}, u32[]{:S(2)}) collective-permute-start(f32[64,256]{1,0:T(8,128)S(1)} %get-tuple-element.27), channel_id=1, source_target_pairs={{0,32},{16,48},{32,0},{48,16},{64,96},{80,112},{96,64},{112,80},{1... | collective-permute-start | bytes 196616 | tf_op jit(solution)/shard_map/ppermute | solution.py:197
  57.9 5.3 %collective-permute-start.12 = (f32[64,256]{1,0:T(8,128)S(1)}, f32[64,256]{1,0:T(8,128)S(1)}, u32[]{:S(2)}, u32[]{:S(2)}) collective-permute-start(f32[64,256]{1,0:T(8,128)S(1)} %get-tuple-element.28), channel_id=1, source_target_pairs={{0,48},{16,32},{32,16},{48,0},{64,112},{80,96},{96,80},{112,64},{1... | collective-permute-start | bytes 196616 | tf_op jit(solution)/shard_map/ppermute | solution.py:197
  63.3 10.5 %collective-permute-start.15 = (f32[64,256]{1,0:T(8,128)S(1)}, f32[64,256]{1,0:T(8,128)S(1)}, u32[]{:S(2)}, u32[]{:S(2)}) collective-permute-start(f32[64,256]{1,0:T(8,128)S(1)} %add_add_fusion.3), channel_id=1, source_target_pairs={{0,192},{16,208},{32,224},{48,240},{64,128},{80,144},{96,160},{112... | collective-permute-start | bytes 196616 | tf_op jit(solution)/shard_map/ppermute | solution.py:197
  70.1 9.2 %collective-permute-start.14 = (f32[64,256]{1,0:T(8,128)S(1)}, f32[64,256]{1,0:T(8,128)S(1)}, u32[]{:S(2)}, u32[]{:S(2)}) collective-permute-start(f32[64,256]{1,0:T(8,128)S(1)} %add_add_fusion.3), channel_id=1, source_target_pairs={{0,128},{16,144},{32,160},{48,176},{64,192},{80,208},{96,224},{112... | collective-permute-start | bytes 196616 | tf_op jit(solution)/shard_map/ppermute | solution.py:197
  70.1 9.2 %collective-permute-start.13 = (f32[64,256]{1,0:T(8,128)S(1)}, f32[64,256]{1,0:T(8,128)S(1)}, u32[]{:S(2)}, u32[]{:S(2)}) collective-permute-start(f32[64,256]{1,0:T(8,128)S(1)} %add_add_fusion.3), channel_id=1, source_target_pairs={{0,64},{16,80},{32,96},{48,112},{64,0},{80,16},{96,32},{112,48},{1... | collective-permute-start | bytes 196616 | tf_op jit(solution)/shard_map/ppermute | solution.py:197
  72.5 10.8 %collective-permute-start.19 = (f32[256,256]{1,0:T(8,128)S(1)}, f32[256,256]{1,0:T(8,128)S(1)}, u32[]{:S(2)}, u32[]{:S(2)}) collective-permute-start(f32[256,256]{1,0:T(8,128)S(1)} %get-tuple-element.29), channel_id=1, source_target_pairs={{14,0},{15,1},{0,2},{1,3},{2,4},{3,5},{4,6},{5,7},{6,8},{7,9},{8,1... | collective-permute-start | bytes 786440 | tf_op jit(solution)/shard_map/ppermute | solution.py:193
  79.3 5.3 %collective-permute-start.18 = (f32[64,256]{1,0:T(8,128)S(1)}, f32[64,256]{1,0:T(8,128)S(1)}, u32[]{:S(2)}, u32[]{:S(2)}) collective-permute-start(f32[64,256]{1,0:T(8,128)S(1)} %add_add_fusion.2.in0), channel_id=1, source_target_pairs={{0,48},{16,32},{32,16},{48,0},{64,112},{80,96},{96,80},{112,64},{1... | collective-permute-start | bytes 196616 | tf_op jit(solution)/shard_map/ppermute | solution.py:197
  79.4 5.3 %collective-permute-start.17 = (f32[64,256]{1,0:T(8,128)S(1)}, f32[64,256]{1,0:T(8,128)S(1)}, u32[]{:S(2)}, u32[]{:S(2)}) collective-permute-start(f32[64,256]{1,0:T(8,128)S(1)} %add_add_fusion.2.in0), channel_id=1, source_target_pairs={{0,32},{16,48},{32,0},{48,16},{64,96},{80,112},{96,64},{112,80},{1... | collective-permute-start | bytes 196616 | tf_op jit(solution)/shard_map/ppermute | solution.py:197
  81.8 4.3 %collective-permute-start.16 = (f32[64,256]{1,0:T(8,128)S(1)}, f32[64,256]{1,0:T(8,128)S(1)}, u32[]{:S(2)}, u32[]{:S(2)}) collective-permute-start(f32[64,256]{1,0:T(8,128)S(1)} %add_add_fusion.2.in0), channel_id=1, source_target_pairs={{0,16},{16,0},{32,48},{48,32},{64,80},{80,64},{96,112},{112,96},{1... | collective-permute-start | bytes 196616 | tf_op jit(solution)/shard_map/ppermute | solution.py:197
  91.6 8.0 %collective-permute-start.20 = (f32[256,256]{1,0:T(8,128)S(1)}, f32[256,256]{1,0:T(8,128)S(1)}, u32[]{:S(2)}, u32[]{:S(2)}) collective-permute-start(f32[256,256]{1,0:T(8,128)S(1)} %get-tuple-element.32), channel_id=1, source_target_pairs={{2,0},{3,1},{4,2},{5,3},{6,4},{7,5},{8,6},{9,7},{10,8},{11,9},{12,... | collective-permute-start | bytes 786440 | tf_op jit(solution)/shard_map/ppermute | solution.py:193

commit v5 on v4

--- a/solution.py
+++ b/solution.py
@@ -57,7 +57,7 @@
     return pltpu.roll(jnp.broadcast_to(vector, (8, vector.shape[1])), back, 1)[:1]
 
 
-def inner_rounds(shift_ref, tl, tr, lr, upper_ref, lower_ref):
+def inner_rounds(shift_ref, tl, tr, lr, upper_ref, lower_ref, angles_ref=None):
     w = tl.shape[0]
 
     def as_rows(vector):
@@ -81,6 +81,9 @@
             (c * a + s * g) * c + (c * g + s * b) * s,
             (c * b - s * g) * c - (c * g - s * a) * s,
         )
+        if angles_ref is not None:
+            angles_ref[2 * r : 2 * r + 1, :] = c
+            angles_ref[2 * r + 1 : 2 * r + 2, :] = s
         c_rows = as_rows(c)
         s_rows = as_rows(s)
         low_left = jnp.transpose(top_right)
@@ -99,6 +102,22 @@
     lr[...] = pltpu.roll(pltpu.roll(lr[...], offset, 1), offset, 0)
 
 
+def replayed_rounds(shift_ref, angles_ref, left, right):
+    w = left.shape[1]
+    offset = jnp.int32(0)
+    for r in range(shift_ref.shape[0]):
+        target = shift_ref[r]
+        back = lax.rem(offset - target + 2 * w, w)
+        offset = target
+        c = angles_ref[2 * r : 2 * r + 1, :]
+        s = angles_ref[2 * r + 1 : 2 * r + 2, :]
+        upper = left[...]
+        lower = pltpu.roll(right[...], back, 1)
+        left[...] = upper * c + lower * s
+        right[...] = lower * c - upper * s
+    right[...] = pltpu.roll(right[...], offset, 1)
+
+
 def full_dot(left, right):
     return lax.dot_general(
         left,
@@ -142,13 +161,13 @@
     hand_out(place_ref, (square, cross, diag), outs)
 
 
-def cross_kernel(place_ref, upper_ref, lower_ref, out0, out1, out2, out3, cross):
-    cross[...] = full_dot(upper_ref[...], lower_ref[...])
+def cross_kernel(place_ref, left_ref, right_ref, out0, out1, out2, out3, cross):
+    cross[...] = full_dot(left_ref[...], right_ref[...])
     hand_out(place_ref, (cross,), (out0, out1, out2, out3))
 
 
 def first_kernel(
-    place_ref, shift_ref, in0, in1, in2, in3, pair_ref, upper_ref, lower_ref, tl, lr, tr, diag
+    place_ref, shift_ref, in0, in1, in2, in3, pair_ref, upper_ref, lower_ref, passed_ref, lr, tl, tr, diag
 ):
     w = tl.shape[0]
     rows, cols = grid_of(w)
@@ -159,32 +178,46 @@
     tl[...] = jnp.where(rows <= cols, square, turned)
     upper_ref[...] = pair_ref[:, :w]
     lower_ref[...] = pair_ref[:, w:]
-    inner_rounds(shift_ref, tl, tr, lr, upper_ref, lower_ref)
+    inner_rounds(shift_ref, tl, tr, lr, upper_ref, lower_ref, passed_ref.at[w:, :])
+    passed_ref[:w, :] = tl[...]
 
 
 def second_kernel(
     place_ref,
-    shift_ref,
+    shifts_ref,
     in0,
     in1,
     in2,
     in3,
-    tl_ref,
+    there_ref,
+    here_ref,
     lr_ref,
     upper_in,
     lower_in,
     upper_ref,
     lower_ref,
+    left,
+    right,
+    left_turned,
+    right_turned,
     tl,
     tr,
     lr,
 ):
-    tl[...] = tl_ref[...]
+    w = tl.shape[0]
+    take_in(place_ref, [piece.at[:, :w] for piece in (in0, in1, in2, in3)], (left,))
+    take_in(place_ref, [piece.at[:, w:] for piece in (in0, in1, in2, in3)], (right,))
+    replayed_rounds(shifts_ref.at[0], here_ref.at[w:, :], left, right)
+    turned = jnp.transpose(right[...])
+    left_turned[...] = turned[:, :w]
+    right_turned[...] = turned[:, w:]
+    replayed_rounds(shifts_ref.at[0], there_ref.at[w:, :], left_turned, right_turned)
+    tr[...] = jnp.transpose(left_turned[...])
+    tl[...] = there_ref[:w, :]
     lr[...] = lr_ref[...]
-    take_in(place_ref, (in0, in1, in2, in3), (tr,))
     upper_ref[...] = upper_in[...]
     lower_ref[...] = lower_in[...]
-    inner_rounds(shift_ref, tl, tr, lr, upper_ref, lower_ref)
+    inner_rounds(shifts_ref.at[1], tl, tr, lr, upper_ref, lower_ref)
 
 
 def passed_along(block, axis, distance):
@@ -197,11 +230,17 @@
     return lax.ppermute(block, axis, [(i, i ^ bits) for i in range(lax.axis_size(axis))])
 
 
-def summed_quarters(outs, axis):
+def within_four(outs, axis):
     sent = [swapped(outs[k], axis, k) for k in (3, 1, 2)]
-    mine = (outs[0] + sent[1]) + (sent[2] + sent[0])
+    return (outs[0] + sent[1]) + (sent[2] + sent[0])
+
+
+def across_fours(mine, axis):
     met = [swapped(mine, axis, k) for k in (8, 4, 12)]
-    mine = (mine + met[1]) + (met[0] + met[2])
+    return (mine + met[1]) + (met[0] + met[2])
+
+
+def shared_in_four(mine, axis):
     shared = [swapped(mine, axis, k) for k in (3, 1, 2)]
     return (mine, shared[1], shared[2], shared[0])
 
@@ -212,23 +251,37 @@
     block = (rows, w)
     square = (w, w)
     diag = (32, w)
+    tall = (2 * w, w)
+    passed = (w + 2 * shifts.shape[1], w)
     place = (lax.axis_index("row") % 4).astype(jnp.int32).reshape(1)
 
-    quarters = kernel_call(
+    other = passed_along(matrix, "col", 2)
+    gram = kernel_call(
         gram_kernel, [(2 * w // 4 + 8, w)] * 4, [SMEM, VMEM], [square, square, diag]
     )(place, matrix)
-    upper, lower, tl, lr = kernel_call(
-        first_kernel, [block, block, square, square], [SMEM, SMEM] + [VMEM] * 5, [square, diag]
-    )(place, shifts[0], *summed_quarters(quarters, "row"), matrix)
+    gram = within_four(gram, "row")
+    cross = kernel_call(
+        cross_kernel, [(width // 4, width)] * 4, [SMEM, VMEM, VMEM], [(width, width)]
+    )(place, other, matrix)
+    gram = across_fours(gram, "row")
+    cross = within_four(cross, "row")
+    gram = shared_in_four(gram, "row")
+    cross = across_fours(cross, "row")
+    upper, lower, here, lr = kernel_call(
+        first_kernel,
+        [block, block, passed, square],
+        [SMEM, SMEM] + [VMEM] * 5,
+        [square, square, diag],
+    )(place, shifts[0], *gram, matrix)
+    there = passed_along(here, "col", 2)
     upper = passed_along(upper, "col", 2)
-    tl = passed_along(tl, "col", 2)
-
-    quarters = kernel_call(
-        cross_kernel, [(w // 4, w)] * 4, [SMEM, VMEM, VMEM], [square]
-    )(place, upper, lower)
+    cross = shared_in_four(cross, "row")
     upper, lower = kernel_call(
-        second_kernel, [block, block], [SMEM, SMEM] + [VMEM] * 8, [square] * 3
-    )(place, shifts[1], *summed_quarters(quarters, "row"), tl, lr, upper, lower)
+        second_kernel,
+        [block, block],
+        [SMEM, SMEM] + [VMEM] * 9,
+        [tall, tall] + [square] * 5,
+    )(place, shifts, *cross, there, here, lr, upper, lower)
     lower = passed_along(lower, "col", -2)
     return jnp.concatenate([upper, lower], axis=1)
 

time: 101 us -> 134 us (1.33)
  the two profiles are of different devices: /device:TPU:8 before, /device:TPU:48 now
where the time goes in v5:
time: 134 us
  waiting for transfers between devices  81.1 us (61%)
  starting transfers between devices  34.4 us (26%)
  Pallas kernels  16 us (12%)
    ppermute x18, waiting for transfers between devices, swapped(): lax.ppermute(block, axis, [(i, i ^ bits) for i in range(lax.axis_size(axi...  58.5 us
    ppermute x18, starting transfers between devices, swapped(): lax.ppermute(block, axis, [(i, i ^ bits) for i in range(lax.axis_size(axi...  28.5 us
    ppermute x4, waiting for transfers between devices, passed_along(): return lax.ppermute(block, axis, route)  22.6 us
    pallas_call x1, Pallas kernels, per_device(): kernel_call(second_kernel, [block, block], [SMEM, SMEM] + [VMEM] * 9, [ta...  8.32 us
    ppermute x4, starting transfers between devices, passed_along(): return lax.ppermute(block, axis, route)  5.91 us
    pallas_call x1, Pallas kernels, per_device(): kernel_call(first_kernel, [block, block, passed, square], [SMEM, SMEM] +...  5.72 us
  transfers between devices with their start and end apart: 22, of which 12 were waited for; matrix products, arithmetic and copies ran while one was open for 0% of the time, Pallas kernels for 6%

profile of v5, /device:TPU:48, one launch (start us, length us, event | category | flops | bytes accessed | tf_op | source)
XLA Modules:
  0.0 133.8 jit_solution(13017961586568058608)
XLA Ops:
  0.0 1.3 collective-permute-start
  1.3 0.0 copy-start
  1.3 1.1 copy-done
  2.3 0.0 copy-start.1
  2.3 0.9 shard_map.29
  3.2 2.3 %collective-permute-start.10 = (f32[136,256]{1,0:T(8,128)S(1)}, f32[136,256]{1,0:T(8,128)S(1)}, u32[]{:S(2)}, u32[]{:S(2)}) collective-permute-start(f32[136,256]{1,0:T(8,128)S(1)} %get-tuple-element.24), channel_id=1, source_target_pairs={{0,16},{16,0},{32,48},{48,32},{64,80},{80,64},{96,112},{112,96},{1... | collective-permute-start | bytes 417800 | tf_op jit(solution)/shard_map/ppermute | solution.py:230
  5.5 0.1 collective-permute-start.11
  5.6 1.5 %collective-permute-start.12 = (f32[136,256]{1,0:T(8,128)S(1)}, f32[136,256]{1,0:T(8,128)S(1)}, u32[]{:S(2)}, u32[]{:S(2)}) collective-permute-start(f32[136,256]{1,0:T(8,128)S(1)} %get-tuple-element.26), channel_id=1, source_target_pairs={{0,48},{16,32},{32,16},{48,0},{64,112},{80,96},{96,80},{112,64},{1... | collective-permute-start | bytes 417800 | tf_op jit(solution)/shard_map/ppermute | solution.py:230
  7.1 15.4 %collective-permute-done.10 = f32[136,256]{1,0:T(8,128)S(1)} collective-permute-done((f32[136,256]{1,0:T(8,128)S(1)}, f32[136,256]{1,0:T(8,128)S(1)}, u32[]{:S(2)}, u32[]{:S(2)}) %collective-permute-start.10) | collective-permute-done | bytes 139296 | tf_op jit(solution)/shard_map/ppermute | solution.py:230
  22.4 0.0 collective-permute-done.11
  22.4 0.0 collective-permute-done.12
  22.5 5.5 %collective-permute-start.15 = (f32[136,256]{1,0:T(8,128)S(1)}, f32[136,256]{1,0:T(8,128)S(1)}, u32[]{:S(2)}, u32[]{:S(2)}) collective-permute-start(f32[136,256]{1,0:T(8,128)S(1)} %add_add_fusion.3), channel_id=1, source_target_pairs={{0,192},{16,208},{32,224},{48,240},{64,128},{80,144},{96,160},{112... | collective-permute-start | bytes 417800 | tf_op jit(solution)/shard_map/ppermute | solution.py:230
  28.0 1.4 %collective-permute-start.14 = (f32[136,256]{1,0:T(8,128)S(1)}, f32[136,256]{1,0:T(8,128)S(1)}, u32[]{:S(2)}, u32[]{:S(2)}) collective-permute-start(f32[136,256]{1,0:T(8,128)S(1)} %add_add_fusion.3), channel_id=1, source_target_pairs={{0,128},{16,144},{32,160},{48,176},{64,192},{80,208},{96,224},{112... | collective-permute-start | bytes 417800 | tf_op jit(solution)/shard_map/ppermute | solution.py:230
  29.4 1.0 collective-permute-start.13
  30.4 0.0 collective-permute-done.left_ref
  30.4 0.0 copy-done.1
  30.4 1.1 shard_map.28
  31.6 0.1 collective-permute-start.1
  31.7 1.1 collective-permute-start.2
  32.8 5.8 %collective-permute-done.15 = f32[136,256]{1,0:T(8,128)S(1)} collective-permute-done((f32[136,256]{1,0:T(8,128)S(1)}, f32[136,256]{1,0:T(8,128)S(1)}, u32[]{:S(2)}, u32[]{:S(2)}) %collective-permute-start.15) | collective-permute-done | bytes 139296 | tf_op jit(solution)/shard_map/ppermute | solution.py:230
  38.6 1.0 collective-permute-start.3
  39.5 2.9 %collective-permute-done.14 = f32[136,256]{1,0:T(8,128)S(1)} collective-permute-done((f32[136,256]{1,0:T(8,128)S(1)}, f32[136,256]{1,0:T(8,128)S(1)}, u32[]{:S(2)}, u32[]{:S(2)}) %collective-permute-start.14) | collective-permute-done | bytes 139296 | tf_op jit(solution)/shard_map/ppermute | solution.py:230
  42.5 0.6 collective-permute-done.13
  43.1 0.7 collective-permute-start.18
  43.8 0.0 collective-permute-done.1
  43.8 4.7 %collective-permute-done.2 = f32[128,512]{1,0:T(8,128)S(1)} collective-permute-done((f32[128,512]{1,0:T(8,128)S(1)}, f32[128,512]{1,0:T(8,128)S(1)}, u32[]{:S(2)}, u32[]{:S(2)}) %collective-permute-start.2) | collective-permute-done | bytes 262176 | tf_op jit(solution)/shard_map/ppermute | solution.py:230
  48.6 4.9 %collective-permute-done.3 = f32[128,512]{1,0:T(8,128)S(1)} collective-permute-done((f32[128,512]{1,0:T(8,128)S(1)}, f32[128,512]{1,0:T(8,128)S(1)}, u32[]{:S(2)}, u32[]{:S(2)}) %collective-permute-start.3) | collective-permute-done | bytes 262176 | tf_op jit(solution)/shard_map/ppermute | solution.py:230
  53.5 0.0 copy-start.2
  53.5 0.1 add_add_fusion.1
  53.6 3.4 %collective-permute-start.6 = (f32[128,512]{1,0:T(8,128)S(1)}, f32[128,512]{1,0:T(8,128)S(1)}, u32[]{:S(2)}, u32[]{:S(2)}) collective-permute-start(f32[128,512]{1,0:T(8,128)S(1)} %add_add_fusion.1), channel_id=1, source_target_pairs={{0,192},{16,208},{32,224},{48,240},{64,128},{80,144},{96,160},{112... | collective-permute-start | bytes 786440 | tf_op jit(solution)/shard_map/ppermute | solution.py:230
  57.0 1.8 %collective-permute-start.5 = (f32[128,512]{1,0:T(8,128)S(1)}, f32[128,512]{1,0:T(8,128)S(1)}, u32[]{:S(2)}, u32[]{:S(2)}) collective-permute-start(f32[128,512]{1,0:T(8,128)S(1)} %add_add_fusion.1), channel_id=1, source_target_pairs={{0,128},{16,144},{32,160},{48,176},{64,192},{80,208},{96,224},{112... | collective-permute-start | bytes 786440 | tf_op jit(solution)/shard_map/ppermute | solution.py:230
  58.8 1.3 collective-permute-start.4
  60.2 1.1 collective-permute-start.17
  61.3 0.0 collective-permute-done.18.in3
  61.3 2.2 %collective-permute-start.16 = (f32[136,256]{1,0:T(8,128)S(1)}, f32[136,256]{1,0:T(8,128)S(1)}, u32[]{:S(2)}, u32[]{:S(2)}) collective-permute-start(f32[136,256]{1,0:T(8,128)S(1)} %add_add_fusion.2.in0), channel_id=1, source_target_pairs={{0,16},{16,0},{32,48},{48,32},{64,80},{80,64},{96,112},{112,96},{1... | collective-permute-start | bytes 417800 | tf_op jit(solution)/shard_map/ppermute | solution.py:230
  63.4 0.0 copy-done.2
  63.4 19.6 %collective-permute-done.17.in2 = f32[136,256]{1,0:T(8,128)S(1)} collective-permute-done((f32[136,256]{1,0:T(8,128)S(1)}, f32[136,256]{1,0:T(8,128)S(1)}, u32[]{:S(2)}, u32[]{:S(2)}) %collective-permute-start.17) | collective-permute-done | bytes 139296 | tf_op jit(solution)/shard_map/ppermute | solution.py:230
  83.0 0.0 collective-permute-done.16.in1
  83.0 5.7 %shard_map.30 = (f32[256,256]{1,0:T(8,128)S(1)}, f32[256,256]{1,0:T(8,128)S(1)}, f32[272,256]{1,0:T(8,128)S(1)}, f32[256,256]{1,0:T(8,128)S(1)}) custom-call(s32[1]{0:T(128)} %bitcast.place_ref, s32[8]{0:T(128)S(1)} %slice_bitcast_fusion.shift_ref, f32[136,256]{1,0:T(8,128)S(1)} %add_add_fusion.2.in0, f32[136,256]{1,0:T(8,128)S(1)} %collective-permute-done.16.in1, ...), custom_call_target="tpu_custom_call" | custom-call | tf_op jit(solution)/shard_map/pallas_call | solution.py:270
  88.7 0.1 collective-permute-start.20
  88.8 3.2 %collective-permute-start.19 = (f32[272,256]{1,0:T(8,128)S(1)}, f32[272,256]{1,0:T(8,128)S(1)}, u32[]{:S(2)}, u32[]{:S(2)}) collective-permute-start(f32[272,256]{1,0:T(8,128)S(1)} %get-tuple-element.27.here_ref), channel_id=1, source_target_pairs={{14,0},{15,1},{0,2},{1,3},{2,4},{3,5},{4,6},{5,7},{6,8},{7,9},{8,1... | collective-permute-start | bytes 835592 | tf_op jit(solution)/shard_map/ppermute | solution.py:226
  92.0 0.0 collective-permute-done.6
  92.0 0.0 collective-permute-done.5
  92.0 0.0 collective-permute-done.4
  92.0 0.1 add_add_fusion.in0
  92.1 1.6 %collective-permute-start.9 = (f32[128,512]{1,0:T(8,128)S(1)}, f32[128,512]{1,0:T(8,128)S(1)}, u32[]{:S(2)}, u32[]{:S(2)}) collective-permute-start(f32[128,512]{1,0:T(8,128)S(1)} %add_add_fusion.in0), channel_id=1, source_target_pairs={{0,48},{16,32},{32,16},{48,0},{64,112},{80,96},{96,80},{112,64},{1... | collective-permute-start | bytes 786440 | tf_op jit(solution)/shard_map/ppermute | solution.py:230
  93.7 2.5 %collective-permute-start.8 = (f32[128,512]{1,0:T(8,128)S(1)}, f32[128,512]{1,0:T(8,128)S(1)}, u32[]{:S(2)}, u32[]{:S(2)}) collective-permute-start(f32[128,512]{1,0:T(8,128)S(1)} %add_add_fusion.in0), channel_id=1, source_target_pairs={{0,32},{16,48},{32,0},{48,16},{64,96},{80,112},{96,64},{112,80},{1... | collective-permute-start | bytes 786440 | tf_op jit(solution)/shard_map/ppermute | solution.py:230
  96.2 0.0 collective-permute-start.7
  96.2 8.9 %collective-permute-done.20.upper_in = f32[256,256]{1,0:T(8,128)S(1)} collective-permute-done((f32[256,256]{1,0:T(8,128)S(1)}, f32[256,256]{1,0:T(8,128)S(1)}, u32[]{:S(2)}, u32[]{:S(2)}) %collective-permute-start.20) | collective-permute-done | bytes 262176 | tf_op jit(solution)/shard_map/ppermute | solution.py:226
  105.1 4.4 %collective-permute-done.19.there_ref = f32[272,256]{1,0:T(8,128)S(1)} collective-permute-done((f32[272,256]{1,0:T(8,128)S(1)}, f32[272,256]{1,0:T(8,128)S(1)}, u32[]{:S(2)}, u32[]{:S(2)}) %collective-permute-start.19) | collective-permute-done | bytes 278560 | tf_op jit(solution)/shard_map/ppermute | solution.py:226
  109.5 0.0 collective-permute-done.9.in3
  109.5 0.4 collective-permute-done.8.in2
  109.9 4.0 %collective-permute-done.7.in1 = f32[128,512]{1,0:T(8,128)S(1)} collective-permute-done((f32[128,512]{1,0:T(8,128)S(1)}, f32[128,512]{1,0:T(8,128)S(1)}, u32[]{:S(2)}, u32[]{:S(2)}) %collective-permute-start.7) | collective-permute-done | bytes 262176 | tf_op jit(solution)/shard_map/ppermute | solution.py:230
  113.9 8.3 %shard_map.31 = (f32[256,256]{1,0:T(8,128)S(1)}, f32[256,256]{1,0:T(8,128)S(1)}) custom-call(s32[1]{0:T(128)} %bitcast.place_ref, s32[2,8]{1,0:T(2,128)S(1)} %copy-done.2, f32[128,512]{1,0:T(8,128)S(1)} %add_add_fusion.in0, f32[128,512]{1,0:T(8,128)S(1)} %collective-permute-done.7.in1, f32[128,512]{1,0:T(8,128)S(1)} %collective-permute-done.8.in2, ...), custom_call_target="tpu_custom_call" | custom-call | tf_op jit(solution)/shard_map/pallas_call | solution.py:279
  122.2 1.4 %collective-permute-start.21 = (f32[256,256]{1,0:T(8,128)S(1)}, f32[256,256]{1,0:T(8,128)S(1)}, u32[]{:S(2)}, u32[]{:S(2)}) collective-permute-start(f32[256,256]{1,0:T(8,128)S(1)} %get-tuple-element.32), channel_id=1, source_target_pairs={{2,0},{3,1},{4,2},{5,3},{6,4},{7,5},{8,6},{9,7},{10,8},{11,9},{12,... | collective-permute-start | bytes 786440 | tf_op jit(solution)/shard_map/ppermute | solution.py:226
  123.6 9.3 %collective-permute-done.21 = f32[256,256]{1,0:T(8,128)S(1)} collective-permute-done((f32[256,256]{1,0:T(8,128)S(1)}, f32[256,256]{1,0:T(8,128)S(1)}, u32[]{:S(2)}, u32[]{:S(2)}) %collective-permute-start.21) | collective-permute-done | bytes 262176 | tf_op jit(solution)/shard_map/ppermute | solution.py:226
  133.0 0.9 pad_maximum_fusion
  (3 shorter events, 0.1 us)
Async XLA Ops:
  0.0 30.4 %collective-permute-start = (f32[256,512]{1,0:T(8,128)}, f32[256,512]{1,0:T(8,128)S(1)}, u32[]{:S(2)}, u32[]{:S(2)}) collective-permute-start(f32[256,512]{1,0:T(8,128)} %pair_ref.3), channel_id=1, source_target_pairs={{14,0},{15,1},{0,2},{1,3},{2,4},{3,5},{4,6},{5,7},{6,8},{7,9},{8,1... | collective-permute-start | bytes 1572872 | tf_op jit(solution)/shard_map/ppermute | solution.py:226
  1.3 1.1 copy-start
  2.3 28.1 %copy-start.1 = (f32[256,512]{1,0:T(8,128)S(1)}, f32[256,512]{1,0:T(8,128)}, u32[]{:S(2)}) copy-start(f32[256,512]{1,0:T(8,128)} %pair_ref.3) | copy-start | bytes 1572868
  3.2 19.2 %collective-permute-start.10 = (f32[136,256]{1,0:T(8,128)S(1)}, f32[136,256]{1,0:T(8,128)S(1)}, u32[]{:S(2)}, u32[]{:S(2)}) collective-permute-start(f32[136,256]{1,0:T(8,128)S(1)} %get-tuple-element.24), channel_id=1, source_target_pairs={{0,16},{16,0},{32,48},{48,32},{64,80},{80,64},{96,112},{112,96},{1... | collective-permute-start | bytes 417800 | tf_op jit(solution)/shard_map/ppermute | solution.py:230
  5.5 16.9 %collective-permute-start.11 = (f32[136,256]{1,0:T(8,128)S(1)}, f32[136,256]{1,0:T(8,128)S(1)}, u32[]{:S(2)}, u32[]{:S(2)}) collective-permute-start(f32[136,256]{1,0:T(8,128)S(1)} %get-tuple-element.25), channel_id=1, source_target_pairs={{0,32},{16,48},{32,0},{48,16},{64,96},{80,112},{96,64},{112,80},{1... | collective-permute-start | bytes 417800 | tf_op jit(solution)/shard_map/ppermute | solution.py:230
  5.6 16.8 %collective-permute-start.12 = (f32[136,256]{1,0:T(8,128)S(1)}, f32[136,256]{1,0:T(8,128)S(1)}, u32[]{:S(2)}, u32[]{:S(2)}) collective-permute-start(f32[136,256]{1,0:T(8,128)S(1)} %get-tuple-element.26), channel_id=1, source_target_pairs={{0,48},{16,32},{32,16},{48,0},{64,112},{80,96},{96,80},{112,64},{1... | collective-permute-start | bytes 417800 | tf_op jit(solution)/shard_map/ppermute | solution.py:230
  22.5 16.1 %collective-permute-start.15 = (f32[136,256]{1,0:T(8,128)S(1)}, f32[136,256]{1,0:T(8,128)S(1)}, u32[]{:S(2)}, u32[]{:S(2)}) collective-permute-start(f32[136,256]{1,0:T(8,128)S(1)} %add_add_fusion.3), channel_id=1, source_target_pairs={{0,192},{16,208},{32,224},{48,240},{64,128},{80,144},{96,160},{112... | collective-permute-start | bytes 417800 | tf_op jit(solution)/shard_map/ppermute | solution.py:230
  28.0 14.5 %collective-permute-start.14 = (f32[136,256]{1,0:T(8,128)S(1)}, f32[136,256]{1,0:T(8,128)S(1)}, u32[]{:S(2)}, u32[]{:S(2)}) collective-permute-start(f32[136,256]{1,0:T(8,128)S(1)} %add_add_fusion.3), channel_id=1, source_target_pairs={{0,128},{16,144},{32,160},{48,176},{64,192},{80,208},{96,224},{112... | collective-permute-start | bytes 417800 | tf_op jit(solution)/shard_map/ppermute | solution.py:230
  29.4 13.7 %collective-permute-start.13 = (f32[136,256]{1,0:T(8,128)S(1)}, f32[136,256]{1,0:T(8,128)S(1)}, u32[]{:S(2)}, u32[]{:S(2)}) collective-permute-start(f32[136,256]{1,0:T(8,128)S(1)} %add_add_fusion.3), channel_id=1, source_target_pairs={{0,64},{16,80},{32,96},{48,112},{64,0},{80,16},{96,32},{112,48},{1... | collective-permute-start | bytes 417800 | tf_op jit(solution)/shard_map/ppermute | solution.py:230
  31.6 12.3 %collective-permute-start.1 = (f32[128,512]{1,0:T(8,128)S(1)}, f32[128,512]{1,0:T(8,128)S(1)}, u32[]{:S(2)}, u32[]{:S(2)}) collective-permute-start(f32[128,512]{1,0:T(8,128)S(1)} %get-tuple-element.20), channel_id=1, source_target_pairs={{0,16},{16,0},{32,48},{48,32},{64,80},{80,64},{96,112},{112,96},{1... | collective-permute-start | bytes 786440 | tf_op jit(solution)/shard_map/ppermute | solution.py:230
  31.7 16.9 %collective-permute-start.2 = (f32[128,512]{1,0:T(8,128)S(1)}, f32[128,512]{1,0:T(8,128)S(1)}, u32[]{:S(2)}, u32[]{:S(2)}) collective-permute-start(f32[128,512]{1,0:T(8,128)S(1)} %get-tuple-element.21), channel_id=1, source_target_pairs={{0,32},{16,48},{32,0},{48,16},{64,96},{80,112},{96,64},{112,80},{1... | collective-permute-start | bytes 786440 | tf_op jit(solution)/shard_map/ppermute | solution.py:230
  38.6 14.9 %collective-permute-start.3 = (f32[128,512]{1,0:T(8,128)S(1)}, f32[128,512]{1,0:T(8,128)S(1)}, u32[]{:S(2)}, u32[]{:S(2)}) collective-permute-start(f32[128,512]{1,0:T(8,128)S(1)} %get-tuple-element.22), channel_id=1, source_target_pairs={{0,48},{16,32},{32,16},{48,0},{64,112},{80,96},{96,80},{112,64},{1... | collective-permute-start | bytes 786440 | tf_op jit(solution)/shard_map/ppermute | solution.py:230
  43.1 18.1 %collective-permute-start.18 = (f32[136,256]{1,0:T(8,128)S(1)}, f32[136,256]{1,0:T(8,128)S(1)}, u32[]{:S(2)}, u32[]{:S(2)}) collective-permute-start(f32[136,256]{1,0:T(8,128)S(1)} %add_add_fusion.2.in0), channel_id=1, source_target_pairs={{0,48},{16,32},{32,16},{48,0},{64,112},{80,96},{96,80},{112,64},{1... | collective-permute-start | bytes 417800 | tf_op jit(solution)/shard_map/ppermute | solution.py:230
  53.5 9.9 %copy-start.2 = (s32[2,8]{1,0:T(2,128)S(1)}, s32[2,8]{1,0:T(2,128)}, u32[]{:S(2)}) copy-start(s32[2,8]{1,0:T(2,128)} %shifts_ref.1) | copy-start | bytes 196
  53.6 38.4 %collective-permute-start.6 = (f32[128,512]{1,0:T(8,128)S(1)}, f32[128,512]{1,0:T(8,128)S(1)}, u32[]{:S(2)}, u32[]{:S(2)}) collective-permute-start(f32[128,512]{1,0:T(8,128)S(1)} %add_add_fusion.1), channel_id=1, source_target_pairs={{0,192},{16,208},{32,224},{48,240},{64,128},{80,144},{96,160},{112... | collective-permute-start | bytes 786440 | tf_op jit(solution)/shard_map/ppermute | solution.py:230
  57.0 35.0 %collective-permute-start.5 = (f32[128,512]{1,0:T(8,128)S(1)}, f32[128,512]{1,0:T(8,128)S(1)}, u32[]{:S(2)}, u32[]{:S(2)}) collective-permute-start(f32[128,512]{1,0:T(8,128)S(1)} %add_add_fusion.1), channel_id=1, source_target_pairs={{0,128},{16,144},{32,160},{48,176},{64,192},{80,208},{96,224},{112... | collective-permute-start | bytes 786440 | tf_op jit(solution)/shard_map/ppermute | solution.py:230
  58.8 33.2 %collective-permute-start.4 = (f32[128,512]{1,0:T(8,128)S(1)}, f32[128,512]{1,0:T(8,128)S(1)}, u32[]{:S(2)}, u32[]{:S(2)}) collective-permute-start(f32[128,512]{1,0:T(8,128)S(1)} %add_add_fusion.1), channel_id=1, source_target_pairs={{0,64},{16,80},{32,96},{48,112},{64,0},{80,16},{96,32},{112,48},{1... | collective-permute-start | bytes 786440 | tf_op jit(solution)/shard_map/ppermute | solution.py:230
  60.2 22.8 %collective-permute-start.17 = (f32[136,256]{1,0:T(8,128)S(1)}, f32[136,256]{1,0:T(8,128)S(1)}, u32[]{:S(2)}, u32[]{:S(2)}) collective-permute-start(f32[136,256]{1,0:T(8,128)S(1)} %add_add_fusion.2.in0), channel_id=1, source_target_pairs={{0,32},{16,48},{32,0},{48,16},{64,96},{80,112},{96,64},{112,80},{1... | collective-permute-start | bytes 417800 | tf_op jit(solution)/shard_map/ppermute | solution.py:230
  61.3 21.7 %collective-permute-start.16 = (f32[136,256]{1,0:T(8,128)S(1)}, f32[136,256]{1,0:T(8,128)S(1)}, u32[]{:S(2)}, u32[]{:S(2)}) collective-permute-start(f32[136,256]{1,0:T(8,128)S(1)} %add_add_fusion.2.in0), channel_id=1, source_target_pairs={{0,16},{16,0},{32,48},{48,32},{64,80},{80,64},{96,112},{112,96},{1... | collective-permute-start | bytes 417800 | tf_op jit(solution)/shard_map/ppermute | solution.py:230
  88.7 16.3 %collective-permute-start.20 = (f32[256,256]{1,0:T(8,128)S(1)}, f32[256,256]{1,0:T(8,128)S(1)}, u32[]{:S(2)}, u32[]{:S(2)}) collective-permute-start(f32[256,256]{1,0:T(8,128)S(1)} %get-tuple-element.29), channel_id=1, source_target_pairs={{14,0},{15,1},{0,2},{1,3},{2,4},{3,5},{4,6},{5,7},{6,8},{7,9},{8,1... | collective-permute-start | bytes 786440 | tf_op jit(solution)/shard_map/ppermute | solution.py:226
  88.8 20.7 %collective-permute-start.19 = (f32[272,256]{1,0:T(8,128)S(1)}, f32[272,256]{1,0:T(8,128)S(1)}, u32[]{:S(2)}, u32[]{:S(2)}) collective-permute-start(f32[272,256]{1,0:T(8,128)S(1)} %get-tuple-element.27.here_ref), channel_id=1, source_target_pairs={{14,0},{15,1},{0,2},{1,3},{2,4},{3,5},{4,6},{5,7},{6,8},{7,9},{8,1... | collective-permute-start | bytes 835592 | tf_op jit(solution)/shard_map/ppermute | solution.py:226
  92.1 17.4 %collective-permute-start.9 = (f32[128,512]{1,0:T(8,128)S(1)}, f32[128,512]{1,0:T(8,128)S(1)}, u32[]{:S(2)}, u32[]{:S(2)}) collective-permute-start(f32[128,512]{1,0:T(8,128)S(1)} %add_add_fusion.in0), channel_id=1, source_target_pairs={{0,48},{16,32},{32,16},{48,0},{64,112},{80,96},{96,80},{112,64},{1... | collective-permute-start | bytes 786440 | tf_op jit(solution)/shard_map/ppermute | solution.py:230
  93.7 16.2 %collective-permute-start.8 = (f32[128,512]{1,0:T(8,128)S(1)}, f32[128,512]{1,0:T(8,128)S(1)}, u32[]{:S(2)}, u32[]{:S(2)}) collective-permute-start(f32[128,512]{1,0:T(8,128)S(1)} %add_add_fusion.in0), channel_id=1, source_target_pairs={{0,32},{16,48},{32,0},{48,16},{64,96},{80,112},{96,64},{112,80},{1... | collective-permute-start | bytes 786440 | tf_op jit(solution)/shard_map/ppermute | solution.py:230
  96.2 17.7 %collective-permute-start.7 = (f32[128,512]{1,0:T(8,128)S(1)}, f32[128,512]{1,0:T(8,128)S(1)}, u32[]{:S(2)}, u32[]{:S(2)}) collective-permute-start(f32[128,512]{1,0:T(8,128)S(1)} %add_add_fusion.in0), channel_id=1, source_target_pairs={{0,16},{16,0},{32,48},{48,32},{64,80},{80,64},{96,112},{112,96},{1... | collective-permute-start | bytes 786440 | tf_op jit(solution)/shard_map/ppermute | solution.py:230
  122.2 10.7 %collective-permute-start.21 = (f32[256,256]{1,0:T(8,128)S(1)}, f32[256,256]{1,0:T(8,128)S(1)}, u32[]{:S(2)}, u32[]{:S(2)}) collective-permute-start(f32[256,256]{1,0:T(8,128)S(1)} %get-tuple-element.32), channel_id=1, source_target_pairs={{2,0},{3,1},{4,2},{5,3},{6,4},{7,5},{8,6},{9,7},{10,8},{11,9},{12,... | collective-permute-start | bytes 786440 | tf_op jit(solution)/shard_map/ppermute | solution.py:226

commit v6 on v4

--- a/solution.py
+++ b/solution.py
@@ -6,6 +6,7 @@
 from jax.sharding import PartitionSpec as P
 
 LANES = 128
+BLK = 256
 VMEM = pl.BlockSpec(memory_space=pltpu.VMEM)
 SMEM = pl.BlockSpec(memory_space=pltpu.SMEM)
 
@@ -57,26 +58,32 @@
     return pltpu.roll(jnp.broadcast_to(vector, (8, vector.shape[1])), back, 1)[:1]
 
 
-def inner_rounds(shift_ref, tl, tr, lr, upper_ref, lower_ref):
+def turns(shift_ref):
+    offset = jnp.int32(0)
+    for r in range(shift_ref.shape[0]):
+        target = shift_ref[r]
+        yield r, lax.rem(offset - target + 2 * BLK, BLK)
+        offset = target
+
+
+def inner_rounds(shift_ref, tl, tr, lr, angles_ref):
     w = tl.shape[0]
 
     def as_rows(vector):
         half = jnp.transpose(jnp.broadcast_to(vector, (LANES, w)))
         return jnp.concatenate([half] * (w // LANES), axis=1)
 
-    offset = jnp.int32(0)
     a = diagonal(tl[...])
     b = diagonal(lr[...])
-    for r in range(shift_ref.shape[0]):
-        target = shift_ref[r]
-        back = lax.rem(offset - target + 2 * w, w)
-        offset = target
+    for r, back in turns(shift_ref):
         top_left = tl[...]
         top_right = pltpu.roll(tr[...], back, 1)
         low_right = pltpu.roll(pltpu.roll(lr[...], back, 1), back, 0)
         g = diagonal(top_right)
         b = turned_along(b, back)
         c, s = half_angle(a - b, 2.0 * g)
+        angles_ref[2 * r : 2 * r + 1, :] = c
+        angles_ref[2 * r + 1 : 2 * r + 2, :] = s
         a, b = (
             (c * a + s * g) * c + (c * g + s * b) * s,
             (c * b - s * g) * c - (c * g - s * a) * s,
@@ -91,12 +98,20 @@
         tl[...] = half_tl * c + half_tr * s
         tr[...] = half_tr * c - half_tl * s
         lr[...] = half_lr * c - half_ll * s
+    offset = shift_ref[shift_ref.shape[0] - 1]
+    lr[...] = pltpu.roll(pltpu.roll(lr[...], offset, 1), offset, 0)
+
+
+def rotated(shift_ref, angles_ref, upper_ref, lower_ref):
+    for r, back in turns(shift_ref):
+        c = angles_ref[2 * r : 2 * r + 1, :]
+        s = angles_ref[2 * r + 1 : 2 * r + 2, :]
         upper = upper_ref[...]
         lower = pltpu.roll(lower_ref[...], back, 1)
         upper_ref[...] = upper * c + lower * s
         lower_ref[...] = lower * c - upper * s
+    offset = shift_ref[shift_ref.shape[0] - 1]
     lower_ref[...] = pltpu.roll(lower_ref[...], offset, 1)
-    lr[...] = pltpu.roll(pltpu.roll(lr[...], offset, 1), offset, 0)
 
 
 def full_dot(left, right):
@@ -142,13 +157,8 @@
     hand_out(place_ref, (square, cross, diag), outs)
 
 
-def cross_kernel(place_ref, upper_ref, lower_ref, out0, out1, out2, out3, cross):
-    cross[...] = full_dot(upper_ref[...], lower_ref[...])
-    hand_out(place_ref, (cross,), (out0, out1, out2, out3))
-
-
 def first_kernel(
-    place_ref, shift_ref, in0, in1, in2, in3, pair_ref, upper_ref, lower_ref, tl, lr, tr, diag
+    place_ref, shift_ref, in0, in1, in2, in3, angles_ref, tl, lr, tr, diag
 ):
     w = tl.shape[0]
     rows, cols = grid_of(w)
@@ -157,34 +167,47 @@
     turned = jnp.transpose(square)
     lr[...] = jnp.where(rows == cols, diag[:1, :], jnp.where(rows > cols, square, turned))
     tl[...] = jnp.where(rows <= cols, square, turned)
+    inner_rounds(shift_ref, tl, tr, lr, angles_ref)
+
+
+def own_kernel(shift_ref, angles_ref, pair_ref, upper_ref, lower_ref):
+    w = upper_ref.shape[1]
     upper_ref[...] = pair_ref[:, :w]
     lower_ref[...] = pair_ref[:, w:]
-    inner_rounds(shift_ref, tl, tr, lr, upper_ref, lower_ref)
-
-
-def second_kernel(
-    place_ref,
-    shift_ref,
-    in0,
-    in1,
-    in2,
-    in3,
-    tl_ref,
-    lr_ref,
-    upper_in,
-    lower_in,
-    upper_ref,
-    lower_ref,
-    tl,
-    tr,
-    lr,
+    rotated(shift_ref, angles_ref, upper_ref, lower_ref)
+
+
+def cross_kernel(
+    place_ref, shift_ref, angles_ref, other_ref, lower_ref, upper_ref, out0, out1, out2, out3, rest, cross
 ):
+    w = upper_ref.shape[1]
+    upper_ref[...] = other_ref[:, :w]
+    rest[...] = other_ref[:, w:]
+    rotated(shift_ref, angles_ref, upper_ref, rest)
+    cross[...] = full_dot(upper_ref[...], lower_ref[...])
+    hand_out(place_ref, (cross,), (out0, out1, out2, out3))
+
+
+def second_kernel(place_ref, shift_ref, in0, in1, in2, in3, tl_ref, lr_ref, angles_ref, tl, tr, lr):
     tl[...] = tl_ref[...]
     lr[...] = lr_ref[...]
     take_in(place_ref, (in0, in1, in2, in3), (tr,))
+    inner_rounds(shift_ref, tl, tr, lr, angles_ref)
+
+
+def upper_kernel(shift_ref, angles_ref, upper_in, lower_in, upper_ref, rest):
     upper_ref[...] = upper_in[...]
-    lower_ref[...] = lower_in[...]
-    inner_rounds(shift_ref, tl, tr, lr, upper_ref, lower_ref)
+    rest[...] = lower_in[...]
+    rotated(shift_ref, angles_ref, upper_ref, rest)
+
+
+def lower_kernel(shift_ref, angles_ref, upper_in, lower_in, done_ref, pair_ref, upper, lower):
+    w = done_ref.shape[1]
+    upper[...] = upper_in[...]
+    lower[...] = lower_in[...]
+    pair_ref[:, :w] = done_ref[...]
+    rotated(shift_ref, angles_ref, upper, lower)
+    pair_ref[:, w:] = lower[...]
 
 
 def passed_along(block, axis, distance):
@@ -197,11 +220,17 @@
     return lax.ppermute(block, axis, [(i, i ^ bits) for i in range(lax.axis_size(axis))])
 
 
-def summed_quarters(outs, axis):
+def within_four(outs, axis):
     sent = [swapped(outs[k], axis, k) for k in (3, 1, 2)]
-    mine = (outs[0] + sent[1]) + (sent[2] + sent[0])
+    return (outs[0] + sent[1]) + (sent[2] + sent[0])
+
+
+def across_fours(mine, axis):
     met = [swapped(mine, axis, k) for k in (8, 4, 12)]
-    mine = (mine + met[1]) + (met[0] + met[2])
+    return (mine + met[1]) + (met[0] + met[2])
+
+
+def shared_in_four(mine, axis):
     shared = [swapped(mine, axis, k) for k in (3, 1, 2)]
     return (mine, shared[1], shared[2], shared[0])
 
@@ -212,25 +241,44 @@
     block = (rows, w)
     square = (w, w)
     diag = (32, w)
+    angles = (2 * shifts.shape[1], w)
     place = (lax.axis_index("row") % 4).astype(jnp.int32).reshape(1)
 
-    quarters = kernel_call(
+    gram = kernel_call(
         gram_kernel, [(2 * w // 4 + 8, w)] * 4, [SMEM, VMEM], [square, square, diag]
     )(place, matrix)
-    upper, lower, tl, lr = kernel_call(
-        first_kernel, [block, block, square, square], [SMEM, SMEM] + [VMEM] * 5, [square, diag]
-    )(place, shifts[0], *summed_quarters(quarters, "row"), matrix)
-    upper = passed_along(upper, "col", 2)
+    gram = within_four(gram, "row")
+    gram, sent = lax.optimization_barrier((gram, matrix))
+    other = passed_along(sent, "col", 2)
+    gram = shared_in_four(across_fours(gram, "row"), "row")
+    here, tl, lr = kernel_call(
+        first_kernel, [angles, square, square], [SMEM, SMEM] + [VMEM] * 4, [square, diag]
+    )(place, shifts[0], *gram)
+    there = passed_along(here, "col", 2)
+    own_upper, lower = kernel_call(own_kernel, [block, block], [SMEM, VMEM, VMEM])(
+        shifts[0], here, matrix
+    )
+    upper, *cross = kernel_call(
+        cross_kernel,
+        [block] + [(w // 4, w)] * 4,
+        [SMEM, SMEM] + [VMEM] * 3,
+        [block, square],
+    )(place, shifts[0], there, other, lower)
+    cross = within_four(cross, "row")
     tl = passed_along(tl, "col", 2)
-
-    quarters = kernel_call(
-        cross_kernel, [(w // 4, w)] * 4, [SMEM, VMEM, VMEM], [square]
-    )(place, upper, lower)
-    upper, lower = kernel_call(
-        second_kernel, [block, block], [SMEM, SMEM] + [VMEM] * 8, [square] * 3
-    )(place, shifts[1], *summed_quarters(quarters, "row"), tl, lr, upper, lower)
-    lower = passed_along(lower, "col", -2)
-    return jnp.concatenate([upper, lower], axis=1)
+    far_lower = passed_along(lower, "col", -2)
+    cross = shared_in_four(across_fours(cross, "row"), "row")
+    (here,) = kernel_call(
+        second_kernel, [angles], [SMEM, SMEM] + [VMEM] * 6, [square] * 3
+    )(place, shifts[1], *cross, tl, lr)
+    there = passed_along(here, "col", -2)
+    (upper,) = kernel_call(upper_kernel, [block], [SMEM] + [VMEM] * 3, [block])(
+        shifts[1], here, upper, lower
+    )
+    (pair,) = kernel_call(
+        lower_kernel, [(rows, width)], [SMEM] + [VMEM] * 4, [block, block]
+    )(shifts[1], there, own_upper, far_lower, upper)
+    return pair
 
 
 def solution(mesh):

time: 101 us -> 96.7 us (0.957)
  waiting for transfers between devices: 50.3 us -> 34.4 us
  Pallas kernels: 12.6 us -> 19.6 us
  starting transfers between devices: 35.4 us -> 41.5 us
  local copies, waits for them, and re-layouts: 1.05 us -> 0.01 us
    ppermute x3 -> x5, starting transfers between devices: 2.71 us -> 12 us  [passed_along(): return lax.ppermute(block, axis, route)]
    ppermute x18, waiting for transfers between devices: 34.5 us -> 26.3 us  [swapped(): lax.ppermute(block, axis, [(i, i ^ bits) for i in range(lax.axis_size(axi...]
    ppermute x3 -> x5, waiting for transfers between devices: 15.8 us -> 8.08 us  [passed_along(): return lax.ppermute(block, axis, route)]
    pallas_call x3 -> x6, Pallas kernels: 11.7 us -> 17.7 us  [the longest x1 5.29 us: per_device(): kernel_call(first_kernel, [angles, square, square], [SMEM, SMEM] + [VMEM]...]
    ppermute x18, starting transfers between devices: 32.6 us -> 29.6 us  [swapped(): lax.ppermute(block, axis, [(i, i ^ bits) for i in range(lax.axis_size(axi...]
    unnamed x4 -> x2, local copies, waits for them, and re-layouts: 1.05 us -> 0.01 us
    pallas_call x1, Pallas kernels: 0.88 us -> 1.91 us  [per_device(): kernel_call(gram_kernel, [(2 * w // 4 + 8, w)] * 4, [SMEM, VMEM], [square...]
  transfers between devices with their start and end apart: 21 -> 23, of which waited for: 19 -> 15; matrix products, arithmetic and copies ran while one was open for 0% -> 0% of each run, Pallas kernels for 0% -> 14%
where the time goes in v6:
time: 96.7 us; the launch traced here: 95.8 us
  starting transfers between devices  41.5 us (43%)
  waiting for transfers between devices  34.4 us (36%)
  Pallas kernels  19.6 us (20%)
    ppermute x18, starting transfers between devices, swapped(): lax.ppermute(block, axis, [(i, i ^ bits) for i in range(lax.axis_size(axi...  29.6 us
    ppermute x18, waiting for transfers between devices, swapped(): lax.ppermute(block, axis, [(i, i ^ bits) for i in range(lax.axis_size(axi...  26.3 us
    ppermute x5, starting transfers between devices, passed_along(): return lax.ppermute(block, axis, route)  12 us
    ppermute x5, waiting for transfers between devices, passed_along(): return lax.ppermute(block, axis, route)  8.08 us
    pallas_call x1, Pallas kernels, per_device(): kernel_call(first_kernel, [angles, square, square], [SMEM, SMEM] + [VMEM]...  5.29 us
    pallas_call x1, Pallas kernels, per_device(): kernel_call(second_kernel, [angles], [SMEM, SMEM] + [VMEM] * 6, [square]...  4.48 us
    pallas_call x1, Pallas kernels, per_device(): kernel_call(lower_kernel, [(rows, width)], [SMEM] + [VMEM] * 4, [block, b...  2.48 us
    pallas_call x1, Pallas kernels, per_device(): kernel_call(own_kernel, [block, block], [SMEM, VMEM, VMEM])  2.24 us
  transfers between devices with their start and end apart: 23, of which 15 were waited for; matrix products, arithmetic and copies ran while one was open for 0% of the time, Pallas kernels for 14%

profile of v6, /device:TPU:8, one launch (start us, length us, event | category | flops | bytes accessed | tf_op | source)
XLA Modules:
  0.0 95.8 jit_solution(6176639924628503377)
XLA Ops:
  0.0 1.9 %shard_map.28 = (f32[136,256]{1,0:T(8,128)S(1)}, f32[136,256]{1,0:T(8,128)S(1)}, f32[136,256]{1,0:T(8,128)S(1)}, f32[136,256]{1,0:T(8,128)S(1)}) custom-call(s32[1]{0:T(128)} %bitcast.1.place_ref, f32[256,512]{1,0:T(8,128)} %pair_ref.3), custom_call_target="tpu_custom_call" | custom-call | tf_op jit(solution)/shard_map/pallas_call | solution.py:247
  1.9 2.0 %collective-permute-start.1 = (f32[136,256]{1,0:T(8,128)S(1)}, f32[136,256]{1,0:T(8,128)S(1)}, u32[]{:S(2)}, u32[]{:S(2)}) collective-permute-start(f32[136,256]{1,0:T(8,128)S(1)} %get-tuple-element.23), channel_id=1, source_target_pairs={{0,32},{16,48},{32,0},{48,16},{64,96},{80,112},{96,64},{112,80},{1... | collective-permute-start | bytes 417800 | tf_op jit(solution)/shard_map/ppermute | solution.py:220
  3.9 1.7 %collective-permute-start.2 = (f32[136,256]{1,0:T(8,128)S(1)}, f32[136,256]{1,0:T(8,128)S(1)}, u32[]{:S(2)}, u32[]{:S(2)}) collective-permute-start(f32[136,256]{1,0:T(8,128)S(1)} %get-tuple-element.24), channel_id=1, source_target_pairs={{0,48},{16,32},{32,16},{48,0},{64,112},{80,96},{96,80},{112,64},{1... | collective-permute-start | bytes 417800 | tf_op jit(solution)/shard_map/ppermute | solution.py:220
  5.6 0.0 collective-permute-start
  5.6 2.9 %collective-permute-done.1 = f32[136,256]{1,0:T(8,128)S(1)} collective-permute-done((f32[136,256]{1,0:T(8,128)S(1)}, f32[136,256]{1,0:T(8,128)S(1)}, u32[]{:S(2)}, u32[]{:S(2)}) %collective-permute-start.1) | collective-permute-done | bytes 139296 | tf_op jit(solution)/shard_map/ppermute | solution.py:220
  8.5 2.9 %collective-permute-done.2 = f32[136,256]{1,0:T(8,128)S(1)} collective-permute-done((f32[136,256]{1,0:T(8,128)S(1)}, f32[136,256]{1,0:T(8,128)S(1)}, u32[]{:S(2)}, u32[]{:S(2)}) %collective-permute-start.2) | collective-permute-done | bytes 139296 | tf_op jit(solution)/shard_map/ppermute | solution.py:220
  11.5 1.0 collective-permute-done
  12.5 0.0 copy-start
  12.5 6.6 %collective-permute-start.4 = (f32[136,256]{1,0:T(8,128)S(1)}, f32[136,256]{1,0:T(8,128)S(1)}, u32[]{:S(2)}, u32[]{:S(2)}) collective-permute-start(f32[136,256]{1,0:T(8,128)S(1)} %add_add_fusion.1), channel_id=1, source_target_pairs={{0,128},{16,144},{32,160},{48,176},{64,192},{80,208},{96,224},{112... | collective-permute-start | bytes 417800 | tf_op jit(solution)/shard_map/ppermute | solution.py:220
  19.1 0.0 collective-permute-start.5
  19.1 1.5 %collective-permute-start.3 = (f32[136,256]{1,0:T(8,128)S(1)}, f32[136,256]{1,0:T(8,128)S(1)}, u32[]{:S(2)}, u32[]{:S(2)}) collective-permute-start(f32[136,256]{1,0:T(8,128)S(1)} %add_add_fusion.1), channel_id=1, source_target_pairs={{0,64},{16,80},{32,96},{48,112},{64,0},{80,16},{96,32},{112,48},{1... | collective-permute-start | bytes 417800 | tf_op jit(solution)/shard_map/ppermute | solution.py:220
  20.6 2.6 %collective-permute-start.10 = (f32[256,512]{1,0:T(8,128)}, f32[256,512]{1,0:T(8,128)S(1)}, u32[]{:S(2)}, u32[]{:S(2)}) collective-permute-start(f32[256,512]{1,0:T(8,128)} %pair_ref.3), channel_id=1, source_target_pairs={{14,0},{15,1},{0,2},{1,3},{2,4},{3,5},{4,6},{5,7},{6,8},{7,9},{8,1... | collective-permute-start | bytes 1572872 | tf_op jit(solution)/shard_map/ppermute | solution.py:216
  23.2 2.5 %collective-permute-done.4 = f32[136,256]{1,0:T(8,128)S(1)} collective-permute-done((f32[136,256]{1,0:T(8,128)S(1)}, f32[136,256]{1,0:T(8,128)S(1)}, u32[]{:S(2)}, u32[]{:S(2)}) %collective-permute-start.4) | collective-permute-done | bytes 139296 | tf_op jit(solution)/shard_map/ppermute | solution.py:220
  25.7 4.3 %collective-permute-done.5 = f32[136,256]{1,0:T(8,128)S(1)} collective-permute-done((f32[136,256]{1,0:T(8,128)S(1)}, f32[136,256]{1,0:T(8,128)S(1)}, u32[]{:S(2)}, u32[]{:S(2)}) %collective-permute-start.5) | collective-permute-done | bytes 139296 | tf_op jit(solution)/shard_map/ppermute | solution.py:220
  29.9 1.5 %collective-permute-done.3 = f32[136,256]{1,0:T(8,128)S(1)} collective-permute-done((f32[136,256]{1,0:T(8,128)S(1)}, f32[136,256]{1,0:T(8,128)S(1)}, u32[]{:S(2)}, u32[]{:S(2)}) %collective-permute-start.3) | collective-permute-done | bytes 139296 | tf_op jit(solution)/shard_map/ppermute | solution.py:220
  31.5 1.7 %collective-permute-start.6 = (f32[136,256]{1,0:T(8,128)S(1)}, f32[136,256]{1,0:T(8,128)S(1)}, u32[]{:S(2)}, u32[]{:S(2)}) collective-permute-start(f32[136,256]{1,0:T(8,128)S(1)} %add_add_fusion.in0), channel_id=1, source_target_pairs={{0,16},{16,0},{32,48},{48,32},{64,80},{80,64},{96,112},{112,96},{1... | collective-permute-start | bytes 417800 | tf_op jit(solution)/shard_map/ppermute | solution.py:220
  33.2 0.8 collective-permute-start.7
  33.9 1.1 %collective-permute-start.8 = (f32[136,256]{1,0:T(8,128)S(1)}, f32[136,256]{1,0:T(8,128)S(1)}, u32[]{:S(2)}, u32[]{:S(2)}) collective-permute-start(f32[136,256]{1,0:T(8,128)S(1)} %add_add_fusion.in0), channel_id=1, source_target_pairs={{0,48},{16,32},{32,16},{48,0},{64,112},{80,96},{96,80},{112,64},{1... | collective-permute-start | bytes 417800 | tf_op jit(solution)/shard_map/ppermute | solution.py:220
  35.1 0.0 copy-done
  35.1 6.4 %collective-permute-done.6.in1 = f32[136,256]{1,0:T(8,128)S(1)} collective-permute-done((f32[136,256]{1,0:T(8,128)S(1)}, f32[136,256]{1,0:T(8,128)S(1)}, u32[]{:S(2)}, u32[]{:S(2)}) %collective-permute-start.6) | collective-permute-done | bytes 139296 | tf_op jit(solution)/shard_map/ppermute | solution.py:220
  41.5 0.0 collective-permute-done.7.in2
  41.5 0.0 collective-permute-done.8.in3
  41.5 5.3 %shard_map.29 = (f32[16,256]{1,0:T(8,128)S(1)}, f32[256,256]{1,0:T(8,128)S(1)}, f32[256,256]{1,0:T(8,128)S(1)}) custom-call(s32[1]{0:T(128)} %bitcast.1.place_ref, s32[8]{0:T(128)S(1)} %get-tuple-element.37.shift_ref, f32[136,256]{1,0:T(8,128)S(1)} %add_add_fusion.in0, f32[136,256]{1,0:T(8,128)S(1)} %collective-permute-done.6.in1, ...), custom_call_target="tpu_custom_call" | custom-call | tf_op jit(solution)/shard_map/pallas_call | solution.py:254
  46.8 2.6 %collective-permute-start.9 = (f32[16,256]{1,0:T(8,128)S(1)}, f32[16,256]{1,0:T(8,128)S(1)}, u32[]{:S(2)}, u32[]{:S(2)}) collective-permute-start(f32[16,256]{1,0:T(8,128)S(1)} %get-tuple-element.26.angles_ref), channel_id=1, source_target_pairs={{14,0},{15,1},{0,2},{1,3},{2,4},{3,5},{4,6},{5,7},{6,8},{7,9},{8,1... | collective-permute-start | bytes 49160 | tf_op jit(solution)/shard_map/ppermute | solution.py:216
  49.4 2.2 %shard_map.30 = (f32[256,256]{1,0:T(8,128)S(1)}, f32[256,256]{1,0:T(8,128)S(1)}) custom-call(s32[8]{0:T(128)S(1)} %get-tuple-element.37.shift_ref, f32[16,256]{1,0:T(8,128)S(1)} %get-tuple-element.26.angles_ref, f32[256,512]{1,0:T(8,128)} %pair_ref.3), custom_call_target="tpu_custom_call" | custom-call | tf_op jit(solution)/shard_map/pallas_call | solution.py:258
  51.7 2.7 %collective-permute-done.9.angles_ref = f32[16,256]{1,0:T(8,128)S(1)} collective-permute-done((f32[16,256]{1,0:T(8,128)S(1)}, f32[16,256]{1,0:T(8,128)S(1)}, u32[]{:S(2)}, u32[]{:S(2)}) %collective-permute-start.9) | collective-permute-done | bytes 16416 | tf_op jit(solution)/shard_map/ppermute | solution.py:216
  54.4 0.0 collective-permute-done.10.other_ref
  54.4 1.6 %shard_map.31 = (f32[256,256]{1,0:T(8,128)S(1)}, f32[64,256]{1,0:T(8,128)S(1)}, f32[64,256]{1,0:T(8,128)S(1)}, f32[64,256]{1,0:T(8,128)S(1)}, f32[64,256]{1,0:T(8,128)S(1)}) custom-call(s32[1]{0:T(128)} %bitcast.1.place_ref, s32[8]{0:T(128)S(1)} %get-tuple-element.37.shift_ref, f32[16,256]{1,0:T(8,128)S(1)} %collective-permute-done.9.angles_ref, ...), custom_call_target="tpu_custom_call" | custom-call | tf_op jit(solution)/shard_map/pallas_call | solution.py:261
  56.0 1.1 %collective-permute-start.12 = (f32[64,256]{1,0:T(8,128)S(1)}, f32[64,256]{1,0:T(8,128)S(1)}, u32[]{:S(2)}, u32[]{:S(2)}) collective-permute-start(f32[64,256]{1,0:T(8,128)S(1)} %get-tuple-element.31), channel_id=1, source_target_pairs={{0,32},{16,48},{32,0},{48,16},{64,96},{80,112},{96,64},{112,80},{1... | collective-permute-start | bytes 196616 | tf_op jit(solution)/shard_map/ppermute | solution.py:220
  57.1 1.8 %collective-permute-start.13 = (f32[64,256]{1,0:T(8,128)S(1)}, f32[64,256]{1,0:T(8,128)S(1)}, u32[]{:S(2)}, u32[]{:S(2)}) collective-permute-start(f32[64,256]{1,0:T(8,128)S(1)} %get-tuple-element.32), channel_id=1, source_target_pairs={{0,48},{16,32},{32,16},{48,0},{64,112},{80,96},{96,80},{112,64},{1... | collective-permute-start | bytes 196616 | tf_op jit(solution)/shard_map/ppermute | solution.py:220
  59.0 0.6 collective-permute-start.11
  59.6 0.8 collective-permute-done.12
  60.4 1.9 %collective-permute-done.13 = f32[64,256]{1,0:T(8,128)S(1)} collective-permute-done((f32[64,256]{1,0:T(8,128)S(1)}, f32[64,256]{1,0:T(8,128)S(1)}, u32[]{:S(2)}, u32[]{:S(2)}) %collective-permute-start.13) | collective-permute-done | bytes 65568 | tf_op jit(solution)/shard_map/ppermute | solution.py:220
  62.3 0.9 collective-permute-done.11
  63.2 4.4 %collective-permute-start.15 = (f32[64,256]{1,0:T(8,128)S(1)}, f32[64,256]{1,0:T(8,128)S(1)}, u32[]{:S(2)}, u32[]{:S(2)}) collective-permute-start(f32[64,256]{1,0:T(8,128)S(1)} %add_add_fusion.3), channel_id=1, source_target_pairs={{0,128},{16,144},{32,160},{48,176},{64,192},{80,208},{96,224},{112... | collective-permute-start | bytes 196616 | tf_op jit(solution)/shard_map/ppermute | solution.py:220
  67.6 0.9 collective-permute-start.16
  68.5 1.3 %collective-permute-start.14 = (f32[64,256]{1,0:T(8,128)S(1)}, f32[64,256]{1,0:T(8,128)S(1)}, u32[]{:S(2)}, u32[]{:S(2)}) collective-permute-start(f32[64,256]{1,0:T(8,128)S(1)} %add_add_fusion.3), channel_id=1, source_target_pairs={{0,64},{16,80},{32,96},{48,112},{64,0},{80,16},{96,32},{112,48},{1... | collective-permute-start | bytes 196616 | tf_op jit(solution)/shard_map/ppermute | solution.py:220
  69.8 2.4 %collective-permute-start.22 = (f32[256,256]{1,0:T(8,128)S(1)}, f32[256,256]{1,0:T(8,128)S(1)}, u32[]{:S(2)}, u32[]{:S(2)}) collective-permute-start(f32[256,256]{1,0:T(8,128)S(1)} %get-tuple-element.28.lower_ref.lower_in), channel_id=1, source_target_pairs={{2,0},{3,1},{4,2},{5,3},{6,4},{7,5},{8,6},{9,7},{10,8},{11,9},{12,... | collective-permute-start | bytes 786440 | tf_op jit(solution)/shard_map/ppermute | solution.py:216
  72.2 1.2 %collective-permute-start.20 = (f32[256,256]{1,0:T(8,128)S(1)}, f32[256,256]{1,0:T(8,128)S(1)}, u32[]{:S(2)}, u32[]{:S(2)}) collective-permute-start(f32[256,256]{1,0:T(8,128)S(1)} %get-tuple-element.33), channel_id=1, source_target_pairs={{14,0},{15,1},{0,2},{1,3},{2,4},{3,5},{4,6},{5,7},{6,8},{7,9},{8,1... | collective-permute-start | bytes 786440 | tf_op jit(solution)/shard_map/ppermute | solution.py:216
  73.4 0.0 collective-permute-done.15
  73.4 0.7 collective-permute-done.16
  74.1 0.0 collective-permute-done.14
  74.1 1.4 %collective-permute-start.17 = (f32[64,256]{1,0:T(8,128)S(1)}, f32[64,256]{1,0:T(8,128)S(1)}, u32[]{:S(2)}, u32[]{:S(2)}) collective-permute-start(f32[64,256]{1,0:T(8,128)S(1)} %add_add_fusion.2.in0), channel_id=1, source_target_pairs={{0,16},{16,0},{32,48},{48,32},{64,80},{80,64},{96,112},{112,96},{1... | collective-permute-start | bytes 196616 | tf_op jit(solution)/shard_map/ppermute | solution.py:220
  75.5 1.5 %collective-permute-start.18 = (f32[64,256]{1,0:T(8,128)S(1)}, f32[64,256]{1,0:T(8,128)S(1)}, u32[]{:S(2)}, u32[]{:S(2)}) collective-permute-start(f32[64,256]{1,0:T(8,128)S(1)} %add_add_fusion.2.in0), channel_id=1, source_target_pairs={{0,32},{16,48},{32,0},{48,16},{64,96},{80,112},{96,64},{112,80},{1... | collective-permute-start | bytes 196616 | tf_op jit(solution)/shard_map/ppermute | solution.py:220
  77.0 1.2 %collective-permute-start.19 = (f32[64,256]{1,0:T(8,128)S(1)}, f32[64,256]{1,0:T(8,128)S(1)}, u32[]{:S(2)}, u32[]{:S(2)}) collective-permute-start(f32[64,256]{1,0:T(8,128)S(1)} %add_add_fusion.2.in0), channel_id=1, source_target_pairs={{0,48},{16,32},{32,16},{48,0},{64,112},{80,96},{96,80},{112,64},{1... | collective-permute-start | bytes 196616 | tf_op jit(solution)/shard_map/ppermute | solution.py:220
  78.2 4.8 %collective-permute-done.20.tl_ref = f32[256,256]{1,0:T(8,128)S(1)} collective-permute-done((f32[256,256]{1,0:T(8,128)S(1)}, f32[256,256]{1,0:T(8,128)S(1)}, u32[]{:S(2)}, u32[]{:S(2)}) %collective-permute-start.20) | collective-permute-done | bytes 262176 | tf_op jit(solution)/shard_map/ppermute | solution.py:216
  83.0 0.5 collective-permute-done.17.in1
  83.4 0.0 collective-permute-done.18.in2
  83.5 0.0 collective-permute-done.19.in3
  83.5 4.5 %shard_map.32.angles_ref = f32[16,256]{1,0:T(8,128)S(1)} custom-call(s32[1]{0:T(128)} %bitcast.1.place_ref, s32[8]{0:T(128)S(1)} %get-tuple-element.38.shift_ref, f32[64,256]{1,0:T(8,128)S(1)} %add_add_fusion.2.in0, f32[64,256]{1,0:T(8,128)S(1)} %collective-permute-done.17.in1, f32[64,256]{1,0:T(8,128)S(1)} %collective-permute-done.18.in2, ...), custom_call_target="tpu_custom_call" | custom-call | tf_op jit(solution)/shard_map/pallas_call | solution.py:271
  87.9 3.2 %collective-permute-start.21 = (f32[16,256]{1,0:T(8,128)S(1)}, f32[16,256]{1,0:T(8,128)S(1)}, u32[]{:S(2)}, u32[]{:S(2)}) collective-permute-start(f32[16,256]{1,0:T(8,128)S(1)} %shard_map.32.angles_ref), channel_id=1, source_target_pairs={{2,0},{3,1},{4,2},{5,3},{6,4},{7,5},{8,6},{9,7},{10,8},{11,9},{12,... | collective-permute-start | bytes 49160 | tf_op jit(solution)/shard_map/ppermute | solution.py:216
  91.1 1.6 %shard_map.33.done_ref = f32[256,256]{1,0:T(8,128)S(1)} custom-call(s32[8]{0:T(128)S(1)} %get-tuple-element.38.shift_ref, f32[16,256]{1,0:T(8,128)S(1)} %shard_map.32.angles_ref, f32[256,256]{1,0:T(8,128)S(1)} %get-tuple-element.36.upper_in, f32[256,256]{1,0:T(8,128)S(1)} %get-tuple-element.28.lower_ref.lower_in), custom_call_target="tpu_custom_call" | custom-call | tf_op jit(solution)/shard_map/pallas_call | solution.py:275
  92.7 0.0 collective-permute-done.22.lower_in
  92.7 0.5 collective-permute-done.21.angles_ref
  93.3 2.5 %shard_map.34 = f32[256,512]{1,0:T(8,128)} custom-call(s32[8]{0:T(128)S(1)} %get-tuple-element.38.shift_ref, f32[16,256]{1,0:T(8,128)S(1)} %collective-permute-done.21.angles_ref, f32[256,256]{1,0:T(8,128)S(1)} %get-tuple-element.35.upper_in, f32[256,256]{1,0:T(8,128)S(1)} %collective-permute-done.22.lower_in, f32[256,256]{1,0:T(8,128)S(1)} %shard_map.33.done_ref), custom_call_target="tpu_custom_call" | custom-call | tf_op jit(solution)/shard_map/pallas_call | solution.py:278
  (5 shorter events, 0.1 us)
Async XLA Ops:
  1.9 6.6 %collective-permute-start.1 = (f32[136,256]{1,0:T(8,128)S(1)}, f32[136,256]{1,0:T(8,128)S(1)}, u32[]{:S(2)}, u32[]{:S(2)}) collective-permute-start(f32[136,256]{1,0:T(8,128)S(1)} %get-tuple-element.23), channel_id=1, source_target_pairs={{0,32},{16,48},{32,0},{48,16},{64,96},{80,112},{96,64},{112,80},{1... | collective-permute-start | bytes 417800 | tf_op jit(solution)/shard_map/ppermute | solution.py:220
  3.9 7.6 %collective-permute-start.2 = (f32[136,256]{1,0:T(8,128)S(1)}, f32[136,256]{1,0:T(8,128)S(1)}, u32[]{:S(2)}, u32[]{:S(2)}) collective-permute-start(f32[136,256]{1,0:T(8,128)S(1)} %get-tuple-element.24), channel_id=1, source_target_pairs={{0,48},{16,32},{32,16},{48,0},{64,112},{80,96},{96,80},{112,64},{1... | collective-permute-start | bytes 417800 | tf_op jit(solution)/shard_map/ppermute | solution.py:220
  5.6 6.8 %collective-permute-start = (f32[136,256]{1,0:T(8,128)S(1)}, f32[136,256]{1,0:T(8,128)S(1)}, u32[]{:S(2)}, u32[]{:S(2)}) collective-permute-start(f32[136,256]{1,0:T(8,128)S(1)} %get-tuple-element.22), channel_id=1, source_target_pairs={{0,16},{16,0},{32,48},{48,32},{64,80},{80,64},{96,112},{112,96},{1... | collective-permute-start | bytes 417800 | tf_op jit(solution)/shard_map/ppermute | solution.py:220
  12.5 22.6 %copy-start = (s32[2,8]{1,0:T(2,128)S(1)}, s32[2,8]{1,0:T(2,128)}, u32[]{:S(2)}) copy-start(s32[2,8]{1,0:T(2,128)} %param.3) | copy-start | bytes 196
  12.5 13.2 %collective-permute-start.4 = (f32[136,256]{1,0:T(8,128)S(1)}, f32[136,256]{1,0:T(8,128)S(1)}, u32[]{:S(2)}, u32[]{:S(2)}) collective-permute-start(f32[136,256]{1,0:T(8,128)S(1)} %add_add_fusion.1), channel_id=1, source_target_pairs={{0,128},{16,144},{32,160},{48,176},{64,192},{80,208},{96,224},{112... | collective-permute-start | bytes 417800 | tf_op jit(solution)/shard_map/ppermute | solution.py:220
  19.1 10.8 %collective-permute-start.5 = (f32[136,256]{1,0:T(8,128)S(1)}, f32[136,256]{1,0:T(8,128)S(1)}, u32[]{:S(2)}, u32[]{:S(2)}) collective-permute-start(f32[136,256]{1,0:T(8,128)S(1)} %add_add_fusion.1), channel_id=1, source_target_pairs={{0,192},{16,208},{32,224},{48,240},{64,128},{80,144},{96,160},{112... | collective-permute-start | bytes 417800 | tf_op jit(solution)/shard_map/ppermute | solution.py:220
  19.1 12.4 %collective-permute-start.3 = (f32[136,256]{1,0:T(8,128)S(1)}, f32[136,256]{1,0:T(8,128)S(1)}, u32[]{:S(2)}, u32[]{:S(2)}) collective-permute-start(f32[136,256]{1,0:T(8,128)S(1)} %add_add_fusion.1), channel_id=1, source_target_pairs={{0,64},{16,80},{32,96},{48,112},{64,0},{80,16},{96,32},{112,48},{1... | collective-permute-start | bytes 417800 | tf_op jit(solution)/shard_map/ppermute | solution.py:220
  20.6 33.8 %collective-permute-start.10 = (f32[256,512]{1,0:T(8,128)}, f32[256,512]{1,0:T(8,128)S(1)}, u32[]{:S(2)}, u32[]{:S(2)}) collective-permute-start(f32[256,512]{1,0:T(8,128)} %pair_ref.3), channel_id=1, source_target_pairs={{14,0},{15,1},{0,2},{1,3},{2,4},{3,5},{4,6},{5,7},{6,8},{7,9},{8,1... | collective-permute-start | bytes 1572872 | tf_op jit(solution)/shard_map/ppermute | solution.py:216
  31.5 10.0 %collective-permute-start.6 = (f32[136,256]{1,0:T(8,128)S(1)}, f32[136,256]{1,0:T(8,128)S(1)}, u32[]{:S(2)}, u32[]{:S(2)}) collective-permute-start(f32[136,256]{1,0:T(8,128)S(1)} %add_add_fusion.in0), channel_id=1, source_target_pairs={{0,16},{16,0},{32,48},{48,32},{64,80},{80,64},{96,112},{112,96},{1... | collective-permute-start | bytes 417800 | tf_op jit(solution)/shard_map/ppermute | solution.py:220
  33.2 8.3 %collective-permute-start.7 = (f32[136,256]{1,0:T(8,128)S(1)}, f32[136,256]{1,0:T(8,128)S(1)}, u32[]{:S(2)}, u32[]{:S(2)}) collective-permute-start(f32[136,256]{1,0:T(8,128)S(1)} %add_add_fusion.in0), channel_id=1, source_target_pairs={{0,32},{16,48},{32,0},{48,16},{64,96},{80,112},{96,64},{112,80},{1... | collective-permute-start | bytes 417800 | tf_op jit(solution)/shard_map/ppermute | solution.py:220
  33.9 7.5 %collective-permute-start.8 = (f32[136,256]{1,0:T(8,128)S(1)}, f32[136,256]{1,0:T(8,128)S(1)}, u32[]{:S(2)}, u32[]{:S(2)}) collective-permute-start(f32[136,256]{1,0:T(8,128)S(1)} %add_add_fusion.in0), channel_id=1, source_target_pairs={{0,48},{16,32},{32,16},{48,0},{64,112},{80,96},{96,80},{112,64},{1... | collective-permute-start | bytes 417800 | tf_op jit(solution)/shard_map/ppermute | solution.py:220
  46.8 7.6 %collective-permute-start.9 = (f32[16,256]{1,0:T(8,128)S(1)}, f32[16,256]{1,0:T(8,128)S(1)}, u32[]{:S(2)}, u32[]{:S(2)}) collective-permute-start(f32[16,256]{1,0:T(8,128)S(1)} %get-tuple-element.26.angles_ref), channel_id=1, source_target_pairs={{14,0},{15,1},{0,2},{1,3},{2,4},{3,5},{4,6},{5,7},{6,8},{7,9},{8,1... | collective-permute-start | bytes 49160 | tf_op jit(solution)/shard_map/ppermute | solution.py:216
  56.0 4.4 %collective-permute-start.12 = (f32[64,256]{1,0:T(8,128)S(1)}, f32[64,256]{1,0:T(8,128)S(1)}, u32[]{:S(2)}, u32[]{:S(2)}) collective-permute-start(f32[64,256]{1,0:T(8,128)S(1)} %get-tuple-element.31), channel_id=1, source_target_pairs={{0,32},{16,48},{32,0},{48,16},{64,96},{80,112},{96,64},{112,80},{1... | collective-permute-start | bytes 196616 | tf_op jit(solution)/shard_map/ppermute | solution.py:220
  57.1 5.2 %collective-permute-start.13 = (f32[64,256]{1,0:T(8,128)S(1)}, f32[64,256]{1,0:T(8,128)S(1)}, u32[]{:S(2)}, u32[]{:S(2)}) collective-permute-start(f32[64,256]{1,0:T(8,128)S(1)} %get-tuple-element.32), channel_id=1, source_target_pairs={{0,48},{16,32},{32,16},{48,0},{64,112},{80,96},{96,80},{112,64},{1... | collective-permute-start | bytes 196616 | tf_op jit(solution)/shard_map/ppermute | solution.py:220
  59.0 4.3 %collective-permute-start.11 = (f32[64,256]{1,0:T(8,128)S(1)}, f32[64,256]{1,0:T(8,128)S(1)}, u32[]{:S(2)}, u32[]{:S(2)}) collective-permute-start(f32[64,256]{1,0:T(8,128)S(1)} %get-tuple-element.30), channel_id=1, source_target_pairs={{0,16},{16,0},{32,48},{48,32},{64,80},{80,64},{96,112},{112,96},{1... | collective-permute-start | bytes 196616 | tf_op jit(solution)/shard_map/ppermute | solution.py:220
  63.2 10.1 %collective-permute-start.15 = (f32[64,256]{1,0:T(8,128)S(1)}, f32[64,256]{1,0:T(8,128)S(1)}, u32[]{:S(2)}, u32[]{:S(2)}) collective-permute-start(f32[64,256]{1,0:T(8,128)S(1)} %add_add_fusion.3), channel_id=1, source_target_pairs={{0,128},{16,144},{32,160},{48,176},{64,192},{80,208},{96,224},{112... | collective-permute-start | bytes 196616 | tf_op jit(solution)/shard_map/ppermute | solution.py:220
  67.6 6.5 %collective-permute-start.16 = (f32[64,256]{1,0:T(8,128)S(1)}, f32[64,256]{1,0:T(8,128)S(1)}, u32[]{:S(2)}, u32[]{:S(2)}) collective-permute-start(f32[64,256]{1,0:T(8,128)S(1)} %add_add_fusion.3), channel_id=1, source_target_pairs={{0,192},{16,208},{32,224},{48,240},{64,128},{80,144},{96,160},{112... | collective-permute-start | bytes 196616 | tf_op jit(solution)/shard_map/ppermute | solution.py:220
  68.5 5.6 %collective-permute-start.14 = (f32[64,256]{1,0:T(8,128)S(1)}, f32[64,256]{1,0:T(8,128)S(1)}, u32[]{:S(2)}, u32[]{:S(2)}) collective-permute-start(f32[64,256]{1,0:T(8,128)S(1)} %add_add_fusion.3), channel_id=1, source_target_pairs={{0,64},{16,80},{32,96},{48,112},{64,0},{80,16},{96,32},{112,48},{1... | collective-permute-start | bytes 196616 | tf_op jit(solution)/shard_map/ppermute | solution.py:220
  69.8 22.9 %collective-permute-start.22 = (f32[256,256]{1,0:T(8,128)S(1)}, f32[256,256]{1,0:T(8,128)S(1)}, u32[]{:S(2)}, u32[]{:S(2)}) collective-permute-start(f32[256,256]{1,0:T(8,128)S(1)} %get-tuple-element.28.lower_ref.lower_in), channel_id=1, source_target_pairs={{2,0},{3,1},{4,2},{5,3},{6,4},{7,5},{8,6},{9,7},{10,8},{11,9},{12,... | collective-permute-start | bytes 786440 | tf_op jit(solution)/shard_map/ppermute | solution.py:216
  72.2 10.8 %collective-permute-start.20 = (f32[256,256]{1,0:T(8,128)S(1)}, f32[256,256]{1,0:T(8,128)S(1)}, u32[]{:S(2)}, u32[]{:S(2)}) collective-permute-start(f32[256,256]{1,0:T(8,128)S(1)} %get-tuple-element.33), channel_id=1, source_target_pairs={{14,0},{15,1},{0,2},{1,3},{2,4},{3,5},{4,6},{5,7},{6,8},{7,9},{8,1... | collective-permute-start | bytes 786440 | tf_op jit(solution)/shard_map/ppermute | solution.py:216
  74.1 9.3 %collective-permute-start.17 = (f32[64,256]{1,0:T(8,128)S(1)}, f32[64,256]{1,0:T(8,128)S(1)}, u32[]{:S(2)}, u32[]{:S(2)}) collective-permute-start(f32[64,256]{1,0:T(8,128)S(1)} %add_add_fusion.2.in0), channel_id=1, source_target_pairs={{0,16},{16,0},{32,48},{48,32},{64,80},{80,64},{96,112},{112,96},{1... | collective-permute-start | bytes 196616 | tf_op jit(solution)/shard_map/ppermute | solution.py:220
  75.5 7.9 %collective-permute-start.18 = (f32[64,256]{1,0:T(8,128)S(1)}, f32[64,256]{1,0:T(8,128)S(1)}, u32[]{:S(2)}, u32[]{:S(2)}) collective-permute-start(f32[64,256]{1,0:T(8,128)S(1)} %add_add_fusion.2.in0), channel_id=1, source_target_pairs={{0,32},{16,48},{32,0},{48,16},{64,96},{80,112},{96,64},{112,80},{1... | collective-permute-start | bytes 196616 | tf_op jit(solution)/shard_map/ppermute | solution.py:220
  77.0 6.4 %collective-permute-start.19 = (f32[64,256]{1,0:T(8,128)S(1)}, f32[64,256]{1,0:T(8,128)S(1)}, u32[]{:S(2)}, u32[]{:S(2)}) collective-permute-start(f32[64,256]{1,0:T(8,128)S(1)} %add_add_fusion.2.in0), channel_id=1, source_target_pairs={{0,48},{16,32},{32,16},{48,0},{64,112},{80,96},{96,80},{112,64},{1... | collective-permute-start | bytes 196616 | tf_op jit(solution)/shard_map/ppermute | solution.py:220
  87.9 5.3 %collective-permute-start.21 = (f32[16,256]{1,0:T(8,128)S(1)}, f32[16,256]{1,0:T(8,128)S(1)}, u32[]{:S(2)}, u32[]{:S(2)}) collective-permute-start(f32[16,256]{1,0:T(8,128)S(1)} %shard_map.32.angles_ref), channel_id=1, source_target_pairs={{2,0},{3,1},{4,2},{5,3},{6,4},{7,5},{8,6},{9,7},{10,8},{11,9},{12,... | collective-permute-start | bytes 49160 | tf_op jit(solution)/shard_map/ppermute | solution.py:216

commit v7 on v6

--- a/solution.py
+++ b/solution.py
@@ -66,7 +66,7 @@
         offset = target
 
 
-def inner_rounds(shift_ref, tl, tr, lr, angles_ref):
+def inner_rounds(shift_ref, tl, tr, lr, angles_ref, keep=False):
     w = tl.shape[0]
 
     def as_rows(vector):
@@ -88,6 +88,9 @@
             (c * a + s * g) * c + (c * g + s * b) * s,
             (c * b - s * g) * c - (c * g - s * a) * s,
         )
+        left = shift_ref.shape[0] - 1 - r
+        if left == 0 and not keep:
+            break
         c_rows = as_rows(c)
         s_rows = as_rows(s)
         low_left = jnp.transpose(top_right)
@@ -95,11 +98,14 @@
         half_tr = c_rows * top_right + s_rows * low_right
         half_ll = c_rows * low_left - s_rows * top_left
         half_lr = c_rows * low_right - s_rows * top_right
-        tl[...] = half_tl * c + half_tr * s
-        tr[...] = half_tr * c - half_tl * s
-        lr[...] = half_lr * c - half_ll * s
-    offset = shift_ref[shift_ref.shape[0] - 1]
-    lr[...] = pltpu.roll(pltpu.roll(lr[...], offset, 1), offset, 0)
+        if left > 0:
+            tr[...] = half_tr * c - half_tl * s
+        if left > 1 or keep:
+            tl[...] = half_tl * c + half_tr * s
+            lr[...] = half_lr * c - half_ll * s
+    if keep:
+        offset = shift_ref[shift_ref.shape[0] - 1]
+        lr[...] = pltpu.roll(pltpu.roll(lr[...], offset, 1), offset, 0)
 
 
 def rotated(shift_ref, angles_ref, upper_ref, lower_ref):
@@ -167,7 +173,7 @@
     turned = jnp.transpose(square)
     lr[...] = jnp.where(rows == cols, diag[:1, :], jnp.where(rows > cols, square, turned))
     tl[...] = jnp.where(rows <= cols, square, turned)
-    inner_rounds(shift_ref, tl, tr, lr, angles_ref)
+    inner_rounds(shift_ref, tl, tr, lr, angles_ref, keep=True)
 
 
 def own_kernel(shift_ref, angles_ref, pair_ref, upper_ref, lower_ref):
@@ -230,6 +236,15 @@
     return (mine + met[1]) + (met[0] + met[2])
 
 
+def met_across(mine, axis):
+    h = mine.shape[0] // 2 // 8 * 8
+    a, b = mine[:h], mine[h:]
+    a1, b1 = swapped(a, axis, 4), swapped(b, axis, 12)
+    a, b = a + a1, b + b1
+    a1, b1 = swapped(a, axis, 12), swapped(b, axis, 4)
+    return jnp.concatenate([a + a1, b + b1], axis=0)
+
+
 def shared_in_four(mine, axis):
     shared = [swapped(mine, axis, k) for k in (3, 1, 2)]
     return (mine, shared[1], shared[2], shared[0])
@@ -250,7 +265,7 @@
     gram = within_four(gram, "row")
     gram, sent = lax.optimization_barrier((gram, matrix))
     other = passed_along(sent, "col", 2)
-    gram = shared_in_four(across_fours(gram, "row"), "row")
+    gram = shared_in_four(met_across(gram, "row"), "row")
     here, tl, lr = kernel_call(
         first_kernel, [angles, square, square], [SMEM, SMEM] + [VMEM] * 4, [square, diag]
     )(place, shifts[0], *gram)

time: 96.7 us -> 94.6 us (0.978)
  waiting for transfers between devices: 34.4 us -> 31.8 us
  starting transfers between devices: 41.5 us -> 43 us
    ppermute x18 -> x19, waiting for transfers between devices: 26.3 us -> 21.2 us  [swapped(): lax.ppermute(block, axis, [(i, i ^ bits) for i in range(lax.axis_size(axi...]
    ppermute x18 -> x19, starting transfers between devices: 29.6 us -> 32.4 us  [swapped(): lax.ppermute(block, axis, [(i, i ^ bits) for i in range(lax.axis_size(axi...]
    ppermute x5, waiting for transfers between devices: 8.08 us -> 10.6 us  [passed_along(): return lax.ppermute(block, axis, route)]
    ppermute x5, starting transfers between devices: 12 us -> 10.6 us  [passed_along(): return lax.ppermute(block, axis, route)]
  transfers between devices with their start and end apart: 23 -> 24, of which waited for: 15 -> 13; matrix products, arithmetic and copies ran while one was open for 0% -> 0% of each run, Pallas kernels for 14% -> 14%
where the time goes in v7:
time: 94.6 us; the launch traced here: 94.3 us
  starting transfers between devices  43 us (45%)
  waiting for transfers between devices  31.8 us (34%)
  Pallas kernels  19.2 us (20%)
    ppermute x19, starting transfers between devices, swapped(): lax.ppermute(block, axis, [(i, i ^ bits) for i in range(lax.axis_size(axi...  32.4 us
    ppermute x19, waiting for transfers between devices, swapped(): lax.ppermute(block, axis, [(i, i ^ bits) for i in range(lax.axis_size(axi...  21.2 us
    ppermute x5, waiting for transfers between devices, passed_along(): return lax.ppermute(block, axis, route)  10.6 us
    ppermute x5, starting transfers between devices, passed_along(): return lax.ppermute(block, axis, route)  10.6 us
    pallas_call x1, Pallas kernels, per_device(): kernel_call(first_kernel, [angles, square, square], [SMEM, SMEM] + [VMEM]...  5.27 us
    pallas_call x1, Pallas kernels, per_device(): kernel_call(second_kernel, [angles], [SMEM, SMEM] + [VMEM] * 6, [square]...  4.16 us
    pallas_call x1, Pallas kernels, per_device(): kernel_call(lower_kernel, [(rows, width)], [SMEM] + [VMEM] * 4, [block, b...  2.48 us
    pallas_call x1, Pallas kernels, per_device(): kernel_call(own_kernel, [block, block], [SMEM, VMEM, VMEM])  2.24 us
  transfers between devices with their start and end apart: 24, of which 13 were waited for; matrix products, arithmetic and copies ran while one was open for 0% of the time, Pallas kernels for 14%

profile of v7, /device:TPU:8, one launch (start us, length us, event | category | flops | bytes accessed | tf_op | source)
XLA Modules:
  0.0 94.3 jit_solution(9359601836446854528)
XLA Ops:
  0.0 1.9 %shard_map.28 = (f32[136,256]{1,0:T(8,128)S(1)}, f32[136,256]{1,0:T(8,128)S(1)}, f32[136,256]{1,0:T(8,128)S(1)}, f32[136,256]{1,0:T(8,128)S(1)}) custom-call(s32[1]{0:T(128)} %bitcast.1.place_ref, f32[256,512]{1,0:T(8,128)} %pair_ref.3), custom_call_target="tpu_custom_call" | custom-call | tf_op jit(solution)/shard_map/pallas_call | solution.py:262
  1.9 2.0 %collective-permute-start.1 = (f32[136,256]{1,0:T(8,128)S(1)}, f32[136,256]{1,0:T(8,128)S(1)}, u32[]{:S(2)}, u32[]{:S(2)}) collective-permute-start(f32[136,256]{1,0:T(8,128)S(1)} %get-tuple-element.23), channel_id=1, source_target_pairs={{0,32},{16,48},{32,0},{48,16},{64,96},{80,112},{96,64},{112,80},{1... | collective-permute-start | bytes 417800 | tf_op jit(solution)/shard_map/ppermute | solution.py:226
  3.9 1.7 %collective-permute-start.2 = (f32[136,256]{1,0:T(8,128)S(1)}, f32[136,256]{1,0:T(8,128)S(1)}, u32[]{:S(2)}, u32[]{:S(2)}) collective-permute-start(f32[136,256]{1,0:T(8,128)S(1)} %get-tuple-element.24), channel_id=1, source_target_pairs={{0,48},{16,32},{32,16},{48,0},{64,112},{80,96},{96,80},{112,64},{1... | collective-permute-start | bytes 417800 | tf_op jit(solution)/shard_map/ppermute | solution.py:226
  5.6 0.0 collective-permute-start
  5.6 2.9 %collective-permute-done.1 = f32[136,256]{1,0:T(8,128)S(1)} collective-permute-done((f32[136,256]{1,0:T(8,128)S(1)}, f32[136,256]{1,0:T(8,128)S(1)}, u32[]{:S(2)}, u32[]{:S(2)}) %collective-permute-start.1) | collective-permute-done | bytes 139296 | tf_op jit(solution)/shard_map/ppermute | solution.py:226
  8.5 2.9 %collective-permute-done.2 = f32[136,256]{1,0:T(8,128)S(1)} collective-permute-done((f32[136,256]{1,0:T(8,128)S(1)}, f32[136,256]{1,0:T(8,128)S(1)}, u32[]{:S(2)}, u32[]{:S(2)}) %collective-permute-start.2) | collective-permute-done | bytes 139296 | tf_op jit(solution)/shard_map/ppermute | solution.py:226
  11.5 1.0 %collective-permute-done = f32[136,256]{1,0:T(8,128)S(1)} collective-permute-done((f32[136,256]{1,0:T(8,128)S(1)}, f32[136,256]{1,0:T(8,128)S(1)}, u32[]{:S(2)}, u32[]{:S(2)}) %collective-permute-start) | collective-permute-done | bytes 139296 | tf_op jit(solution)/shard_map/ppermute | solution.py:226
  12.5 5.7 %collective-permute-start.5 = (f32[72,256]{1,0:T(8,128)S(1)}, f32[72,256]{1,0:T(8,128)S(1)}, u32[]{:S(2)}, u32[]{:S(2)}) collective-permute-start(f32[72,256]{1,0:T(8,128)S(1)} %slice.19), channel_id=1, source_target_pairs={{0,192},{16,208},{32,224},{48,240},{64,128},{80,144},{96,160},{112... | collective-permute-start | bytes 221192 | tf_op jit(solution)/shard_map/ppermute | solution.py:226
  18.2 1.5 %collective-permute-start.3 = (f32[64,256]{1,0:T(8,128)S(1)}, f32[64,256]{1,0:T(8,128)S(1)}, u32[]{:S(2)}, u32[]{:S(2)}) collective-permute-start(f32[64,256]{1,0:T(8,128)S(1)} %slice.18), channel_id=1, source_target_pairs={{0,64},{16,80},{32,96},{48,112},{64,0},{80,16},{96,32},{112,48},{1... | collective-permute-start | bytes 196616 | tf_op jit(solution)/shard_map/ppermute | solution.py:226
  19.7 2.6 %collective-permute-start.11 = (f32[256,512]{1,0:T(8,128)}, f32[256,512]{1,0:T(8,128)S(1)}, u32[]{:S(2)}, u32[]{:S(2)}) collective-permute-start(f32[256,512]{1,0:T(8,128)} %pair_ref.3), channel_id=1, source_target_pairs={{14,0},{15,1},{0,2},{1,3},{2,4},{3,5},{4,6},{5,7},{6,8},{7,9},{8,1... | collective-permute-start | bytes 1572872 | tf_op jit(solution)/shard_map/ppermute | solution.py:222
  22.2 0.0 collective-permute-done.5
  22.3 1.6 %collective-permute-start.6 = (f32[72,256]{1,0:T(8,128)S(1)}, f32[72,256]{1,0:T(8,128)S(1)}, u32[]{:S(2)}, u32[]{:S(2)}) collective-permute-start(f32[72,256]{1,0:T(8,128)S(1)} %slice_add_fusion.1), channel_id=1, source_target_pairs={{0,64},{16,80},{32,96},{48,112},{64,0},{80,16},{96,32},{112,48},{1... | collective-permute-start | bytes 221192 | tf_op jit(solution)/shard_map/ppermute | solution.py:226
  23.8 0.2 collective-permute-done.3
  24.1 2.6 %collective-permute-start.4 = (f32[64,256]{1,0:T(8,128)S(1)}, f32[64,256]{1,0:T(8,128)S(1)}, u32[]{:S(2)}, u32[]{:S(2)}) collective-permute-start(f32[64,256]{1,0:T(8,128)S(1)} %slice_add_fusion), channel_id=1, source_target_pairs={{0,192},{16,208},{32,224},{48,240},{64,128},{80,144},{96,160},{112... | collective-permute-start | bytes 196616 | tf_op jit(solution)/shard_map/ppermute | solution.py:226
  26.7 3.8 %collective-permute-done.4 = f32[64,256]{1,0:T(8,128)S(1)} collective-permute-done((f32[64,256]{1,0:T(8,128)S(1)}, f32[64,256]{1,0:T(8,128)S(1)}, u32[]{:S(2)}, u32[]{:S(2)}) %collective-permute-start.4) | collective-permute-done | bytes 65568 | tf_op jit(solution)/shard_map/ppermute | solution.py:226
  30.6 0.0 collective-permute-done.6
  30.6 0.0 copy-start
  30.6 1.8 %collective-permute-start.7 = (f32[136,256]{1,0:T(8,128)S(1)}, f32[136,256]{1,0:T(8,128)S(1)}, u32[]{:S(2)}, u32[]{:S(2)}) collective-permute-start(f32[136,256]{1,0:T(8,128)S(1)} %pad_maximum_fusion.in0), channel_id=1, source_target_pairs={{0,16},{16,0},{32,48},{48,32},{64,80},{80,64},{96,112},{112,96},{1... | collective-permute-start | bytes 417800 | tf_op jit(solution)/shard_map/ppermute | solution.py:226
  32.5 1.6 %collective-permute-start.8 = (f32[136,256]{1,0:T(8,128)S(1)}, f32[136,256]{1,0:T(8,128)S(1)}, u32[]{:S(2)}, u32[]{:S(2)}) collective-permute-start(f32[136,256]{1,0:T(8,128)S(1)} %pad_maximum_fusion.in0), channel_id=1, source_target_pairs={{0,32},{16,48},{32,0},{48,16},{64,96},{80,112},{96,64},{112,80},{1... | collective-permute-start | bytes 417800 | tf_op jit(solution)/shard_map/ppermute | solution.py:226
  34.1 0.1 collective-permute-start.9
  34.2 0.0 copy-done
  34.2 6.4 %collective-permute-done.7.in1 = f32[136,256]{1,0:T(8,128)S(1)} collective-permute-done((f32[136,256]{1,0:T(8,128)S(1)}, f32[136,256]{1,0:T(8,128)S(1)}, u32[]{:S(2)}, u32[]{:S(2)}) %collective-permute-start.7) | collective-permute-done | bytes 139296 | tf_op jit(solution)/shard_map/ppermute | solution.py:226
  40.6 0.0 collective-permute-done.8.in2
  40.6 0.0 collective-permute-done.9.in3
  40.6 5.3 %shard_map.29 = (f32[16,256]{1,0:T(8,128)S(1)}, f32[256,256]{1,0:T(8,128)S(1)}, f32[256,256]{1,0:T(8,128)S(1)}) custom-call(s32[1]{0:T(128)} %bitcast.1.place_ref, s32[8]{0:T(128)S(1)} %get-tuple-element.37.shift_ref, f32[136,256]{1,0:T(8,128)S(1)} %pad_maximum_fusion.in0, f32[136,256]{1,0:T(8,128)S(1)} %collective-permute-done.7.in1, ...), custom_call_target="tpu_custom_call" | custom-call | tf_op jit(solution)/shard_map/pallas_call | solution.py:269
  45.9 2.4 %collective-permute-start.10 = (f32[16,256]{1,0:T(8,128)S(1)}, f32[16,256]{1,0:T(8,128)S(1)}, u32[]{:S(2)}, u32[]{:S(2)}) collective-permute-start(f32[16,256]{1,0:T(8,128)S(1)} %get-tuple-element.26.angles_ref), channel_id=1, source_target_pairs={{14,0},{15,1},{0,2},{1,3},{2,4},{3,5},{4,6},{5,7},{6,8},{7,9},{8,1... | collective-permute-start | bytes 49160 | tf_op jit(solution)/shard_map/ppermute | solution.py:222
  48.2 2.2 %shard_map.30 = (f32[256,256]{1,0:T(8,128)S(1)}, f32[256,256]{1,0:T(8,128)S(1)}) custom-call(s32[8]{0:T(128)S(1)} %get-tuple-element.37.shift_ref, f32[16,256]{1,0:T(8,128)S(1)} %get-tuple-element.26.angles_ref, f32[256,512]{1,0:T(8,128)} %pair_ref.3), custom_call_target="tpu_custom_call" | custom-call | tf_op jit(solution)/shard_map/pallas_call | solution.py:273
  50.5 3.0 %collective-permute-done.10.angles_ref = f32[16,256]{1,0:T(8,128)S(1)} collective-permute-done((f32[16,256]{1,0:T(8,128)S(1)}, f32[16,256]{1,0:T(8,128)S(1)}, u32[]{:S(2)}, u32[]{:S(2)}) %collective-permute-start.10) | collective-permute-done | bytes 16416 | tf_op jit(solution)/shard_map/ppermute | solution.py:222
  53.5 0.0 collective-permute-done.11.other_ref
  53.5 1.6 %shard_map.31 = (f32[256,256]{1,0:T(8,128)S(1)}, f32[64,256]{1,0:T(8,128)S(1)}, f32[64,256]{1,0:T(8,128)S(1)}, f32[64,256]{1,0:T(8,128)S(1)}, f32[64,256]{1,0:T(8,128)S(1)}) custom-call(s32[1]{0:T(128)} %bitcast.1.place_ref, s32[8]{0:T(128)S(1)} %get-tuple-element.37.shift_ref, f32[16,256]{1,0:T(8,128)S(1)} %collective-permute-done.10.angles_ref, ...), custom_call_target="tpu_custom_call" | custom-call | tf_op jit(solution)/shard_map/pallas_call | solution.py:276
  55.1 1.1 %collective-permute-start.13 = (f32[64,256]{1,0:T(8,128)S(1)}, f32[64,256]{1,0:T(8,128)S(1)}, u32[]{:S(2)}, u32[]{:S(2)}) collective-permute-start(f32[64,256]{1,0:T(8,128)S(1)} %get-tuple-element.31), channel_id=1, source_target_pairs={{0,32},{16,48},{32,0},{48,16},{64,96},{80,112},{96,64},{112,80},{1... | collective-permute-start | bytes 196616 | tf_op jit(solution)/shard_map/ppermute | solution.py:226
  56.2 1.1 %collective-permute-start.14 = (f32[64,256]{1,0:T(8,128)S(1)}, f32[64,256]{1,0:T(8,128)S(1)}, u32[]{:S(2)}, u32[]{:S(2)}) collective-permute-start(f32[64,256]{1,0:T(8,128)S(1)} %get-tuple-element.32), channel_id=1, source_target_pairs={{0,48},{16,32},{32,16},{48,0},{64,112},{80,96},{96,80},{112,64},{1... | collective-permute-start | bytes 196616 | tf_op jit(solution)/shard_map/ppermute | solution.py:226
  57.3 1.4 %collective-permute-start.12 = (f32[64,256]{1,0:T(8,128)S(1)}, f32[64,256]{1,0:T(8,128)S(1)}, u32[]{:S(2)}, u32[]{:S(2)}) collective-permute-start(f32[64,256]{1,0:T(8,128)S(1)} %get-tuple-element.30), channel_id=1, source_target_pairs={{0,16},{16,0},{32,48},{48,32},{64,80},{80,64},{96,112},{112,96},{1... | collective-permute-start | bytes 196616 | tf_op jit(solution)/shard_map/ppermute | solution.py:226
  58.7 0.8 collective-permute-done.13
  59.4 2.6 %collective-permute-done.14 = f32[64,256]{1,0:T(8,128)S(1)} collective-permute-done((f32[64,256]{1,0:T(8,128)S(1)}, f32[64,256]{1,0:T(8,128)S(1)}, u32[]{:S(2)}, u32[]{:S(2)}) %collective-permute-start.14) | collective-permute-done | bytes 65568 | tf_op jit(solution)/shard_map/ppermute | solution.py:226
  62.1 0.0 collective-permute-done.12
  62.1 2.4 %collective-permute-start.16 = (f32[64,256]{1,0:T(8,128)S(1)}, f32[64,256]{1,0:T(8,128)S(1)}, u32[]{:S(2)}, u32[]{:S(2)}) collective-permute-start(f32[64,256]{1,0:T(8,128)S(1)} %add_add_fusion.2), channel_id=1, source_target_pairs={{0,128},{16,144},{32,160},{48,176},{64,192},{80,208},{96,224},{112... | collective-permute-start | bytes 196616 | tf_op jit(solution)/shard_map/ppermute | solution.py:226
  64.5 2.8 %collective-permute-start.17 = (f32[64,256]{1,0:T(8,128)S(1)}, f32[64,256]{1,0:T(8,128)S(1)}, u32[]{:S(2)}, u32[]{:S(2)}) collective-permute-start(f32[64,256]{1,0:T(8,128)S(1)} %add_add_fusion.2), channel_id=1, source_target_pairs={{0,192},{16,208},{32,224},{48,240},{64,128},{80,144},{96,160},{112... | collective-permute-start | bytes 196616 | tf_op jit(solution)/shard_map/ppermute | solution.py:226
  67.2 1.5 %collective-permute-start.15 = (f32[64,256]{1,0:T(8,128)S(1)}, f32[64,256]{1,0:T(8,128)S(1)}, u32[]{:S(2)}, u32[]{:S(2)}) collective-permute-start(f32[64,256]{1,0:T(8,128)S(1)} %add_add_fusion.2), channel_id=1, source_target_pairs={{0,64},{16,80},{32,96},{48,112},{64,0},{80,16},{96,32},{112,48},{1... | collective-permute-start | bytes 196616 | tf_op jit(solution)/shard_map/ppermute | solution.py:226
  68.7 3.1 %collective-permute-start.23 = (f32[256,256]{1,0:T(8,128)S(1)}, f32[256,256]{1,0:T(8,128)S(1)}, u32[]{:S(2)}, u32[]{:S(2)}) collective-permute-start(f32[256,256]{1,0:T(8,128)S(1)} %get-tuple-element.28.lower_ref.lower_in), channel_id=1, source_target_pairs={{2,0},{3,1},{4,2},{5,3},{6,4},{7,5},{8,6},{9,7},{10,8},{11,9},{12,... | collective-permute-start | bytes 786440 | tf_op jit(solution)/shard_map/ppermute | solution.py:222
  71.7 0.5 collective-permute-start.21
  72.2 0.0 collective-permute-done.16
  72.2 0.0 collective-permute-done.17
  72.2 0.4 collective-permute-done.15
  72.6 1.5 %collective-permute-start.18 = (f32[64,256]{1,0:T(8,128)S(1)}, f32[64,256]{1,0:T(8,128)S(1)}, u32[]{:S(2)}, u32[]{:S(2)}) collective-permute-start(f32[64,256]{1,0:T(8,128)S(1)} %add_add_fusion.1.in0), channel_id=1, source_target_pairs={{0,16},{16,0},{32,48},{48,32},{64,80},{80,64},{96,112},{112,96},{1... | collective-permute-start | bytes 196616 | tf_op jit(solution)/shard_map/ppermute | solution.py:226
  74.1 1.4 %collective-permute-start.19 = (f32[64,256]{1,0:T(8,128)S(1)}, f32[64,256]{1,0:T(8,128)S(1)}, u32[]{:S(2)}, u32[]{:S(2)}) collective-permute-start(f32[64,256]{1,0:T(8,128)S(1)} %add_add_fusion.1.in0), channel_id=1, source_target_pairs={{0,32},{16,48},{32,0},{48,16},{64,96},{80,112},{96,64},{112,80},{1... | collective-permute-start | bytes 196616 | tf_op jit(solution)/shard_map/ppermute | solution.py:226
  75.5 0.7 collective-permute-start.20
  76.2 6.0 %collective-permute-done.21.tl_ref = f32[256,256]{1,0:T(8,128)S(1)} collective-permute-done((f32[256,256]{1,0:T(8,128)S(1)}, f32[256,256]{1,0:T(8,128)S(1)}, u32[]{:S(2)}, u32[]{:S(2)}) %collective-permute-start.21) | collective-permute-done | bytes 262176 | tf_op jit(solution)/shard_map/ppermute | solution.py:222
  82.2 0.1 collective-permute-done.18.in1
  82.3 0.0 collective-permute-done.19.in2
  82.3 0.0 collective-permute-done.20.in3
  82.3 4.2 %shard_map.32.angles_ref = f32[16,256]{1,0:T(8,128)S(1)} custom-call(s32[1]{0:T(128)} %bitcast.1.place_ref, s32[8]{0:T(128)S(1)} %get-tuple-element.38.shift_ref, f32[64,256]{1,0:T(8,128)S(1)} %add_add_fusion.1.in0, f32[64,256]{1,0:T(8,128)S(1)} %collective-permute-done.18.in1, f32[64,256]{1,0:T(8,128)S(1)} %collective-permute-done.19.in2, ...), custom_call_target="tpu_custom_call" | custom-call | tf_op jit(solution)/shard_map/pallas_call | solution.py:286
  86.5 2.1 %collective-permute-start.22 = (f32[16,256]{1,0:T(8,128)S(1)}, f32[16,256]{1,0:T(8,128)S(1)}, u32[]{:S(2)}, u32[]{:S(2)}) collective-permute-start(f32[16,256]{1,0:T(8,128)S(1)} %shard_map.32.angles_ref), channel_id=1, source_target_pairs={{2,0},{3,1},{4,2},{5,3},{6,4},{7,5},{8,6},{9,7},{10,8},{11,9},{12,... | collective-permute-start | bytes 49160 | tf_op jit(solution)/shard_map/ppermute | solution.py:222
  88.6 1.6 %shard_map.33.done_ref = f32[256,256]{1,0:T(8,128)S(1)} custom-call(s32[8]{0:T(128)S(1)} %get-tuple-element.38.shift_ref, f32[16,256]{1,0:T(8,128)S(1)} %shard_map.32.angles_ref, f32[256,256]{1,0:T(8,128)S(1)} %get-tuple-element.36.upper_in, f32[256,256]{1,0:T(8,128)S(1)} %get-tuple-element.28.lower_ref.lower_in), custom_call_target="tpu_custom_call" | custom-call | tf_op jit(solution)/shard_map/pallas_call | solution.py:290
  90.2 0.0 collective-permute-done.23.lower_in
  90.2 1.6 %collective-permute-done.22.angles_ref = f32[16,256]{1,0:T(8,128)S(1)} collective-permute-done((f32[16,256]{1,0:T(8,128)S(1)}, f32[16,256]{1,0:T(8,128)S(1)}, u32[]{:S(2)}, u32[]{:S(2)}) %collective-permute-start.22) | collective-permute-done | bytes 16416 | tf_op jit(solution)/shard_map/ppermute | solution.py:222
  91.8 2.5 %shard_map.34 = f32[256,512]{1,0:T(8,128)} custom-call(s32[8]{0:T(128)S(1)} %get-tuple-element.38.shift_ref, f32[16,256]{1,0:T(8,128)S(1)} %collective-permute-done.22.angles_ref, f32[256,256]{1,0:T(8,128)S(1)} %get-tuple-element.35.upper_in, f32[256,256]{1,0:T(8,128)S(1)} %collective-permute-done.23.lower_in, f32[256,256]{1,0:T(8,128)S(1)} %shard_map.33.done_ref), custom_call_target="tpu_custom_call" | custom-call | tf_op jit(solution)/shard_map/pallas_call | solution.py:293
  (11 shorter events, 0.1 us)
Async XLA Ops:
  1.9 6.6 %collective-permute-start.1 = (f32[136,256]{1,0:T(8,128)S(1)}, f32[136,256]{1,0:T(8,128)S(1)}, u32[]{:S(2)}, u32[]{:S(2)}) collective-permute-start(f32[136,256]{1,0:T(8,128)S(1)} %get-tuple-element.23), channel_id=1, source_target_pairs={{0,32},{16,48},{32,0},{48,16},{64,96},{80,112},{96,64},{112,80},{1... | collective-permute-start | bytes 417800 | tf_op jit(solution)/shard_map/ppermute | solution.py:226
  3.9 7.6 %collective-permute-start.2 = (f32[136,256]{1,0:T(8,128)S(1)}, f32[136,256]{1,0:T(8,128)S(1)}, u32[]{:S(2)}, u32[]{:S(2)}) collective-permute-start(f32[136,256]{1,0:T(8,128)S(1)} %get-tuple-element.24), channel_id=1, source_target_pairs={{0,48},{16,32},{32,16},{48,0},{64,112},{80,96},{96,80},{112,64},{1... | collective-permute-start | bytes 417800 | tf_op jit(solution)/shard_map/ppermute | solution.py:226
  5.6 6.8 %collective-permute-start = (f32[136,256]{1,0:T(8,128)S(1)}, f32[136,256]{1,0:T(8,128)S(1)}, u32[]{:S(2)}, u32[]{:S(2)}) collective-permute-start(f32[136,256]{1,0:T(8,128)S(1)} %get-tuple-element.22), channel_id=1, source_target_pairs={{0,16},{16,0},{32,48},{48,32},{64,80},{80,64},{96,112},{112,96},{1... | collective-permute-start | bytes 417800 | tf_op jit(solution)/shard_map/ppermute | solution.py:226
  12.5 9.8 %collective-permute-start.5 = (f32[72,256]{1,0:T(8,128)S(1)}, f32[72,256]{1,0:T(8,128)S(1)}, u32[]{:S(2)}, u32[]{:S(2)}) collective-permute-start(f32[72,256]{1,0:T(8,128)S(1)} %slice.19), channel_id=1, source_target_pairs={{0,192},{16,208},{32,224},{48,240},{64,128},{80,144},{96,160},{112... | collective-permute-start | bytes 221192 | tf_op jit(solution)/shard_map/ppermute | solution.py:226
  18.2 5.9 %collective-permute-start.3 = (f32[64,256]{1,0:T(8,128)S(1)}, f32[64,256]{1,0:T(8,128)S(1)}, u32[]{:S(2)}, u32[]{:S(2)}) collective-permute-start(f32[64,256]{1,0:T(8,128)S(1)} %slice.18), channel_id=1, source_target_pairs={{0,64},{16,80},{32,96},{48,112},{64,0},{80,16},{96,32},{112,48},{1... | collective-permute-start | bytes 196616 | tf_op jit(solution)/shard_map/ppermute | solution.py:226
  19.7 33.8 %collective-permute-start.11 = (f32[256,512]{1,0:T(8,128)}, f32[256,512]{1,0:T(8,128)S(1)}, u32[]{:S(2)}, u32[]{:S(2)}) collective-permute-start(f32[256,512]{1,0:T(8,128)} %pair_ref.3), channel_id=1, source_target_pairs={{14,0},{15,1},{0,2},{1,3},{2,4},{3,5},{4,6},{5,7},{6,8},{7,9},{8,1... | collective-permute-start | bytes 1572872 | tf_op jit(solution)/shard_map/ppermute | solution.py:222
  22.3 8.3 %collective-permute-start.6 = (f32[72,256]{1,0:T(8,128)S(1)}, f32[72,256]{1,0:T(8,128)S(1)}, u32[]{:S(2)}, u32[]{:S(2)}) collective-permute-start(f32[72,256]{1,0:T(8,128)S(1)} %slice_add_fusion.1), channel_id=1, source_target_pairs={{0,64},{16,80},{32,96},{48,112},{64,0},{80,16},{96,32},{112,48},{1... | collective-permute-start | bytes 221192 | tf_op jit(solution)/shard_map/ppermute | solution.py:226
  24.1 6.5 %collective-permute-start.4 = (f32[64,256]{1,0:T(8,128)S(1)}, f32[64,256]{1,0:T(8,128)S(1)}, u32[]{:S(2)}, u32[]{:S(2)}) collective-permute-start(f32[64,256]{1,0:T(8,128)S(1)} %slice_add_fusion), channel_id=1, source_target_pairs={{0,192},{16,208},{32,224},{48,240},{64,128},{80,144},{96,160},{112... | collective-permute-start | bytes 196616 | tf_op jit(solution)/shard_map/ppermute | solution.py:226
  30.6 3.6 %copy-start = (s32[2,8]{1,0:T(2,128)S(1)}, s32[2,8]{1,0:T(2,128)}, u32[]{:S(2)}) copy-start(s32[2,8]{1,0:T(2,128)} %param.3) | copy-start | bytes 196
  30.6 9.9 %collective-permute-start.7 = (f32[136,256]{1,0:T(8,128)S(1)}, f32[136,256]{1,0:T(8,128)S(1)}, u32[]{:S(2)}, u32[]{:S(2)}) collective-permute-start(f32[136,256]{1,0:T(8,128)S(1)} %pad_maximum_fusion.in0), channel_id=1, source_target_pairs={{0,16},{16,0},{32,48},{48,32},{64,80},{80,64},{96,112},{112,96},{1... | collective-permute-start | bytes 417800 | tf_op jit(solution)/shard_map/ppermute | solution.py:226
  32.5 8.1 %collective-permute-start.8 = (f32[136,256]{1,0:T(8,128)S(1)}, f32[136,256]{1,0:T(8,128)S(1)}, u32[]{:S(2)}, u32[]{:S(2)}) collective-permute-start(f32[136,256]{1,0:T(8,128)S(1)} %pad_maximum_fusion.in0), channel_id=1, source_target_pairs={{0,32},{16,48},{32,0},{48,16},{64,96},{80,112},{96,64},{112,80},{1... | collective-permute-start | bytes 417800 | tf_op jit(solution)/shard_map/ppermute | solution.py:226
  34.1 6.5 %collective-permute-start.9 = (f32[136,256]{1,0:T(8,128)S(1)}, f32[136,256]{1,0:T(8,128)S(1)}, u32[]{:S(2)}, u32[]{:S(2)}) collective-permute-start(f32[136,256]{1,0:T(8,128)S(1)} %pad_maximum_fusion.in0), channel_id=1, source_target_pairs={{0,48},{16,32},{32,16},{48,0},{64,112},{80,96},{96,80},{112,64},{1... | collective-permute-start | bytes 417800 | tf_op jit(solution)/shard_map/ppermute | solution.py:226
  45.9 7.6 %collective-permute-start.10 = (f32[16,256]{1,0:T(8,128)S(1)}, f32[16,256]{1,0:T(8,128)S(1)}, u32[]{:S(2)}, u32[]{:S(2)}) collective-permute-start(f32[16,256]{1,0:T(8,128)S(1)} %get-tuple-element.26.angles_ref), channel_id=1, source_target_pairs={{14,0},{15,1},{0,2},{1,3},{2,4},{3,5},{4,6},{5,7},{6,8},{7,9},{8,1... | collective-permute-start | bytes 49160 | tf_op jit(solution)/shard_map/ppermute | solution.py:222
  55.1 4.4 %collective-permute-start.13 = (f32[64,256]{1,0:T(8,128)S(1)}, f32[64,256]{1,0:T(8,128)S(1)}, u32[]{:S(2)}, u32[]{:S(2)}) collective-permute-start(f32[64,256]{1,0:T(8,128)S(1)} %get-tuple-element.31), channel_id=1, source_target_pairs={{0,32},{16,48},{32,0},{48,16},{64,96},{80,112},{96,64},{112,80},{1... | collective-permute-start | bytes 196616 | tf_op jit(solution)/shard_map/ppermute | solution.py:226
  56.2 5.9 %collective-permute-start.14 = (f32[64,256]{1,0:T(8,128)S(1)}, f32[64,256]{1,0:T(8,128)S(1)}, u32[]{:S(2)}, u32[]{:S(2)}) collective-permute-start(f32[64,256]{1,0:T(8,128)S(1)} %get-tuple-element.32), channel_id=1, source_target_pairs={{0,48},{16,32},{32,16},{48,0},{64,112},{80,96},{96,80},{112,64},{1... | collective-permute-start | bytes 196616 | tf_op jit(solution)/shard_map/ppermute | solution.py:226
  57.3 4.8 %collective-permute-start.12 = (f32[64,256]{1,0:T(8,128)S(1)}, f32[64,256]{1,0:T(8,128)S(1)}, u32[]{:S(2)}, u32[]{:S(2)}) collective-permute-start(f32[64,256]{1,0:T(8,128)S(1)} %get-tuple-element.30), channel_id=1, source_target_pairs={{0,16},{16,0},{32,48},{48,32},{64,80},{80,64},{96,112},{112,96},{1... | collective-permute-start | bytes 196616 | tf_op jit(solution)/shard_map/ppermute | solution.py:226
  62.1 10.1 %collective-permute-start.16 = (f32[64,256]{1,0:T(8,128)S(1)}, f32[64,256]{1,0:T(8,128)S(1)}, u32[]{:S(2)}, u32[]{:S(2)}) collective-permute-start(f32[64,256]{1,0:T(8,128)S(1)} %add_add_fusion.2), channel_id=1, source_target_pairs={{0,128},{16,144},{32,160},{48,176},{64,192},{80,208},{96,224},{112... | collective-permute-start | bytes 196616 | tf_op jit(solution)/shard_map/ppermute | solution.py:226
  64.5 7.7 %collective-permute-start.17 = (f32[64,256]{1,0:T(8,128)S(1)}, f32[64,256]{1,0:T(8,128)S(1)}, u32[]{:S(2)}, u32[]{:S(2)}) collective-permute-start(f32[64,256]{1,0:T(8,128)S(1)} %add_add_fusion.2), channel_id=1, source_target_pairs={{0,192},{16,208},{32,224},{48,240},{64,128},{80,144},{96,160},{112... | collective-permute-start | bytes 196616 | tf_op jit(solution)/shard_map/ppermute | solution.py:226
  67.2 5.4 %collective-permute-start.15 = (f32[64,256]{1,0:T(8,128)S(1)}, f32[64,256]{1,0:T(8,128)S(1)}, u32[]{:S(2)}, u32[]{:S(2)}) collective-permute-start(f32[64,256]{1,0:T(8,128)S(1)} %add_add_fusion.2), channel_id=1, source_target_pairs={{0,64},{16,80},{32,96},{48,112},{64,0},{80,16},{96,32},{112,48},{1... | collective-permute-start | bytes 196616 | tf_op jit(solution)/shard_map/ppermute | solution.py:226
  68.7 21.5 %collective-permute-start.23 = (f32[256,256]{1,0:T(8,128)S(1)}, f32[256,256]{1,0:T(8,128)S(1)}, u32[]{:S(2)}, u32[]{:S(2)}) collective-permute-start(f32[256,256]{1,0:T(8,128)S(1)} %get-tuple-element.28.lower_ref.lower_in), channel_id=1, source_target_pairs={{2,0},{3,1},{4,2},{5,3},{6,4},{7,5},{8,6},{9,7},{10,8},{11,9},{12,... | collective-permute-start | bytes 786440 | tf_op jit(solution)/shard_map/ppermute | solution.py:222
  71.7 10.5 %collective-permute-start.21 = (f32[256,256]{1,0:T(8,128)S(1)}, f32[256,256]{1,0:T(8,128)S(1)}, u32[]{:S(2)}, u32[]{:S(2)}) collective-permute-start(f32[256,256]{1,0:T(8,128)S(1)} %get-tuple-element.33), channel_id=1, source_target_pairs={{14,0},{15,1},{0,2},{1,3},{2,4},{3,5},{4,6},{5,7},{6,8},{7,9},{8,1... | collective-permute-start | bytes 786440 | tf_op jit(solution)/shard_map/ppermute | solution.py:222
  72.6 9.7 %collective-permute-start.18 = (f32[64,256]{1,0:T(8,128)S(1)}, f32[64,256]{1,0:T(8,128)S(1)}, u32[]{:S(2)}, u32[]{:S(2)}) collective-permute-start(f32[64,256]{1,0:T(8,128)S(1)} %add_add_fusion.1.in0), channel_id=1, source_target_pairs={{0,16},{16,0},{32,48},{48,32},{64,80},{80,64},{96,112},{112,96},{1... | collective-permute-start | bytes 196616 | tf_op jit(solution)/shard_map/ppermute | solution.py:226
  74.1 8.2 %collective-permute-start.19 = (f32[64,256]{1,0:T(8,128)S(1)}, f32[64,256]{1,0:T(8,128)S(1)}, u32[]{:S(2)}, u32[]{:S(2)}) collective-permute-start(f32[64,256]{1,0:T(8,128)S(1)} %add_add_fusion.1.in0), channel_id=1, source_target_pairs={{0,32},{16,48},{32,0},{48,16},{64,96},{80,112},{96,64},{112,80},{1... | collective-permute-start | bytes 196616 | tf_op jit(solution)/shard_map/ppermute | solution.py:226
  75.5 6.9 %collective-permute-start.20 = (f32[64,256]{1,0:T(8,128)S(1)}, f32[64,256]{1,0:T(8,128)S(1)}, u32[]{:S(2)}, u32[]{:S(2)}) collective-permute-start(f32[64,256]{1,0:T(8,128)S(1)} %add_add_fusion.1.in0), channel_id=1, source_target_pairs={{0,48},{16,32},{32,16},{48,0},{64,112},{80,96},{96,80},{112,64},{1... | collective-permute-start | bytes 196616 | tf_op jit(solution)/shard_map/ppermute | solution.py:226
  86.5 5.3 %collective-permute-start.22 = (f32[16,256]{1,0:T(8,128)S(1)}, f32[16,256]{1,0:T(8,128)S(1)}, u32[]{:S(2)}, u32[]{:S(2)}) collective-permute-start(f32[16,256]{1,0:T(8,128)S(1)} %shard_map.32.angles_ref), channel_id=1, source_target_pairs={{2,0},{3,1},{4,2},{5,3},{6,4},{7,5},{8,6},{9,7},{10,8},{11,9},{12,... | collective-permute-start | bytes 49160 | tf_op jit(solution)/shard_map/ppermute | solution.py:222

commit v8 on v7

--- a/solution.py
+++ b/solution.py
@@ -9,6 +9,7 @@
 BLK = 256
 VMEM = pl.BlockSpec(memory_space=pltpu.VMEM)
 SMEM = pl.BlockSpec(memory_space=pltpu.SMEM)
+ANY = pl.BlockSpec(memory_space=pl.ANY)
 
 
 def kernel_call(kernel, outs, ins, scratch=()):
@@ -18,6 +19,19 @@
         in_specs=ins,
         out_specs=[VMEM] * len(outs),
         scratch_shapes=[pltpu.VMEM(shape, jnp.float32) for shape in scratch],
+        compiler_params=pltpu.CompilerParams(vmem_limit_bytes=32 * 1024 * 1024),
+    )
+
+
+def output_call(kernel, like, ins, scratch, aliases={}):
+    return pl.pallas_call(
+        kernel,
+        out_shape=jax.ShapeDtypeStruct(like.shape, jnp.float32),
+        in_specs=[SMEM] + ins,
+        out_specs=ANY,
+        scratch_shapes=[pltpu.VMEM(shape, jnp.float32) for shape in scratch]
+        + [pltpu.SemaphoreType.DMA],
+        input_output_aliases=aliases,
         compiler_params=pltpu.CompilerParams(vmem_limit_bytes=32 * 1024 * 1024),
     )
 
@@ -58,6 +72,12 @@
     return pltpu.roll(jnp.broadcast_to(vector, (8, vector.shape[1])), back, 1)[:1]
 
 
+def as_rows(vector):
+    w = vector.shape[1]
+    half = jnp.transpose(jnp.broadcast_to(vector, (LANES, w)))
+    return jnp.concatenate([half] * (w // LANES), axis=1)
+
+
 def turns(shift_ref):
     offset = jnp.int32(0)
     for r in range(shift_ref.shape[0]):
@@ -66,12 +86,8 @@
         offset = target
 
 
-def inner_rounds(shift_ref, tl, tr, lr, angles_ref, keep=False):
+def inner_rounds(shift_ref, tl, tr, lr, angles_ref, finished_later=False):
     w = tl.shape[0]
-
-    def as_rows(vector):
-        half = jnp.transpose(jnp.broadcast_to(vector, (LANES, w)))
-        return jnp.concatenate([half] * (w // LANES), axis=1)
 
     a = diagonal(tl[...])
     b = diagonal(lr[...])
@@ -89,7 +105,7 @@
             (c * b - s * g) * c - (c * g - s * a) * s,
         )
         left = shift_ref.shape[0] - 1 - r
-        if left == 0 and not keep:
+        if left == 0:
             break
         c_rows = as_rows(c)
         s_rows = as_rows(s)
@@ -98,14 +114,34 @@
         half_tr = c_rows * top_right + s_rows * low_right
         half_ll = c_rows * low_left - s_rows * top_left
         half_lr = c_rows * low_right - s_rows * top_right
-        if left > 0:
-            tr[...] = half_tr * c - half_tl * s
-        if left > 1 or keep:
+        tr[...] = half_tr * c - half_tl * s
+        if left > 1 or finished_later:
             tl[...] = half_tl * c + half_tr * s
             lr[...] = half_lr * c - half_ll * s
-    if keep:
-        offset = shift_ref[shift_ref.shape[0] - 1]
-        lr[...] = pltpu.roll(pltpu.roll(lr[...], offset, 1), offset, 0)
+
+
+def last_update(shift_ref, angles_ref, tl, tr, lr):
+    w = tl.shape[0]
+    last = shift_ref.shape[0] - 1
+    back = lax.rem(shift_ref[last - 1] - shift_ref[last] + 2 * BLK, BLK)
+    c = angles_ref[2 * last : 2 * last + 1, :]
+    s = angles_ref[2 * last + 1 : 2 * last + 2, :]
+    c_rows = as_rows(c)
+    s_rows = as_rows(s)
+    top_left = tl[...]
+    top_right = pltpu.roll(tr[...], back, 1)
+    low_left = jnp.transpose(top_right)
+    low_right = pltpu.roll(pltpu.roll(lr[...], back, 1), back, 0)
+    half_tl = c_rows * top_left + s_rows * low_left
+    half_tr = c_rows * top_right + s_rows * low_right
+    half_ll = c_rows * low_left - s_rows * top_left
+    half_lr = c_rows * low_right - s_rows * top_right
+    offset = shift_ref[last]
+    low_right = half_lr * c - half_ll * s
+    return (
+        half_tl * c + half_tr * s,
+        pltpu.roll(pltpu.roll(low_right, offset, 1), offset, 0),
+    )
 
 
 def rotated(shift_ref, angles_ref, upper_ref, lower_ref):
@@ -164,7 +200,7 @@
 
 
 def first_kernel(
-    place_ref, shift_ref, in0, in1, in2, in3, angles_ref, tl, lr, tr, diag
+    place_ref, shift_ref, in0, in1, in2, in3, angles_ref, tl, tr, lr, diag
 ):
     w = tl.shape[0]
     rows, cols = grid_of(w)
@@ -173,7 +209,12 @@
     turned = jnp.transpose(square)
     lr[...] = jnp.where(rows == cols, diag[:1, :], jnp.where(rows > cols, square, turned))
     tl[...] = jnp.where(rows <= cols, square, turned)
-    inner_rounds(shift_ref, tl, tr, lr, angles_ref, keep=True)
+    inner_rounds(shift_ref, tl, tr, lr, angles_ref, finished_later=True)
+
+
+def last_kernel(shift_ref, angles_ref, tl, tr, lr, tl_ref, lr_ref):
+    top_left, lr_ref[...] = last_update(shift_ref, angles_ref, tl, tr, lr)
+    tl_ref[...] = packed(top_left)
 
 
 def own_kernel(shift_ref, angles_ref, pair_ref, upper_ref, lower_ref):
@@ -194,26 +235,53 @@
     hand_out(place_ref, (cross,), (out0, out1, out2, out3))
 
 
+def packed(block):
+    h = block.shape[0] // 2
+    q = h // 2
+    low = block[h:, h:]
+    return jnp.concatenate([block[:h], jnp.concatenate([low[:q], low[q:]], axis=1)], axis=0)
+
+
+def unpacked(parts):
+    h = parts.shape[1] // 2
+    q = h // 2
+    top = parts[:h]
+    low = jnp.concatenate([parts[h:, :h], parts[h:, h:]], axis=0)
+    low = jnp.concatenate([jnp.transpose(top[:, h:]), low], axis=1)
+    return jnp.concatenate([top, low], axis=0)
+
+
 def second_kernel(place_ref, shift_ref, in0, in1, in2, in3, tl_ref, lr_ref, angles_ref, tl, tr, lr):
-    tl[...] = tl_ref[...]
+    tl[...] = unpacked(tl_ref[...])
     lr[...] = lr_ref[...]
     take_in(place_ref, (in0, in1, in2, in3), (tr,))
     inner_rounds(shift_ref, tl, tr, lr, angles_ref)
 
 
-def upper_kernel(shift_ref, angles_ref, upper_in, lower_in, upper_ref, rest):
-    upper_ref[...] = upper_in[...]
+def upper_kernel(shift_ref, angles_ref, upper_in, lower_in, pair_ref, upper, rest, sem):
+    upper[...] = upper_in[...]
     rest[...] = lower_in[...]
-    rotated(shift_ref, angles_ref, upper_ref, rest)
-
-
-def lower_kernel(shift_ref, angles_ref, upper_in, lower_in, done_ref, pair_ref, upper, lower):
-    w = done_ref.shape[1]
-    upper[...] = upper_in[...]
-    lower[...] = lower_in[...]
-    pair_ref[:, :w] = done_ref[...]
-    rotated(shift_ref, angles_ref, upper, lower)
-    pair_ref[:, w:] = lower[...]
+    rotated(shift_ref, angles_ref, upper, rest)
+    copy = pltpu.make_async_copy(upper, pair_ref.at[:, : upper.shape[1]], sem)
+    copy.start()
+    copy.wait()
+
+
+def lower_kernel(shift_ref, angles_ref, upper_in, lower_in, half_ref, pair_ref, done, sem):
+    w = done.shape[1]
+    rounds = list(turns(shift_ref))
+    for t in range(0, done.shape[0], 8):
+        upper = upper_in[t : t + 8, :]
+        lower = lower_in[t : t + 8, :]
+        for r, back in rounds:
+            c = angles_ref[2 * r : 2 * r + 1, :]
+            s = angles_ref[2 * r + 1 : 2 * r + 2, :]
+            lower = pltpu.roll(lower, back, 1)
+            upper, lower = upper * c + lower * s, lower * c - upper * s
+        done[t : t + 8, :] = pltpu.roll(lower, shift_ref[shift_ref.shape[0] - 1], 1)
+    copy = pltpu.make_async_copy(done, pair_ref.at[:, w:], sem)
+    copy.start()
+    copy.wait()
 
 
 def passed_along(block, axis, distance):
@@ -266,12 +334,15 @@
     gram, sent = lax.optimization_barrier((gram, matrix))
     other = passed_along(sent, "col", 2)
     gram = shared_in_four(met_across(gram, "row"), "row")
-    here, tl, lr = kernel_call(
-        first_kernel, [angles, square, square], [SMEM, SMEM] + [VMEM] * 4, [square, diag]
+    here, *state = kernel_call(
+        first_kernel, [angles] + [square] * 3, [SMEM, SMEM] + [VMEM] * 4, [diag]
     )(place, shifts[0], *gram)
     there = passed_along(here, "col", 2)
     own_upper, lower = kernel_call(own_kernel, [block, block], [SMEM, VMEM, VMEM])(
         shifts[0], here, matrix
+    )
+    tl, lr = kernel_call(last_kernel, [(3 * w // 4, w), square], [SMEM] + [VMEM] * 4)(
+        shifts[0], here, *state
     )
     upper, *cross = kernel_call(
         cross_kernel,
@@ -281,19 +352,19 @@
     )(place, shifts[0], there, other, lower)
     cross = within_four(cross, "row")
     tl = passed_along(tl, "col", 2)
-    far_lower = passed_along(lower, "col", -2)
+    tl, sent = lax.optimization_barrier((tl, lower))
+    far_lower = passed_along(sent, "col", -2)
     cross = shared_in_four(across_fours(cross, "row"), "row")
     (here,) = kernel_call(
         second_kernel, [angles], [SMEM, SMEM] + [VMEM] * 6, [square] * 3
     )(place, shifts[1], *cross, tl, lr)
     there = passed_along(here, "col", -2)
-    (upper,) = kernel_call(upper_kernel, [block], [SMEM] + [VMEM] * 3, [block])(
+    half = output_call(upper_kernel, matrix, [VMEM] * 3, [block, block])(
         shifts[1], here, upper, lower
     )
-    (pair,) = kernel_call(
-        lower_kernel, [(rows, width)], [SMEM] + [VMEM] * 4, [block, block]
-    )(shifts[1], there, own_upper, far_lower, upper)
-    return pair
+    return output_call(lower_kernel, matrix, [VMEM] * 3 + [ANY], [block], {4: 0})(
+        shifts[1], there, own_upper, far_lower, half
+    )
 
 
 def solution(mesh):

time: 94.6 us -> 93.2 us (0.985)
  waiting for transfers between devices: 31.8 us -> 30 us
  starting transfers between devices: 43 us -> 41.5 us
  Pallas kernels: 19.2 us -> 20.4 us
    ppermute x5, waiting for transfers between devices: 10.6 us -> 3.61 us  [passed_along(): return lax.ppermute(block, axis, route)]
    ppermute x19, waiting for transfers between devices: 21.2 us -> 26.4 us  [swapped(): lax.ppermute(block, axis, [(i, i ^ bits) for i in range(lax.axis_size(axi...]
    ppermute x5, starting transfers between devices: 10.6 us -> 9.42 us  [passed_along(): return lax.ppermute(block, axis, route)]
    pallas_call x3 -> x4, Pallas kernels: 9.31 us -> 10.4 us  [the longest x1 4.76 us: per_device(): kernel_call(first_kernel, [angles] + [square] * 3, [SMEM, SMEM] + [VMEM]...]
  transfers between devices with their start and end apart: 24 -> 24, of which waited for: 13 -> 14; matrix products, arithmetic and copies ran while one was open for 0% -> 0% of each run, Pallas kernels for 14% -> 16%
where the time goes in v8:
time: 93.2 us; the launch traced here: 92.3 us
  starting transfers between devices  41.5 us (45%)
  waiting for transfers between devices  30 us (32%)
  Pallas kernels  20.4 us (22%)
    ppermute x19, starting transfers between devices, swapped(): lax.ppermute(block, axis, [(i, i ^ bits) for i in range(lax.axis_size(axi...  32 us
    ppermute x19, waiting for transfers between devices, swapped(): lax.ppermute(block, axis, [(i, i ^ bits) for i in range(lax.axis_size(axi...  26.4 us
    ppermute x5, starting transfers between devices, passed_along(): return lax.ppermute(block, axis, route)  9.42 us
    pallas_call x1, Pallas kernels, per_device(): kernel_call(first_kernel, [angles] + [square] * 3, [SMEM, SMEM] + [VMEM]...  4.76 us
    pallas_call x1, Pallas kernels, per_device(): kernel_call(second_kernel, [angles], [SMEM, SMEM] + [VMEM] * 6, [square]...  4.19 us
    ppermute x5, waiting for transfers between devices, passed_along(): return lax.ppermute(block, axis, route)  3.61 us
    pallas_call x1, Pallas kernels, per_device(): output_call(upper_kernel, matrix, [VMEM] * 3, [block, block])  2.27 us
    pallas_call x1, Pallas kernels, per_device(): kernel_call(own_kernel, [block, block], [SMEM, VMEM, VMEM])  2.24 us
  transfers between devices with their start and end apart: 24, of which 14 were waited for; matrix products, arithmetic and copies ran while one was open for 0% of the time, Pallas kernels for 16%

profile of v8, /device:TPU:8, one launch (start us, length us, event | category | flops | bytes accessed | tf_op | source)
XLA Modules:
  0.0 92.3 jit_solution(6473229407503801401)
XLA Ops:
  0.0 1.9 %shard_map.28 = (f32[136,256]{1,0:T(8,128)S(1)}, f32[136,256]{1,0:T(8,128)S(1)}, f32[136,256]{1,0:T(8,128)S(1)}, f32[136,256]{1,0:T(8,128)S(1)}) custom-call(s32[1]{0:T(128)} %bitcast.1.place_ref, f32[256,512]{1,0:T(8,128)} %pair_ref.3), custom_call_target="tpu_custom_call" | custom-call | tf_op jit(solution)/shard_map/pallas_call | solution.py:330
  1.9 2.3 %collective-permute-start = (f32[136,256]{1,0:T(8,128)S(1)}, f32[136,256]{1,0:T(8,128)S(1)}, u32[]{:S(2)}, u32[]{:S(2)}) collective-permute-start(f32[136,256]{1,0:T(8,128)S(1)} %get-tuple-element.27), channel_id=1, source_target_pairs={{0,16},{16,0},{32,48},{48,32},{64,80},{80,64},{96,112},{112,96},{1... | collective-permute-start | bytes 417800 | tf_op jit(solution)/shard_map/ppermute | solution.py:294
  4.2 0.2 collective-permute-start.1
  4.4 1.4 %collective-permute-start.2 = (f32[136,256]{1,0:T(8,128)S(1)}, f32[136,256]{1,0:T(8,128)S(1)}, u32[]{:S(2)}, u32[]{:S(2)}) collective-permute-start(f32[136,256]{1,0:T(8,128)S(1)} %get-tuple-element.29), channel_id=1, source_target_pairs={{0,48},{16,32},{32,16},{48,0},{64,112},{80,96},{96,80},{112,64},{1... | collective-permute-start | bytes 417800 | tf_op jit(solution)/shard_map/ppermute | solution.py:294
  5.7 1.9 %collective-permute-done = f32[136,256]{1,0:T(8,128)S(1)} collective-permute-done((f32[136,256]{1,0:T(8,128)S(1)}, f32[136,256]{1,0:T(8,128)S(1)}, u32[]{:S(2)}, u32[]{:S(2)}) %collective-permute-start) | collective-permute-done | bytes 139296 | tf_op jit(solution)/shard_map/ppermute | solution.py:294
  7.6 2.6 %collective-permute-done.1 = f32[136,256]{1,0:T(8,128)S(1)} collective-permute-done((f32[136,256]{1,0:T(8,128)S(1)}, f32[136,256]{1,0:T(8,128)S(1)}, u32[]{:S(2)}, u32[]{:S(2)}) %collective-permute-start.1) | collective-permute-done | bytes 139296 | tf_op jit(solution)/shard_map/ppermute | solution.py:294
  10.2 1.5 %collective-permute-done.2 = f32[136,256]{1,0:T(8,128)S(1)} collective-permute-done((f32[136,256]{1,0:T(8,128)S(1)}, f32[136,256]{1,0:T(8,128)S(1)}, u32[]{:S(2)}, u32[]{:S(2)}) %collective-permute-start.2) | collective-permute-done | bytes 139296 | tf_op jit(solution)/shard_map/ppermute | solution.py:294
  11.8 6.2 %collective-permute-start.5 = (f32[72,256]{1,0:T(8,128)S(1)}, f32[72,256]{1,0:T(8,128)S(1)}, u32[]{:S(2)}, u32[]{:S(2)}) collective-permute-start(f32[72,256]{1,0:T(8,128)S(1)} %slice.20), channel_id=1, source_target_pairs={{0,192},{16,208},{32,224},{48,240},{64,128},{80,144},{96,160},{112... | collective-permute-start | bytes 221192 | tf_op jit(solution)/shard_map/ppermute | solution.py:294
  18.0 1.4 %collective-permute-start.3 = (f32[64,256]{1,0:T(8,128)S(1)}, f32[64,256]{1,0:T(8,128)S(1)}, u32[]{:S(2)}, u32[]{:S(2)}) collective-permute-start(f32[64,256]{1,0:T(8,128)S(1)} %slice.19), channel_id=1, source_target_pairs={{0,64},{16,80},{32,96},{48,112},{64,0},{80,16},{96,32},{112,48},{1... | collective-permute-start | bytes 196616 | tf_op jit(solution)/shard_map/ppermute | solution.py:294
  19.5 2.3 %collective-permute-start.11 = (f32[256,512]{1,0:T(8,128)}, f32[256,512]{1,0:T(8,128)S(1)}, u32[]{:S(2)}, u32[]{:S(2)}) collective-permute-start(f32[256,512]{1,0:T(8,128)} %pair_ref.3), channel_id=1, source_target_pairs={{14,0},{15,1},{0,2},{1,3},{2,4},{3,5},{4,6},{5,7},{6,8},{7,9},{8,1... | collective-permute-start | bytes 1572872 | tf_op jit(solution)/shard_map/ppermute | solution.py:290
  21.8 0.0 collective-permute-done.5
  21.8 1.6 %collective-permute-start.6 = (f32[72,256]{1,0:T(8,128)S(1)}, f32[72,256]{1,0:T(8,128)S(1)}, u32[]{:S(2)}, u32[]{:S(2)}) collective-permute-start(f32[72,256]{1,0:T(8,128)S(1)} %slice_add_fusion.1), channel_id=1, source_target_pairs={{0,64},{16,80},{32,96},{48,112},{64,0},{80,16},{96,32},{112,48},{1... | collective-permute-start | bytes 221192 | tf_op jit(solution)/shard_map/ppermute | solution.py:294
  23.4 1.5 %collective-permute-done.3 = f32[64,256]{1,0:T(8,128)S(1)} collective-permute-done((f32[64,256]{1,0:T(8,128)S(1)}, f32[64,256]{1,0:T(8,128)S(1)}, u32[]{:S(2)}, u32[]{:S(2)}) %collective-permute-start.3) | collective-permute-done | bytes 65568 | tf_op jit(solution)/shard_map/ppermute | solution.py:294
  24.9 1.7 %collective-permute-start.4 = (f32[64,256]{1,0:T(8,128)S(1)}, f32[64,256]{1,0:T(8,128)S(1)}, u32[]{:S(2)}, u32[]{:S(2)}) collective-permute-start(f32[64,256]{1,0:T(8,128)S(1)} %slice_add_fusion), channel_id=1, source_target_pairs={{0,192},{16,208},{32,224},{48,240},{64,128},{80,144},{96,160},{112... | collective-permute-start | bytes 196616 | tf_op jit(solution)/shard_map/ppermute | solution.py:294
  26.6 4.8 %collective-permute-done.4 = f32[64,256]{1,0:T(8,128)S(1)} collective-permute-done((f32[64,256]{1,0:T(8,128)S(1)}, f32[64,256]{1,0:T(8,128)S(1)}, u32[]{:S(2)}, u32[]{:S(2)}) %collective-permute-start.4) | collective-permute-done | bytes 65568 | tf_op jit(solution)/shard_map/ppermute | solution.py:294
  31.4 0.0 collective-permute-done.6
  31.4 0.0 copy-start
  31.4 0.1 collective-permute-start.7
  31.5 1.5 %collective-permute-start.8 = (f32[136,256]{1,0:T(8,128)S(1)}, f32[136,256]{1,0:T(8,128)S(1)}, u32[]{:S(2)}, u32[]{:S(2)}) collective-permute-start(f32[136,256]{1,0:T(8,128)S(1)} %pad_maximum_fusion.in0), channel_id=1, source_target_pairs={{0,32},{16,48},{32,0},{48,16},{64,96},{80,112},{96,64},{112,80},{1... | collective-permute-start | bytes 417800 | tf_op jit(solution)/shard_map/ppermute | solution.py:294
  33.1 1.9 %collective-permute-start.9 = (f32[136,256]{1,0:T(8,128)S(1)}, f32[136,256]{1,0:T(8,128)S(1)}, u32[]{:S(2)}, u32[]{:S(2)}) collective-permute-start(f32[136,256]{1,0:T(8,128)S(1)} %pad_maximum_fusion.in0), channel_id=1, source_target_pairs={{0,48},{16,32},{32,16},{48,0},{64,112},{80,96},{96,80},{112,64},{1... | collective-permute-start | bytes 417800 | tf_op jit(solution)/shard_map/ppermute | solution.py:294
  35.0 0.0 copy-done
  35.0 2.7 %collective-permute-done.7.in1 = f32[136,256]{1,0:T(8,128)S(1)} collective-permute-done((f32[136,256]{1,0:T(8,128)S(1)}, f32[136,256]{1,0:T(8,128)S(1)}, u32[]{:S(2)}, u32[]{:S(2)}) %collective-permute-start.7) | collective-permute-done | bytes 139296 | tf_op jit(solution)/shard_map/ppermute | solution.py:294
  37.7 0.0 collective-permute-done.8.in2
  37.7 1.8 %collective-permute-done.9.in3 = f32[136,256]{1,0:T(8,128)S(1)} collective-permute-done((f32[136,256]{1,0:T(8,128)S(1)}, f32[136,256]{1,0:T(8,128)S(1)}, u32[]{:S(2)}, u32[]{:S(2)}) %collective-permute-start.9) | collective-permute-done | bytes 139296 | tf_op jit(solution)/shard_map/ppermute | solution.py:294
  39.5 4.8 %shard_map.29 = (f32[16,256]{1,0:T(8,128)S(1)}, f32[256,256]{1,0:T(8,128)S(1)}, f32[256,256]{1,0:T(8,128)S(1)}, f32[256,256]{1,0:T(8,128)S(1)}) custom-call(s32[1]{0:T(128)} %bitcast.1.place_ref, s32[8]{0:T(128)S(1)} %get-tuple-element.47.shift_ref, f32[136,256]{1,0:T(8,128)S(1)} %pad_maximum_fusion.in0, f32[136,256]{1,0:T(8,128)S(1)} %collective-permute-done.7.in1, ...), custom_call_target="tpu_custom_call" | custom-call | tf_op jit(solution)/shard_map/pallas_call | solution.py:337
  44.3 2.6 %collective-permute-start.10 = (f32[16,256]{1,0:T(8,128)S(1)}, f32[16,256]{1,0:T(8,128)S(1)}, u32[]{:S(2)}, u32[]{:S(2)}) collective-permute-start(f32[16,256]{1,0:T(8,128)S(1)} %get-tuple-element.31.angles_ref), channel_id=1, source_target_pairs={{14,0},{15,1},{0,2},{1,3},{2,4},{3,5},{4,6},{5,7},{6,8},{7,9},{8,1... | collective-permute-start | bytes 49160 | tf_op jit(solution)/shard_map/ppermute | solution.py:290
  46.9 2.2 %shard_map.30 = (f32[256,256]{1,0:T(8,128)S(1)}, f32[256,256]{1,0:T(8,128)S(1)}) custom-call(s32[8]{0:T(128)S(1)} %get-tuple-element.47.shift_ref, f32[16,256]{1,0:T(8,128)S(1)} %get-tuple-element.31.angles_ref, f32[256,512]{1,0:T(8,128)} %pair_ref.3), custom_call_target="tpu_custom_call" | custom-call | tf_op jit(solution)/shard_map/pallas_call | solution.py:341
  49.1 2.8 %collective-permute-done.10.angles_ref = f32[16,256]{1,0:T(8,128)S(1)} collective-permute-done((f32[16,256]{1,0:T(8,128)S(1)}, f32[16,256]{1,0:T(8,128)S(1)}, u32[]{:S(2)}, u32[]{:S(2)}) %collective-permute-start.10) | collective-permute-done | bytes 16416 | tf_op jit(solution)/shard_map/ppermute | solution.py:290
  51.9 0.0 collective-permute-done.11.other_ref
  51.9 1.6 %shard_map.31 = (f32[256,256]{1,0:T(8,128)S(1)}, f32[64,256]{1,0:T(8,128)S(1)}, f32[64,256]{1,0:T(8,128)S(1)}, f32[64,256]{1,0:T(8,128)S(1)}, f32[64,256]{1,0:T(8,128)S(1)}) custom-call(s32[1]{0:T(128)} %bitcast.1.place_ref, s32[8]{0:T(128)S(1)} %get-tuple-element.47.shift_ref, f32[16,256]{1,0:T(8,128)S(1)} %collective-permute-done.10.angles_ref, ...), custom_call_target="tpu_custom_call" | custom-call | tf_op jit(solution)/shard_map/pallas_call | solution.py:347
  53.5 0.5 collective-permute-start.12
  54.0 1.6 %collective-permute-start.13 = (f32[64,256]{1,0:T(8,128)S(1)}, f32[64,256]{1,0:T(8,128)S(1)}, u32[]{:S(2)}, u32[]{:S(2)}) collective-permute-start(f32[64,256]{1,0:T(8,128)S(1)} %get-tuple-element.36), channel_id=1, source_target_pairs={{0,32},{16,48},{32,0},{48,16},{64,96},{80,112},{96,64},{112,80},{1... | collective-permute-start | bytes 196616 | tf_op jit(solution)/shard_map/ppermute | solution.py:294
  55.6 1.5 %collective-permute-start.14 = (f32[64,256]{1,0:T(8,128)S(1)}, f32[64,256]{1,0:T(8,128)S(1)}, u32[]{:S(2)}, u32[]{:S(2)}) collective-permute-start(f32[64,256]{1,0:T(8,128)S(1)} %get-tuple-element.37), channel_id=1, source_target_pairs={{0,48},{16,32},{32,16},{48,0},{64,112},{80,96},{96,80},{112,64},{1... | collective-permute-start | bytes 196616 | tf_op jit(solution)/shard_map/ppermute | solution.py:294
  57.1 1.2 %shard_map.32 = (f32[192,256]{1,0:T(8,128)S(1)}, f32[256,256]{1,0:T(8,128)S(1)}) custom-call(s32[8]{0:T(128)S(1)} %get-tuple-element.47.shift_ref, f32[16,256]{1,0:T(8,128)S(1)} %get-tuple-element.31.angles_ref, f32[256,256]{1,0:T(8,128)S(1)} %get-tuple-element.38.tl, f32[256,256]{1,0:T(8,128)S(1)} %get-tuple-element.39.tr, f32[256,256]{1,0:T(8,128)S(1)} %get-tuple-element.40.lr), custom_call_target="tpu_custom_call" | custom-call | tf_op jit(solution)/shard_map/pallas_call | solution.py:344
  58.3 0.3 collective-permute-start.21
  58.6 0.0 collective-permute-done.12
  58.6 0.0 collective-permute-done.13
  58.6 3.4 %collective-permute-done.14 = f32[64,256]{1,0:T(8,128)S(1)} collective-permute-done((f32[64,256]{1,0:T(8,128)S(1)}, f32[64,256]{1,0:T(8,128)S(1)}, u32[]{:S(2)}, u32[]{:S(2)}) %collective-permute-start.14) | collective-permute-done | bytes 65568 | tf_op jit(solution)/shard_map/ppermute | solution.py:294
  62.1 0.1 collective-permute-start.15
  62.2 3.5 %collective-permute-start.16 = (f32[64,256]{1,0:T(8,128)S(1)}, f32[64,256]{1,0:T(8,128)S(1)}, u32[]{:S(2)}, u32[]{:S(2)}) collective-permute-start(f32[64,256]{1,0:T(8,128)S(1)} %add_add_fusion.2), channel_id=1, source_target_pairs={{0,128},{16,144},{32,160},{48,176},{64,192},{80,208},{96,224},{112... | collective-permute-start | bytes 196616 | tf_op jit(solution)/shard_map/ppermute | solution.py:294
  65.7 3.0 %collective-permute-start.17 = (f32[64,256]{1,0:T(8,128)S(1)}, f32[64,256]{1,0:T(8,128)S(1)}, u32[]{:S(2)}, u32[]{:S(2)}) collective-permute-start(f32[64,256]{1,0:T(8,128)S(1)} %add_add_fusion.2), channel_id=1, source_target_pairs={{0,192},{16,208},{32,224},{48,240},{64,128},{80,144},{96,160},{112... | collective-permute-start | bytes 196616 | tf_op jit(solution)/shard_map/ppermute | solution.py:294
  68.6 0.0 collective-permute-done.21.tl_ref
  68.6 2.0 %collective-permute-start.23 = (f32[256,256]{1,0:T(8,128)S(1)}, f32[256,256]{1,0:T(8,128)S(1)}, u32[]{:S(2)}, u32[]{:S(2)}) collective-permute-start(f32[256,256]{1,0:T(8,128)S(1)} %get-tuple-element.45.lower_ref.lower_in), channel_id=1, source_target_pairs={{2,0},{3,1},{4,2},{5,3},{6,4},{7,5},{8,6},{9,7},{10,8},{11,9},{12,... | collective-permute-start | bytes 786440 | tf_op jit(solution)/shard_map/ppermute | solution.py:290
  70.7 0.0 collective-permute-done.15
  70.7 0.0 collective-permute-done.16
  70.7 1.5 %collective-permute-done.17 = f32[64,256]{1,0:T(8,128)S(1)} collective-permute-done((f32[64,256]{1,0:T(8,128)S(1)}, f32[64,256]{1,0:T(8,128)S(1)}, u32[]{:S(2)}, u32[]{:S(2)}) %collective-permute-start.17) | collective-permute-done | bytes 65568 | tf_op jit(solution)/shard_map/ppermute | solution.py:294
  72.1 1.1 %collective-permute-start.18 = (f32[64,256]{1,0:T(8,128)S(1)}, f32[64,256]{1,0:T(8,128)S(1)}, u32[]{:S(2)}, u32[]{:S(2)}) collective-permute-start(f32[64,256]{1,0:T(8,128)S(1)} %add_add_fusion.1.in0), channel_id=1, source_target_pairs={{0,16},{16,0},{32,48},{48,32},{64,80},{80,64},{96,112},{112,96},{1... | collective-permute-start | bytes 196616 | tf_op jit(solution)/shard_map/ppermute | solution.py:294
  73.2 2.0 %collective-permute-start.19 = (f32[64,256]{1,0:T(8,128)S(1)}, f32[64,256]{1,0:T(8,128)S(1)}, u32[]{:S(2)}, u32[]{:S(2)}) collective-permute-start(f32[64,256]{1,0:T(8,128)S(1)} %add_add_fusion.1.in0), channel_id=1, source_target_pairs={{0,32},{16,48},{32,0},{48,16},{64,96},{80,112},{96,64},{112,80},{1... | collective-permute-start | bytes 196616 | tf_op jit(solution)/shard_map/ppermute | solution.py:294
  75.3 0.4 collective-permute-start.20
  75.7 0.8 collective-permute-done.18.in1
  76.5 1.0 %collective-permute-done.19.in2 = f32[64,256]{1,0:T(8,128)S(1)} collective-permute-done((f32[64,256]{1,0:T(8,128)S(1)}, f32[64,256]{1,0:T(8,128)S(1)}, u32[]{:S(2)}, u32[]{:S(2)}) %collective-permute-start.19) | collective-permute-done | bytes 65568 | tf_op jit(solution)/shard_map/ppermute | solution.py:294
  77.5 2.9 %collective-permute-done.20.in3 = f32[64,256]{1,0:T(8,128)S(1)} collective-permute-done((f32[64,256]{1,0:T(8,128)S(1)}, f32[64,256]{1,0:T(8,128)S(1)}, u32[]{:S(2)}, u32[]{:S(2)}) %collective-permute-start.20) | collective-permute-done | bytes 65568 | tf_op jit(solution)/shard_map/ppermute | solution.py:294
  80.4 4.2 %shard_map.33.angles_ref = f32[16,256]{1,0:T(8,128)S(1)} custom-call(s32[1]{0:T(128)} %bitcast.1.place_ref, s32[8]{0:T(128)S(1)} %get-tuple-element.48.shift_ref, f32[64,256]{1,0:T(8,128)S(1)} %add_add_fusion.1.in0, f32[64,256]{1,0:T(8,128)S(1)} %collective-permute-done.18.in1, f32[64,256]{1,0:T(8,128)S(1)} %collective-permute-done.19.in2, ...), custom_call_target="tpu_custom_call" | custom-call | tf_op jit(solution)/shard_map/pallas_call | solution.py:358
  84.6 2.2 %collective-permute-start.22 = (f32[16,256]{1,0:T(8,128)S(1)}, f32[16,256]{1,0:T(8,128)S(1)}, u32[]{:S(2)}, u32[]{:S(2)}) collective-permute-start(f32[16,256]{1,0:T(8,128)S(1)} %shard_map.33.angles_ref), channel_id=1, source_target_pairs={{2,0},{3,1},{4,2},{5,3},{6,4},{7,5},{8,6},{9,7},{10,8},{11,9},{12,... | collective-permute-start | bytes 49160 | tf_op jit(solution)/shard_map/ppermute | solution.py:290
  86.9 2.3 %shard_map.34.half_ref = f32[256,512]{1,0:T(8,128)} custom-call(s32[8]{0:T(128)S(1)} %get-tuple-element.48.shift_ref, f32[16,256]{1,0:T(8,128)S(1)} %shard_map.33.angles_ref, f32[256,256]{1,0:T(8,128)S(1)} %get-tuple-element.46.upper_in, f32[256,256]{1,0:T(8,128)S(1)} %get-tuple-element.45.lower_ref.lower_in), custom_call_target="tpu_custom_call" | custom-call | tf_op jit(solution)/shard_map/pallas_call | solution.py:362
  89.1 0.8 collective-permute-done.22.angles_ref
  90.0 0.0 collective-permute-done.23.lower_in
  90.0 2.2 %shard_map.35 = f32[256,512]{1,0:T(8,128)} custom-call(s32[8]{0:T(128)S(1)} %get-tuple-element.48.shift_ref, f32[16,256]{1,0:T(8,128)S(1)} %collective-permute-done.22.angles_ref, f32[256,256]{1,0:T(8,128)S(1)} %get-tuple-element.44.upper_in, f32[256,256]{1,0:T(8,128)S(1)} %collective-permute-done.23.lower_in, ...), custom_call_target="tpu_custom_call", output_to_operand_aliasing={{}: (4, {})} | custom-call | tf_op jit(solution)/shard_map/pallas_call | solution.py:365
  (11 shorter events, 0.1 us)
Async XLA Ops:
  1.9 5.7 %collective-permute-start = (f32[136,256]{1,0:T(8,128)S(1)}, f32[136,256]{1,0:T(8,128)S(1)}, u32[]{:S(2)}, u32[]{:S(2)}) collective-permute-start(f32[136,256]{1,0:T(8,128)S(1)} %get-tuple-element.27), channel_id=1, source_target_pairs={{0,16},{16,0},{32,48},{48,32},{64,80},{80,64},{96,112},{112,96},{1... | collective-permute-start | bytes 417800 | tf_op jit(solution)/shard_map/ppermute | solution.py:294
  4.2 6.0 %collective-permute-start.1 = (f32[136,256]{1,0:T(8,128)S(1)}, f32[136,256]{1,0:T(8,128)S(1)}, u32[]{:S(2)}, u32[]{:S(2)}) collective-permute-start(f32[136,256]{1,0:T(8,128)S(1)} %get-tuple-element.28), channel_id=1, source_target_pairs={{0,32},{16,48},{32,0},{48,16},{64,96},{80,112},{96,64},{112,80},{1... | collective-permute-start | bytes 417800 | tf_op jit(solution)/shard_map/ppermute | solution.py:294
  4.4 7.4 %collective-permute-start.2 = (f32[136,256]{1,0:T(8,128)S(1)}, f32[136,256]{1,0:T(8,128)S(1)}, u32[]{:S(2)}, u32[]{:S(2)}) collective-permute-start(f32[136,256]{1,0:T(8,128)S(1)} %get-tuple-element.29), channel_id=1, source_target_pairs={{0,48},{16,32},{32,16},{48,0},{64,112},{80,96},{96,80},{112,64},{1... | collective-permute-start | bytes 417800 | tf_op jit(solution)/shard_map/ppermute | solution.py:294
  11.8 10.0 %collective-permute-start.5 = (f32[72,256]{1,0:T(8,128)S(1)}, f32[72,256]{1,0:T(8,128)S(1)}, u32[]{:S(2)}, u32[]{:S(2)}) collective-permute-start(f32[72,256]{1,0:T(8,128)S(1)} %slice.20), channel_id=1, source_target_pairs={{0,192},{16,208},{32,224},{48,240},{64,128},{80,144},{96,160},{112... | collective-permute-start | bytes 221192 | tf_op jit(solution)/shard_map/ppermute | solution.py:294
  18.0 6.8 %collective-permute-start.3 = (f32[64,256]{1,0:T(8,128)S(1)}, f32[64,256]{1,0:T(8,128)S(1)}, u32[]{:S(2)}, u32[]{:S(2)}) collective-permute-start(f32[64,256]{1,0:T(8,128)S(1)} %slice.19), channel_id=1, source_target_pairs={{0,64},{16,80},{32,96},{48,112},{64,0},{80,16},{96,32},{112,48},{1... | collective-permute-start | bytes 196616 | tf_op jit(solution)/shard_map/ppermute | solution.py:294
  19.5 32.4 %collective-permute-start.11 = (f32[256,512]{1,0:T(8,128)}, f32[256,512]{1,0:T(8,128)S(1)}, u32[]{:S(2)}, u32[]{:S(2)}) collective-permute-start(f32[256,512]{1,0:T(8,128)} %pair_ref.3), channel_id=1, source_target_pairs={{14,0},{15,1},{0,2},{1,3},{2,4},{3,5},{4,6},{5,7},{6,8},{7,9},{8,1... | collective-permute-start | bytes 1572872 | tf_op jit(solution)/shard_map/ppermute | solution.py:290
  21.8 9.6 %collective-permute-start.6 = (f32[72,256]{1,0:T(8,128)S(1)}, f32[72,256]{1,0:T(8,128)S(1)}, u32[]{:S(2)}, u32[]{:S(2)}) collective-permute-start(f32[72,256]{1,0:T(8,128)S(1)} %slice_add_fusion.1), channel_id=1, source_target_pairs={{0,64},{16,80},{32,96},{48,112},{64,0},{80,16},{96,32},{112,48},{1... | collective-permute-start | bytes 221192 | tf_op jit(solution)/shard_map/ppermute | solution.py:294
  24.9 6.5 %collective-permute-start.4 = (f32[64,256]{1,0:T(8,128)S(1)}, f32[64,256]{1,0:T(8,128)S(1)}, u32[]{:S(2)}, u32[]{:S(2)}) collective-permute-start(f32[64,256]{1,0:T(8,128)S(1)} %slice_add_fusion), channel_id=1, source_target_pairs={{0,192},{16,208},{32,224},{48,240},{64,128},{80,144},{96,160},{112... | collective-permute-start | bytes 196616 | tf_op jit(solution)/shard_map/ppermute | solution.py:294
  31.4 3.6 %copy-start = (s32[2,8]{1,0:T(2,128)S(1)}, s32[2,8]{1,0:T(2,128)}, u32[]{:S(2)}) copy-start(s32[2,8]{1,0:T(2,128)} %param.3) | copy-start | bytes 196
  31.4 6.3 %collective-permute-start.7 = (f32[136,256]{1,0:T(8,128)S(1)}, f32[136,256]{1,0:T(8,128)S(1)}, u32[]{:S(2)}, u32[]{:S(2)}) collective-permute-start(f32[136,256]{1,0:T(8,128)S(1)} %pad_maximum_fusion.in0), channel_id=1, source_target_pairs={{0,16},{16,0},{32,48},{48,32},{64,80},{80,64},{96,112},{112,96},{1... | collective-permute-start | bytes 417800 | tf_op jit(solution)/shard_map/ppermute | solution.py:294
  31.5 6.2 %collective-permute-start.8 = (f32[136,256]{1,0:T(8,128)S(1)}, f32[136,256]{1,0:T(8,128)S(1)}, u32[]{:S(2)}, u32[]{:S(2)}) collective-permute-start(f32[136,256]{1,0:T(8,128)S(1)} %pad_maximum_fusion.in0), channel_id=1, source_target_pairs={{0,32},{16,48},{32,0},{48,16},{64,96},{80,112},{96,64},{112,80},{1... | collective-permute-start | bytes 417800 | tf_op jit(solution)/shard_map/ppermute | solution.py:294
  33.1 6.5 %collective-permute-start.9 = (f32[136,256]{1,0:T(8,128)S(1)}, f32[136,256]{1,0:T(8,128)S(1)}, u32[]{:S(2)}, u32[]{:S(2)}) collective-permute-start(f32[136,256]{1,0:T(8,128)S(1)} %pad_maximum_fusion.in0), channel_id=1, source_target_pairs={{0,48},{16,32},{32,16},{48,0},{64,112},{80,96},{96,80},{112,64},{1... | collective-permute-start | bytes 417800 | tf_op jit(solution)/shard_map/ppermute | solution.py:294
  44.3 7.6 %collective-permute-start.10 = (f32[16,256]{1,0:T(8,128)S(1)}, f32[16,256]{1,0:T(8,128)S(1)}, u32[]{:S(2)}, u32[]{:S(2)}) collective-permute-start(f32[16,256]{1,0:T(8,128)S(1)} %get-tuple-element.31.angles_ref), channel_id=1, source_target_pairs={{14,0},{15,1},{0,2},{1,3},{2,4},{3,5},{4,6},{5,7},{6,8},{7,9},{8,1... | collective-permute-start | bytes 49160 | tf_op jit(solution)/shard_map/ppermute | solution.py:290
  53.5 5.1 %collective-permute-start.12 = (f32[64,256]{1,0:T(8,128)S(1)}, f32[64,256]{1,0:T(8,128)S(1)}, u32[]{:S(2)}, u32[]{:S(2)}) collective-permute-start(f32[64,256]{1,0:T(8,128)S(1)} %get-tuple-element.35), channel_id=1, source_target_pairs={{0,16},{16,0},{32,48},{48,32},{64,80},{80,64},{96,112},{112,96},{1... | collective-permute-start | bytes 196616 | tf_op jit(solution)/shard_map/ppermute | solution.py:294
  54.0 4.6 %collective-permute-start.13 = (f32[64,256]{1,0:T(8,128)S(1)}, f32[64,256]{1,0:T(8,128)S(1)}, u32[]{:S(2)}, u32[]{:S(2)}) collective-permute-start(f32[64,256]{1,0:T(8,128)S(1)} %get-tuple-element.36), channel_id=1, source_target_pairs={{0,32},{16,48},{32,0},{48,16},{64,96},{80,112},{96,64},{112,80},{1... | collective-permute-start | bytes 196616 | tf_op jit(solution)/shard_map/ppermute | solution.py:294
  55.6 6.4 %collective-permute-start.14 = (f32[64,256]{1,0:T(8,128)S(1)}, f32[64,256]{1,0:T(8,128)S(1)}, u32[]{:S(2)}, u32[]{:S(2)}) collective-permute-start(f32[64,256]{1,0:T(8,128)S(1)} %get-tuple-element.37), channel_id=1, source_target_pairs={{0,48},{16,32},{32,16},{48,0},{64,112},{80,96},{96,80},{112,64},{1... | collective-permute-start | bytes 196616 | tf_op jit(solution)/shard_map/ppermute | solution.py:294
  58.3 10.3 %collective-permute-start.21 = (f32[192,256]{1,0:T(8,128)S(1)}, f32[192,256]{1,0:T(8,128)S(1)}, u32[]{:S(2)}, u32[]{:S(2)}) collective-permute-start(f32[192,256]{1,0:T(8,128)S(1)} %get-tuple-element.41), channel_id=1, source_target_pairs={{14,0},{15,1},{0,2},{1,3},{2,4},{3,5},{4,6},{5,7},{6,8},{7,9},{8,1... | collective-permute-start | bytes 589832 | tf_op jit(solution)/shard_map/ppermute | solution.py:290
  62.1 8.6 %collective-permute-start.15 = (f32[64,256]{1,0:T(8,128)S(1)}, f32[64,256]{1,0:T(8,128)S(1)}, u32[]{:S(2)}, u32[]{:S(2)}) collective-permute-start(f32[64,256]{1,0:T(8,128)S(1)} %add_add_fusion.2), channel_id=1, source_target_pairs={{0,64},{16,80},{32,96},{48,112},{64,0},{80,16},{96,32},{112,48},{1... | collective-permute-start | bytes 196616 | tf_op jit(solution)/shard_map/ppermute | solution.py:294
  62.2 8.5 %collective-permute-start.16 = (f32[64,256]{1,0:T(8,128)S(1)}, f32[64,256]{1,0:T(8,128)S(1)}, u32[]{:S(2)}, u32[]{:S(2)}) collective-permute-start(f32[64,256]{1,0:T(8,128)S(1)} %add_add_fusion.2), channel_id=1, source_target_pairs={{0,128},{16,144},{32,160},{48,176},{64,192},{80,208},{96,224},{112... | collective-permute-start | bytes 196616 | tf_op jit(solution)/shard_map/ppermute | solution.py:294
  65.7 6.4 %collective-permute-start.17 = (f32[64,256]{1,0:T(8,128)S(1)}, f32[64,256]{1,0:T(8,128)S(1)}, u32[]{:S(2)}, u32[]{:S(2)}) collective-permute-start(f32[64,256]{1,0:T(8,128)S(1)} %add_add_fusion.2), channel_id=1, source_target_pairs={{0,192},{16,208},{32,224},{48,240},{64,128},{80,144},{96,160},{112... | collective-permute-start | bytes 196616 | tf_op jit(solution)/shard_map/ppermute | solution.py:294
  68.6 21.3 %collective-permute-start.23 = (f32[256,256]{1,0:T(8,128)S(1)}, f32[256,256]{1,0:T(8,128)S(1)}, u32[]{:S(2)}, u32[]{:S(2)}) collective-permute-start(f32[256,256]{1,0:T(8,128)S(1)} %get-tuple-element.45.lower_ref.lower_in), channel_id=1, source_target_pairs={{2,0},{3,1},{4,2},{5,3},{6,4},{7,5},{8,6},{9,7},{10,8},{11,9},{12,... | collective-permute-start | bytes 786440 | tf_op jit(solution)/shard_map/ppermute | solution.py:290
  72.1 4.4 %collective-permute-start.18 = (f32[64,256]{1,0:T(8,128)S(1)}, f32[64,256]{1,0:T(8,128)S(1)}, u32[]{:S(2)}, u32[]{:S(2)}) collective-permute-start(f32[64,256]{1,0:T(8,128)S(1)} %add_add_fusion.1.in0), channel_id=1, source_target_pairs={{0,16},{16,0},{32,48},{48,32},{64,80},{80,64},{96,112},{112,96},{1... | collective-permute-start | bytes 196616 | tf_op jit(solution)/shard_map/ppermute | solution.py:294
  73.2 4.3 %collective-permute-start.19 = (f32[64,256]{1,0:T(8,128)S(1)}, f32[64,256]{1,0:T(8,128)S(1)}, u32[]{:S(2)}, u32[]{:S(2)}) collective-permute-start(f32[64,256]{1,0:T(8,128)S(1)} %add_add_fusion.1.in0), channel_id=1, source_target_pairs={{0,32},{16,48},{32,0},{48,16},{64,96},{80,112},{96,64},{112,80},{1... | collective-permute-start | bytes 196616 | tf_op jit(solution)/shard_map/ppermute | solution.py:294
  75.3 5.2 %collective-permute-start.20 = (f32[64,256]{1,0:T(8,128)S(1)}, f32[64,256]{1,0:T(8,128)S(1)}, u32[]{:S(2)}, u32[]{:S(2)}) collective-permute-start(f32[64,256]{1,0:T(8,128)S(1)} %add_add_fusion.1.in0), channel_id=1, source_target_pairs={{0,48},{16,32},{32,16},{48,0},{64,112},{80,96},{96,80},{112,64},{1... | collective-permute-start | bytes 196616 | tf_op jit(solution)/shard_map/ppermute | solution.py:294
  84.6 5.3 %collective-permute-start.22 = (f32[16,256]{1,0:T(8,128)S(1)}, f32[16,256]{1,0:T(8,128)S(1)}, u32[]{:S(2)}, u32[]{:S(2)}) collective-permute-start(f32[16,256]{1,0:T(8,128)S(1)} %shard_map.33.angles_ref), channel_id=1, source_target_pairs={{2,0},{3,1},{4,2},{5,3},{6,4},{7,5},{8,6},{9,7},{10,8},{11,9},{12,... | collective-permute-start | bytes 49160 | tf_op jit(solution)/shard_map/ppermute | solution.py:290

commit v9 on v8

--- a/solution.py
+++ b/solution.py
@@ -300,8 +300,8 @@
 
 
 def across_fours(mine, axis):
-    met = [swapped(mine, axis, k) for k in (8, 4, 12)]
-    return (mine + met[1]) + (met[0] + met[2])
+    met = [swapped(mine, axis, k) for k in (4, 12, 8)]
+    return (mine + met[0]) + (met[1] + met[2])
 
 
 def met_across(mine, axis):
@@ -330,9 +330,10 @@
     gram = kernel_call(
         gram_kernel, [(2 * w // 4 + 8, w)] * 4, [SMEM, VMEM], [square, square, diag]
     )(place, matrix)
-    gram = within_four(gram, "row")
-    gram, sent = lax.optimization_barrier((gram, matrix))
-    other = passed_along(sent, "col", 2)
+    sent = [swapped(gram[k], "row", k) for k in (3, 1, 2)]
+    sent[2], moved = lax.optimization_barrier((sent[2], matrix))
+    other = passed_along(moved, "col", 2)
+    gram = (gram[0] + sent[1]) + (sent[2] + sent[0])
     gram = shared_in_four(met_across(gram, "row"), "row")
     here, *state = kernel_call(
         first_kernel, [angles] + [square] * 3, [SMEM, SMEM] + [VMEM] * 4, [diag]
@@ -350,7 +351,9 @@
         [SMEM, SMEM] + [VMEM] * 3,
         [block, square],
     )(place, shifts[0], there, other, lower)
-    cross = within_four(cross, "row")
+    sent = [swapped(cross[k], "row", k) for k in (3, 1, 2)]
+    sent[2], tl = lax.optimization_barrier((sent[2], tl))
+    cross = (cross[0] + sent[1]) + (sent[2] + sent[0])
     tl = passed_along(tl, "col", 2)
     tl, sent = lax.optimization_barrier((tl, lower))
     far_lower = passed_along(sent, "col", -2)

time: 93.2 us -> 91 us (0.976)
  waiting for transfers between devices: 30 us -> 26.4 us
  starting transfers between devices: 41.5 us -> 43.1 us
    ppermute x19, waiting for transfers between devices: 26.4 us -> 23.1 us  [swapped(): lax.ppermute(block, axis, [(i, i ^ bits) for i in range(lax.axis_size(axi...]
    ppermute x5, starting transfers between devices: 9.42 us -> 11.6 us  [passed_along(): return lax.ppermute(block, axis, route)]
where the time goes in v9:
time: 91 us; the launch traced here: 90.3 us
  starting transfers between devices  43.1 us (47%)
  waiting for transfers between devices  26.4 us (29%)
  Pallas kernels  20.4 us (22%)
    ppermute x19, starting transfers between devices, swapped(): lax.ppermute(block, axis, [(i, i ^ bits) for i in range(lax.axis_size(axi...  31.4 us
    ppermute x19, waiting for transfers between devices, swapped(): lax.ppermute(block, axis, [(i, i ^ bits) for i in range(lax.axis_size(axi...  23.1 us
    ppermute x5, starting transfers between devices, passed_along(): return lax.ppermute(block, axis, route)  11.6 us
    pallas_call x1, Pallas kernels, per_device(): kernel_call(first_kernel, [angles] + [square] * 3, [SMEM, SMEM] + [VMEM]...  4.76 us
    pallas_call x1, Pallas kernels, per_device(): kernel_call(second_kernel, [angles], [SMEM, SMEM] + [VMEM] * 6, [square]...  4.19 us
    ppermute x5, waiting for transfers between devices, passed_along(): return lax.ppermute(block, axis, route)  3.27 us
    pallas_call x1, Pallas kernels, per_device(): output_call(upper_kernel, matrix, [VMEM] * 3, [block, block])  2.27 us
    pallas_call x1, Pallas kernels, per_device(): kernel_call(own_kernel, [block, block], [SMEM, VMEM, VMEM])  2.24 us
  transfers between devices with their start and end apart: 24, of which 14 were waited for; matrix products, arithmetic and copies ran while one was open for 0% of the time, Pallas kernels for 16%

profile of v9, /device:TPU:8, one launch (start us, length us, event | category | flops | bytes accessed | tf_op | source)
XLA Modules:
  0.0 90.3 jit_solution(15778010339748969635)
XLA Ops:
  0.0 1.9 %shard_map.28 = (f32[136,256]{1,0:T(8,128)S(1)}, f32[136,256]{1,0:T(8,128)S(1)}, f32[136,256]{1,0:T(8,128)S(1)}, f32[136,256]{1,0:T(8,128)S(1)}) custom-call(s32[1]{0:T(128)} %bitcast.1.place_ref, f32[256,512]{1,0:T(8,128)} %pair_ref.3), custom_call_target="tpu_custom_call" | custom-call | tf_op jit(solution)/shard_map/pallas_call | solution.py:330
  1.9 2.0 %collective-permute-start.1 = (f32[136,256]{1,0:T(8,128)S(1)}, f32[136,256]{1,0:T(8,128)S(1)}, u32[]{:S(2)}, u32[]{:S(2)}) collective-permute-start(f32[136,256]{1,0:T(8,128)S(1)} %get-tuple-element.30), channel_id=1, source_target_pairs={{0,32},{16,48},{32,0},{48,16},{64,96},{80,112},{96,64},{112,80},{1... | collective-permute-start | bytes 417800 | tf_op jit(solution)/shard_map/ppermute | solution.py:294
  3.9 0.4 collective-permute-start
  4.4 1.3 %collective-permute-start.2 = (f32[136,256]{1,0:T(8,128)S(1)}, f32[136,256]{1,0:T(8,128)S(1)}, u32[]{:S(2)}, u32[]{:S(2)}) collective-permute-start(f32[136,256]{1,0:T(8,128)S(1)} %get-tuple-element.32), channel_id=1, source_target_pairs={{0,48},{16,32},{32,16},{48,0},{64,112},{80,96},{96,80},{112,64},{1... | collective-permute-start | bytes 417800 | tf_op jit(solution)/shard_map/ppermute | solution.py:294
  5.6 2.4 %collective-permute-done.1 = f32[136,256]{1,0:T(8,128)S(1)} collective-permute-done((f32[136,256]{1,0:T(8,128)S(1)}, f32[136,256]{1,0:T(8,128)S(1)}, u32[]{:S(2)}, u32[]{:S(2)}) %collective-permute-start.1) | collective-permute-done | bytes 139296 | tf_op jit(solution)/shard_map/ppermute | solution.py:294
  8.0 4.0 %collective-permute-done = f32[136,256]{1,0:T(8,128)S(1)} collective-permute-done((f32[136,256]{1,0:T(8,128)S(1)}, f32[136,256]{1,0:T(8,128)S(1)}, u32[]{:S(2)}, u32[]{:S(2)}) %collective-permute-start) | collective-permute-done | bytes 139296 | tf_op jit(solution)/shard_map/ppermute | solution.py:294
  12.0 0.0 collective-permute-done.2
  12.1 5.5 %collective-permute-start.5 = (f32[72,256]{1,0:T(8,128)S(1)}, f32[72,256]{1,0:T(8,128)S(1)}, u32[]{:S(2)}, u32[]{:S(2)}) collective-permute-start(f32[72,256]{1,0:T(8,128)S(1)} %slice.22), channel_id=1, source_target_pairs={{0,192},{16,208},{32,224},{48,240},{64,128},{80,144},{96,160},{112... | collective-permute-start | bytes 221192 | tf_op jit(solution)/shard_map/ppermute | solution.py:294
  17.6 1.5 %collective-permute-start.3 = (f32[64,256]{1,0:T(8,128)S(1)}, f32[64,256]{1,0:T(8,128)S(1)}, u32[]{:S(2)}, u32[]{:S(2)}) collective-permute-start(f32[64,256]{1,0:T(8,128)S(1)} %slice.21), channel_id=1, source_target_pairs={{0,64},{16,80},{32,96},{48,112},{64,0},{80,16},{96,32},{112,48},{1... | collective-permute-start | bytes 196616 | tf_op jit(solution)/shard_map/ppermute | solution.py:294
  19.0 2.3 %collective-permute-start.11 = (f32[256,512]{1,0:T(8,128)}, f32[256,512]{1,0:T(8,128)S(1)}, u32[]{:S(2)}, u32[]{:S(2)}) collective-permute-start(f32[256,512]{1,0:T(8,128)} %pair_ref.3), channel_id=1, source_target_pairs={{14,0},{15,1},{0,2},{1,3},{2,4},{3,5},{4,6},{5,7},{6,8},{7,9},{8,1... | collective-permute-start | bytes 1572872 | tf_op jit(solution)/shard_map/ppermute | solution.py:290
  21.3 0.0 collective-permute-done.5
  21.4 1.6 %collective-permute-start.6 = (f32[72,256]{1,0:T(8,128)S(1)}, f32[72,256]{1,0:T(8,128)S(1)}, u32[]{:S(2)}, u32[]{:S(2)}) collective-permute-start(f32[72,256]{1,0:T(8,128)S(1)} %slice_add_fusion.1), channel_id=1, source_target_pairs={{0,64},{16,80},{32,96},{48,112},{64,0},{80,16},{96,32},{112,48},{1... | collective-permute-start | bytes 221192 | tf_op jit(solution)/shard_map/ppermute | solution.py:294
  22.9 1.6 %collective-permute-done.3 = f32[64,256]{1,0:T(8,128)S(1)} collective-permute-done((f32[64,256]{1,0:T(8,128)S(1)}, f32[64,256]{1,0:T(8,128)S(1)}, u32[]{:S(2)}, u32[]{:S(2)}) %collective-permute-start.3) | collective-permute-done | bytes 65568 | tf_op jit(solution)/shard_map/ppermute | solution.py:294
  24.5 1.3 %collective-permute-start.4 = (f32[64,256]{1,0:T(8,128)S(1)}, f32[64,256]{1,0:T(8,128)S(1)}, u32[]{:S(2)}, u32[]{:S(2)}) collective-permute-start(f32[64,256]{1,0:T(8,128)S(1)} %slice_add_fusion), channel_id=1, source_target_pairs={{0,192},{16,208},{32,224},{48,240},{64,128},{80,144},{96,160},{112... | collective-permute-start | bytes 196616 | tf_op jit(solution)/shard_map/ppermute | solution.py:294
  25.9 5.1 %collective-permute-done.4 = f32[64,256]{1,0:T(8,128)S(1)} collective-permute-done((f32[64,256]{1,0:T(8,128)S(1)}, f32[64,256]{1,0:T(8,128)S(1)}, u32[]{:S(2)}, u32[]{:S(2)}) %collective-permute-start.4) | collective-permute-done | bytes 65568 | tf_op jit(solution)/shard_map/ppermute | solution.py:294
  31.0 0.0 collective-permute-done.6
  31.0 0.0 copy-start
  31.1 1.1 %collective-permute-start.9 = (f32[136,256]{1,0:T(8,128)S(1)}, f32[136,256]{1,0:T(8,128)S(1)}, u32[]{:S(2)}, u32[]{:S(2)}) collective-permute-start(f32[136,256]{1,0:T(8,128)S(1)} %pad_maximum_fusion.in0), channel_id=1, source_target_pairs={{0,48},{16,32},{32,16},{48,0},{64,112},{80,96},{96,80},{112,64},{1... | collective-permute-start | bytes 417800 | tf_op jit(solution)/shard_map/ppermute | solution.py:294
  32.1 0.3 collective-permute-start.8
  32.5 2.2 %collective-permute-start.7 = (f32[136,256]{1,0:T(8,128)S(1)}, f32[136,256]{1,0:T(8,128)S(1)}, u32[]{:S(2)}, u32[]{:S(2)}) collective-permute-start(f32[136,256]{1,0:T(8,128)S(1)} %pad_maximum_fusion.in0), channel_id=1, source_target_pairs={{0,16},{16,0},{32,48},{48,32},{64,80},{80,64},{96,112},{112,96},{1... | collective-permute-start | bytes 417800 | tf_op jit(solution)/shard_map/ppermute | solution.py:294
  34.7 0.0 copy-done
  34.7 2.6 %collective-permute-done.9.in3 = f32[136,256]{1,0:T(8,128)S(1)} collective-permute-done((f32[136,256]{1,0:T(8,128)S(1)}, f32[136,256]{1,0:T(8,128)S(1)}, u32[]{:S(2)}, u32[]{:S(2)}) %collective-permute-start.9) | collective-permute-done | bytes 139296 | tf_op jit(solution)/shard_map/ppermute | solution.py:294
  37.2 0.0 collective-permute-done.8.in2
  37.2 1.9 %collective-permute-done.7.in1 = f32[136,256]{1,0:T(8,128)S(1)} collective-permute-done((f32[136,256]{1,0:T(8,128)S(1)}, f32[136,256]{1,0:T(8,128)S(1)}, u32[]{:S(2)}, u32[]{:S(2)}) %collective-permute-start.7) | collective-permute-done | bytes 139296 | tf_op jit(solution)/shard_map/ppermute | solution.py:294
  39.1 4.8 %shard_map.29 = (f32[16,256]{1,0:T(8,128)S(1)}, f32[256,256]{1,0:T(8,128)S(1)}, f32[256,256]{1,0:T(8,128)S(1)}, f32[256,256]{1,0:T(8,128)S(1)}) custom-call(s32[1]{0:T(128)} %bitcast.1.place_ref, s32[8]{0:T(128)S(1)} %get-tuple-element.51.shift_ref, f32[136,256]{1,0:T(8,128)S(1)} %pad_maximum_fusion.in0, f32[136,256]{1,0:T(8,128)S(1)} %collective-permute-done.7.in1, ...), custom_call_target="tpu_custom_call" | custom-call | tf_op jit(solution)/shard_map/pallas_call | solution.py:338
  43.9 2.6 %collective-permute-start.10 = (f32[16,256]{1,0:T(8,128)S(1)}, f32[16,256]{1,0:T(8,128)S(1)}, u32[]{:S(2)}, u32[]{:S(2)}) collective-permute-start(f32[16,256]{1,0:T(8,128)S(1)} %get-tuple-element.33.angles_ref), channel_id=1, source_target_pairs={{14,0},{15,1},{0,2},{1,3},{2,4},{3,5},{4,6},{5,7},{6,8},{7,9},{8,1... | collective-permute-start | bytes 49160 | tf_op jit(solution)/shard_map/ppermute | solution.py:290
  46.4 2.2 %shard_map.30 = (f32[256,256]{1,0:T(8,128)S(1)}, f32[256,256]{1,0:T(8,128)S(1)}) custom-call(s32[8]{0:T(128)S(1)} %get-tuple-element.51.shift_ref, f32[16,256]{1,0:T(8,128)S(1)} %get-tuple-element.33.angles_ref, f32[256,512]{1,0:T(8,128)} %pair_ref.3), custom_call_target="tpu_custom_call" | custom-call | tf_op jit(solution)/shard_map/pallas_call | solution.py:342
  48.7 2.8 %collective-permute-done.10.angles_ref = f32[16,256]{1,0:T(8,128)S(1)} collective-permute-done((f32[16,256]{1,0:T(8,128)S(1)}, f32[16,256]{1,0:T(8,128)S(1)}, u32[]{:S(2)}, u32[]{:S(2)}) %collective-permute-start.10) | collective-permute-done | bytes 16416 | tf_op jit(solution)/shard_map/ppermute | solution.py:290
  51.5 0.0 collective-permute-done.11.other_ref
  51.5 1.6 %shard_map.31 = (f32[256,256]{1,0:T(8,128)S(1)}, f32[64,256]{1,0:T(8,128)S(1)}, f32[64,256]{1,0:T(8,128)S(1)}, f32[64,256]{1,0:T(8,128)S(1)}, f32[64,256]{1,0:T(8,128)S(1)}) custom-call(s32[1]{0:T(128)} %bitcast.1.place_ref, s32[8]{0:T(128)S(1)} %get-tuple-element.51.shift_ref, f32[16,256]{1,0:T(8,128)S(1)} %collective-permute-done.10.angles_ref, ...), custom_call_target="tpu_custom_call" | custom-call | tf_op jit(solution)/shard_map/pallas_call | solution.py:348
  53.1 1.1 %collective-permute-start.13 = (f32[64,256]{1,0:T(8,128)S(1)}, f32[64,256]{1,0:T(8,128)S(1)}, u32[]{:S(2)}, u32[]{:S(2)}) collective-permute-start(f32[64,256]{1,0:T(8,128)S(1)} %get-tuple-element.38), channel_id=1, source_target_pairs={{0,32},{16,48},{32,0},{48,16},{64,96},{80,112},{96,64},{112,80},{1... | collective-permute-start | bytes 196616 | tf_op jit(solution)/shard_map/ppermute | solution.py:294
  54.2 0.1 collective-permute-start.12
  54.3 2.4 %collective-permute-start.14 = (f32[64,256]{1,0:T(8,128)S(1)}, f32[64,256]{1,0:T(8,128)S(1)}, u32[]{:S(2)}, u32[]{:S(2)}) collective-permute-start(f32[64,256]{1,0:T(8,128)S(1)} %get-tuple-element.44), channel_id=1, source_target_pairs={{0,48},{16,32},{32,16},{48,0},{64,112},{80,96},{96,80},{112,64},{1... | collective-permute-start | bytes 196616 | tf_op jit(solution)/shard_map/ppermute | solution.py:294
  56.7 1.2 %shard_map.32 = (f32[192,256]{1,0:T(8,128)S(1)}, f32[256,256]{1,0:T(8,128)S(1)}) custom-call(s32[8]{0:T(128)S(1)} %get-tuple-element.51.shift_ref, f32[16,256]{1,0:T(8,128)S(1)} %get-tuple-element.33.angles_ref, f32[256,256]{1,0:T(8,128)S(1)} %get-tuple-element.39.tl, f32[256,256]{1,0:T(8,128)S(1)} %get-tuple-element.40.tr, f32[256,256]{1,0:T(8,128)S(1)} %get-tuple-element.41.lr), custom_call_target="tpu_custom_call" | custom-call | tf_op jit(solution)/shard_map/pallas_call | solution.py:345
  57.9 0.0 collective-permute-done.13
  57.9 0.3 collective-permute-start.21
  58.2 1.0 %collective-permute-done.12 = f32[64,256]{1,0:T(8,128)S(1)} collective-permute-done((f32[64,256]{1,0:T(8,128)S(1)}, f32[64,256]{1,0:T(8,128)S(1)}, u32[]{:S(2)}, u32[]{:S(2)}) %collective-permute-start.12) | collective-permute-done | bytes 65568 | tf_op jit(solution)/shard_map/ppermute | solution.py:294
  59.2 1.1 %collective-permute-done.14 = f32[64,256]{1,0:T(8,128)S(1)} collective-permute-done((f32[64,256]{1,0:T(8,128)S(1)}, f32[64,256]{1,0:T(8,128)S(1)}, u32[]{:S(2)}, u32[]{:S(2)}) %collective-permute-start.14) | collective-permute-done | bytes 65568 | tf_op jit(solution)/shard_map/ppermute | solution.py:294
  60.3 2.7 %collective-permute-start.17 = (f32[64,256]{1,0:T(8,128)S(1)}, f32[64,256]{1,0:T(8,128)S(1)}, u32[]{:S(2)}, u32[]{:S(2)}) collective-permute-start(f32[64,256]{1,0:T(8,128)S(1)} %add_add_fusion.2), channel_id=1, source_target_pairs={{0,128},{16,144},{32,160},{48,176},{64,192},{80,208},{96,224},{112... | collective-permute-start | bytes 196616 | tf_op jit(solution)/shard_map/ppermute | solution.py:294
  63.0 2.2 %collective-permute-start.16 = (f32[64,256]{1,0:T(8,128)S(1)}, f32[64,256]{1,0:T(8,128)S(1)}, u32[]{:S(2)}, u32[]{:S(2)}) collective-permute-start(f32[64,256]{1,0:T(8,128)S(1)} %add_add_fusion.2), channel_id=1, source_target_pairs={{0,192},{16,208},{32,224},{48,240},{64,128},{80,144},{96,160},{112... | collective-permute-start | bytes 196616 | tf_op jit(solution)/shard_map/ppermute | solution.py:294
  65.1 1.8 %collective-permute-start.15 = (f32[64,256]{1,0:T(8,128)S(1)}, f32[64,256]{1,0:T(8,128)S(1)}, u32[]{:S(2)}, u32[]{:S(2)}) collective-permute-start(f32[64,256]{1,0:T(8,128)S(1)} %add_add_fusion.2), channel_id=1, source_target_pairs={{0,64},{16,80},{32,96},{48,112},{64,0},{80,16},{96,32},{112,48},{1... | collective-permute-start | bytes 196616 | tf_op jit(solution)/shard_map/ppermute | solution.py:294
  66.9 0.5 collective-permute-done.21.tl_ref
  67.4 2.9 %collective-permute-start.23 = (f32[256,256]{1,0:T(8,128)S(1)}, f32[256,256]{1,0:T(8,128)S(1)}, u32[]{:S(2)}, u32[]{:S(2)}) collective-permute-start(f32[256,256]{1,0:T(8,128)S(1)} %get-tuple-element.49.lower_ref.lower_in), channel_id=1, source_target_pairs={{2,0},{3,1},{4,2},{5,3},{6,4},{7,5},{8,6},{9,7},{10,8},{11,9},{12,... | collective-permute-start | bytes 786440 | tf_op jit(solution)/shard_map/ppermute | solution.py:290
  70.2 0.0 collective-permute-done.17
  70.2 0.0 collective-permute-done.16
  70.2 0.2 collective-permute-done.15
  70.4 2.7 %collective-permute-start.20 = (f32[64,256]{1,0:T(8,128)S(1)}, f32[64,256]{1,0:T(8,128)S(1)}, u32[]{:S(2)}, u32[]{:S(2)}) collective-permute-start(f32[64,256]{1,0:T(8,128)S(1)} %add_add_fusion.1.in0), channel_id=1, source_target_pairs={{0,48},{16,32},{32,16},{48,0},{64,112},{80,96},{96,80},{112,64},{1... | collective-permute-start | bytes 196616 | tf_op jit(solution)/shard_map/ppermute | solution.py:294
  73.2 0.3 collective-permute-start.19
  73.5 1.1 %collective-permute-start.18 = (f32[64,256]{1,0:T(8,128)S(1)}, f32[64,256]{1,0:T(8,128)S(1)}, u32[]{:S(2)}, u32[]{:S(2)}) collective-permute-start(f32[64,256]{1,0:T(8,128)S(1)} %add_add_fusion.1.in0), channel_id=1, source_target_pairs={{0,16},{16,0},{32,48},{48,32},{64,80},{80,64},{96,112},{112,96},{1... | collective-permute-start | bytes 196616 | tf_op jit(solution)/shard_map/ppermute | solution.py:294
  74.6 1.1 %collective-permute-done.20.in3 = f32[64,256]{1,0:T(8,128)S(1)} collective-permute-done((f32[64,256]{1,0:T(8,128)S(1)}, f32[64,256]{1,0:T(8,128)S(1)}, u32[]{:S(2)}, u32[]{:S(2)}) %collective-permute-start.20) | collective-permute-done | bytes 65568 | tf_op jit(solution)/shard_map/ppermute | solution.py:294
  75.7 1.7 %collective-permute-done.19.in2 = f32[64,256]{1,0:T(8,128)S(1)} collective-permute-done((f32[64,256]{1,0:T(8,128)S(1)}, f32[64,256]{1,0:T(8,128)S(1)}, u32[]{:S(2)}, u32[]{:S(2)}) %collective-permute-start.19) | collective-permute-done | bytes 65568 | tf_op jit(solution)/shard_map/ppermute | solution.py:294
  77.4 0.3 collective-permute-done.18.in1
  77.8 4.2 %shard_map.33.angles_ref = f32[16,256]{1,0:T(8,128)S(1)} custom-call(s32[1]{0:T(128)} %bitcast.1.place_ref, s32[8]{0:T(128)S(1)} %get-tuple-element.52.shift_ref, f32[64,256]{1,0:T(8,128)S(1)} %add_add_fusion.1.in0, f32[64,256]{1,0:T(8,128)S(1)} %collective-permute-done.18.in1, f32[64,256]{1,0:T(8,128)S(1)} %collective-permute-done.19.in2, ...), custom_call_target="tpu_custom_call" | custom-call | tf_op jit(solution)/shard_map/pallas_call | solution.py:361
  82.0 3.7 %collective-permute-start.22 = (f32[16,256]{1,0:T(8,128)S(1)}, f32[16,256]{1,0:T(8,128)S(1)}, u32[]{:S(2)}, u32[]{:S(2)}) collective-permute-start(f32[16,256]{1,0:T(8,128)S(1)} %shard_map.33.angles_ref), channel_id=1, source_target_pairs={{2,0},{3,1},{4,2},{5,3},{6,4},{7,5},{8,6},{9,7},{10,8},{11,9},{12,... | collective-permute-start | bytes 49160 | tf_op jit(solution)/shard_map/ppermute | solution.py:290
  85.6 2.3 %shard_map.34.half_ref = f32[256,512]{1,0:T(8,128)} custom-call(s32[8]{0:T(128)S(1)} %get-tuple-element.52.shift_ref, f32[16,256]{1,0:T(8,128)S(1)} %shard_map.33.angles_ref, f32[256,256]{1,0:T(8,128)S(1)} %get-tuple-element.50.upper_in, f32[256,256]{1,0:T(8,128)S(1)} %get-tuple-element.49.lower_ref.lower_in), custom_call_target="tpu_custom_call" | custom-call | tf_op jit(solution)/shard_map/pallas_call | solution.py:365
  87.9 0.0 collective-permute-done.22.angles_ref
  87.9 0.0 collective-permute-done.23.lower_in
  87.9 2.2 %shard_map.35 = f32[256,512]{1,0:T(8,128)} custom-call(s32[8]{0:T(128)S(1)} %get-tuple-element.52.shift_ref, f32[16,256]{1,0:T(8,128)S(1)} %collective-permute-done.22.angles_ref, f32[256,256]{1,0:T(8,128)S(1)} %get-tuple-element.48.upper_in, f32[256,256]{1,0:T(8,128)S(1)} %collective-permute-done.23.lower_in, ...), custom_call_target="tpu_custom_call", output_to_operand_aliasing={{}: (4, {})} | custom-call | tf_op jit(solution)/shard_map/pallas_call | solution.py:368
  (11 shorter events, 0.1 us)
Async XLA Ops:
  1.9 6.1 %collective-permute-start.1 = (f32[136,256]{1,0:T(8,128)S(1)}, f32[136,256]{1,0:T(8,128)S(1)}, u32[]{:S(2)}, u32[]{:S(2)}) collective-permute-start(f32[136,256]{1,0:T(8,128)S(1)} %get-tuple-element.30), channel_id=1, source_target_pairs={{0,32},{16,48},{32,0},{48,16},{64,96},{80,112},{96,64},{112,80},{1... | collective-permute-start | bytes 417800 | tf_op jit(solution)/shard_map/ppermute | solution.py:294
  3.9 8.1 %collective-permute-start = (f32[136,256]{1,0:T(8,128)S(1)}, f32[136,256]{1,0:T(8,128)S(1)}, u32[]{:S(2)}, u32[]{:S(2)}) collective-permute-start(f32[136,256]{1,0:T(8,128)S(1)} %get-tuple-element.29), channel_id=1, source_target_pairs={{0,16},{16,0},{32,48},{48,32},{64,80},{80,64},{96,112},{112,96},{1... | collective-permute-start | bytes 417800 | tf_op jit(solution)/shard_map/ppermute | solution.py:294
  4.4 7.7 %collective-permute-start.2 = (f32[136,256]{1,0:T(8,128)S(1)}, f32[136,256]{1,0:T(8,128)S(1)}, u32[]{:S(2)}, u32[]{:S(2)}) collective-permute-start(f32[136,256]{1,0:T(8,128)S(1)} %get-tuple-element.32), channel_id=1, source_target_pairs={{0,48},{16,32},{32,16},{48,0},{64,112},{80,96},{96,80},{112,64},{1... | collective-permute-start | bytes 417800 | tf_op jit(solution)/shard_map/ppermute | solution.py:294
  12.1 9.3 %collective-permute-start.5 = (f32[72,256]{1,0:T(8,128)S(1)}, f32[72,256]{1,0:T(8,128)S(1)}, u32[]{:S(2)}, u32[]{:S(2)}) collective-permute-start(f32[72,256]{1,0:T(8,128)S(1)} %slice.22), channel_id=1, source_target_pairs={{0,192},{16,208},{32,224},{48,240},{64,128},{80,144},{96,160},{112... | collective-permute-start | bytes 221192 | tf_op jit(solution)/shard_map/ppermute | solution.py:294
  17.6 6.9 %collective-permute-start.3 = (f32[64,256]{1,0:T(8,128)S(1)}, f32[64,256]{1,0:T(8,128)S(1)}, u32[]{:S(2)}, u32[]{:S(2)}) collective-permute-start(f32[64,256]{1,0:T(8,128)S(1)} %slice.21), channel_id=1, source_target_pairs={{0,64},{16,80},{32,96},{48,112},{64,0},{80,16},{96,32},{112,48},{1... | collective-permute-start | bytes 196616 | tf_op jit(solution)/shard_map/ppermute | solution.py:294
  19.0 32.4 %collective-permute-start.11 = (f32[256,512]{1,0:T(8,128)}, f32[256,512]{1,0:T(8,128)S(1)}, u32[]{:S(2)}, u32[]{:S(2)}) collective-permute-start(f32[256,512]{1,0:T(8,128)} %pair_ref.3), channel_id=1, source_target_pairs={{14,0},{15,1},{0,2},{1,3},{2,4},{3,5},{4,6},{5,7},{6,8},{7,9},{8,1... | collective-permute-start | bytes 1572872 | tf_op jit(solution)/shard_map/ppermute | solution.py:290
  21.4 9.7 %collective-permute-start.6 = (f32[72,256]{1,0:T(8,128)S(1)}, f32[72,256]{1,0:T(8,128)S(1)}, u32[]{:S(2)}, u32[]{:S(2)}) collective-permute-start(f32[72,256]{1,0:T(8,128)S(1)} %slice_add_fusion.1), channel_id=1, source_target_pairs={{0,64},{16,80},{32,96},{48,112},{64,0},{80,16},{96,32},{112,48},{1... | collective-permute-start | bytes 221192 | tf_op jit(solution)/shard_map/ppermute | solution.py:294
  24.5 6.5 %collective-permute-start.4 = (f32[64,256]{1,0:T(8,128)S(1)}, f32[64,256]{1,0:T(8,128)S(1)}, u32[]{:S(2)}, u32[]{:S(2)}) collective-permute-start(f32[64,256]{1,0:T(8,128)S(1)} %slice_add_fusion), channel_id=1, source_target_pairs={{0,192},{16,208},{32,224},{48,240},{64,128},{80,144},{96,160},{112... | collective-permute-start | bytes 196616 | tf_op jit(solution)/shard_map/ppermute | solution.py:294
  31.0 3.6 %copy-start = (s32[2,8]{1,0:T(2,128)S(1)}, s32[2,8]{1,0:T(2,128)}, u32[]{:S(2)}) copy-start(s32[2,8]{1,0:T(2,128)} %param.3) | copy-start | bytes 196
  31.1 6.1 %collective-permute-start.9 = (f32[136,256]{1,0:T(8,128)S(1)}, f32[136,256]{1,0:T(8,128)S(1)}, u32[]{:S(2)}, u32[]{:S(2)}) collective-permute-start(f32[136,256]{1,0:T(8,128)S(1)} %pad_maximum_fusion.in0), channel_id=1, source_target_pairs={{0,48},{16,32},{32,16},{48,0},{64,112},{80,96},{96,80},{112,64},{1... | collective-permute-start | bytes 417800 | tf_op jit(solution)/shard_map/ppermute | solution.py:294
  32.1 5.1 %collective-permute-start.8 = (f32[136,256]{1,0:T(8,128)S(1)}, f32[136,256]{1,0:T(8,128)S(1)}, u32[]{:S(2)}, u32[]{:S(2)}) collective-permute-start(f32[136,256]{1,0:T(8,128)S(1)} %pad_maximum_fusion.in0), channel_id=1, source_target_pairs={{0,32},{16,48},{32,0},{48,16},{64,96},{80,112},{96,64},{112,80},{1... | collective-permute-start | bytes 417800 | tf_op jit(solution)/shard_map/ppermute | solution.py:294
  32.5 6.6 %collective-permute-start.7 = (f32[136,256]{1,0:T(8,128)S(1)}, f32[136,256]{1,0:T(8,128)S(1)}, u32[]{:S(2)}, u32[]{:S(2)}) collective-permute-start(f32[136,256]{1,0:T(8,128)S(1)} %pad_maximum_fusion.in0), channel_id=1, source_target_pairs={{0,16},{16,0},{32,48},{48,32},{64,80},{80,64},{96,112},{112,96},{1... | collective-permute-start | bytes 417800 | tf_op jit(solution)/shard_map/ppermute | solution.py:294
  43.9 7.6 %collective-permute-start.10 = (f32[16,256]{1,0:T(8,128)S(1)}, f32[16,256]{1,0:T(8,128)S(1)}, u32[]{:S(2)}, u32[]{:S(2)}) collective-permute-start(f32[16,256]{1,0:T(8,128)S(1)} %get-tuple-element.33.angles_ref), channel_id=1, source_target_pairs={{14,0},{15,1},{0,2},{1,3},{2,4},{3,5},{4,6},{5,7},{6,8},{7,9},{8,1... | collective-permute-start | bytes 49160 | tf_op jit(solution)/shard_map/ppermute | solution.py:290
  53.1 4.8 %collective-permute-start.13 = (f32[64,256]{1,0:T(8,128)S(1)}, f32[64,256]{1,0:T(8,128)S(1)}, u32[]{:S(2)}, u32[]{:S(2)}) collective-permute-start(f32[64,256]{1,0:T(8,128)S(1)} %get-tuple-element.38), channel_id=1, source_target_pairs={{0,32},{16,48},{32,0},{48,16},{64,96},{80,112},{96,64},{112,80},{1... | collective-permute-start | bytes 196616 | tf_op jit(solution)/shard_map/ppermute | solution.py:294
  54.2 5.0 %collective-permute-start.12 = (f32[64,256]{1,0:T(8,128)S(1)}, f32[64,256]{1,0:T(8,128)S(1)}, u32[]{:S(2)}, u32[]{:S(2)}) collective-permute-start(f32[64,256]{1,0:T(8,128)S(1)} %get-tuple-element.37), channel_id=1, source_target_pairs={{0,16},{16,0},{32,48},{48,32},{64,80},{80,64},{96,112},{112,96},{1... | collective-permute-start | bytes 196616 | tf_op jit(solution)/shard_map/ppermute | solution.py:294
  54.3 6.0 %collective-permute-start.14 = (f32[64,256]{1,0:T(8,128)S(1)}, f32[64,256]{1,0:T(8,128)S(1)}, u32[]{:S(2)}, u32[]{:S(2)}) collective-permute-start(f32[64,256]{1,0:T(8,128)S(1)} %get-tuple-element.44), channel_id=1, source_target_pairs={{0,48},{16,32},{32,16},{48,0},{64,112},{80,96},{96,80},{112,64},{1... | collective-permute-start | bytes 196616 | tf_op jit(solution)/shard_map/ppermute | solution.py:294
  57.9 9.5 %collective-permute-start.21 = (f32[192,256]{1,0:T(8,128)S(1)}, f32[192,256]{1,0:T(8,128)S(1)}, u32[]{:S(2)}, u32[]{:S(2)}) collective-permute-start(f32[192,256]{1,0:T(8,128)S(1)} %get-tuple-element.45), channel_id=1, source_target_pairs={{14,0},{15,1},{0,2},{1,3},{2,4},{3,5},{4,6},{5,7},{6,8},{7,9},{8,1... | collective-permute-start | bytes 589832 | tf_op jit(solution)/shard_map/ppermute | solution.py:290
  60.3 9.9 %collective-permute-start.17 = (f32[64,256]{1,0:T(8,128)S(1)}, f32[64,256]{1,0:T(8,128)S(1)}, u32[]{:S(2)}, u32[]{:S(2)}) collective-permute-start(f32[64,256]{1,0:T(8,128)S(1)} %add_add_fusion.2), channel_id=1, source_target_pairs={{0,128},{16,144},{32,160},{48,176},{64,192},{80,208},{96,224},{112... | collective-permute-start | bytes 196616 | tf_op jit(solution)/shard_map/ppermute | solution.py:294
  63.0 7.3 %collective-permute-start.16 = (f32[64,256]{1,0:T(8,128)S(1)}, f32[64,256]{1,0:T(8,128)S(1)}, u32[]{:S(2)}, u32[]{:S(2)}) collective-permute-start(f32[64,256]{1,0:T(8,128)S(1)} %add_add_fusion.2), channel_id=1, source_target_pairs={{0,192},{16,208},{32,224},{48,240},{64,128},{80,144},{96,160},{112... | collective-permute-start | bytes 196616 | tf_op jit(solution)/shard_map/ppermute | solution.py:294
  65.1 5.3 %collective-permute-start.15 = (f32[64,256]{1,0:T(8,128)S(1)}, f32[64,256]{1,0:T(8,128)S(1)}, u32[]{:S(2)}, u32[]{:S(2)}) collective-permute-start(f32[64,256]{1,0:T(8,128)S(1)} %add_add_fusion.2), channel_id=1, source_target_pairs={{0,64},{16,80},{32,96},{48,112},{64,0},{80,16},{96,32},{112,48},{1... | collective-permute-start | bytes 196616 | tf_op jit(solution)/shard_map/ppermute | solution.py:294
  67.4 20.5 %collective-permute-start.23 = (f32[256,256]{1,0:T(8,128)S(1)}, f32[256,256]{1,0:T(8,128)S(1)}, u32[]{:S(2)}, u32[]{:S(2)}) collective-permute-start(f32[256,256]{1,0:T(8,128)S(1)} %get-tuple-element.49.lower_ref.lower_in), channel_id=1, source_target_pairs={{2,0},{3,1},{4,2},{5,3},{6,4},{7,5},{8,6},{9,7},{10,8},{11,9},{12,... | collective-permute-start | bytes 786440 | tf_op jit(solution)/shard_map/ppermute | solution.py:290
  70.4 5.3 %collective-permute-start.20 = (f32[64,256]{1,0:T(8,128)S(1)}, f32[64,256]{1,0:T(8,128)S(1)}, u32[]{:S(2)}, u32[]{:S(2)}) collective-permute-start(f32[64,256]{1,0:T(8,128)S(1)} %add_add_fusion.1.in0), channel_id=1, source_target_pairs={{0,48},{16,32},{32,16},{48,0},{64,112},{80,96},{96,80},{112,64},{1... | collective-permute-start | bytes 196616 | tf_op jit(solution)/shard_map/ppermute | solution.py:294
  73.2 4.3 %collective-permute-start.19 = (f32[64,256]{1,0:T(8,128)S(1)}, f32[64,256]{1,0:T(8,128)S(1)}, u32[]{:S(2)}, u32[]{:S(2)}) collective-permute-start(f32[64,256]{1,0:T(8,128)S(1)} %add_add_fusion.1.in0), channel_id=1, source_target_pairs={{0,32},{16,48},{32,0},{48,16},{64,96},{80,112},{96,64},{112,80},{1... | collective-permute-start | bytes 196616 | tf_op jit(solution)/shard_map/ppermute | solution.py:294
  73.5 4.3 %collective-permute-start.18 = (f32[64,256]{1,0:T(8,128)S(1)}, f32[64,256]{1,0:T(8,128)S(1)}, u32[]{:S(2)}, u32[]{:S(2)}) collective-permute-start(f32[64,256]{1,0:T(8,128)S(1)} %add_add_fusion.1.in0), channel_id=1, source_target_pairs={{0,16},{16,0},{32,48},{48,32},{64,80},{80,64},{96,112},{112,96},{1... | collective-permute-start | bytes 196616 | tf_op jit(solution)/shard_map/ppermute | solution.py:294
  82.0 5.9 %collective-permute-start.22 = (f32[16,256]{1,0:T(8,128)S(1)}, f32[16,256]{1,0:T(8,128)S(1)}, u32[]{:S(2)}, u32[]{:S(2)}) collective-permute-start(f32[16,256]{1,0:T(8,128)S(1)} %shard_map.33.angles_ref), channel_id=1, source_target_pairs={{2,0},{3,1},{4,2},{5,3},{6,4},{7,5},{8,6},{9,7},{10,8},{11,9},{12,... | collective-permute-start | bytes 49160 | tf_op jit(solution)/shard_map/ppermute | solution.py:290

commit v10 on v9

--- a/solution.py
+++ b/solution.py
@@ -156,6 +156,20 @@
     lower_ref[...] = pltpu.roll(lower_ref[...], offset, 1)
 
 
+def rotated_rows(shift_ref, angles_ref, upper_ref, lower_ref):
+    rounds = list(turns(shift_ref))
+    for t in range(0, upper_ref.shape[0], 8):
+        part = slice(t, t + 8)
+        upper = upper_ref[part, :]
+        lower = lower_ref[part, :]
+        for r, back in rounds:
+            c = angles_ref[2 * r : 2 * r + 1, :]
+            s = angles_ref[2 * r + 1 : 2 * r + 2, :]
+            lower = pltpu.roll(lower, back, 1)
+            upper, lower = upper * c + lower * s, lower * c - upper * s
+        yield part, upper, pltpu.roll(lower, shift_ref[shift_ref.shape[0] - 1], 1)
+
+
 def full_dot(left, right):
     return lax.dot_general(
         left,
@@ -225,12 +239,12 @@
 
 
 def cross_kernel(
-    place_ref, shift_ref, angles_ref, other_ref, lower_ref, upper_ref, out0, out1, out2, out3, rest, cross
+    place_ref, shift_ref, angles_ref, other_ref, lower_ref, upper_ref, out0, out1, out2, out3, cross
 ):
     w = upper_ref.shape[1]
-    upper_ref[...] = other_ref[:, :w]
-    rest[...] = other_ref[:, w:]
-    rotated(shift_ref, angles_ref, upper_ref, rest)
+    halves = (other_ref.at[:, :w], other_ref.at[:, w:])
+    for part, upper, _ in rotated_rows(shift_ref, angles_ref, *halves):
+        upper_ref[part, :] = upper
     cross[...] = full_dot(upper_ref[...], lower_ref[...])
     hand_out(place_ref, (cross,), (out0, out1, out2, out3))
 
@@ -269,16 +283,8 @@
 
 def lower_kernel(shift_ref, angles_ref, upper_in, lower_in, half_ref, pair_ref, done, sem):
     w = done.shape[1]
-    rounds = list(turns(shift_ref))
-    for t in range(0, done.shape[0], 8):
-        upper = upper_in[t : t + 8, :]
-        lower = lower_in[t : t + 8, :]
-        for r, back in rounds:
-            c = angles_ref[2 * r : 2 * r + 1, :]
-            s = angles_ref[2 * r + 1 : 2 * r + 2, :]
-            lower = pltpu.roll(lower, back, 1)
-            upper, lower = upper * c + lower * s, lower * c - upper * s
-        done[t : t + 8, :] = pltpu.roll(lower, shift_ref[shift_ref.shape[0] - 1], 1)
+    for part, _, lower in rotated_rows(shift_ref, angles_ref, upper_in, lower_in):
+        done[part, :] = lower
     copy = pltpu.make_async_copy(done, pair_ref.at[:, w:], sem)
     copy.start()
     copy.wait()
@@ -314,8 +320,8 @@
 
 
 def shared_in_four(mine, axis):
-    shared = [swapped(mine, axis, k) for k in (3, 1, 2)]
-    return (mine, shared[1], shared[2], shared[0])
+    shared = [swapped(mine, axis, k) for k in (2, 3, 1)]
+    return (mine, shared[2], shared[0], shared[1])
 
 
 def per_device(matrix, shifts):
@@ -330,10 +336,10 @@
     gram = kernel_call(
         gram_kernel, [(2 * w // 4 + 8, w)] * 4, [SMEM, VMEM], [square, square, diag]
     )(place, matrix)
-    sent = [swapped(gram[k], "row", k) for k in (3, 1, 2)]
-    sent[2], moved = lax.optimization_barrier((sent[2], matrix))
+    sent = [swapped(gram[k], "row", k) for k in (2, 1, 3)]
+    sent[0], moved = lax.optimization_barrier((sent[0], matrix))
     other = passed_along(moved, "col", 2)
-    gram = (gram[0] + sent[1]) + (sent[2] + sent[0])
+    gram = (gram[0] + sent[1]) + (sent[0] + sent[2])
     gram = shared_in_four(met_across(gram, "row"), "row")
     here, *state = kernel_call(
         first_kernel, [angles] + [square] * 3, [SMEM, SMEM] + [VMEM] * 4, [diag]
@@ -349,7 +355,7 @@
         cross_kernel,
         [block] + [(w // 4, w)] * 4,
         [SMEM, SMEM] + [VMEM] * 3,
-        [block, square],
+        [square],
     )(place, shifts[0], there, other, lower)
     sent = [swapped(cross[k], "row", k) for k in (3, 1, 2)]
     sent[2], tl = lax.optimization_barrier((sent[2], tl))

time: 91 us -> 91 us (level)
  no operation moved by 1% of the time
where the time goes in v10:
time: 91 us; the launch traced here: 90.3 us
  starting transfers between devices  43.1 us (47%)
  waiting for transfers between devices  26.4 us (29%)
  Pallas kernels  20.4 us (22%)
    ppermute x19, starting transfers between devices, swapped(): lax.ppermute(block, axis, [(i, i ^ bits) for i in range(lax.axis_size(axi...  31.4 us
    ppermute x19, waiting for transfers between devices, swapped(): lax.ppermute(block, axis, [(i, i ^ bits) for i in range(lax.axis_size(axi...  23.1 us
    ppermute x5, starting transfers between devices, passed_along(): return lax.ppermute(block, axis, route)  11.6 us
    pallas_call x1, Pallas kernels, per_device(): kernel_call(first_kernel, [angles] + [square] * 3, [SMEM, SMEM] + [VMEM]...  4.76 us
    pallas_call x1, Pallas kernels, per_device(): kernel_call(second_kernel, [angles], [SMEM, SMEM] + [VMEM] * 6, [square]...  4.19 us
    ppermute x5, waiting for transfers between devices, passed_along(): return lax.ppermute(block, axis, route)  3.27 us
    pallas_call x1, Pallas kernels, per_device(): output_call(upper_kernel, matrix, [VMEM] * 3, [block, block])  2.27 us
    pallas_call x1, Pallas kernels, per_device(): kernel_call(own_kernel, [block, block], [SMEM, VMEM, VMEM])  2.24 us
  transfers between devices with their start and end apart: 24, of which 14 were waited for; matrix products, arithmetic and copies ran while one was open for 0% of the time, Pallas kernels for 16%

profile of v10, /device:TPU:8, one launch (start us, length us, event | category | flops | bytes accessed | tf_op | source)
XLA Modules:
  0.0 90.3 jit_solution(2530093821770380762)
XLA Ops:
  0.0 1.9 %shard_map.28 = (f32[136,256]{1,0:T(8,128)S(1)}, f32[136,256]{1,0:T(8,128)S(1)}, f32[136,256]{1,0:T(8,128)S(1)}, f32[136,256]{1,0:T(8,128)S(1)}) custom-call(s32[1]{0:T(128)} %bitcast.1.place_ref, f32[256,512]{1,0:T(8,128)} %pair_ref.3), custom_call_target="tpu_custom_call" | custom-call | tf_op jit(solution)/shard_map/pallas_call | solution.py:336
  1.9 2.0 %collective-permute-start.1 = (f32[136,256]{1,0:T(8,128)S(1)}, f32[136,256]{1,0:T(8,128)S(1)}, u32[]{:S(2)}, u32[]{:S(2)}) collective-permute-start(f32[136,256]{1,0:T(8,128)S(1)} %get-tuple-element.30), channel_id=1, source_target_pairs={{0,32},{16,48},{32,0},{48,16},{64,96},{80,112},{96,64},{112,80},{1... | collective-permute-start | bytes 417800 | tf_op jit(solution)/shard_map/ppermute | solution.py:300
  3.9 0.4 collective-permute-start
  4.4 1.3 %collective-permute-start.2 = (f32[136,256]{1,0:T(8,128)S(1)}, f32[136,256]{1,0:T(8,128)S(1)}, u32[]{:S(2)}, u32[]{:S(2)}) collective-permute-start(f32[136,256]{1,0:T(8,128)S(1)} %get-tuple-element.32), channel_id=1, source_target_pairs={{0,48},{16,32},{32,16},{48,0},{64,112},{80,96},{96,80},{112,64},{1... | collective-permute-start | bytes 417800 | tf_op jit(solution)/shard_map/ppermute | solution.py:300
  5.6 2.4 %collective-permute-done.1 = f32[136,256]{1,0:T(8,128)S(1)} collective-permute-done((f32[136,256]{1,0:T(8,128)S(1)}, f32[136,256]{1,0:T(8,128)S(1)}, u32[]{:S(2)}, u32[]{:S(2)}) %collective-permute-start.1) | collective-permute-done | bytes 139296 | tf_op jit(solution)/shard_map/ppermute | solution.py:300
  8.0 4.0 %collective-permute-done = f32[136,256]{1,0:T(8,128)S(1)} collective-permute-done((f32[136,256]{1,0:T(8,128)S(1)}, f32[136,256]{1,0:T(8,128)S(1)}, u32[]{:S(2)}, u32[]{:S(2)}) %collective-permute-start) | collective-permute-done | bytes 139296 | tf_op jit(solution)/shard_map/ppermute | solution.py:300
  12.0 0.0 collective-permute-done.2
  12.1 5.5 %collective-permute-start.5 = (f32[72,256]{1,0:T(8,128)S(1)}, f32[72,256]{1,0:T(8,128)S(1)}, u32[]{:S(2)}, u32[]{:S(2)}) collective-permute-start(f32[72,256]{1,0:T(8,128)S(1)} %slice.22), channel_id=1, source_target_pairs={{0,192},{16,208},{32,224},{48,240},{64,128},{80,144},{96,160},{112... | collective-permute-start | bytes 221192 | tf_op jit(solution)/shard_map/ppermute | solution.py:300
  17.6 1.5 %collective-permute-start.3 = (f32[64,256]{1,0:T(8,128)S(1)}, f32[64,256]{1,0:T(8,128)S(1)}, u32[]{:S(2)}, u32[]{:S(2)}) collective-permute-start(f32[64,256]{1,0:T(8,128)S(1)} %slice.21), channel_id=1, source_target_pairs={{0,64},{16,80},{32,96},{48,112},{64,0},{80,16},{96,32},{112,48},{1... | collective-permute-start | bytes 196616 | tf_op jit(solution)/shard_map/ppermute | solution.py:300
  19.0 2.3 %collective-permute-start.11 = (f32[256,512]{1,0:T(8,128)}, f32[256,512]{1,0:T(8,128)S(1)}, u32[]{:S(2)}, u32[]{:S(2)}) collective-permute-start(f32[256,512]{1,0:T(8,128)} %pair_ref.3), channel_id=1, source_target_pairs={{14,0},{15,1},{0,2},{1,3},{2,4},{3,5},{4,6},{5,7},{6,8},{7,9},{8,1... | collective-permute-start | bytes 1572872 | tf_op jit(solution)/shard_map/ppermute | solution.py:296
  21.3 0.0 collective-permute-done.5
  21.4 1.6 %collective-permute-start.6 = (f32[72,256]{1,0:T(8,128)S(1)}, f32[72,256]{1,0:T(8,128)S(1)}, u32[]{:S(2)}, u32[]{:S(2)}) collective-permute-start(f32[72,256]{1,0:T(8,128)S(1)} %slice_add_fusion.1), channel_id=1, source_target_pairs={{0,64},{16,80},{32,96},{48,112},{64,0},{80,16},{96,32},{112,48},{1... | collective-permute-start | bytes 221192 | tf_op jit(solution)/shard_map/ppermute | solution.py:300
  22.9 1.6 %collective-permute-done.3 = f32[64,256]{1,0:T(8,128)S(1)} collective-permute-done((f32[64,256]{1,0:T(8,128)S(1)}, f32[64,256]{1,0:T(8,128)S(1)}, u32[]{:S(2)}, u32[]{:S(2)}) %collective-permute-start.3) | collective-permute-done | bytes 65568 | tf_op jit(solution)/shard_map/ppermute | solution.py:300
  24.5 1.3 %collective-permute-start.4 = (f32[64,256]{1,0:T(8,128)S(1)}, f32[64,256]{1,0:T(8,128)S(1)}, u32[]{:S(2)}, u32[]{:S(2)}) collective-permute-start(f32[64,256]{1,0:T(8,128)S(1)} %slice_add_fusion), channel_id=1, source_target_pairs={{0,192},{16,208},{32,224},{48,240},{64,128},{80,144},{96,160},{112... | collective-permute-start | bytes 196616 | tf_op jit(solution)/shard_map/ppermute | solution.py:300
  25.9 5.1 %collective-permute-done.4 = f32[64,256]{1,0:T(8,128)S(1)} collective-permute-done((f32[64,256]{1,0:T(8,128)S(1)}, f32[64,256]{1,0:T(8,128)S(1)}, u32[]{:S(2)}, u32[]{:S(2)}) %collective-permute-start.4) | collective-permute-done | bytes 65568 | tf_op jit(solution)/shard_map/ppermute | solution.py:300
  31.0 0.0 collective-permute-done.6
  31.0 0.0 copy-start
  31.1 1.1 %collective-permute-start.9 = (f32[136,256]{1,0:T(8,128)S(1)}, f32[136,256]{1,0:T(8,128)S(1)}, u32[]{:S(2)}, u32[]{:S(2)}) collective-permute-start(f32[136,256]{1,0:T(8,128)S(1)} %pad_maximum_fusion.in0), channel_id=1, source_target_pairs={{0,48},{16,32},{32,16},{48,0},{64,112},{80,96},{96,80},{112,64},{1... | collective-permute-start | bytes 417800 | tf_op jit(solution)/shard_map/ppermute | solution.py:300
  32.1 0.3 collective-permute-start.8
  32.5 2.2 %collective-permute-start.7 = (f32[136,256]{1,0:T(8,128)S(1)}, f32[136,256]{1,0:T(8,128)S(1)}, u32[]{:S(2)}, u32[]{:S(2)}) collective-permute-start(f32[136,256]{1,0:T(8,128)S(1)} %pad_maximum_fusion.in0), channel_id=1, source_target_pairs={{0,16},{16,0},{32,48},{48,32},{64,80},{80,64},{96,112},{112,96},{1... | collective-permute-start | bytes 417800 | tf_op jit(solution)/shard_map/ppermute | solution.py:300
  34.7 0.0 copy-done
  34.7 2.6 %collective-permute-done.9.in3 = f32[136,256]{1,0:T(8,128)S(1)} collective-permute-done((f32[136,256]{1,0:T(8,128)S(1)}, f32[136,256]{1,0:T(8,128)S(1)}, u32[]{:S(2)}, u32[]{:S(2)}) %collective-permute-start.9) | collective-permute-done | bytes 139296 | tf_op jit(solution)/shard_map/ppermute | solution.py:300
  37.2 0.0 collective-permute-done.8.in2
  37.2 1.9 %collective-permute-done.7.in1 = f32[136,256]{1,0:T(8,128)S(1)} collective-permute-done((f32[136,256]{1,0:T(8,128)S(1)}, f32[136,256]{1,0:T(8,128)S(1)}, u32[]{:S(2)}, u32[]{:S(2)}) %collective-permute-start.7) | collective-permute-done | bytes 139296 | tf_op jit(solution)/shard_map/ppermute | solution.py:300
  39.1 4.8 %shard_map.29 = (f32[16,256]{1,0:T(8,128)S(1)}, f32[256,256]{1,0:T(8,128)S(1)}, f32[256,256]{1,0:T(8,128)S(1)}, f32[256,256]{1,0:T(8,128)S(1)}) custom-call(s32[1]{0:T(128)} %bitcast.1.place_ref, s32[8]{0:T(128)S(1)} %get-tuple-element.51.shift_ref, f32[136,256]{1,0:T(8,128)S(1)} %pad_maximum_fusion.in0, f32[136,256]{1,0:T(8,128)S(1)} %collective-permute-done.7.in1, ...), custom_call_target="tpu_custom_call" | custom-call | tf_op jit(solution)/shard_map/pallas_call | solution.py:344
  43.9 2.6 %collective-permute-start.10 = (f32[16,256]{1,0:T(8,128)S(1)}, f32[16,256]{1,0:T(8,128)S(1)}, u32[]{:S(2)}, u32[]{:S(2)}) collective-permute-start(f32[16,256]{1,0:T(8,128)S(1)} %get-tuple-element.33.angles_ref), channel_id=1, source_target_pairs={{14,0},{15,1},{0,2},{1,3},{2,4},{3,5},{4,6},{5,7},{6,8},{7,9},{8,1... | collective-permute-start | bytes 49160 | tf_op jit(solution)/shard_map/ppermute | solution.py:296
  46.4 2.2 %shard_map.30 = (f32[256,256]{1,0:T(8,128)S(1)}, f32[256,256]{1,0:T(8,128)S(1)}) custom-call(s32[8]{0:T(128)S(1)} %get-tuple-element.51.shift_ref, f32[16,256]{1,0:T(8,128)S(1)} %get-tuple-element.33.angles_ref, f32[256,512]{1,0:T(8,128)} %pair_ref.3), custom_call_target="tpu_custom_call" | custom-call | tf_op jit(solution)/shard_map/pallas_call | solution.py:348
  48.7 2.8 %collective-permute-done.10.angles_ref = f32[16,256]{1,0:T(8,128)S(1)} collective-permute-done((f32[16,256]{1,0:T(8,128)S(1)}, f32[16,256]{1,0:T(8,128)S(1)}, u32[]{:S(2)}, u32[]{:S(2)}) %collective-permute-start.10) | collective-permute-done | bytes 16416 | tf_op jit(solution)/shard_map/ppermute | solution.py:296
  51.5 0.0 collective-permute-done.11.other_ref
  51.5 1.6 %shard_map.31 = (f32[256,256]{1,0:T(8,128)S(1)}, f32[64,256]{1,0:T(8,128)S(1)}, f32[64,256]{1,0:T(8,128)S(1)}, f32[64,256]{1,0:T(8,128)S(1)}, f32[64,256]{1,0:T(8,128)S(1)}) custom-call(s32[1]{0:T(128)} %bitcast.1.place_ref, s32[8]{0:T(128)S(1)} %get-tuple-element.51.shift_ref, f32[16,256]{1,0:T(8,128)S(1)} %collective-permute-done.10.angles_ref, ...), custom_call_target="tpu_custom_call" | custom-call | tf_op jit(solution)/shard_map/pallas_call | solution.py:354
  53.1 1.1 %collective-permute-start.13 = (f32[64,256]{1,0:T(8,128)S(1)}, f32[64,256]{1,0:T(8,128)S(1)}, u32[]{:S(2)}, u32[]{:S(2)}) collective-permute-start(f32[64,256]{1,0:T(8,128)S(1)} %get-tuple-element.38), channel_id=1, source_target_pairs={{0,32},{16,48},{32,0},{48,16},{64,96},{80,112},{96,64},{112,80},{1... | collective-permute-start | bytes 196616 | tf_op jit(solution)/shard_map/ppermute | solution.py:300
  54.2 0.1 collective-permute-start.12
  54.3 2.4 %collective-permute-start.14 = (f32[64,256]{1,0:T(8,128)S(1)}, f32[64,256]{1,0:T(8,128)S(1)}, u32[]{:S(2)}, u32[]{:S(2)}) collective-permute-start(f32[64,256]{1,0:T(8,128)S(1)} %get-tuple-element.44), channel_id=1, source_target_pairs={{0,48},{16,32},{32,16},{48,0},{64,112},{80,96},{96,80},{112,64},{1... | collective-permute-start | bytes 196616 | tf_op jit(solution)/shard_map/ppermute | solution.py:300
  56.7 1.2 %shard_map.32 = (f32[192,256]{1,0:T(8,128)S(1)}, f32[256,256]{1,0:T(8,128)S(1)}) custom-call(s32[8]{0:T(128)S(1)} %get-tuple-element.51.shift_ref, f32[16,256]{1,0:T(8,128)S(1)} %get-tuple-element.33.angles_ref, f32[256,256]{1,0:T(8,128)S(1)} %get-tuple-element.39.tl, f32[256,256]{1,0:T(8,128)S(1)} %get-tuple-element.40.tr, f32[256,256]{1,0:T(8,128)S(1)} %get-tuple-element.41.lr), custom_call_target="tpu_custom_call" | custom-call | tf_op jit(solution)/shard_map/pallas_call | solution.py:351
  57.9 0.0 collective-permute-done.13
  57.9 0.3 collective-permute-start.21
  58.2 1.0 %collective-permute-done.12 = f32[64,256]{1,0:T(8,128)S(1)} collective-permute-done((f32[64,256]{1,0:T(8,128)S(1)}, f32[64,256]{1,0:T(8,128)S(1)}, u32[]{:S(2)}, u32[]{:S(2)}) %collective-permute-start.12) | collective-permute-done | bytes 65568 | tf_op jit(solution)/shard_map/ppermute | solution.py:300
  59.2 1.1 %collective-permute-done.14 = f32[64,256]{1,0:T(8,128)S(1)} collective-permute-done((f32[64,256]{1,0:T(8,128)S(1)}, f32[64,256]{1,0:T(8,128)S(1)}, u32[]{:S(2)}, u32[]{:S(2)}) %collective-permute-start.14) | collective-permute-done | bytes 65568 | tf_op jit(solution)/shard_map/ppermute | solution.py:300
  60.3 2.7 %collective-permute-start.17 = (f32[64,256]{1,0:T(8,128)S(1)}, f32[64,256]{1,0:T(8,128)S(1)}, u32[]{:S(2)}, u32[]{:S(2)}) collective-permute-start(f32[64,256]{1,0:T(8,128)S(1)} %add_add_fusion.2), channel_id=1, source_target_pairs={{0,128},{16,144},{32,160},{48,176},{64,192},{80,208},{96,224},{112... | collective-permute-start | bytes 196616 | tf_op jit(solution)/shard_map/ppermute | solution.py:300
  63.0 2.2 %collective-permute-start.16 = (f32[64,256]{1,0:T(8,128)S(1)}, f32[64,256]{1,0:T(8,128)S(1)}, u32[]{:S(2)}, u32[]{:S(2)}) collective-permute-start(f32[64,256]{1,0:T(8,128)S(1)} %add_add_fusion.2), channel_id=1, source_target_pairs={{0,192},{16,208},{32,224},{48,240},{64,128},{80,144},{96,160},{112... | collective-permute-start | bytes 196616 | tf_op jit(solution)/shard_map/ppermute | solution.py:300
  65.1 1.8 %collective-permute-start.15 = (f32[64,256]{1,0:T(8,128)S(1)}, f32[64,256]{1,0:T(8,128)S(1)}, u32[]{:S(2)}, u32[]{:S(2)}) collective-permute-start(f32[64,256]{1,0:T(8,128)S(1)} %add_add_fusion.2), channel_id=1, source_target_pairs={{0,64},{16,80},{32,96},{48,112},{64,0},{80,16},{96,32},{112,48},{1... | collective-permute-start | bytes 196616 | tf_op jit(solution)/shard_map/ppermute | solution.py:300
  66.9 0.5 collective-permute-done.21.tl_ref
  67.4 2.9 %collective-permute-start.23 = (f32[256,256]{1,0:T(8,128)S(1)}, f32[256,256]{1,0:T(8,128)S(1)}, u32[]{:S(2)}, u32[]{:S(2)}) collective-permute-start(f32[256,256]{1,0:T(8,128)S(1)} %get-tuple-element.49.lower_ref.lower_in), channel_id=1, source_target_pairs={{2,0},{3,1},{4,2},{5,3},{6,4},{7,5},{8,6},{9,7},{10,8},{11,9},{12,... | collective-permute-start | bytes 786440 | tf_op jit(solution)/shard_map/ppermute | solution.py:296
  70.2 0.0 collective-permute-done.17
  70.2 0.0 collective-permute-done.16
  70.2 0.2 collective-permute-done.15
  70.4 2.7 %collective-permute-start.20 = (f32[64,256]{1,0:T(8,128)S(1)}, f32[64,256]{1,0:T(8,128)S(1)}, u32[]{:S(2)}, u32[]{:S(2)}) collective-permute-start(f32[64,256]{1,0:T(8,128)S(1)} %add_add_fusion.1.in0), channel_id=1, source_target_pairs={{0,48},{16,32},{32,16},{48,0},{64,112},{80,96},{96,80},{112,64},{1... | collective-permute-start | bytes 196616 | tf_op jit(solution)/shard_map/ppermute | solution.py:300
  73.2 0.3 collective-permute-start.19
  73.5 1.1 %collective-permute-start.18 = (f32[64,256]{1,0:T(8,128)S(1)}, f32[64,256]{1,0:T(8,128)S(1)}, u32[]{:S(2)}, u32[]{:S(2)}) collective-permute-start(f32[64,256]{1,0:T(8,128)S(1)} %add_add_fusion.1.in0), channel_id=1, source_target_pairs={{0,16},{16,0},{32,48},{48,32},{64,80},{80,64},{96,112},{112,96},{1... | collective-permute-start | bytes 196616 | tf_op jit(solution)/shard_map/ppermute | solution.py:300
  74.6 1.1 %collective-permute-done.20.in3 = f32[64,256]{1,0:T(8,128)S(1)} collective-permute-done((f32[64,256]{1,0:T(8,128)S(1)}, f32[64,256]{1,0:T(8,128)S(1)}, u32[]{:S(2)}, u32[]{:S(2)}) %collective-permute-start.20) | collective-permute-done | bytes 65568 | tf_op jit(solution)/shard_map/ppermute | solution.py:300
  75.7 1.7 %collective-permute-done.19.in2 = f32[64,256]{1,0:T(8,128)S(1)} collective-permute-done((f32[64,256]{1,0:T(8,128)S(1)}, f32[64,256]{1,0:T(8,128)S(1)}, u32[]{:S(2)}, u32[]{:S(2)}) %collective-permute-start.19) | collective-permute-done | bytes 65568 | tf_op jit(solution)/shard_map/ppermute | solution.py:300
  77.4 0.3 collective-permute-done.18.in1
  77.8 4.2 %shard_map.33.angles_ref = f32[16,256]{1,0:T(8,128)S(1)} custom-call(s32[1]{0:T(128)} %bitcast.1.place_ref, s32[8]{0:T(128)S(1)} %get-tuple-element.52.shift_ref, f32[64,256]{1,0:T(8,128)S(1)} %add_add_fusion.1.in0, f32[64,256]{1,0:T(8,128)S(1)} %collective-permute-done.18.in1, f32[64,256]{1,0:T(8,128)S(1)} %collective-permute-done.19.in2, ...), custom_call_target="tpu_custom_call" | custom-call | tf_op jit(solution)/shard_map/pallas_call | solution.py:367
  82.0 3.7 %collective-permute-start.22 = (f32[16,256]{1,0:T(8,128)S(1)}, f32[16,256]{1,0:T(8,128)S(1)}, u32[]{:S(2)}, u32[]{:S(2)}) collective-permute-start(f32[16,256]{1,0:T(8,128)S(1)} %shard_map.33.angles_ref), channel_id=1, source_target_pairs={{2,0},{3,1},{4,2},{5,3},{6,4},{7,5},{8,6},{9,7},{10,8},{11,9},{12,... | collective-permute-start | bytes 49160 | tf_op jit(solution)/shard_map/ppermute | solution.py:296
  85.6 2.3 %shard_map.34.half_ref = f32[256,512]{1,0:T(8,128)} custom-call(s32[8]{0:T(128)S(1)} %get-tuple-element.52.shift_ref, f32[16,256]{1,0:T(8,128)S(1)} %shard_map.33.angles_ref, f32[256,256]{1,0:T(8,128)S(1)} %get-tuple-element.50.upper_in, f32[256,256]{1,0:T(8,128)S(1)} %get-tuple-element.49.lower_ref.lower_in), custom_call_target="tpu_custom_call" | custom-call | tf_op jit(solution)/shard_map/pallas_call | solution.py:371
  87.9 0.0 collective-permute-done.22.angles_ref
  87.9 0.0 collective-permute-done.23.lower_in
  87.9 2.2 %shard_map.35 = f32[256,512]{1,0:T(8,128)} custom-call(s32[8]{0:T(128)S(1)} %get-tuple-element.52.shift_ref, f32[16,256]{1,0:T(8,128)S(1)} %collective-permute-done.22.angles_ref, f32[256,256]{1,0:T(8,128)S(1)} %get-tuple-element.48.upper_in, f32[256,256]{1,0:T(8,128)S(1)} %collective-permute-done.23.lower_in, ...), custom_call_target="tpu_custom_call", output_to_operand_aliasing={{}: (4, {})} | custom-call | tf_op jit(solution)/shard_map/pallas_call | solution.py:374
  (11 shorter events, 0.1 us)
Async XLA Ops:
  1.9 6.1 %collective-permute-start.1 = (f32[136,256]{1,0:T(8,128)S(1)}, f32[136,256]{1,0:T(8,128)S(1)}, u32[]{:S(2)}, u32[]{:S(2)}) collective-permute-start(f32[136,256]{1,0:T(8,128)S(1)} %get-tuple-element.30), channel_id=1, source_target_pairs={{0,32},{16,48},{32,0},{48,16},{64,96},{80,112},{96,64},{112,80},{1... | collective-permute-start | bytes 417800 | tf_op jit(solution)/shard_map/ppermute | solution.py:300
  3.9 8.1 %collective-permute-start = (f32[136,256]{1,0:T(8,128)S(1)}, f32[136,256]{1,0:T(8,128)S(1)}, u32[]{:S(2)}, u32[]{:S(2)}) collective-permute-start(f32[136,256]{1,0:T(8,128)S(1)} %get-tuple-element.29), channel_id=1, source_target_pairs={{0,16},{16,0},{32,48},{48,32},{64,80},{80,64},{96,112},{112,96},{1... | collective-permute-start | bytes 417800 | tf_op jit(solution)/shard_map/ppermute | solution.py:300
  4.4 7.7 %collective-permute-start.2 = (f32[136,256]{1,0:T(8,128)S(1)}, f32[136,256]{1,0:T(8,128)S(1)}, u32[]{:S(2)}, u32[]{:S(2)}) collective-permute-start(f32[136,256]{1,0:T(8,128)S(1)} %get-tuple-element.32), channel_id=1, source_target_pairs={{0,48},{16,32},{32,16},{48,0},{64,112},{80,96},{96,80},{112,64},{1... | collective-permute-start | bytes 417800 | tf_op jit(solution)/shard_map/ppermute | solution.py:300
  12.1 9.3 %collective-permute-start.5 = (f32[72,256]{1,0:T(8,128)S(1)}, f32[72,256]{1,0:T(8,128)S(1)}, u32[]{:S(2)}, u32[]{:S(2)}) collective-permute-start(f32[72,256]{1,0:T(8,128)S(1)} %slice.22), channel_id=1, source_target_pairs={{0,192},{16,208},{32,224},{48,240},{64,128},{80,144},{96,160},{112... | collective-permute-start | bytes 221192 | tf_op jit(solution)/shard_map/ppermute | solution.py:300
  17.6 6.9 %collective-permute-start.3 = (f32[64,256]{1,0:T(8,128)S(1)}, f32[64,256]{1,0:T(8,128)S(1)}, u32[]{:S(2)}, u32[]{:S(2)}) collective-permute-start(f32[64,256]{1,0:T(8,128)S(1)} %slice.21), channel_id=1, source_target_pairs={{0,64},{16,80},{32,96},{48,112},{64,0},{80,16},{96,32},{112,48},{1... | collective-permute-start | bytes 196616 | tf_op jit(solution)/shard_map/ppermute | solution.py:300
  19.0 32.4 %collective-permute-start.11 = (f32[256,512]{1,0:T(8,128)}, f32[256,512]{1,0:T(8,128)S(1)}, u32[]{:S(2)}, u32[]{:S(2)}) collective-permute-start(f32[256,512]{1,0:T(8,128)} %pair_ref.3), channel_id=1, source_target_pairs={{14,0},{15,1},{0,2},{1,3},{2,4},{3,5},{4,6},{5,7},{6,8},{7,9},{8,1... | collective-permute-start | bytes 1572872 | tf_op jit(solution)/shard_map/ppermute | solution.py:296
  21.4 9.7 %collective-permute-start.6 = (f32[72,256]{1,0:T(8,128)S(1)}, f32[72,256]{1,0:T(8,128)S(1)}, u32[]{:S(2)}, u32[]{:S(2)}) collective-permute-start(f32[72,256]{1,0:T(8,128)S(1)} %slice_add_fusion.1), channel_id=1, source_target_pairs={{0,64},{16,80},{32,96},{48,112},{64,0},{80,16},{96,32},{112,48},{1... | collective-permute-start | bytes 221192 | tf_op jit(solution)/shard_map/ppermute | solution.py:300
  24.5 6.5 %collective-permute-start.4 = (f32[64,256]{1,0:T(8,128)S(1)}, f32[64,256]{1,0:T(8,128)S(1)}, u32[]{:S(2)}, u32[]{:S(2)}) collective-permute-start(f32[64,256]{1,0:T(8,128)S(1)} %slice_add_fusion), channel_id=1, source_target_pairs={{0,192},{16,208},{32,224},{48,240},{64,128},{80,144},{96,160},{112... | collective-permute-start | bytes 196616 | tf_op jit(solution)/shard_map/ppermute | solution.py:300
  31.0 3.6 %copy-start = (s32[2,8]{1,0:T(2,128)S(1)}, s32[2,8]{1,0:T(2,128)}, u32[]{:S(2)}) copy-start(s32[2,8]{1,0:T(2,128)} %param.3) | copy-start | bytes 196
  31.1 6.1 %collective-permute-start.9 = (f32[136,256]{1,0:T(8,128)S(1)}, f32[136,256]{1,0:T(8,128)S(1)}, u32[]{:S(2)}, u32[]{:S(2)}) collective-permute-start(f32[136,256]{1,0:T(8,128)S(1)} %pad_maximum_fusion.in0), channel_id=1, source_target_pairs={{0,48},{16,32},{32,16},{48,0},{64,112},{80,96},{96,80},{112,64},{1... | collective-permute-start | bytes 417800 | tf_op jit(solution)/shard_map/ppermute | solution.py:300
  32.1 5.1 %collective-permute-start.8 = (f32[136,256]{1,0:T(8,128)S(1)}, f32[136,256]{1,0:T(8,128)S(1)}, u32[]{:S(2)}, u32[]{:S(2)}) collective-permute-start(f32[136,256]{1,0:T(8,128)S(1)} %pad_maximum_fusion.in0), channel_id=1, source_target_pairs={{0,32},{16,48},{32,0},{48,16},{64,96},{80,112},{96,64},{112,80},{1... | collective-permute-start | bytes 417800 | tf_op jit(solution)/shard_map/ppermute | solution.py:300
  32.5 6.6 %collective-permute-start.7 = (f32[136,256]{1,0:T(8,128)S(1)}, f32[136,256]{1,0:T(8,128)S(1)}, u32[]{:S(2)}, u32[]{:S(2)}) collective-permute-start(f32[136,256]{1,0:T(8,128)S(1)} %pad_maximum_fusion.in0), channel_id=1, source_target_pairs={{0,16},{16,0},{32,48},{48,32},{64,80},{80,64},{96,112},{112,96},{1... | collective-permute-start | bytes 417800 | tf_op jit(solution)/shard_map/ppermute | solution.py:300
  43.9 7.6 %collective-permute-start.10 = (f32[16,256]{1,0:T(8,128)S(1)}, f32[16,256]{1,0:T(8,128)S(1)}, u32[]{:S(2)}, u32[]{:S(2)}) collective-permute-start(f32[16,256]{1,0:T(8,128)S(1)} %get-tuple-element.33.angles_ref), channel_id=1, source_target_pairs={{14,0},{15,1},{0,2},{1,3},{2,4},{3,5},{4,6},{5,7},{6,8},{7,9},{8,1... | collective-permute-start | bytes 49160 | tf_op jit(solution)/shard_map/ppermute | solution.py:296
  53.1 4.8 %collective-permute-start.13 = (f32[64,256]{1,0:T(8,128)S(1)}, f32[64,256]{1,0:T(8,128)S(1)}, u32[]{:S(2)}, u32[]{:S(2)}) collective-permute-start(f32[64,256]{1,0:T(8,128)S(1)} %get-tuple-element.38), channel_id=1, source_target_pairs={{0,32},{16,48},{32,0},{48,16},{64,96},{80,112},{96,64},{112,80},{1... | collective-permute-start | bytes 196616 | tf_op jit(solution)/shard_map/ppermute | solution.py:300
  54.2 5.0 %collective-permute-start.12 = (f32[64,256]{1,0:T(8,128)S(1)}, f32[64,256]{1,0:T(8,128)S(1)}, u32[]{:S(2)}, u32[]{:S(2)}) collective-permute-start(f32[64,256]{1,0:T(8,128)S(1)} %get-tuple-element.37), channel_id=1, source_target_pairs={{0,16},{16,0},{32,48},{48,32},{64,80},{80,64},{96,112},{112,96},{1... | collective-permute-start | bytes 196616 | tf_op jit(solution)/shard_map/ppermute | solution.py:300
  54.3 6.0 %collective-permute-start.14 = (f32[64,256]{1,0:T(8,128)S(1)}, f32[64,256]{1,0:T(8,128)S(1)}, u32[]{:S(2)}, u32[]{:S(2)}) collective-permute-start(f32[64,256]{1,0:T(8,128)S(1)} %get-tuple-element.44), channel_id=1, source_target_pairs={{0,48},{16,32},{32,16},{48,0},{64,112},{80,96},{96,80},{112,64},{1... | collective-permute-start | bytes 196616 | tf_op jit(solution)/shard_map/ppermute | solution.py:300
  57.9 9.5 %collective-permute-start.21 = (f32[192,256]{1,0:T(8,128)S(1)}, f32[192,256]{1,0:T(8,128)S(1)}, u32[]{:S(2)}, u32[]{:S(2)}) collective-permute-start(f32[192,256]{1,0:T(8,128)S(1)} %get-tuple-element.45), channel_id=1, source_target_pairs={{14,0},{15,1},{0,2},{1,3},{2,4},{3,5},{4,6},{5,7},{6,8},{7,9},{8,1... | collective-permute-start | bytes 589832 | tf_op jit(solution)/shard_map/ppermute | solution.py:296
  60.3 9.9 %collective-permute-start.17 = (f32[64,256]{1,0:T(8,128)S(1)}, f32[64,256]{1,0:T(8,128)S(1)}, u32[]{:S(2)}, u32[]{:S(2)}) collective-permute-start(f32[64,256]{1,0:T(8,128)S(1)} %add_add_fusion.2), channel_id=1, source_target_pairs={{0,128},{16,144},{32,160},{48,176},{64,192},{80,208},{96,224},{112... | collective-permute-start | bytes 196616 | tf_op jit(solution)/shard_map/ppermute | solution.py:300
  63.0 7.3 %collective-permute-start.16 = (f32[64,256]{1,0:T(8,128)S(1)}, f32[64,256]{1,0:T(8,128)S(1)}, u32[]{:S(2)}, u32[]{:S(2)}) collective-permute-start(f32[64,256]{1,0:T(8,128)S(1)} %add_add_fusion.2), channel_id=1, source_target_pairs={{0,192},{16,208},{32,224},{48,240},{64,128},{80,144},{96,160},{112... | collective-permute-start | bytes 196616 | tf_op jit(solution)/shard_map/ppermute | solution.py:300
  65.1 5.3 %collective-permute-start.15 = (f32[64,256]{1,0:T(8,128)S(1)}, f32[64,256]{1,0:T(8,128)S(1)}, u32[]{:S(2)}, u32[]{:S(2)}) collective-permute-start(f32[64,256]{1,0:T(8,128)S(1)} %add_add_fusion.2), channel_id=1, source_target_pairs={{0,64},{16,80},{32,96},{48,112},{64,0},{80,16},{96,32},{112,48},{1... | collective-permute-start | bytes 196616 | tf_op jit(solution)/shard_map/ppermute | solution.py:300
  67.4 20.5 %collective-permute-start.23 = (f32[256,256]{1,0:T(8,128)S(1)}, f32[256,256]{1,0:T(8,128)S(1)}, u32[]{:S(2)}, u32[]{:S(2)}) collective-permute-start(f32[256,256]{1,0:T(8,128)S(1)} %get-tuple-element.49.lower_ref.lower_in), channel_id=1, source_target_pairs={{2,0},{3,1},{4,2},{5,3},{6,4},{7,5},{8,6},{9,7},{10,8},{11,9},{12,... | collective-permute-start | bytes 786440 | tf_op jit(solution)/shard_map/ppermute | solution.py:296
  70.4 5.3 %collective-permute-start.20 = (f32[64,256]{1,0:T(8,128)S(1)}, f32[64,256]{1,0:T(8,128)S(1)}, u32[]{:S(2)}, u32[]{:S(2)}) collective-permute-start(f32[64,256]{1,0:T(8,128)S(1)} %add_add_fusion.1.in0), channel_id=1, source_target_pairs={{0,48},{16,32},{32,16},{48,0},{64,112},{80,96},{96,80},{112,64},{1... | collective-permute-start | bytes 196616 | tf_op jit(solution)/shard_map/ppermute | solution.py:300
  73.2 4.3 %collective-permute-start.19 = (f32[64,256]{1,0:T(8,128)S(1)}, f32[64,256]{1,0:T(8,128)S(1)}, u32[]{:S(2)}, u32[]{:S(2)}) collective-permute-start(f32[64,256]{1,0:T(8,128)S(1)} %add_add_fusion.1.in0), channel_id=1, source_target_pairs={{0,32},{16,48},{32,0},{48,16},{64,96},{80,112},{96,64},{112,80},{1... | collective-permute-start | bytes 196616 | tf_op jit(solution)/shard_map/ppermute | solution.py:300
  73.5 4.3 %collective-permute-start.18 = (f32[64,256]{1,0:T(8,128)S(1)}, f32[64,256]{1,0:T(8,128)S(1)}, u32[]{:S(2)}, u32[]{:S(2)}) collective-permute-start(f32[64,256]{1,0:T(8,128)S(1)} %add_add_fusion.1.in0), channel_id=1, source_target_pairs={{0,16},{16,0},{32,48},{48,32},{64,80},{80,64},{96,112},{112,96},{1... | collective-permute-start | bytes 196616 | tf_op jit(solution)/shard_map/ppermute | solution.py:300
  82.0 5.9 %collective-permute-start.22 = (f32[16,256]{1,0:T(8,128)S(1)}, f32[16,256]{1,0:T(8,128)S(1)}, u32[]{:S(2)}, u32[]{:S(2)}) collective-permute-start(f32[16,256]{1,0:T(8,128)S(1)} %shard_map.33.angles_ref), channel_id=1, source_target_pairs={{2,0},{3,1},{4,2},{5,3},{6,4},{7,5},{8,6},{9,7},{10,8},{11,9},{12,... | collective-permute-start | bytes 49160 | tf_op jit(solution)/shard_map/ppermute | solution.py:296

commit v11 on v10

--- a/solution.py
+++ b/solution.py
@@ -357,9 +357,9 @@
         [SMEM, SMEM] + [VMEM] * 3,
         [square],
     )(place, shifts[0], there, other, lower)
-    sent = [swapped(cross[k], "row", k) for k in (3, 1, 2)]
-    sent[2], tl = lax.optimization_barrier((sent[2], tl))
-    cross = (cross[0] + sent[1]) + (sent[2] + sent[0])
+    sent = [swapped(cross[k], "row", k) for k in (2, 1, 3)]
+    sent[0], tl = lax.optimization_barrier((sent[0], tl))
+    cross = (cross[0] + sent[1]) + (sent[0] + sent[2])
     tl = passed_along(tl, "col", 2)
     tl, sent = lax.optimization_barrier((tl, lower))
     far_lower = passed_along(sent, "col", -2)

time: 91 us -> 91 us (level)
  no operation moved by 1% of the time
where the time goes in v11:
time: 91 us; the launch traced here: 90.3 us
  starting transfers between devices  43.1 us (47%)
  waiting for transfers between devices  26.4 us (29%)
  Pallas kernels  20.4 us (22%)
    ppermute x19, starting transfers between devices, swapped(): lax.ppermute(block, axis, [(i, i ^ bits) for i in range(lax.axis_size(axi...  31.4 us
    ppermute x19, waiting for transfers between devices, swapped(): lax.ppermute(block, axis, [(i, i ^ bits) for i in range(lax.axis_size(axi...  23.1 us
    ppermute x5, starting transfers between devices, passed_along(): return lax.ppermute(block, axis, route)  11.6 us
    pallas_call x1, Pallas kernels, per_device(): kernel_call(first_kernel, [angles] + [square] * 3, [SMEM, SMEM] + [VMEM]...  4.76 us
    pallas_call x1, Pallas kernels, per_device(): kernel_call(second_kernel, [angles], [SMEM, SMEM] + [VMEM] * 6, [square]...  4.19 us
    ppermute x5, waiting for transfers between devices, passed_along(): return lax.ppermute(block, axis, route)  3.27 us
    pallas_call x1, Pallas kernels, per_device(): output_call(upper_kernel, matrix, [VMEM] * 3, [block, block])  2.27 us
    pallas_call x1, Pallas kernels, per_device(): kernel_call(own_kernel, [block, block], [SMEM, VMEM, VMEM])  2.24 us
  transfers between devices with their start and end apart: 24, of which 14 were waited for; matrix products, arithmetic and copies ran while one was open for 0% of the time, Pallas kernels for 16%

profile of v11, /device:TPU:8, one launch (start us, length us, event | category | flops | bytes accessed | tf_op | source)
XLA Modules:
  0.0 90.3 jit_solution(2530093821770380762)
XLA Ops:
  0.0 1.9 %shard_map.28 = (f32[136,256]{1,0:T(8,128)S(1)}, f32[136,256]{1,0:T(8,128)S(1)}, f32[136,256]{1,0:T(8,128)S(1)}, f32[136,256]{1,0:T(8,128)S(1)}) custom-call(s32[1]{0:T(128)} %bitcast.1.place_ref, f32[256,512]{1,0:T(8,128)} %pair_ref.3), custom_call_target="tpu_custom_call" | custom-call | tf_op jit(solution)/shard_map/pallas_call | solution.py:336
  1.9 2.0 %collective-permute-start.1 = (f32[136,256]{1,0:T(8,128)S(1)}, f32[136,256]{1,0:T(8,128)S(1)}, u32[]{:S(2)}, u32[]{:S(2)}) collective-permute-start(f32[136,256]{1,0:T(8,128)S(1)} %get-tuple-element.30), channel_id=1, source_target_pairs={{0,32},{16,48},{32,0},{48,16},{64,96},{80,112},{96,64},{112,80},{1... | collective-permute-start | bytes 417800 | tf_op jit(solution)/shard_map/ppermute | solution.py:300
  3.9 0.4 collective-permute-start
  4.4 1.3 %collective-permute-start.2 = (f32[136,256]{1,0:T(8,128)S(1)}, f32[136,256]{1,0:T(8,128)S(1)}, u32[]{:S(2)}, u32[]{:S(2)}) collective-permute-start(f32[136,256]{1,0:T(8,128)S(1)} %get-tuple-element.32), channel_id=1, source_target_pairs={{0,48},{16,32},{32,16},{48,0},{64,112},{80,96},{96,80},{112,64},{1... | collective-permute-start | bytes 417800 | tf_op jit(solution)/shard_map/ppermute | solution.py:300
  5.6 2.4 %collective-permute-done.1 = f32[136,256]{1,0:T(8,128)S(1)} collective-permute-done((f32[136,256]{1,0:T(8,128)S(1)}, f32[136,256]{1,0:T(8,128)S(1)}, u32[]{:S(2)}, u32[]{:S(2)}) %collective-permute-start.1) | collective-permute-done | bytes 139296 | tf_op jit(solution)/shard_map/ppermute | solution.py:300
  8.0 4.0 %collective-permute-done = f32[136,256]{1,0:T(8,128)S(1)} collective-permute-done((f32[136,256]{1,0:T(8,128)S(1)}, f32[136,256]{1,0:T(8,128)S(1)}, u32[]{:S(2)}, u32[]{:S(2)}) %collective-permute-start) | collective-permute-done | bytes 139296 | tf_op jit(solution)/shard_map/ppermute | solution.py:300
  12.0 0.0 collective-permute-done.2
  12.1 5.5 %collective-permute-start.5 = (f32[72,256]{1,0:T(8,128)S(1)}, f32[72,256]{1,0:T(8,128)S(1)}, u32[]{:S(2)}, u32[]{:S(2)}) collective-permute-start(f32[72,256]{1,0:T(8,128)S(1)} %slice.22), channel_id=1, source_target_pairs={{0,192},{16,208},{32,224},{48,240},{64,128},{80,144},{96,160},{112... | collective-permute-start | bytes 221192 | tf_op jit(solution)/shard_map/ppermute | solution.py:300
  17.6 1.5 %collective-permute-start.3 = (f32[64,256]{1,0:T(8,128)S(1)}, f32[64,256]{1,0:T(8,128)S(1)}, u32[]{:S(2)}, u32[]{:S(2)}) collective-permute-start(f32[64,256]{1,0:T(8,128)S(1)} %slice.21), channel_id=1, source_target_pairs={{0,64},{16,80},{32,96},{48,112},{64,0},{80,16},{96,32},{112,48},{1... | collective-permute-start | bytes 196616 | tf_op jit(solution)/shard_map/ppermute | solution.py:300
  19.0 2.3 %collective-permute-start.11 = (f32[256,512]{1,0:T(8,128)}, f32[256,512]{1,0:T(8,128)S(1)}, u32[]{:S(2)}, u32[]{:S(2)}) collective-permute-start(f32[256,512]{1,0:T(8,128)} %pair_ref.3), channel_id=1, source_target_pairs={{14,0},{15,1},{0,2},{1,3},{2,4},{3,5},{4,6},{5,7},{6,8},{7,9},{8,1... | collective-permute-start | bytes 1572872 | tf_op jit(solution)/shard_map/ppermute | solution.py:296
  21.3 0.0 collective-permute-done.5
  21.4 1.6 %collective-permute-start.6 = (f32[72,256]{1,0:T(8,128)S(1)}, f32[72,256]{1,0:T(8,128)S(1)}, u32[]{:S(2)}, u32[]{:S(2)}) collective-permute-start(f32[72,256]{1,0:T(8,128)S(1)} %slice_add_fusion.1), channel_id=1, source_target_pairs={{0,64},{16,80},{32,96},{48,112},{64,0},{80,16},{96,32},{112,48},{1... | collective-permute-start | bytes 221192 | tf_op jit(solution)/shard_map/ppermute | solution.py:300
  22.9 1.6 %collective-permute-done.3 = f32[64,256]{1,0:T(8,128)S(1)} collective-permute-done((f32[64,256]{1,0:T(8,128)S(1)}, f32[64,256]{1,0:T(8,128)S(1)}, u32[]{:S(2)}, u32[]{:S(2)}) %collective-permute-start.3) | collective-permute-done | bytes 65568 | tf_op jit(solution)/shard_map/ppermute | solution.py:300
  24.5 1.3 %collective-permute-start.4 = (f32[64,256]{1,0:T(8,128)S(1)}, f32[64,256]{1,0:T(8,128)S(1)}, u32[]{:S(2)}, u32[]{:S(2)}) collective-permute-start(f32[64,256]{1,0:T(8,128)S(1)} %slice_add_fusion), channel_id=1, source_target_pairs={{0,192},{16,208},{32,224},{48,240},{64,128},{80,144},{96,160},{112... | collective-permute-start | bytes 196616 | tf_op jit(solution)/shard_map/ppermute | solution.py:300
  25.9 5.1 %collective-permute-done.4 = f32[64,256]{1,0:T(8,128)S(1)} collective-permute-done((f32[64,256]{1,0:T(8,128)S(1)}, f32[64,256]{1,0:T(8,128)S(1)}, u32[]{:S(2)}, u32[]{:S(2)}) %collective-permute-start.4) | collective-permute-done | bytes 65568 | tf_op jit(solution)/shard_map/ppermute | solution.py:300
  31.0 0.0 collective-permute-done.6
  31.0 0.0 copy-start
  31.1 1.1 %collective-permute-start.9 = (f32[136,256]{1,0:T(8,128)S(1)}, f32[136,256]{1,0:T(8,128)S(1)}, u32[]{:S(2)}, u32[]{:S(2)}) collective-permute-start(f32[136,256]{1,0:T(8,128)S(1)} %pad_maximum_fusion.in0), channel_id=1, source_target_pairs={{0,48},{16,32},{32,16},{48,0},{64,112},{80,96},{96,80},{112,64},{1... | collective-permute-start | bytes 417800 | tf_op jit(solution)/shard_map/ppermute | solution.py:300
  32.1 0.3 collective-permute-start.8
  32.5 2.2 %collective-permute-start.7 = (f32[136,256]{1,0:T(8,128)S(1)}, f32[136,256]{1,0:T(8,128)S(1)}, u32[]{:S(2)}, u32[]{:S(2)}) collective-permute-start(f32[136,256]{1,0:T(8,128)S(1)} %pad_maximum_fusion.in0), channel_id=1, source_target_pairs={{0,16},{16,0},{32,48},{48,32},{64,80},{80,64},{96,112},{112,96},{1... | collective-permute-start | bytes 417800 | tf_op jit(solution)/shard_map/ppermute | solution.py:300
  34.7 0.0 copy-done
  34.7 2.6 %collective-permute-done.9.in3 = f32[136,256]{1,0:T(8,128)S(1)} collective-permute-done((f32[136,256]{1,0:T(8,128)S(1)}, f32[136,256]{1,0:T(8,128)S(1)}, u32[]{:S(2)}, u32[]{:S(2)}) %collective-permute-start.9) | collective-permute-done | bytes 139296 | tf_op jit(solution)/shard_map/ppermute | solution.py:300
  37.2 0.0 collective-permute-done.8.in2
  37.2 1.9 %collective-permute-done.7.in1 = f32[136,256]{1,0:T(8,128)S(1)} collective-permute-done((f32[136,256]{1,0:T(8,128)S(1)}, f32[136,256]{1,0:T(8,128)S(1)}, u32[]{:S(2)}, u32[]{:S(2)}) %collective-permute-start.7) | collective-permute-done | bytes 139296 | tf_op jit(solution)/shard_map/ppermute | solution.py:300
  39.1 4.8 %shard_map.29 = (f32[16,256]{1,0:T(8,128)S(1)}, f32[256,256]{1,0:T(8,128)S(1)}, f32[256,256]{1,0:T(8,128)S(1)}, f32[256,256]{1,0:T(8,128)S(1)}) custom-call(s32[1]{0:T(128)} %bitcast.1.place_ref, s32[8]{0:T(128)S(1)} %get-tuple-element.51.shift_ref, f32[136,256]{1,0:T(8,128)S(1)} %pad_maximum_fusion.in0, f32[136,256]{1,0:T(8,128)S(1)} %collective-permute-done.7.in1, ...), custom_call_target="tpu_custom_call" | custom-call | tf_op jit(solution)/shard_map/pallas_call | solution.py:344
  43.9 2.6 %collective-permute-start.10 = (f32[16,256]{1,0:T(8,128)S(1)}, f32[16,256]{1,0:T(8,128)S(1)}, u32[]{:S(2)}, u32[]{:S(2)}) collective-permute-start(f32[16,256]{1,0:T(8,128)S(1)} %get-tuple-element.33.angles_ref), channel_id=1, source_target_pairs={{14,0},{15,1},{0,2},{1,3},{2,4},{3,5},{4,6},{5,7},{6,8},{7,9},{8,1... | collective-permute-start | bytes 49160 | tf_op jit(solution)/shard_map/ppermute | solution.py:296
  46.4 2.2 %shard_map.30 = (f32[256,256]{1,0:T(8,128)S(1)}, f32[256,256]{1,0:T(8,128)S(1)}) custom-call(s32[8]{0:T(128)S(1)} %get-tuple-element.51.shift_ref, f32[16,256]{1,0:T(8,128)S(1)} %get-tuple-element.33.angles_ref, f32[256,512]{1,0:T(8,128)} %pair_ref.3), custom_call_target="tpu_custom_call" | custom-call | tf_op jit(solution)/shard_map/pallas_call | solution.py:348
  48.7 2.8 %collective-permute-done.10.angles_ref = f32[16,256]{1,0:T(8,128)S(1)} collective-permute-done((f32[16,256]{1,0:T(8,128)S(1)}, f32[16,256]{1,0:T(8,128)S(1)}, u32[]{:S(2)}, u32[]{:S(2)}) %collective-permute-start.10) | collective-permute-done | bytes 16416 | tf_op jit(solution)/shard_map/ppermute | solution.py:296
  51.5 0.0 collective-permute-done.11.other_ref
  51.5 1.6 %shard_map.31 = (f32[256,256]{1,0:T(8,128)S(1)}, f32[64,256]{1,0:T(8,128)S(1)}, f32[64,256]{1,0:T(8,128)S(1)}, f32[64,256]{1,0:T(8,128)S(1)}, f32[64,256]{1,0:T(8,128)S(1)}) custom-call(s32[1]{0:T(128)} %bitcast.1.place_ref, s32[8]{0:T(128)S(1)} %get-tuple-element.51.shift_ref, f32[16,256]{1,0:T(8,128)S(1)} %collective-permute-done.10.angles_ref, ...), custom_call_target="tpu_custom_call" | custom-call | tf_op jit(solution)/shard_map/pallas_call | solution.py:354
  53.1 1.1 %collective-permute-start.13 = (f32[64,256]{1,0:T(8,128)S(1)}, f32[64,256]{1,0:T(8,128)S(1)}, u32[]{:S(2)}, u32[]{:S(2)}) collective-permute-start(f32[64,256]{1,0:T(8,128)S(1)} %get-tuple-element.38), channel_id=1, source_target_pairs={{0,32},{16,48},{32,0},{48,16},{64,96},{80,112},{96,64},{112,80},{1... | collective-permute-start | bytes 196616 | tf_op jit(solution)/shard_map/ppermute | solution.py:300
  54.2 0.1 collective-permute-start.12
  54.3 2.4 %collective-permute-start.14 = (f32[64,256]{1,0:T(8,128)S(1)}, f32[64,256]{1,0:T(8,128)S(1)}, u32[]{:S(2)}, u32[]{:S(2)}) collective-permute-start(f32[64,256]{1,0:T(8,128)S(1)} %get-tuple-element.44), channel_id=1, source_target_pairs={{0,48},{16,32},{32,16},{48,0},{64,112},{80,96},{96,80},{112,64},{1... | collective-permute-start | bytes 196616 | tf_op jit(solution)/shard_map/ppermute | solution.py:300
  56.7 1.2 %shard_map.32 = (f32[192,256]{1,0:T(8,128)S(1)}, f32[256,256]{1,0:T(8,128)S(1)}) custom-call(s32[8]{0:T(128)S(1)} %get-tuple-element.51.shift_ref, f32[16,256]{1,0:T(8,128)S(1)} %get-tuple-element.33.angles_ref, f32[256,256]{1,0:T(8,128)S(1)} %get-tuple-element.39.tl, f32[256,256]{1,0:T(8,128)S(1)} %get-tuple-element.40.tr, f32[256,256]{1,0:T(8,128)S(1)} %get-tuple-element.41.lr), custom_call_target="tpu_custom_call" | custom-call | tf_op jit(solution)/shard_map/pallas_call | solution.py:351
  57.9 0.0 collective-permute-done.13
  57.9 0.3 collective-permute-start.21
  58.2 1.0 %collective-permute-done.12 = f32[64,256]{1,0:T(8,128)S(1)} collective-permute-done((f32[64,256]{1,0:T(8,128)S(1)}, f32[64,256]{1,0:T(8,128)S(1)}, u32[]{:S(2)}, u32[]{:S(2)}) %collective-permute-start.12) | collective-permute-done | bytes 65568 | tf_op jit(solution)/shard_map/ppermute | solution.py:300
  59.2 1.1 %collective-permute-done.14 = f32[64,256]{1,0:T(8,128)S(1)} collective-permute-done((f32[64,256]{1,0:T(8,128)S(1)}, f32[64,256]{1,0:T(8,128)S(1)}, u32[]{:S(2)}, u32[]{:S(2)}) %collective-permute-start.14) | collective-permute-done | bytes 65568 | tf_op jit(solution)/shard_map/ppermute | solution.py:300
  60.3 2.7 %collective-permute-start.17 = (f32[64,256]{1,0:T(8,128)S(1)}, f32[64,256]{1,0:T(8,128)S(1)}, u32[]{:S(2)}, u32[]{:S(2)}) collective-permute-start(f32[64,256]{1,0:T(8,128)S(1)} %add_add_fusion.2), channel_id=1, source_target_pairs={{0,128},{16,144},{32,160},{48,176},{64,192},{80,208},{96,224},{112... | collective-permute-start | bytes 196616 | tf_op jit(solution)/shard_map/ppermute | solution.py:300
  63.0 2.2 %collective-permute-start.16 = (f32[64,256]{1,0:T(8,128)S(1)}, f32[64,256]{1,0:T(8,128)S(1)}, u32[]{:S(2)}, u32[]{:S(2)}) collective-permute-start(f32[64,256]{1,0:T(8,128)S(1)} %add_add_fusion.2), channel_id=1, source_target_pairs={{0,192},{16,208},{32,224},{48,240},{64,128},{80,144},{96,160},{112... | collective-permute-start | bytes 196616 | tf_op jit(solution)/shard_map/ppermute | solution.py:300
  65.1 1.8 %collective-permute-start.15 = (f32[64,256]{1,0:T(8,128)S(1)}, f32[64,256]{1,0:T(8,128)S(1)}, u32[]{:S(2)}, u32[]{:S(2)}) collective-permute-start(f32[64,256]{1,0:T(8,128)S(1)} %add_add_fusion.2), channel_id=1, source_target_pairs={{0,64},{16,80},{32,96},{48,112},{64,0},{80,16},{96,32},{112,48},{1... | collective-permute-start | bytes 196616 | tf_op jit(solution)/shard_map/ppermute | solution.py:300
  66.9 0.5 collective-permute-done.21.tl_ref
  67.4 2.9 %collective-permute-start.23 = (f32[256,256]{1,0:T(8,128)S(1)}, f32[256,256]{1,0:T(8,128)S(1)}, u32[]{:S(2)}, u32[]{:S(2)}) collective-permute-start(f32[256,256]{1,0:T(8,128)S(1)} %get-tuple-element.49.lower_ref.lower_in), channel_id=1, source_target_pairs={{2,0},{3,1},{4,2},{5,3},{6,4},{7,5},{8,6},{9,7},{10,8},{11,9},{12,... | collective-permute-start | bytes 786440 | tf_op jit(solution)/shard_map/ppermute | solution.py:296
  70.2 0.0 collective-permute-done.17
  70.2 0.0 collective-permute-done.16
  70.2 0.2 collective-permute-done.15
  70.4 2.7 %collective-permute-start.20 = (f32[64,256]{1,0:T(8,128)S(1)}, f32[64,256]{1,0:T(8,128)S(1)}, u32[]{:S(2)}, u32[]{:S(2)}) collective-permute-start(f32[64,256]{1,0:T(8,128)S(1)} %add_add_fusion.1.in0), channel_id=1, source_target_pairs={{0,48},{16,32},{32,16},{48,0},{64,112},{80,96},{96,80},{112,64},{1... | collective-permute-start | bytes 196616 | tf_op jit(solution)/shard_map/ppermute | solution.py:300
  73.2 0.3 collective-permute-start.19
  73.5 1.1 %collective-permute-start.18 = (f32[64,256]{1,0:T(8,128)S(1)}, f32[64,256]{1,0:T(8,128)S(1)}, u32[]{:S(2)}, u32[]{:S(2)}) collective-permute-start(f32[64,256]{1,0:T(8,128)S(1)} %add_add_fusion.1.in0), channel_id=1, source_target_pairs={{0,16},{16,0},{32,48},{48,32},{64,80},{80,64},{96,112},{112,96},{1... | collective-permute-start | bytes 196616 | tf_op jit(solution)/shard_map/ppermute | solution.py:300
  74.6 1.1 %collective-permute-done.20.in3 = f32[64,256]{1,0:T(8,128)S(1)} collective-permute-done((f32[64,256]{1,0:T(8,128)S(1)}, f32[64,256]{1,0:T(8,128)S(1)}, u32[]{:S(2)}, u32[]{:S(2)}) %collective-permute-start.20) | collective-permute-done | bytes 65568 | tf_op jit(solution)/shard_map/ppermute | solution.py:300
  75.7 1.7 %collective-permute-done.19.in2 = f32[64,256]{1,0:T(8,128)S(1)} collective-permute-done((f32[64,256]{1,0:T(8,128)S(1)}, f32[64,256]{1,0:T(8,128)S(1)}, u32[]{:S(2)}, u32[]{:S(2)}) %collective-permute-start.19) | collective-permute-done | bytes 65568 | tf_op jit(solution)/shard_map/ppermute | solution.py:300
  77.4 0.3 collective-permute-done.18.in1
  77.8 4.2 %shard_map.33.angles_ref = f32[16,256]{1,0:T(8,128)S(1)} custom-call(s32[1]{0:T(128)} %bitcast.1.place_ref, s32[8]{0:T(128)S(1)} %get-tuple-element.52.shift_ref, f32[64,256]{1,0:T(8,128)S(1)} %add_add_fusion.1.in0, f32[64,256]{1,0:T(8,128)S(1)} %collective-permute-done.18.in1, f32[64,256]{1,0:T(8,128)S(1)} %collective-permute-done.19.in2, ...), custom_call_target="tpu_custom_call" | custom-call | tf_op jit(solution)/shard_map/pallas_call | solution.py:367
  82.0 3.7 %collective-permute-start.22 = (f32[16,256]{1,0:T(8,128)S(1)}, f32[16,256]{1,0:T(8,128)S(1)}, u32[]{:S(2)}, u32[]{:S(2)}) collective-permute-start(f32[16,256]{1,0:T(8,128)S(1)} %shard_map.33.angles_ref), channel_id=1, source_target_pairs={{2,0},{3,1},{4,2},{5,3},{6,4},{7,5},{8,6},{9,7},{10,8},{11,9},{12,... | collective-permute-start | bytes 49160 | tf_op jit(solution)/shard_map/ppermute | solution.py:296
  85.6 2.3 %shard_map.34.half_ref = f32[256,512]{1,0:T(8,128)} custom-call(s32[8]{0:T(128)S(1)} %get-tuple-element.52.shift_ref, f32[16,256]{1,0:T(8,128)S(1)} %shard_map.33.angles_ref, f32[256,256]{1,0:T(8,128)S(1)} %get-tuple-element.50.upper_in, f32[256,256]{1,0:T(8,128)S(1)} %get-tuple-element.49.lower_ref.lower_in), custom_call_target="tpu_custom_call" | custom-call | tf_op jit(solution)/shard_map/pallas_call | solution.py:371
  87.9 0.0 collective-permute-done.22.angles_ref
  87.9 0.0 collective-permute-done.23.lower_in
  87.9 2.2 %shard_map.35 = f32[256,512]{1,0:T(8,128)} custom-call(s32[8]{0:T(128)S(1)} %get-tuple-element.52.shift_ref, f32[16,256]{1,0:T(8,128)S(1)} %collective-permute-done.22.angles_ref, f32[256,256]{1,0:T(8,128)S(1)} %get-tuple-element.48.upper_in, f32[256,256]{1,0:T(8,128)S(1)} %collective-permute-done.23.lower_in, ...), custom_call_target="tpu_custom_call", output_to_operand_aliasing={{}: (4, {})} | custom-call | tf_op jit(solution)/shard_map/pallas_call | solution.py:374
  (11 shorter events, 0.1 us)
Async XLA Ops:
  1.9 6.1 %collective-permute-start.1 = (f32[136,256]{1,0:T(8,128)S(1)}, f32[136,256]{1,0:T(8,128)S(1)}, u32[]{:S(2)}, u32[]{:S(2)}) collective-permute-start(f32[136,256]{1,0:T(8,128)S(1)} %get-tuple-element.30), channel_id=1, source_target_pairs={{0,32},{16,48},{32,0},{48,16},{64,96},{80,112},{96,64},{112,80},{1... | collective-permute-start | bytes 417800 | tf_op jit(solution)/shard_map/ppermute | solution.py:300
  3.9 8.1 %collective-permute-start = (f32[136,256]{1,0:T(8,128)S(1)}, f32[136,256]{1,0:T(8,128)S(1)}, u32[]{:S(2)}, u32[]{:S(2)}) collective-permute-start(f32[136,256]{1,0:T(8,128)S(1)} %get-tuple-element.29), channel_id=1, source_target_pairs={{0,16},{16,0},{32,48},{48,32},{64,80},{80,64},{96,112},{112,96},{1... | collective-permute-start | bytes 417800 | tf_op jit(solution)/shard_map/ppermute | solution.py:300
  4.4 7.7 %collective-permute-start.2 = (f32[136,256]{1,0:T(8,128)S(1)}, f32[136,256]{1,0:T(8,128)S(1)}, u32[]{:S(2)}, u32[]{:S(2)}) collective-permute-start(f32[136,256]{1,0:T(8,128)S(1)} %get-tuple-element.32), channel_id=1, source_target_pairs={{0,48},{16,32},{32,16},{48,0},{64,112},{80,96},{96,80},{112,64},{1... | collective-permute-start | bytes 417800 | tf_op jit(solution)/shard_map/ppermute | solution.py:300
  12.1 9.3 %collective-permute-start.5 = (f32[72,256]{1,0:T(8,128)S(1)}, f32[72,256]{1,0:T(8,128)S(1)}, u32[]{:S(2)}, u32[]{:S(2)}) collective-permute-start(f32[72,256]{1,0:T(8,128)S(1)} %slice.22), channel_id=1, source_target_pairs={{0,192},{16,208},{32,224},{48,240},{64,128},{80,144},{96,160},{112... | collective-permute-start | bytes 221192 | tf_op jit(solution)/shard_map/ppermute | solution.py:300
  17.6 6.9 %collective-permute-start.3 = (f32[64,256]{1,0:T(8,128)S(1)}, f32[64,256]{1,0:T(8,128)S(1)}, u32[]{:S(2)}, u32[]{:S(2)}) collective-permute-start(f32[64,256]{1,0:T(8,128)S(1)} %slice.21), channel_id=1, source_target_pairs={{0,64},{16,80},{32,96},{48,112},{64,0},{80,16},{96,32},{112,48},{1... | collective-permute-start | bytes 196616 | tf_op jit(solution)/shard_map/ppermute | solution.py:300
  19.0 32.4 %collective-permute-start.11 = (f32[256,512]{1,0:T(8,128)}, f32[256,512]{1,0:T(8,128)S(1)}, u32[]{:S(2)}, u32[]{:S(2)}) collective-permute-start(f32[256,512]{1,0:T(8,128)} %pair_ref.3), channel_id=1, source_target_pairs={{14,0},{15,1},{0,2},{1,3},{2,4},{3,5},{4,6},{5,7},{6,8},{7,9},{8,1... | collective-permute-start | bytes 1572872 | tf_op jit(solution)/shard_map/ppermute | solution.py:296
  21.4 9.7 %collective-permute-start.6 = (f32[72,256]{1,0:T(8,128)S(1)}, f32[72,256]{1,0:T(8,128)S(1)}, u32[]{:S(2)}, u32[]{:S(2)}) collective-permute-start(f32[72,256]{1,0:T(8,128)S(1)} %slice_add_fusion.1), channel_id=1, source_target_pairs={{0,64},{16,80},{32,96},{48,112},{64,0},{80,16},{96,32},{112,48},{1... | collective-permute-start | bytes 221192 | tf_op jit(solution)/shard_map/ppermute | solution.py:300
  24.5 6.5 %collective-permute-start.4 = (f32[64,256]{1,0:T(8,128)S(1)}, f32[64,256]{1,0:T(8,128)S(1)}, u32[]{:S(2)}, u32[]{:S(2)}) collective-permute-start(f32[64,256]{1,0:T(8,128)S(1)} %slice_add_fusion), channel_id=1, source_target_pairs={{0,192},{16,208},{32,224},{48,240},{64,128},{80,144},{96,160},{112... | collective-permute-start | bytes 196616 | tf_op jit(solution)/shard_map/ppermute | solution.py:300
  31.0 3.6 %copy-start = (s32[2,8]{1,0:T(2,128)S(1)}, s32[2,8]{1,0:T(2,128)}, u32[]{:S(2)}) copy-start(s32[2,8]{1,0:T(2,128)} %param.3) | copy-start | bytes 196
  31.1 6.1 %collective-permute-start.9 = (f32[136,256]{1,0:T(8,128)S(1)}, f32[136,256]{1,0:T(8,128)S(1)}, u32[]{:S(2)}, u32[]{:S(2)}) collective-permute-start(f32[136,256]{1,0:T(8,128)S(1)} %pad_maximum_fusion.in0), channel_id=1, source_target_pairs={{0,48},{16,32},{32,16},{48,0},{64,112},{80,96},{96,80},{112,64},{1... | collective-permute-start | bytes 417800 | tf_op jit(solution)/shard_map/ppermute | solution.py:300
  32.1 5.1 %collective-permute-start.8 = (f32[136,256]{1,0:T(8,128)S(1)}, f32[136,256]{1,0:T(8,128)S(1)}, u32[]{:S(2)}, u32[]{:S(2)}) collective-permute-start(f32[136,256]{1,0:T(8,128)S(1)} %pad_maximum_fusion.in0), channel_id=1, source_target_pairs={{0,32},{16,48},{32,0},{48,16},{64,96},{80,112},{96,64},{112,80},{1... | collective-permute-start | bytes 417800 | tf_op jit(solution)/shard_map/ppermute | solution.py:300
  32.5 6.6 %collective-permute-start.7 = (f32[136,256]{1,0:T(8,128)S(1)}, f32[136,256]{1,0:T(8,128)S(1)}, u32[]{:S(2)}, u32[]{:S(2)}) collective-permute-start(f32[136,256]{1,0:T(8,128)S(1)} %pad_maximum_fusion.in0), channel_id=1, source_target_pairs={{0,16},{16,0},{32,48},{48,32},{64,80},{80,64},{96,112},{112,96},{1... | collective-permute-start | bytes 417800 | tf_op jit(solution)/shard_map/ppermute | solution.py:300
  43.9 7.6 %collective-permute-start.10 = (f32[16,256]{1,0:T(8,128)S(1)}, f32[16,256]{1,0:T(8,128)S(1)}, u32[]{:S(2)}, u32[]{:S(2)}) collective-permute-start(f32[16,256]{1,0:T(8,128)S(1)} %get-tuple-element.33.angles_ref), channel_id=1, source_target_pairs={{14,0},{15,1},{0,2},{1,3},{2,4},{3,5},{4,6},{5,7},{6,8},{7,9},{8,1... | collective-permute-start | bytes 49160 | tf_op jit(solution)/shard_map/ppermute | solution.py:296
  53.1 4.8 %collective-permute-start.13 = (f32[64,256]{1,0:T(8,128)S(1)}, f32[64,256]{1,0:T(8,128)S(1)}, u32[]{:S(2)}, u32[]{:S(2)}) collective-permute-start(f32[64,256]{1,0:T(8,128)S(1)} %get-tuple-element.38), channel_id=1, source_target_pairs={{0,32},{16,48},{32,0},{48,16},{64,96},{80,112},{96,64},{112,80},{1... | collective-permute-start | bytes 196616 | tf_op jit(solution)/shard_map/ppermute | solution.py:300
  54.2 5.0 %collective-permute-start.12 = (f32[64,256]{1,0:T(8,128)S(1)}, f32[64,256]{1,0:T(8,128)S(1)}, u32[]{:S(2)}, u32[]{:S(2)}) collective-permute-start(f32[64,256]{1,0:T(8,128)S(1)} %get-tuple-element.37), channel_id=1, source_target_pairs={{0,16},{16,0},{32,48},{48,32},{64,80},{80,64},{96,112},{112,96},{1... | collective-permute-start | bytes 196616 | tf_op jit(solution)/shard_map/ppermute | solution.py:300
  54.3 6.0 %collective-permute-start.14 = (f32[64,256]{1,0:T(8,128)S(1)}, f32[64,256]{1,0:T(8,128)S(1)}, u32[]{:S(2)}, u32[]{:S(2)}) collective-permute-start(f32[64,256]{1,0:T(8,128)S(1)} %get-tuple-element.44), channel_id=1, source_target_pairs={{0,48},{16,32},{32,16},{48,0},{64,112},{80,96},{96,80},{112,64},{1... | collective-permute-start | bytes 196616 | tf_op jit(solution)/shard_map/ppermute | solution.py:300
  57.9 9.5 %collective-permute-start.21 = (f32[192,256]{1,0:T(8,128)S(1)}, f32[192,256]{1,0:T(8,128)S(1)}, u32[]{:S(2)}, u32[]{:S(2)}) collective-permute-start(f32[192,256]{1,0:T(8,128)S(1)} %get-tuple-element.45), channel_id=1, source_target_pairs={{14,0},{15,1},{0,2},{1,3},{2,4},{3,5},{4,6},{5,7},{6,8},{7,9},{8,1... | collective-permute-start | bytes 589832 | tf_op jit(solution)/shard_map/ppermute | solution.py:296
  60.3 9.9 %collective-permute-start.17 = (f32[64,256]{1,0:T(8,128)S(1)}, f32[64,256]{1,0:T(8,128)S(1)}, u32[]{:S(2)}, u32[]{:S(2)}) collective-permute-start(f32[64,256]{1,0:T(8,128)S(1)} %add_add_fusion.2), channel_id=1, source_target_pairs={{0,128},{16,144},{32,160},{48,176},{64,192},{80,208},{96,224},{112... | collective-permute-start | bytes 196616 | tf_op jit(solution)/shard_map/ppermute | solution.py:300
  63.0 7.3 %collective-permute-start.16 = (f32[64,256]{1,0:T(8,128)S(1)}, f32[64,256]{1,0:T(8,128)S(1)}, u32[]{:S(2)}, u32[]{:S(2)}) collective-permute-start(f32[64,256]{1,0:T(8,128)S(1)} %add_add_fusion.2), channel_id=1, source_target_pairs={{0,192},{16,208},{32,224},{48,240},{64,128},{80,144},{96,160},{112... | collective-permute-start | bytes 196616 | tf_op jit(solution)/shard_map/ppermute | solution.py:300
  65.1 5.3 %collective-permute-start.15 = (f32[64,256]{1,0:T(8,128)S(1)}, f32[64,256]{1,0:T(8,128)S(1)}, u32[]{:S(2)}, u32[]{:S(2)}) collective-permute-start(f32[64,256]{1,0:T(8,128)S(1)} %add_add_fusion.2), channel_id=1, source_target_pairs={{0,64},{16,80},{32,96},{48,112},{64,0},{80,16},{96,32},{112,48},{1... | collective-permute-start | bytes 196616 | tf_op jit(solution)/shard_map/ppermute | solution.py:300
  67.4 20.5 %collective-permute-start.23 = (f32[256,256]{1,0:T(8,128)S(1)}, f32[256,256]{1,0:T(8,128)S(1)}, u32[]{:S(2)}, u32[]{:S(2)}) collective-permute-start(f32[256,256]{1,0:T(8,128)S(1)} %get-tuple-element.49.lower_ref.lower_in), channel_id=1, source_target_pairs={{2,0},{3,1},{4,2},{5,3},{6,4},{7,5},{8,6},{9,7},{10,8},{11,9},{12,... | collective-permute-start | bytes 786440 | tf_op jit(solution)/shard_map/ppermute | solution.py:296
  70.4 5.3 %collective-permute-start.20 = (f32[64,256]{1,0:T(8,128)S(1)}, f32[64,256]{1,0:T(8,128)S(1)}, u32[]{:S(2)}, u32[]{:S(2)}) collective-permute-start(f32[64,256]{1,0:T(8,128)S(1)} %add_add_fusion.1.in0), channel_id=1, source_target_pairs={{0,48},{16,32},{32,16},{48,0},{64,112},{80,96},{96,80},{112,64},{1... | collective-permute-start | bytes 196616 | tf_op jit(solution)/shard_map/ppermute | solution.py:300
  73.2 4.3 %collective-permute-start.19 = (f32[64,256]{1,0:T(8,128)S(1)}, f32[64,256]{1,0:T(8,128)S(1)}, u32[]{:S(2)}, u32[]{:S(2)}) collective-permute-start(f32[64,256]{1,0:T(8,128)S(1)} %add_add_fusion.1.in0), channel_id=1, source_target_pairs={{0,32},{16,48},{32,0},{48,16},{64,96},{80,112},{96,64},{112,80},{1... | collective-permute-start | bytes 196616 | tf_op jit(solution)/shard_map/ppermute | solution.py:300
  73.5 4.3 %collective-permute-start.18 = (f32[64,256]{1,0:T(8,128)S(1)}, f32[64,256]{1,0:T(8,128)S(1)}, u32[]{:S(2)}, u32[]{:S(2)}) collective-permute-start(f32[64,256]{1,0:T(8,128)S(1)} %add_add_fusion.1.in0), channel_id=1, source_target_pairs={{0,16},{16,0},{32,48},{48,32},{64,80},{80,64},{96,112},{112,96},{1... | collective-permute-start | bytes 196616 | tf_op jit(solution)/shard_map/ppermute | solution.py:300
  82.0 5.9 %collective-permute-start.22 = (f32[16,256]{1,0:T(8,128)S(1)}, f32[16,256]{1,0:T(8,128)S(1)}, u32[]{:S(2)}, u32[]{:S(2)}) collective-permute-start(f32[16,256]{1,0:T(8,128)S(1)} %shard_map.33.angles_ref), channel_id=1, source_target_pairs={{2,0},{3,1},{4,2},{5,3},{6,4},{7,5},{8,6},{9,7},{10,8},{11,9},{12,... | collective-permute-start | bytes 49160 | tf_op jit(solution)/shard_map/ppermute | solution.py:296
